TPU v7x, 256 devices: a whole 4x4x8 slice. The times are simulated.
256 devices in a mesh: lon: 32 (over y_lo, z, core), lat: 8 (over x, y_hi).
Axes of the slice: x: 4, y: 4 (y_hi: 2, y_lo: 2; y = y_hi * 2 + y_lo), z: 8, core: 2. Of those that a mesh axis runs over, the one named last changes fastest.
Arguments:
- features: bfloat16 [2, 16, 4096, 256], P(None, 'lat', 'lon'), may hold values from -6 to 6
- out_grad: bfloat16 [2, 16, 4096, 256], P(None, 'lat', 'lon'), may hold values from -8 to 8
- first_kernel: bfloat16 [3, 3, 256, 256], replicated, may hold values from -0.125 to 0.125
- second_kernel: bfloat16 [3, 3, 256, 256], replicated, may hold values from -0.125 to 0.125
- strides: int32 [2, 16, 3], replicated, may hold values from 1 to 16, as said below
Outputs:
- input_grad: bfloat16 [2, 16, 4096, 256], P(None, 'lat', 'lon')
- first_grad: float32 [3, 3, 256, 256], replicated
- second_grad: float32 [3, 3, 256, 256], replicated
Inputs may be any that keep to these rules, and one draw needn't show every extreme that they name: strides[s, p, k] is 16 where the source row of p and k is the polar row; with d the source row's distance from the pole it is otherwise within one of (16 + d) // (2 d + 1) and below 16.
All inputs are finite; a program needn't handle non-finite values.
Results may differ from a plain program's by a relative error of at most 0.0033.
Values may be sent and summed in bfloat16 or wider, within the bound.
No kernel may reach another device: no remote copies, remote signals or barrier semaphores. Data moves between devices by JAX's collectives and lax.ppermute only.
A program may use at most 64 MiB of HBM per device.

v0:
```python
import math

import jax
import jax.numpy as jnp
from jax import lax
from jax.sharding import PartitionSpec as P

POLE = 16
SPAN = 16


def with_halo(cells, sides, width, closed):
    for axis, dim in sides:
        count = lax.axis_size(axis)
        ends = count if closed else count - 1
        head = lax.slice_in_dim(cells, 0, width, axis=dim)
        tail = lax.slice_in_dim(cells, cells.shape[dim] - width, cells.shape[dim], axis=dim)
        cells = jnp.concatenate(
            [
                lax.ppermute(tail, axis, [(i, (i + 1) % count) for i in range(ends)]),
                cells,
                lax.ppermute(head, axis, [((i + 1) % count, i) for i in range(ends)]),
            ],
            axis=dim,
        )
    return cells


def shifted(value, axis, by):
    size = lax.axis_size(axis)
    return lax.ppermute(value, axis, [(i, (i + by) % size) for i in range(size)])


def shifted_rows(band_rows, starts, col_width):

    def one_row(row_data, offset):
        return lax.dynamic_slice_in_dim(row_data, offset, col_width, 0)

    return jax.vmap(one_row)(band_rows, starts)


def extend(field_in, lat_pos, lon_count, span_cols):
    row_count = field_in.shape[2]
    padded = with_halo(field_in, (("lat", 2),), 1, False)
    crossed = shifted(field_in[:, :, 0], "lon", lon_count // 2)
    top_row = jnp.where(lat_pos == 0, crossed, padded[:, :, 0])
    bottom_row = padded[:, :, row_count + 1]
    extended = jnp.concatenate([top_row[:, :, None], field_in, bottom_row[:, :, None]], axis=2)
    extended = with_halo(extended, (("lon", 3),), span_cols, True)
    return extended


def forward_taps(context, row_strides, span_cols):
    row_count = context.shape[0] - 2
    col_width = context.shape[1] - 2 * span_cols
    tap_list = []
    for kernel_row in range(3):
        band_rows = context[kernel_row : kernel_row + row_count]
        for kernel_col in range(3):
            starts = span_cols + (kernel_col - 1) * row_strides[:, kernel_row]
            tap_list.append(shifted_rows(band_rows, starts, col_width))
    return jnp.concatenate(tap_list, axis=-1).reshape(row_count * col_width, -1)


def adjoint(context, kernel, above_strides, centre_strides, below_strides, top_mirror, span_cols):
    row_count = context.shape[0] - 2
    col_width = context.shape[1] - 2 * span_cols
    chan_count = context.shape[2]
    flipped = jnp.transpose(kernel, (0, 1, 3, 2)).reshape(3, 3 * chan_count, chan_count)
    slot_strides = (above_strides, centre_strides, below_strides)
    slot_taps = []
    for slot_index in range(3):
        band_rows = context[slot_index : slot_index + row_count]
        tap_list = [
            shifted_rows(
                band_rows, span_cols - (kernel_col - 1) * slot_strides[slot_index], col_width
            )
            for kernel_col in range(3)
        ]
        slot_taps.append(jnp.concatenate(tap_list, axis=-1))

    def project(tap_block, kernel_row):
        result = jnp.dot(
            tap_block.reshape(-1, 3 * chan_count),
            flipped[kernel_row],
            preferred_element_type=jnp.float32,
        )
        return result.reshape(row_count, col_width, chan_count)

    upper_part = project(slot_taps[0], 2)
    centre_part = project(slot_taps[1], 1)
    lower_part = project(slot_taps[2], 0)
    upper_edge = jnp.dot(slot_taps[0][0], flipped[0], preferred_element_type=jnp.float32)
    upper_part = upper_part.at[0].set(jnp.where(top_mirror, upper_edge, upper_part[0]))
    return upper_part + centre_part + lower_part


def local(features, out_grad, first_kernel, second_kernel, strides):
    slab_count, row_count, col_width, chan_count = features.shape
    lat_count = lax.axis_size("lat")
    lon_count = lax.axis_size("lon")
    lat_pos = lax.axis_index("lat")
    first_row = lat_pos * row_count
    global_rows = first_row + jnp.arange(row_count, dtype=jnp.int32)
    span_cols = SPAN
    row_strides = lax.dynamic_slice_in_dim(strides, first_row, row_count, 1)
    above_rows = jnp.maximum(global_rows - 1, 0)
    below_rows = jnp.minimum(global_rows + 1, POLE - 1)
    above_strides = jnp.where(
        global_rows[None, :] == 0, strides[:, 0:1, 0], strides[:, above_rows, 2]
    )
    below_strides = strides[:, below_rows, 0]
    centre_strides = row_strides[:, :, 1]
    top_mirror = lat_pos == 0
    contract_rows = (((0,), (0,)), ((), ()))

    def taps_of(context):
        return jax.vmap(
            lambda part_ctx, part_strides: forward_taps(part_ctx, part_strides, span_cols)
        )(context, row_strides).reshape(-1, 9 * chan_count)

    def adjoint_of(context, kernel):
        return jax.vmap(
            lambda part_ctx, above_part, centre_part, below_part: adjoint(
                part_ctx, kernel, above_part, centre_part, below_part, top_mirror, span_cols
            )
        )(context, above_strides, centre_strides, below_strides)

    first_context = extend(jnp.stack([features, out_grad]), lat_pos, lon_count, span_cols)
    feature_taps = taps_of(first_context[0])
    flat_kernel = first_kernel.reshape(9 * chan_count, chan_count)
    pre_act = jnp.dot(feature_taps, flat_kernel, preferred_element_type=jnp.float32)
    pre_act = pre_act.reshape(slab_count, row_count, col_width, chan_count)
    activated = jax.nn.gelu(pre_act).astype(jnp.bfloat16)
    act_grad = adjoint_of(first_context[1], second_kernel)
    _, pullback = jax.vjp(jax.nn.gelu, pre_act)
    pre_grad = pullback(act_grad)[0].astype(jnp.bfloat16)
    second_context = extend(jnp.stack([activated, pre_grad]), lat_pos, lon_count, span_cols)
    act_taps = taps_of(second_context[0])
    second_local = lax.dot_general(
        act_taps,
        out_grad.reshape(-1, chan_count),
        contract_rows,
        preferred_element_type=jnp.float32,
    )
    back_term = adjoint_of(second_context[1], first_kernel)
    input_grad = (out_grad.astype(jnp.float32) + back_term).astype(jnp.bfloat16)
    first_local = lax.dot_general(
        feature_taps,
        pre_grad.reshape(-1, chan_count),
        contract_rows,
        preferred_element_type=jnp.float32,
    )
    first_sum, second_sum = lax.psum((first_local, second_local), ("lon", "lat"))
    cells_total = slab_count * row_count * lat_count * col_width * lon_count
    grad_scale = 1.0 / math.sqrt(cells_total)
    first_grad = (first_sum * grad_scale).reshape(3, 3, chan_count, chan_count)
    second_grad = (second_sum * grad_scale).reshape(3, 3, chan_count, chan_count)
    return (input_grad, first_grad, second_grad)


def solution(mesh):
    return jax.shard_map(
        local,
        mesh=mesh,
        in_specs=(P(None, "lat", "lon", None), P(None, "lat", "lon", None), P(), P(), P()),
        out_specs=(P(None, "lat", "lon", None), P(), P()),
        check_vma=False,
    )
```

profile of v0, /device:TPU:1, one launch (start us, length us, event | category | flops | bytes accessed | tf_op | source)
XLA Modules:
  0.0 437.8 jit_solution(18306430620331662633)
XLA Ops:
  10.4 2.2 collective-permute-start
  12.6 6.8 %collective-permute-start.1 = (bf16[2,2,1,128,256]{4,3,1,0,2:T(8,128)(2,1)}, bf16[2,2,1,128,256]{4,3,1,0,2:T(8,128)(2,1)}, u32[]{:S(2)}, u32[]{:S(2)}) collective-permute-start(bf16[2,2,1,128,256]{4,3,1,0,2:T(8,128)(2,1)} %get-tuple-element.59), channel_id=1, source_target_pairs={{0,1},{1,2},{2,3},{3,4},{4,5},{5,6},{6,7},{8,9},{9,10},{10,11},{11... | collective-permute-start | bytes 786440 | tf_op jit(solution)/shard_map/ppermute | solution.py:20
  27.0 1.8 collective-permute-done.1
  29.9 1.8 collective-permute-start.4
  31.7 1.8 collective-permute-start.3
  37.6 1.4 gather_fusion.2
  41.3 1.4 gather_fusion.4
  43.1 1.4 gather_fusion.6
  44.5 1.4 gather_fusion.5
  46.0 1.4 gather_fusion.7
  47.8 1.4 gather_fusion.9
  49.2 1.4 gather_fusion.8
  53.3 1.4 gather_fusion.12
  54.7 1.8 gather_fusion.13
  59.5 1.5 fusion.6
  63.5 1.4 gather_fusion.16
  65.7 1.4 gather_fusion.14
  69.6 1.4 gather_fusion.19
  71.8 1.4 gather_fusion.17
  79.1 2.6 fusion.114
  84.9 5.5 %collective-permute-start.6 = (bf16[2,2,1,128,256]{4,3,1,0,2:T(8,128)(2,1)S(1)}, bf16[2,2,1,128,256]{4,3,1,0,2:T(8,128)(2,1)S(1)}, u32[]{:S(2)}, u32[]{:S(2)}) collective-permute-start(bf16[2,2,1,128,256]{4,3,1,0,2:T(8,128)(2,1)S(1)} %get-tuple-element.57), channel_id=1, source_target_pairs={{0,1},{1,2},{2,3},{3,4},{4,5},{5,6},{6,7},{8,9},{9,10},{10,11},{11... | collective-permute-start | bytes 786440 | tf_op jit(solution)/shard_map/ppermute | solution.py:20
  91.8 4.2 collective-permute-done.6
  96.0 5.2 %collective-permute-done.7 = bf16[2,2,1,128,256]{4,3,2,1,0:T(8,128)(2,1)S(1)} collective-permute-done((bf16[2,2,1,128,256]{4,3,2,1,0:T(8,128)(2,1)S(1)}, bf16[2,2,1,128,256]{4,3,2,1,0:T(8,128)(2,1)S(1)}, u32[]{:S(2)}, u32[]{:S(2)}) %collective-permute-start.7) | collective-permute-done | bytes 262176 | tf_op jit(solution)/shard_map/ppermute | solution.py:22
  101.2 5.6 %collective-permute-start.9 = (bf16[2,2,4,16,256]{4,3,2,1,0:T(8,128)(2,1)S(1)}, bf16[2,2,4,16,256]{4,3,2,1,0:T(8,128)(2,1)S(1)}, u32[]{:S(2)}, u32[]{:S(2)}) collective-permute-start(bf16[2,2,4,16,256]{4,3,2,1,0:T(8,128)(2,1)S(1)} %get-tuple-element.42), channel_id=1, source_target_pairs={{8,0},{16,8},{24,16},{32,24},{40,32},{48,40},{56,48},{64,56},{72,6... | collective-permute-start | bytes 393224 | tf_op jit(solution)/shard_map/ppermute | solution.py:22
  107.0 2.2 convolution_bitcast_fusion.1
  111.3 2.1 gather_fusion.30
  115.2 2.1 gather_fusion.32
  117.3 2.1 gather_fusion.33
  119.4 2.1 gather_fusion.34
  121.8 2.1 gather_fusion.35
  123.9 2.1 gather_fusion.36
  126.0 2.1 gather_fusion.37
  128.3 1.8 copy.86
  131.1 1.8 copy.90
  132.9 1.8 copy.92
  134.7 1.8 copy.94
  136.5 1.8 copy.96
  138.3 1.8 copy.98
  146.7 2.2 convolution_bitcast_fusion
  154.2 1.4 gather_fusion.21
  155.6 1.4 gather_fusion.20
  157.4 1.4 gather_fusion.25
  160.2 1.4 gather_fusion.23
  163.4 1.4 gather_fusion.27
  164.8 1.4 gather_fusion.26
  169.8 255.9 %all-reduce.17.cloned.1.call-done = (f32[2304,256]{1,0:T(8,128)}, f32[2304,256]{1,0:T(8,128)}) async-done(((f32[2304,256]{1,0:T(8,128)}, f32[2304,256]{1,0:T(8,128)}), (f32[2304,256]{1,0:T(8,128)}, f32[2304,256]{1,0:T(8,128)})) %all-reduce.17.cloned.1.call-update) | async-done | bytes 4718608 | tf_op jit(solution)/shard_map/psum | solution.py:154
  425.7 3.4 broadcast_multiply_fusion.1
  429.1 1.6 broadcast_multiply_fusion
  (230 shorter events, 65.3 us)
Async XLA Ops:
  7.2 15.2 %copy-start.42 = (s32[2,16,3]{1,0,2:T(2,128)S(1)}, s32[2,16,3]{1,0,2:T(2,128)}, u32[]{:S(2)}) copy-start(s32[2,16,3]{1,0,2:T(2,128)} %param.13) | copy-start | bytes 1156
  7.2 14.5 %copy-start.1 = (bf16[3,3,256,256]{3,2,1,0:T(8,128)(2,1)S(1)}, bf16[3,3,256,256]{3,2,1,0:T(8,128)(2,1)}, u32[]{:S(2)}) copy-start(bf16[3,3,256,256]{3,2,1,0:T(8,128)(2,1)} %param.12) | copy-start | bytes 3538948
  7.2 418.5 %all-reduce.17.cloned.1.call-start = ((), (), s32[]{:S(2)}) async-start(), calls=%async_computation | async-start | bytes 9437184 | tf_op jit(solution)/shard_map/psum | solution.py:154
  9.1 20.7 %collective-permute-start.2 = (bf16[2,2,1,128,256]{4,3,1,0,2:T(8,128)(2,1)S(1)}, bf16[2,2,1,128,256]{4,3,1,0,2:T(8,128)(2,1)S(1)}, u32[]{:S(2)}, u32[]{:S(2)}) collective-permute-start(bf16[2,2,1,128,256]{4,3,1,0,2:T(8,128)(2,1)S(1)} %get-tuple-element.60), channel_id=1, source_target_pairs={{1,0},{2,1},{3,2},{4,3},{5,4},{6,5},{7,6},{9,8},{10,9},{11,10},{12... | collective-permute-start | bytes 786440 | tf_op jit(solution)/shard_map/ppermute | solution.py:22
  10.4 16.6 %collective-permute-start = (bf16[2,2,128,256]{3,2,1,0:T(8,128)(2,1)S(1)}, bf16[2,2,128,256]{3,2,1,0:T(8,128)(2,1)}, u32[]{:S(2)}, u32[]{:S(2)}) collective-permute-start(bf16[2,2,128,256]{3,2,1,0:T(8,128)(2,1)S(1)} %bitcast.267), channel_id=1, source_target_pairs={{0,128},{8,136},{16,144},{24,152},{32,160},{40,168},{48,176},{56,1... | collective-permute-start | bytes 786440 | tf_op jit(solution)/shard_map/ppermute | solution.py:31
  12.6 16.1 %collective-permute-start.1 = (bf16[2,2,1,128,256]{4,3,1,0,2:T(8,128)(2,1)}, bf16[2,2,1,128,256]{4,3,1,0,2:T(8,128)(2,1)}, u32[]{:S(2)}, u32[]{:S(2)}) collective-permute-start(bf16[2,2,1,128,256]{4,3,1,0,2:T(8,128)(2,1)} %get-tuple-element.59), channel_id=1, source_target_pairs={{0,1},{1,2},{2,3},{3,4},{4,5},{5,6},{6,7},{8,9},{9,10},{10,11},{11... | collective-permute-start | bytes 786440 | tf_op jit(solution)/shard_map/ppermute | solution.py:20
  22.6 15.0 %copy-start.39 = (s32[4]{0:T(128)}, s32[4]{0:T(128)S(1)}, u32[]{:S(2)}) copy-start(s32[4]{0:T(128)S(1)} %reshape.354) | copy-start | bytes 52
  22.7 18.6 %copy-start.37 = (s32[4]{0:T(128)}, s32[4]{0:T(128)S(1)}, u32[]{:S(2)}) copy-start(s32[4]{0:T(128)S(1)} %reshape.366) | copy-start | bytes 52
  22.8 21.7 %copy-start.35 = (s32[4]{0:T(128)}, s32[4]{0:T(128)S(1)}, u32[]{:S(2)}) copy-start(s32[4]{0:T(128)S(1)} %reshape.372) | copy-start | bytes 52
  22.8 23.1 %copy-start.33 = (s32[4]{0:T(128)}, s32[4]{0:T(128)S(1)}, u32[]{:S(2)}) copy-start(s32[4]{0:T(128)S(1)} %reshape.384) | copy-start | bytes 52
  22.9 26.3 %copy-start.31 = (s32[4]{0:T(128)}, s32[4]{0:T(128)S(1)}, u32[]{:S(2)}) copy-start(s32[4]{0:T(128)S(1)} %reshape.390) | copy-start | bytes 52
  23.0 27.7 %copy-start.29 = (s32[4]{0:T(128)}, s32[4]{0:T(128)S(1)}, u32[]{:S(2)}) copy-start(s32[4]{0:T(128)S(1)} %reshape.402) | copy-start | bytes 52
  29.9 6.0 %collective-permute-start.4 = (bf16[2,2,4,16,256]{4,3,1,0,2:T(8,128)(2,1)S(1)}, bf16[2,2,4,16,256]{4,3,1,0,2:T(8,128)(2,1)S(1)}, u32[]{:S(2)}, u32[]{:S(2)}) collective-permute-start(bf16[2,2,4,16,256]{4,3,1,0,2:T(8,128)(2,1)S(1)} %get-tuple-element.44), channel_id=1, source_target_pairs={{8,0},{16,8},{24,16},{32,24},{40,32},{48,40},{56,48},{64,56},{72,6... | collective-permute-start | bytes 393224 | tf_op jit(solution)/shard_map/ppermute | solution.py:22
  31.7 5.3 %collective-permute-start.3 = (bf16[2,2,4,16,256]{4,3,1,0,2:T(8,128)(2,1)S(1)}, bf16[2,2,4,16,256]{4,3,1,0,2:T(8,128)(2,1)S(1)}, u32[]{:S(2)}, u32[]{:S(2)}) collective-permute-start(bf16[2,2,4,16,256]{4,3,1,0,2:T(8,128)(2,1)S(1)} %get-tuple-element.43), channel_id=1, source_target_pairs={{0,8},{8,16},{16,24},{24,32},{32,40},{40,48},{48,56},{56,64},{64,7... | collective-permute-start | bytes 393224 | tf_op jit(solution)/shard_map/ppermute | solution.py:20
  37.3 2.5 copy-start.4
  57.3 2.2 copy-start.11
  59.5 1.6 copy-start.16
  62.1 3.6 copy-start.23
  67.1 2.5 copy-start.27
  68.2 3.6 copy-start.25
  73.2 5.1 %copy-start.6 = (bf16[4,128,256]{2,1,0:T(8,128)(2,1)S(1)}, bf16[4,128,256]{2,1,0:T(8,128)(2,1)}, u32[]{:S(2)}) copy-start(bf16[4,128,256]{2,1,0:T(8,128)(2,1)} %copy.27) | copy-start | bytes 786436
  73.3 5.8 %copy-start.2 = (bf16[3,3,256,256]{3,2,1,0:T(8,128)(2,1)S(1)}, bf16[3,3,256,256]{3,2,1,0:T(8,128)(2,1)}, u32[]{:S(2)}) copy-start(bf16[3,3,256,256]{3,2,1,0:T(8,128)(2,1)} %param.11) | copy-start | bytes 3538948
  79.1 2.8 copy-start.9
  79.1 2.9 copy-start.14
  79.1 2.9 copy-start.15
  79.1 2.9 copy-start.17
  79.1 2.9 copy-start.22
  79.1 3.1 copy-start.10
  79.1 3.1 copy-start.18
  79.1 3.1 copy-start.19
  83.4 23.5 %copy-start.41 = (bf16[2,2,128,2304]{3,2,1,0:T(8,128)(2,1)S(1)}, bf16[2,2,128,2304]{3,2,1,0:T(8,128)(2,1)}, u32[]{:S(2)}) copy-start(bf16[2,2,128,2304]{3,2,1,0:T(8,128)(2,1)} %constant_dynamic-update-slice_fusion) | copy-start | bytes 7077892
  83.5 8.2 %collective-permute-start.5 = (bf16[2,2,128,256]{3,2,1,0:T(8,128)(2,1)S(1)}, bf16[2,2,128,256]{3,2,1,0:T(8,128)(2,1)S(1)}, u32[]{:S(2)}, u32[]{:S(2)}) collective-permute-start(bf16[2,2,128,256]{3,2,1,0:T(8,128)(2,1)S(1)} %bitcast.268), channel_id=1, source_target_pairs={{0,128},{8,136},{16,144},{24,152},{32,160},{40,168},{48,176},{56,1... | collective-permute-start | bytes 786440 | tf_op jit(solution)/shard_map/ppermute | solution.py:31
  84.9 11.1 %collective-permute-start.6 = (bf16[2,2,1,128,256]{4,3,1,0,2:T(8,128)(2,1)S(1)}, bf16[2,2,1,128,256]{4,3,1,0,2:T(8,128)(2,1)S(1)}, u32[]{:S(2)}, u32[]{:S(2)}) collective-permute-start(bf16[2,2,1,128,256]{4,3,1,0,2:T(8,128)(2,1)S(1)} %get-tuple-element.57), channel_id=1, source_target_pairs={{0,1},{1,2},{2,3},{3,4},{4,5},{5,6},{6,7},{8,9},{9,10},{10,11},{11... | collective-permute-start | bytes 786440 | tf_op jit(solution)/shard_map/ppermute | solution.py:20
  90.4 10.8 %collective-permute-start.7 = (bf16[2,2,1,128,256]{4,3,2,1,0:T(8,128)(2,1)S(1)}, bf16[2,2,1,128,256]{4,3,2,1,0:T(8,128)(2,1)S(1)}, u32[]{:S(2)}, u32[]{:S(2)}) collective-permute-start(bf16[2,2,1,128,256]{4,3,2,1,0:T(8,128)(2,1)S(1)} %get-tuple-element.58), channel_id=1, source_target_pairs={{1,0},{2,1},{3,2},{4,3},{5,4},{6,5},{7,6},{9,8},{10,9},{11,10},{12... | collective-permute-start | bytes 786440 | tf_op jit(solution)/shard_map/ppermute | solution.py:22
  101.2 8.0 %collective-permute-start.9 = (bf16[2,2,4,16,256]{4,3,2,1,0:T(8,128)(2,1)S(1)}, bf16[2,2,4,16,256]{4,3,2,1,0:T(8,128)(2,1)S(1)}, u32[]{:S(2)}, u32[]{:S(2)}) collective-permute-start(bf16[2,2,4,16,256]{4,3,2,1,0:T(8,128)(2,1)S(1)} %get-tuple-element.42), channel_id=1, source_target_pairs={{8,0},{16,8},{24,16},{32,24},{40,32},{48,40},{56,48},{64,56},{72,6... | collective-permute-start | bytes 393224 | tf_op jit(solution)/shard_map/ppermute | solution.py:22
  106.8 2.4 collective-permute-start.8
  109.9 3.5 copy-start.38
  111.3 3.9 copy-start.36
  115.2 4.2 copy-start.34
  117.3 4.5 %copy-start.32 = (s32[4]{0:T(128)S(1)}, s32[4]{0:T(128)}, u32[]{:S(2)}) copy-start(s32[4]{0:T(128)} %copy-done.31) | copy-start | bytes 52
  121.8 4.2 copy-start.30
  140.2 6.6 %copy-start.5 = (bf16[2,2,128,256]{3,2,1,0:T(8,128)(2,1)S(1)}, bf16[2,2,128,256]{3,2,1,0:T(8,128)(2,1)}, u32[]{:S(2)}) copy-start(bf16[2,2,128,256]{3,2,1,0:T(8,128)(2,1)} %param.10) | copy-start | bytes 786436
  141.6 5.0 %copy-start.8 = (bf16[4,128,256]{1,2,0:T(8,128)(2,1)S(1)}, bf16[4,128,256]{1,2,0:T(8,128)(2,1)}, u32[]{:S(2)}) copy-start(bf16[4,128,256]{1,2,0:T(8,128)(2,1)} %copy.96) | copy-start | bytes 786436
  141.6 5.1 %copy-start.7 = (bf16[4,128,256]{1,2,0:T(8,128)(2,1)S(1)}, bf16[4,128,256]{1,2,0:T(8,128)(2,1)}, u32[]{:S(2)}) copy-start(bf16[4,128,256]{1,2,0:T(8,128)(2,1)} %copy.98) | copy-start | bytes 786436
  157.4 2.8 copy-start.24
  158.8 3.2 copy-start.28
  162.0 2.8 copy-start.26
  425.7 3.4 copy-start
  (6 other events, 5.7 us)
Sparse Core Ops, SparseCore 0:
  149.1 276.5 all-reduce.16
where the time goes:
time: 443 us; the launch traced here: 438 us
  waiting for transfers between devices  269 us (61%)
  local copies, waits for them, and re-layouts  106 us (24%)
  starting transfers between devices  27.9 us (6%)
  between operations  15.5 us (3%)
  matrix products  11.8 us (3%)
  other arithmetic  7.48 us (2%)
    psum x1, waiting for transfers between devices, local(): lax.psum((first_local, second_local), ('lon', 'lat'))  256 us
    gather x84, local copies, waits for them, and re-layouts, one_row(): return lax.dynamic_slice_in_dim(row_data, offset, col_width, 0)  76.9 us
    unnamed x103, local copies, waits for them, and re-layouts  15.1 us
    ppermute x4, starting transfers between devices, with_halo(): lax.ppermute(tail, axis, [(i, (i + 1) % count) for i in range(ends)])  14.3 us
    ppermute x4, starting transfers between devices, with_halo(): lax.ppermute(head, axis, [((i + 1) % count, i) for i in range(ends)])  9.94 us
  transfers between devices with their start and end apart: 11, of which 6 were waited for; matrix products, arithmetic and copies ran while one was open for 7% of the time, Pallas kernels for 0%

commit v1 on v0

v1 whole, which is shorter than its diff:
```python
import functools
import math

import jax
import jax.numpy as jnp
from jax import lax
from jax.experimental import pallas as pl
from jax.experimental.pallas import tpu as pltpu
from jax.sharding import Mesh
from jax.sharding import PartitionSpec as P

POLE = 16
SPAN = 16
ALL = ("yl", "z", "core", "x", "yh")
PLANE = ("x", "yh", "yl")
NN = (((1,), (0,)), ((), ()))
NT = (((1,), (1,)), ((), ()))
TN = (((0,), (0,)), ((), ()))
ROOT = math.sqrt(2.0 / math.pi)
CUBIC = 0.044715


def dot(a, b, dims):
    return lax.dot_general(a, b, dims, preferred_element_type=jnp.float32)


def fill(ext, field, own, down, cross, bottom, left, right, mirror):
    width = own.shape[2]
    for s in range(2):
        for row in range(4):
            place = ext.at[s * 4 + row]
            if row == 0:
                above, across = down[field, s].astype(jnp.float32), cross[field, s].astype(jnp.float32)
                middle = jnp.where(mirror, across, above)
            elif row == 3:
                middle = bottom[field, s].astype(jnp.float32)
            else:
                middle = own[s, row - 1].astype(jnp.float32)
            place[:SPAN] = left[field, s, row].astype(jnp.float32)
            place[SPAN : SPAN + width] = middle
            place[SPAN + width : 2 * SPAN + width] = right[field, s, row].astype(jnp.float32)


def tap(ext, s, row, shift, width):
    if isinstance(shift, int):
        return ext[s * 4 + row, SPAN + shift : SPAN + shift + width, :].astype(jnp.bfloat16)
    start = SPAN + shift
    rest = lax.rem(start, 8)
    span = ext[s * 4 + row, pl.ds(pl.multiple_of(start - rest, 8), width + 8), :]
    chans = span.shape[-1]
    turned = pltpu.roll(span.reshape(width // 8 + 1, 8, chans), lax.rem(8 - rest, 8), 1)
    lane = lax.broadcasted_iota(jnp.int32, (1, 8, chans), 1)
    moved = jnp.where(lane < 8 - rest, turned[:-1], turned[1:])
    return moved.reshape(width, chans).astype(jnp.bfloat16)


def adjoint_stride(strides, s, row, slot, lat):
    here = lat * 2 + row
    if slot == 0:
        if row == 1:
            return strides[s, lat * 2, 2]
        return jnp.where(lat == 0, strides[s, 0, 0], strides[s, jnp.maximum(here - 1, 0), 2])
    if slot == 1:
        return strides[s, here, 1]
    return strides[s, jnp.minimum(here + 1, POLE - 1), 0]


def adjoint_taps(ext, taps, strides, lat, width):
    for row in range(2):
        for s in range(2):
            at = (row * 2 + s) * width
            for slot in range(3):
                stride = adjoint_stride(strides, s, row, slot, lat)
                for col in range(3):
                    shift = 0 if col == 1 else -(col - 1) * stride
                    taps[slot * 3 + col, at : at + width] = tap(ext, s, row + slot, shift, width)


def adjoint_product(taps, kernel, mirror, row, half):
    total = None
    at = row * half
    for slot in range(3):
        for col in range(3):
            weight = kernel[2 - slot, col]
            if slot == 0 and row == 0:
                weight = jnp.where(mirror, kernel[0, col], weight)
            term = dot(taps[slot * 3 + col, at : at + half], weight, NT)
            total = term if total is None else total + term
    return total


def main_kernel(where, strides, feat, grad, down, cross, bottom, left, right, first_kernel, second_kernel,
                keep, send, pre_grad, ext_f, ext_g, taps_f, taps_g, act):
    lat, core = where[0], where[1]
    mirror = lat == 0
    width = feat.shape[2]
    half = 2 * width
    fill(ext_f, 0, feat, down, cross, bottom, left, right, mirror)
    for row in range(2):
        for s in range(2):
            at = (row * 2 + s) * width
            for k in range(3):
                stride = strides[s, lat * 2 + row, k]
                for col in range(3):
                    shift = 0 if col == 1 else (col - 1) * stride
                    taps_f[k * 3 + col, at : at + width] = tap(ext_f, s, row + k, shift, width)
    fill(ext_g, 1, grad, down, cross, bottom, left, right, mirror)
    adjoint_taps(ext_g, taps_g, strides, lat, width)

    for row in range(2):
        at = row * half
        pre = None
        for k in range(3):
            for col in range(3):
                term = dot(taps_f[k * 3 + col, at : at + half], first_kernel[k, col], NN)
                pre = term if pre is None else pre + term
        square = pre * pre
        bend = jnp.tanh(ROOT * (pre + CUBIC * (pre * square)))
        act[at : at + half] = (0.5 * pre * (1.0 + bend)).astype(jnp.bfloat16)
        slope = 0.5 * (1.0 + bend) + 0.5 * pre * (1.0 - bend * bend) * (ROOT * (1.0 + 3.0 * CUBIC * square))
        back = adjoint_product(taps_g, second_kernel, mirror, row, half)
        result = (back * slope).astype(jnp.bfloat16)
        for s in range(2):
            pre_grad[s, row] = result[s * width : (s + 1) * width]

    def place(value, k, col, owner):
        at = (k * 3 + col) * 256

        @pl.when(core == owner)
        def _():
            keep[at : at + 256] = value

        @pl.when(core != owner)
        def _():
            send[at : at + 256] = value.astype(jnp.bfloat16)

    activated = act[...]
    for col in range(3):
        edge = dot(activated[:half], taps_g[col, :half], TN)
        upper = dot(activated[half:], taps_g[col, half:], TN)
        lower = dot(activated, taps_g[6 + col], TN)
        place(dot(activated, taps_g[3 + col], TN), 1, col, 1)
        place(lower + jnp.where(mirror, edge, 0.0), 0, col, 1)
        place(upper + jnp.where(mirror, 0.0, edge), 2, col, 1)
    cells = [pre_grad[s, row] for row in range(2) for s in range(2)]
    pre_all = jnp.concatenate(cells, axis=0)
    for k in range(3):
        for col in range(3):
            place(dot(taps_f[k * 3 + col], pre_all, TN), k, col, 0)


def back_kernel(where, strides, grad, pre, down, cross, bottom, left, right, first_kernel, out, ext, taps):
    lat = where[0]
    mirror = lat == 0
    width = grad.shape[2]
    fill(ext, 0, pre, down, cross, bottom, left, right, mirror)
    adjoint_taps(ext, taps, strides, lat, width)
    for row in range(2):
        total = adjoint_product(taps, first_kernel, mirror, row, 2 * width)
        for s in range(2):
            own = grad[s, row].astype(jnp.float32)
            out[s, row] = (own + total[s * width : (s + 1) * width]).astype(jnp.bfloat16)


def halos(fields, lon_count, lat_count):
    n, _, _, width, _ = fields.shape
    at = lambda lon, lat: (lon % lon_count) * lat_count + lat
    lons = range(lon_count)
    down = lax.ppermute(fields[:, :, 1], ALL, [(at(i, k), at(i, k + 1)) for i in lons for k in range(lat_count - 1)])
    bottom = lax.ppermute(fields[:, :, 0], ALL, [(at(i, k + 1), at(i, k)) for i in lons for k in range(lat_count - 1)])
    cross = lax.ppermute(fields[:, :, 0], ALL, [(at(i, 0), at(i + lon_count // 2, 0)) for i in lons])
    lat = lax.axis_index(("x", "yh"))
    top = jnp.where(lat == 0, cross, down)

    def edge(cut):
        return jnp.concatenate([cut(top)[:, :, None], cut(fields), cut(bottom)[:, :, None]], axis=2)

    head = edge(lambda a: lax.slice_in_dim(a, 0, SPAN, axis=a.ndim - 2))
    tail = edge(lambda a: lax.slice_in_dim(a, width - SPAN, width, axis=a.ndim - 2))
    lats = range(lat_count)
    left = lax.ppermute(tail, ALL, [(at(i, k), at(i + 1, k)) for i in lons for k in lats])
    right = lax.ppermute(head, ALL, [(at(i + 1, k), at(i, k)) for i in lons for k in lats])
    return down, cross, bottom, left, right


def summed(keep, send):
    core = lax.axis_index("core")
    swap = [(0, 1), (1, 0)]
    total = keep + lax.ppermute(send, "core", swap).astype(jnp.float32)
    planes = lax.axis_size(PLANE)
    rows, cols = total.shape
    spread = lax.all_to_all(total.astype(jnp.bfloat16).reshape(planes, rows // planes, cols), PLANE, 0, 0, tiled=True)
    part = jnp.sum(spread.astype(jnp.float32), axis=0)
    count = lax.axis_size("z")
    reach = 1
    while reach < count:
        reach *= 2
        part = part + lax.ppermute(part, "z", [(i, i ^ (reach - 1)) for i in range(count)])
    part = part.astype(jnp.bfloat16)
    copies = jnp.broadcast_to(part[None], (planes,) + part.shape)
    mine = lax.all_to_all(copies, PLANE, 0, 0, tiled=True).reshape(rows, cols)
    other = lax.ppermute(mine, "core", swap)
    first = jnp.where(core == 0, mine, other).astype(jnp.float32)
    second = jnp.where(core == 0, other, mine).astype(jnp.float32)
    return first, second


def local(features, out_grad, first_kernel, second_kernel, strides):
    slabs, rows, width, chans = features.shape
    lat_axes, lon_axes = ("x", "yh"), ("yl", "z", "core")
    lat_count, lon_count = lax.axis_size(lat_axes), lax.axis_size(lon_axes)
    where = jnp.stack([lax.axis_index(lat_axes), lax.axis_index("core")]).astype(jnp.int32)
    smem = pl.BlockSpec(memory_space=pltpu.SMEM)
    vmem = pl.BlockSpec(memory_space=pltpu.VMEM)
    cells = slabs * rows * width
    ext = pltpu.VMEM((slabs * (rows + 2), width + 2 * SPAN + 8, chans), jnp.float32)
    taps = pltpu.VMEM((9, cells, chans), jnp.bfloat16)
    params = pltpu.CompilerParams(vmem_limit_bytes=48 * 1024 * 1024)
    grads = (9 * chans, chans)

    around = halos(jnp.stack([features, out_grad]), lon_count, lat_count)
    keep, send, pre_grad = pl.pallas_call(
        main_kernel,
        out_shape=[
            jax.ShapeDtypeStruct(grads, jnp.float32),
            jax.ShapeDtypeStruct(grads, jnp.bfloat16),
            jax.ShapeDtypeStruct(features.shape, jnp.bfloat16),
        ],
        in_specs=[smem, smem] + [vmem] * 9,
        out_specs=[vmem] * 3,
        scratch_shapes=[ext, ext, taps, taps, pltpu.VMEM((cells, chans), jnp.bfloat16)],
        compiler_params=params,
        name="main",
    )(where, strides, features, out_grad, *around, first_kernel, second_kernel)

    first, second = summed(keep, send)

    around = halos(pre_grad[None], lon_count, lat_count)
    input_grad = pl.pallas_call(
        back_kernel,
        out_shape=jax.ShapeDtypeStruct(features.shape, jnp.bfloat16),
        in_specs=[smem, smem] + [vmem] * 8,
        out_specs=vmem,
        scratch_shapes=[ext, taps],
        compiler_params=params,
        name="back",
    )(where, strides, out_grad, pre_grad, *around, first_kernel)

    scale = 1.0 / math.sqrt(cells * lat_count * lon_count)
    shape = first_kernel.shape
    return input_grad, (first * scale).reshape(shape), (second * scale).reshape(shape)


def solution(mesh):
    wide = Mesh(mesh.devices.reshape(2, 8, 2, 4, 2), ALL)
    field = P(None, ("x", "yh"), ("yl", "z", "core"), None)
    return jax.shard_map(
        local,
        mesh=wide,
        in_specs=(field, field, P(), P(), P()),
        out_specs=(field, P(), P()),
        check_vma=False,
    )
```

time: 443 us -> 141 us (0.32)
  waiting for transfers between devices: 269 us -> 45.5 us
  local copies, waits for them, and re-layouts: 106 us -> 5.43 us
  blocking collectives: 0 us -> 20.5 us
  starting transfers between devices: 27.9 us -> 45.9 us
  between operations: 15.5 us -> 0.91 us
  matrix products: 11.8 us -> 0 us
  Pallas kernels: 0 us -> 11.8 us
    psum x1 -> x0, waiting for transfers between devices: 256 us -> none  [local(): lax.psum((first_local, second_local), ('lon', 'lat'))]
    gather x87 -> x0, local copies, waits for them, and re-layouts: 78.1 us -> none  [the longest x84 76.9 us: one_row(): return lax.dynamic_slice_in_dim(row_data, offset, col_width, 0)]
    ppermute x10 -> x15, waiting for transfers between devices: 13.4 us -> 40.6 us  [the longest x2 12.3 us: halos(): lax.ppermute(fields[:, :, 0], ALL, [(at(i, 0), at(i + lon_count // 2, 0))...]
    all_to_all x0 -> x1, blocking collectives: none -> 20.5 us  [summed(): lax.all_to_all(total.astype(jnp.bfloat16).reshape(planes, rows // planes,...]
    unnamed x103 -> x21, local copies, waits for them, and re-layouts: 15.1 us -> 0.82 us
    ppermute x10 -> x15, starting transfers between devices: 27.8 us -> 42 us  [the longest x2 10.4 us: halos(): lax.ppermute(fields[:, :, 1], ALL, [(at(i, k), at(i, k + 1)) for i in lon...]
    dot_general x11 -> x0, matrix products: 11.8 us -> none  [the longest x6 4.26 us: project(): jnp.dot(tap_block.reshape(-1, 3 * chan_count), flipped[kernel_row], prefe...]
    pallas_call x0 -> x2, Pallas kernels: none -> 11.8 us  [the longest x1 9.4 us: local(): pl.pallas_call(main_kernel, out_shape=[jax.ShapeDtypeStruct(grads, jnp.fl...]
  transfers between devices with their start and end apart: 11 -> 16, of which waited for: 6 -> 12; matrix products, arithmetic and copies ran while one was open for 7% -> 3% of each run, Pallas kernels for 0% -> 2%
where the time goes in v1:
time: 141 us; the launch traced here: 140 us
  starting transfers between devices  45.9 us (33%)
  waiting for transfers between devices  45.5 us (32%)
  blocking collectives  20.5 us (15%)
  Pallas kernels  11.8 us (8%)
  other arithmetic  10 us (7%)
  local copies, waits for them, and re-layouts  5.43 us (4%)
    all_to_all x1, blocking collectives, summed(): lax.all_to_all(total.astype(jnp.bfloat16).reshape(planes, rows // planes,...  20.5 us
    ppermute x2, waiting for transfers between devices, halos(): lax.ppermute(fields[:, :, 0], ALL, [(at(i, 0), at(i + lon_count // 2, 0))...  12.3 us
    ppermute x3, waiting for transfers between devices, summed(): lax.ppermute(part, 'z', [(i, i ^ reach - 1) for i in range(count)])  10.7 us
    ppermute x2, starting transfers between devices, halos(): lax.ppermute(fields[:, :, 1], ALL, [(at(i, k), at(i, k + 1)) for i in lon...  10.4 us
    pallas_call x1, Pallas kernels, local(): pl.pallas_call(main_kernel, out_shape=[jax.ShapeDtypeStruct(grads, jnp.fl...  9.4 us
    ppermute x2, starting transfers between devices, halos(): lax.ppermute(tail, ALL, [(at(i, k), at(i + 1, k)) for i in lons for k in...  8.44 us
    ppermute x1, starting transfers between devices, summed(): other = lax.ppermute(mine, 'core', swap)  7.68 us
    ppermute x2, waiting for transfers between devices, halos(): lax.ppermute(fields[:, :, 0], ALL, [(at(i, k + 1), at(i, k)) for i in lon...  7.36 us
  transfers between devices with their start and end apart: 16, of which 12 were waited for; matrix products, arithmetic and copies ran while one was open for 3% of the time, Pallas kernels for 2%

profile of v1, /device:TPU:1, one launch (start us, length us, event | category | flops | bytes accessed | tf_op | source)
XLA Modules:
  0.0 140.0 jit_solution(58444041051324246)
XLA Ops:
  0.6 1.1 copy_bitcast_fusion.1
  1.7 0.0 copy-start.8
  1.7 0.0 copy-start.2
  1.7 0.8 fusion.3
  2.6 5.7 %collective-permute-start = (bf16[2,2,128,256]{3,2,1,0:T(8,128)(2,1)}, bf16[2,2,128,256]{3,2,1,0:T(8,128)(2,1)S(1)}, u32[]{:S(2)}, u32[]{:S(2)}) collective-permute-start(bf16[2,2,128,256]{3,2,1,0:T(8,128)(2,1)} %get-tuple-element.14), channel_id=1, source_target_pairs={{0,1},{1,2},{2,3},{3,4},{4,5},{5,6},{6,7},{8,9},{9,10},{10,11},{11... | collective-permute-start | bytes 786440 | tf_op jit(solution)/shard_map/ppermute | solution.py:169
  8.2 2.3 %collective-permute-start.1 = (bf16[2,2,128,256]{3,2,1,0:T(8,128)(2,1)}, bf16[2,2,128,256]{3,2,1,0:T(8,128)(2,1)S(1)}, u32[]{:S(2)}, u32[]{:S(2)}) collective-permute-start(bf16[2,2,128,256]{3,2,1,0:T(8,128)(2,1)} %get-tuple-element.13), channel_id=1, source_target_pairs={{0,128},{8,136},{16,144},{24,152},{32,160},{40,168},{48,176},{56,1... | collective-permute-start | bytes 786440 | tf_op jit(solution)/shard_map/ppermute | solution.py:171
  10.6 1.3 collective-permute-start.2
  11.9 0.0 copy-start.1
  11.9 0.0 copy-start.3
  11.9 0.9 pad_maximum_fusion.2
  12.9 0.6 collective-permute-done.down
  13.5 12.3 %collective-permute-done.1.cross = bf16[2,2,128,256]{3,2,1,0:T(8,128)(2,1)S(1)} collective-permute-done((bf16[2,2,128,256]{3,2,1,0:T(8,128)(2,1)}, bf16[2,2,128,256]{3,2,1,0:T(8,128)(2,1)S(1)}, u32[]{:S(2)}, u32[]{:S(2)}) %collective-permute-start.1) | collective-permute-done | bytes 262176 | tf_op jit(solution)/shard_map/ppermute | solution.py:171
  25.8 0.8 slice_bitcast_fusion.2
  26.6 0.7 pad_maximum_fusion
  27.3 3.1 %collective-permute-start.3 = (bf16[2,2,4,16,256]{4,3,1,0,2:T(8,128)(2,1)}, bf16[2,2,4,16,256]{4,3,1,0,2:T(8,128)(2,1)}, u32[]{:S(2)}, u32[]{:S(2)}) collective-permute-start(bf16[2,2,4,16,256]{4,3,1,0,2:T(8,128)(2,1)} %pad_maximum_fusion), channel_id=1, source_target_pairs={{0,8},{1,9},{2,10},{3,11},{4,12},{5,13},{6,14},{7,15},{8,16},{9,17... | collective-permute-start | bytes 393224 | tf_op jit(solution)/shard_map/ppermute | solution.py:181
  30.3 0.7 pad_maximum_fusion.1
  31.0 0.8 copy.17.strides
  31.8 0.1 pad_add_fusion.where
  31.8 0.8 collective-permute-done.3
  32.6 0.9 copy.13.left
  33.5 2.5 %collective-permute-done.4.right = bf16[2,2,4,16,256]{4,3,2,1,0:T(8,128)(2,1)S(1)} collective-permute-done((bf16[2,2,4,16,256]{4,3,2,1,0:T(8,128)(2,1)}, bf16[2,2,4,16,256]{4,3,2,1,0:T(8,128)(2,1)S(1)}, u32[]{:S(2)}, u32[]{:S(2)}) %collective-permute-start.4) | collective-permute-done | bytes 131104 | tf_op jit(solution)/shard_map/ppermute | solution.py:182
  36.0 9.4 %main.1 = (f32[2304,256]{1,0:T(8,128)}, bf16[2304,256]{1,0:T(8,128)(2,1)S(1)}, bf16[2,2,128,256]{3,2,1,0:T(8,128)(2,1)S(1)}) custom-call(s32[2]{0:T(128)S(1)} %pad_add_fusion.where, s32[2,16,3]{2,1,0:T(8,128)S(1)} %copy.17.strides, bf16[2,2,128,256]{3,2,1,0:T(8,128)(2,1)S(1)} %copy-done.3, bf16[2,2,128,256]{3,2,1,0:T(8,128)(2,1)S(1)} %copy-done.1, ...), custom_call_target="tpu_custom_call" | custom-call | tf_op jit(solution)/shard_map/main/pallas_call | solution.py:222
  45.4 1.9 %collective-permute-start.10 = (bf16[2304,256]{1,0:T(8,128)(2,1)S(1)}, bf16[2304,256]{1,0:T(8,128)(2,1)S(1)}, u32[]{:S(2)}, u32[]{:S(2)}) collective-permute-start(bf16[2304,256]{1,0:T(8,128)(2,1)S(1)} %get-tuple-element.8), channel_id=1, source_target_pairs={{0,8},{8,0},{1,9},{9,1},{2,10},{10,2},{3,11},{11,3},{4,12},{12,4},... | collective-permute-start | bytes 3538952 | tf_op jit(solution)/shard_map/ppermute | solution.py:189
  47.3 2.5 %collective-permute-done.10 = bf16[2304,256]{1,0:T(8,128)(2,1)S(1)} collective-permute-done((bf16[2304,256]{1,0:T(8,128)(2,1)S(1)}, bf16[2304,256]{1,0:T(8,128)(2,1)S(1)}, u32[]{:S(2)}, u32[]{:S(2)}) %collective-permute-start.10) | collective-permute-done | bytes 1179680 | tf_op jit(solution)/shard_map/ppermute | solution.py:189
  49.8 2.0 %add_convert_fusion = bf16[2304,256]{1,0:T(8,128)(2,1)S(1)} fusion(f32[2304,256]{1,0:T(8,128)} %get-tuple-element.7, bf16[2304,256]{1,0:T(8,128)(2,1)S(1)} %collective-permute-done.10), kind=kLoop, calls=%fused_computation.3 | loop fusion | flops 1769472 | bytes 4718592 | tf_op jit(solution)/shard_map/convert_element_type | solution.py:192
  51.8 20.5 %all_to_all.10 = bf16[16,144,256]{2,1,0:T(8,128)(2,1)S(1)} all-to-all(bf16[16,144,256]{2,1,0:T(8,128)(2,1)S(1)} %bitcast.44), channel_id=1, replica_groups=mesh['yl'=2,'z'=8,'core'=2,'x'=4,'yh'=2] {'x','yh','yl'}, dimensions={0} | all-to-all | bytes 2359296 | tf_op jit(solution)/shard_map/all_to_all | solution.py:192
  72.3 0.2 convert_reduce_fusion
  72.5 0.1 collective-permute-start.11
  72.6 4.0 %collective-permute-done.11 = f32[144,256]{1,0:T(8,128)S(1)} collective-permute-done((f32[144,256]{1,0:T(8,128)S(1)}, f32[144,256]{1,0:T(8,128)S(1)}, u32[]{:S(2)}, u32[]{:S(2)}) %collective-permute-start.11) | collective-permute-done | bytes 147488 | tf_op jit(solution)/shard_map/ppermute | solution.py:198
  76.6 5.2 %collective-permute-start.12 = (f32[144,256]{1,0:T(8,128)S(1)}, f32[144,256]{1,0:T(8,128)S(1)}, u32[]{:S(2)}, u32[]{:S(2)}) collective-permute-start(f32[144,256]{1,0:T(8,128)S(1)} %add.19), channel_id=1, source_target_pairs={{0,48},{16,32},{32,16},{48,0},{64,112},{80,96},{96,80},{112,64},{1... | collective-permute-start | bytes 442376 | tf_op jit(solution)/shard_map/ppermute | solution.py:198
  81.8 2.6 %collective-permute-done.12 = f32[144,256]{1,0:T(8,128)S(1)} collective-permute-done((f32[144,256]{1,0:T(8,128)S(1)}, f32[144,256]{1,0:T(8,128)S(1)}, u32[]{:S(2)}, u32[]{:S(2)}) %collective-permute-start.12) | collective-permute-done | bytes 147488 | tf_op jit(solution)/shard_map/ppermute | solution.py:198
  84.4 1.2 collective-permute-start.13
  85.6 4.1 %collective-permute-done.13 = f32[144,256]{1,0:T(8,128)S(1)} collective-permute-done((f32[144,256]{1,0:T(8,128)S(1)}, f32[144,256]{1,0:T(8,128)S(1)}, u32[]{:S(2)}, u32[]{:S(2)}) %collective-permute-start.13) | collective-permute-done | bytes 147488 | tf_op jit(solution)/shard_map/ppermute | solution.py:198
  89.7 1.1 broadcast_in_dim.42
  90.8 4.0 %all-to-all-start.1 = ((bf16[16,144,256]{2,1,0:T(8,128)(2,1)}), bf16[16,144,256]{2,1,0:T(8,128)(2,1)S(1)}, u32[]{:S(2)}, u32[]{:S(2)}) async-start(bf16[16,144,256]{2,1,0:T(8,128)(2,1)} %broadcast_in_dim.42), calls=%async_computation.1 | async-start | bytes 2359296 | tf_op jit(solution)/shard_map/all_to_all | solution.py:201
  94.8 0.7 slice_bitcast_fusion
  95.6 4.8 %collective-permute-start.5 = (bf16[1,2,128,256]{3,2,1,0:T(8,128)(2,1)}, bf16[1,2,128,256]{3,2,1,0:T(8,128)(2,1)S(1)}, u32[]{:S(2)}, u32[]{:S(2)}) collective-permute-start(bf16[1,2,128,256]{3,2,1,0:T(8,128)(2,1)} %get-tuple-element.18), channel_id=1, source_target_pairs={{0,1},{1,2},{2,3},{3,4},{4,5},{5,6},{6,7},{8,9},{9,10},{10,11},{11... | collective-permute-start | bytes 393224 | tf_op jit(solution)/shard_map/ppermute | solution.py:169
  100.3 2.2 %collective-permute-start.6 = (bf16[1,2,128,256]{3,2,1,0:T(8,128)(2,1)}, bf16[1,2,128,256]{3,2,1,0:T(8,128)(2,1)S(1)}, u32[]{:S(2)}, u32[]{:S(2)}) collective-permute-start(bf16[1,2,128,256]{3,2,1,0:T(8,128)(2,1)} %get-tuple-element.17), channel_id=1, source_target_pairs={{0,128},{8,136},{16,144},{24,152},{32,160},{40,168},{48,176},{56,1... | collective-permute-start | bytes 393224 | tf_op jit(solution)/shard_map/ppermute | solution.py:171
  102.5 4.9 %all-to-all-done.1 = bf16[16,144,256]{2,1,0:T(8,128)(2,1)S(1)} async-done(((bf16[16,144,256]{2,1,0:T(8,128)(2,1)}), bf16[16,144,256]{2,1,0:T(8,128)(2,1)S(1)}, u32[]{:S(2)}, u32[]{:S(2)}) %all-to-all-start.1) | async-done | bytes 1179680 | tf_op jit(solution)/shard_map/all_to_all | solution.py:201
  107.4 7.7 %collective-permute-start.14 = (bf16[2304,256]{1,0:T(8,128)(2,1)S(1)}, bf16[2304,256]{1,0:T(8,128)(2,1)}, u32[]{:S(2)}, u32[]{:S(2)}) collective-permute-start(bf16[2304,256]{1,0:T(8,128)(2,1)S(1)} %bitcast.43), channel_id=1, source_target_pairs={{0,8},{8,0},{1,9},{9,1},{2,10},{10,2},{3,11},{11,3},{4,12},{12,4},... | collective-permute-start | bytes 3538952 | tf_op jit(solution)/shard_map/ppermute | solution.py:202
  115.1 1.3 collective-permute-start.7
  116.5 7.4 %collective-permute-done.7.bottom = bf16[1,2,128,256]{3,2,1,0:T(8,128)(2,1)S(1)} collective-permute-done((bf16[1,2,128,256]{3,2,1,0:T(8,128)(2,1)}, bf16[1,2,128,256]{3,2,1,0:T(8,128)(2,1)S(1)}, u32[]{:S(2)}, u32[]{:S(2)}) %collective-permute-start.7) | collective-permute-done | bytes 131104 | tf_op jit(solution)/shard_map/ppermute | solution.py:170
  123.9 5.4 %collective-permute-start.8 = (bf16[1,2,4,16,256]{4,3,1,2,0:T(8,128)(2,1)S(1)}, bf16[1,2,4,16,256]{4,3,1,2,0:T(8,128)(2,1)S(1)}, u32[]{:S(2)}, u32[]{:S(2)}) collective-permute-start(bf16[1,2,4,16,256]{4,3,1,2,0:T(8,128)(2,1)S(1)} %pad_maximum_fusion.3), channel_id=1, source_target_pairs={{0,8},{1,9},{2,10},{3,11},{4,12},{5,13},{6,14},{7,15},{8,16},{9,17... | collective-permute-start | bytes 196616 | tf_op jit(solution)/shard_map/ppermute | solution.py:181
  129.2 0.6 pad_maximum_fusion.4
  129.9 0.7 collective-permute-done.8
  130.6 3.2 %collective-permute-done.9.right = bf16[1,2,4,16,256]{4,3,2,1,0:T(8,128)(2,1)S(1)} collective-permute-done((bf16[1,2,4,16,256]{4,3,2,1,0:T(8,128)(2,1)}, bf16[1,2,4,16,256]{4,3,2,1,0:T(8,128)(2,1)S(1)}, u32[]{:S(2)}, u32[]{:S(2)}) %collective-permute-start.9) | collective-permute-done | bytes 65568 | tf_op jit(solution)/shard_map/ppermute | solution.py:182
  133.8 2.4 %back.1 = bf16[2,2,128,256]{3,2,1,0:T(8,128)(2,1)} custom-call(s32[2]{0:T(128)S(1)} %copy-done.7, s32[2,16,3]{2,1,0:T(8,128)S(1)} %copy.17.strides, bf16[2,2,128,256]{3,2,1,0:T(8,128)(2,1)S(1)} %copy-done.1, bf16[2,2,128,256]{3,2,1,0:T(8,128)(2,1)S(1)} %copy-done.5, bf16[1,2,128,256]{3,2,1,0:T(8,128)(2,1)S(1)} %collective-permute-done.5.down, ...), custom_call_target="tpu_custom_call" | custom-call | tf_op jit(solution)/shard_map/back/pallas_call | solution.py:239
  136.1 3.9 %convert_multiply_fusion = (f32[2304,256]{1,0:T(8,128)}, f32[2304,256]{1,0:T(8,128)}) fusion(bf16[2304,256]{1,0:T(8,128)(2,1)} %collective-permute-done.14, pred[]{:T(512)S(6)} %eq.9, bf16[16,144,256]{2,1,0:T(8,128)(2,1)S(1)} %all-to-all-done.1), kind=kLoop, calls=%fused_computation | loop fusion | flops 3538944 | bytes 7077889 | tf_op jit(solution)/shard_map/mul | solution.py:251
  (34 shorter events, 0.2 us)
Async XLA Ops:
  1.7 6.5 %copy-start.8 = (bf16[1,2,2,128,256]{4,3,1,0,2:T(8,128)(2,1)}, bf16[1,2,2,128,256]{4,3,1,0,2:T(8,128)(2,1)S(1)}, u32[]{:S(2)}) copy-start(bf16[1,2,2,128,256]{4,3,1,0,2:T(8,128)(2,1)S(1)} %get-tuple-element.27) | copy-start | bytes 786436
  1.7 6.5 %copy-start.9 = (bf16[1,2,2,128,256]{4,3,1,0,2:T(8,128)(2,1)}, bf16[1,2,2,128,256]{4,3,1,0,2:T(8,128)(2,1)S(1)}, u32[]{:S(2)}) copy-start(bf16[1,2,2,128,256]{4,3,1,0,2:T(8,128)(2,1)S(1)} %get-tuple-element.28) | copy-start | bytes 786436
  1.7 34.3 %copy-start.2 = (bf16[3,3,256,256]{3,2,1,0:T(8,128)(2,1)S(1)}, bf16[3,3,256,256]{3,2,1,0:T(8,128)(2,1)}, u32[]{:S(2)}) copy-start(bf16[3,3,256,256]{3,2,1,0:T(8,128)(2,1)} %second_kernel.1) | copy-start | bytes 3538948
  2.6 10.9 %collective-permute-start = (bf16[2,2,128,256]{3,2,1,0:T(8,128)(2,1)}, bf16[2,2,128,256]{3,2,1,0:T(8,128)(2,1)S(1)}, u32[]{:S(2)}, u32[]{:S(2)}) collective-permute-start(bf16[2,2,128,256]{3,2,1,0:T(8,128)(2,1)} %get-tuple-element.14), channel_id=1, source_target_pairs={{0,1},{1,2},{2,3},{3,4},{4,5},{5,6},{6,7},{8,9},{9,10},{10,11},{11... | collective-permute-start | bytes 786440 | tf_op jit(solution)/shard_map/ppermute | solution.py:169
  8.2 17.5 %collective-permute-start.1 = (bf16[2,2,128,256]{3,2,1,0:T(8,128)(2,1)}, bf16[2,2,128,256]{3,2,1,0:T(8,128)(2,1)S(1)}, u32[]{:S(2)}, u32[]{:S(2)}) collective-permute-start(bf16[2,2,128,256]{3,2,1,0:T(8,128)(2,1)} %get-tuple-element.13), channel_id=1, source_target_pairs={{0,128},{8,136},{16,144},{24,152},{32,160},{40,168},{48,176},{56,1... | collective-permute-start | bytes 786440 | tf_op jit(solution)/shard_map/ppermute | solution.py:171
  10.6 15.2 %collective-permute-start.2 = (bf16[2,2,128,256]{3,2,1,0:T(8,128)(2,1)}, bf16[2,2,128,256]{3,2,1,0:T(8,128)(2,1)}, u32[]{:S(2)}, u32[]{:S(2)}) collective-permute-start(bf16[2,2,128,256]{3,2,1,0:T(8,128)(2,1)} %get-tuple-element.13), channel_id=1, source_target_pairs={{1,0},{2,1},{3,2},{4,3},{5,4},{6,5},{7,6},{9,8},{10,9},{11,10},{12... | collective-permute-start | bytes 786440 | tf_op jit(solution)/shard_map/ppermute | solution.py:170
  11.9 24.1 %copy-start = (bf16[3,3,256,256]{3,2,1,0:T(8,128)(2,1)S(1)}, bf16[3,3,256,256]{3,2,1,0:T(8,128)(2,1)}, u32[]{:S(2)}) copy-start(bf16[3,3,256,256]{3,2,1,0:T(8,128)(2,1)} %first_kernel.3) | copy-start | bytes 3538948
  11.9 24.1 %copy-start.1 = (bf16[2,2,128,256]{3,2,1,0:T(8,128)(2,1)S(1)}, bf16[2,2,128,256]{3,2,1,0:T(8,128)(2,1)}, u32[]{:S(2)}) copy-start(bf16[2,2,128,256]{3,2,1,0:T(8,128)(2,1)} %grad.3) | copy-start | bytes 786436
  11.9 24.1 %copy-start.3 = (bf16[2,2,128,256]{3,2,1,0:T(8,128)(2,1)S(1)}, bf16[2,2,128,256]{3,2,1,0:T(8,128)(2,1)}, u32[]{:S(2)}) copy-start(bf16[2,2,128,256]{3,2,1,0:T(8,128)(2,1)} %feat.1) | copy-start | bytes 786436
  27.3 5.3 %collective-permute-start.3 = (bf16[2,2,4,16,256]{4,3,1,0,2:T(8,128)(2,1)}, bf16[2,2,4,16,256]{4,3,1,0,2:T(8,128)(2,1)}, u32[]{:S(2)}, u32[]{:S(2)}) collective-permute-start(bf16[2,2,4,16,256]{4,3,1,0,2:T(8,128)(2,1)} %pad_maximum_fusion), channel_id=1, source_target_pairs={{0,8},{1,9},{2,10},{3,11},{4,12},{5,13},{6,14},{7,15},{8,16},{9,17... | collective-permute-start | bytes 393224 | tf_op jit(solution)/shard_map/ppermute | solution.py:181
  31.0 5.0 %collective-permute-start.4 = (bf16[2,2,4,16,256]{4,3,2,1,0:T(8,128)(2,1)}, bf16[2,2,4,16,256]{4,3,2,1,0:T(8,128)(2,1)S(1)}, u32[]{:S(2)}, u32[]{:S(2)}) collective-permute-start(bf16[2,2,4,16,256]{4,3,2,1,0:T(8,128)(2,1)} %pad_maximum_fusion.1), channel_id=1, source_target_pairs={{8,0},{9,1},{10,2},{11,3},{12,4},{13,5},{14,6},{15,7},{16,8},{17,9... | collective-permute-start | bytes 393224 | tf_op jit(solution)/shard_map/ppermute | solution.py:182
  31.8 13.6 %copy-start.6 = (s32[2]{0:T(128)}, s32[2]{0:T(128)S(1)}, u32[]{:S(2)}) copy-start(s32[2]{0:T(128)S(1)} %pad_add_fusion.where) | copy-start | bytes 28
  45.4 6.4 %copy-start.4 = (bf16[2,2,128,256]{3,2,1,0:T(8,128)(2,1)}, bf16[2,2,128,256]{3,2,1,0:T(8,128)(2,1)S(1)}, u32[]{:S(2)}) copy-start(bf16[2,2,128,256]{3,2,1,0:T(8,128)(2,1)S(1)} %get-tuple-element.6.pre) | copy-start | bytes 786436
  45.4 4.4 %collective-permute-start.10 = (bf16[2304,256]{1,0:T(8,128)(2,1)S(1)}, bf16[2304,256]{1,0:T(8,128)(2,1)S(1)}, u32[]{:S(2)}, u32[]{:S(2)}) collective-permute-start(bf16[2304,256]{1,0:T(8,128)(2,1)S(1)} %get-tuple-element.8), channel_id=1, source_target_pairs={{0,8},{8,0},{1,9},{9,1},{2,10},{10,2},{3,11},{11,3},{4,12},{12,4},... | collective-permute-start | bytes 3538952 | tf_op jit(solution)/shard_map/ppermute | solution.py:189
  72.5 4.1 %collective-permute-start.11 = (f32[144,256]{1,0:T(8,128)S(1)}, f32[144,256]{1,0:T(8,128)S(1)}, u32[]{:S(2)}, u32[]{:S(2)}) collective-permute-start(f32[144,256]{1,0:T(8,128)S(1)} %convert_reduce_fusion), channel_id=1, source_target_pairs={{0,16},{16,0},{32,48},{48,32},{64,80},{80,64},{96,112},{112,96},{1... | collective-permute-start | bytes 442376 | tf_op jit(solution)/shard_map/ppermute | solution.py:198
  76.6 7.8 %collective-permute-start.12 = (f32[144,256]{1,0:T(8,128)S(1)}, f32[144,256]{1,0:T(8,128)S(1)}, u32[]{:S(2)}, u32[]{:S(2)}) collective-permute-start(f32[144,256]{1,0:T(8,128)S(1)} %add.19), channel_id=1, source_target_pairs={{0,48},{16,32},{32,16},{48,0},{64,112},{80,96},{96,80},{112,64},{1... | collective-permute-start | bytes 442376 | tf_op jit(solution)/shard_map/ppermute | solution.py:198
  84.4 5.3 %collective-permute-start.13 = (f32[144,256]{1,0:T(8,128)S(1)}, f32[144,256]{1,0:T(8,128)S(1)}, u32[]{:S(2)}, u32[]{:S(2)}) collective-permute-start(f32[144,256]{1,0:T(8,128)S(1)} %add.20), channel_id=1, source_target_pairs={{0,112},{16,96},{32,80},{48,64},{64,48},{80,32},{96,16},{112,0},{1... | collective-permute-start | bytes 442376 | tf_op jit(solution)/shard_map/ppermute | solution.py:198
  90.8 4.0 %copy-start.5 = (bf16[2,2,128,256]{3,2,1,0:T(8,128)(2,1)S(1)}, bf16[2,2,128,256]{3,2,1,0:T(8,128)(2,1)}, u32[]{:S(2)}) copy-start(bf16[2,2,128,256]{3,2,1,0:T(8,128)(2,1)} %copy-done.4) | copy-start | bytes 786436
  90.8 16.6 %all-to-all-start.1 = ((bf16[16,144,256]{2,1,0:T(8,128)(2,1)}), bf16[16,144,256]{2,1,0:T(8,128)(2,1)S(1)}, u32[]{:S(2)}, u32[]{:S(2)}) async-start(bf16[16,144,256]{2,1,0:T(8,128)(2,1)} %broadcast_in_dim.42), calls=%async_computation.1 | async-start | bytes 2359296 | tf_op jit(solution)/shard_map/all_to_all | solution.py:201
  94.8 39.0 %copy-start.7 = (s32[2]{0:T(128)S(1)}, s32[2]{0:T(128)}, u32[]{:S(2)}) copy-start(s32[2]{0:T(128)} %copy-done.6) | copy-start | bytes 28
  95.6 20.9 %collective-permute-start.5 = (bf16[1,2,128,256]{3,2,1,0:T(8,128)(2,1)}, bf16[1,2,128,256]{3,2,1,0:T(8,128)(2,1)S(1)}, u32[]{:S(2)}, u32[]{:S(2)}) collective-permute-start(bf16[1,2,128,256]{3,2,1,0:T(8,128)(2,1)} %get-tuple-element.18), channel_id=1, source_target_pairs={{0,1},{1,2},{2,3},{3,4},{4,5},{5,6},{6,7},{8,9},{9,10},{10,11},{11... | collective-permute-start | bytes 393224 | tf_op jit(solution)/shard_map/ppermute | solution.py:169
  100.3 16.1 %collective-permute-start.6 = (bf16[1,2,128,256]{3,2,1,0:T(8,128)(2,1)}, bf16[1,2,128,256]{3,2,1,0:T(8,128)(2,1)S(1)}, u32[]{:S(2)}, u32[]{:S(2)}) collective-permute-start(bf16[1,2,128,256]{3,2,1,0:T(8,128)(2,1)} %get-tuple-element.17), channel_id=1, source_target_pairs={{0,128},{8,136},{16,144},{24,152},{32,160},{40,168},{48,176},{56,1... | collective-permute-start | bytes 393224 | tf_op jit(solution)/shard_map/ppermute | solution.py:171
  107.4 28.7 %collective-permute-start.14 = (bf16[2304,256]{1,0:T(8,128)(2,1)S(1)}, bf16[2304,256]{1,0:T(8,128)(2,1)}, u32[]{:S(2)}, u32[]{:S(2)}) collective-permute-start(bf16[2304,256]{1,0:T(8,128)(2,1)S(1)} %bitcast.43), channel_id=1, source_target_pairs={{0,8},{8,0},{1,9},{9,1},{2,10},{10,2},{3,11},{11,3},{4,12},{12,4},... | collective-permute-start | bytes 3538952 | tf_op jit(solution)/shard_map/ppermute | solution.py:202
  115.1 8.7 %collective-permute-start.7 = (bf16[1,2,128,256]{3,2,1,0:T(8,128)(2,1)}, bf16[1,2,128,256]{3,2,1,0:T(8,128)(2,1)S(1)}, u32[]{:S(2)}, u32[]{:S(2)}) collective-permute-start(bf16[1,2,128,256]{3,2,1,0:T(8,128)(2,1)} %get-tuple-element.17), channel_id=1, source_target_pairs={{1,0},{2,1},{3,2},{4,3},{5,4},{6,5},{7,6},{9,8},{10,9},{11,10},{12... | collective-permute-start | bytes 393224 | tf_op jit(solution)/shard_map/ppermute | solution.py:170
  123.9 6.7 %collective-permute-start.8 = (bf16[1,2,4,16,256]{4,3,1,2,0:T(8,128)(2,1)S(1)}, bf16[1,2,4,16,256]{4,3,1,2,0:T(8,128)(2,1)S(1)}, u32[]{:S(2)}, u32[]{:S(2)}) collective-permute-start(bf16[1,2,4,16,256]{4,3,1,2,0:T(8,128)(2,1)S(1)} %pad_maximum_fusion.3), channel_id=1, source_target_pairs={{0,8},{1,9},{2,10},{3,11},{4,12},{5,13},{6,14},{7,15},{8,16},{9,17... | collective-permute-start | bytes 196616 | tf_op jit(solution)/shard_map/ppermute | solution.py:181
  129.9 3.9 %collective-permute-start.9 = (bf16[1,2,4,16,256]{4,3,2,1,0:T(8,128)(2,1)}, bf16[1,2,4,16,256]{4,3,2,1,0:T(8,128)(2,1)S(1)}, u32[]{:S(2)}, u32[]{:S(2)}) collective-permute-start(bf16[1,2,4,16,256]{4,3,2,1,0:T(8,128)(2,1)} %pad_maximum_fusion.4), channel_id=1, source_target_pairs={{8,0},{9,1},{10,2},{11,3},{12,4},{13,5},{14,6},{15,7},{16,8},{17,9... | collective-permute-start | bytes 196616 | tf_op jit(solution)/shard_map/ppermute | solution.py:182

commit v2 on v1

--- a/solution.py
+++ b/solution.py
@@ -1,4 +1,3 @@
-import functools
 import math
 
 import jax
@@ -24,21 +23,22 @@
     return lax.dot_general(a, b, dims, preferred_element_type=jnp.float32)
 
 
-def fill(ext, field, own, down, cross, bottom, left, right, mirror):
+def fill(ext, field, own, halo, where):
+    pair, next_pair, in_chip, next_chip = halo
     width = own.shape[2]
+    odd, core = where[2] == 1, where[1] == 1
     for s in range(2):
         for row in range(4):
             place = ext.at[s * 4 + row]
-            if row == 0:
-                above, across = down[field, s].astype(jnp.float32), cross[field, s].astype(jnp.float32)
-                middle = jnp.where(mirror, across, above)
-            elif row == 3:
-                middle = bottom[field, s].astype(jnp.float32)
+            if row in (0, 3):
+                one, other = pair[field, s].astype(jnp.float32), next_pair[field, s].astype(jnp.float32)
+                middle = jnp.where(odd, one, other) if row == 0 else jnp.where(odd, other, one)
             else:
                 middle = own[s, row - 1].astype(jnp.float32)
-            place[:SPAN] = left[field, s, row].astype(jnp.float32)
+            near, far = in_chip[field, s, row].astype(jnp.float32), next_chip[field, s, row].astype(jnp.float32)
+            place[:SPAN] = jnp.where(core, near, far)
             place[SPAN : SPAN + width] = middle
-            place[SPAN + width : 2 * SPAN + width] = right[field, s, row].astype(jnp.float32)
+            place[SPAN + width : 2 * SPAN + width] = jnp.where(core, far, near)
 
 
 def tap(ext, s, row, shift, width):
@@ -89,13 +89,14 @@
     return total
 
 
-def main_kernel(where, strides, feat, grad, down, cross, bottom, left, right, first_kernel, second_kernel,
+def main_kernel(where, strides, feat, grad, pair, next_pair, in_chip, next_chip, first_kernel, second_kernel,
                 keep, send, pre_grad, ext_f, ext_g, taps_f, taps_g, act):
     lat, core = where[0], where[1]
     mirror = lat == 0
     width = feat.shape[2]
     half = 2 * width
-    fill(ext_f, 0, feat, down, cross, bottom, left, right, mirror)
+    halo = (pair, next_pair, in_chip, next_chip)
+    fill(ext_f, 0, feat, halo, where)
     for row in range(2):
         for s in range(2):
             at = (row * 2 + s) * width
@@ -104,7 +105,7 @@
                 for col in range(3):
                     shift = 0 if col == 1 else (col - 1) * stride
                     taps_f[k * 3 + col, at : at + width] = tap(ext_f, s, row + k, shift, width)
-    fill(ext_g, 1, grad, down, cross, bottom, left, right, mirror)
+    fill(ext_g, 1, grad, halo, where)
     adjoint_taps(ext_g, taps_g, strides, lat, width)
 
     for row in range(2):
@@ -149,11 +150,11 @@
             place(dot(taps_f[k * 3 + col], pre_all, TN), k, col, 0)
 
 
-def back_kernel(where, strides, grad, pre, down, cross, bottom, left, right, first_kernel, out, ext, taps):
+def back_kernel(where, strides, grad, pre, pair, next_pair, in_chip, next_chip, first_kernel, out, ext, taps):
     lat = where[0]
     mirror = lat == 0
     width = grad.shape[2]
-    fill(ext, 0, pre, down, cross, bottom, left, right, mirror)
+    fill(ext, 0, pre, (pair, next_pair, in_chip, next_chip), where)
     adjoint_taps(ext, taps, strides, lat, width)
     for row in range(2):
         total = adjoint_product(taps, first_kernel, mirror, row, 2 * width)
@@ -162,54 +163,56 @@
             out[s, row] = (own + total[s * width : (s + 1) * width]).astype(jnp.bfloat16)
 
 
-def halos(fields, lon_count, lat_count):
-    n, _, _, width, _ = fields.shape
+def both_ways(pairs):
+    return pairs + [(b, a) for a, b in pairs]
+
+
+def row_halos(fields, lon_count, lat_count):
     at = lambda lon, lat: (lon % lon_count) * lat_count + lat
     lons = range(lon_count)
-    down = lax.ppermute(fields[:, :, 1], ALL, [(at(i, k), at(i, k + 1)) for i in lons for k in range(lat_count - 1)])
-    bottom = lax.ppermute(fields[:, :, 0], ALL, [(at(i, k + 1), at(i, k)) for i in lons for k in range(lat_count - 1)])
-    cross = lax.ppermute(fields[:, :, 0], ALL, [(at(i, 0), at(i + lon_count // 2, 0)) for i in lons])
-    lat = lax.axis_index(("x", "yh"))
-    top = jnp.where(lat == 0, cross, down)
-
-    def edge(cut):
-        return jnp.concatenate([cut(top)[:, :, None], cut(fields), cut(bottom)[:, :, None]], axis=2)
-
-    head = edge(lambda a: lax.slice_in_dim(a, 0, SPAN, axis=a.ndim - 2))
-    tail = edge(lambda a: lax.slice_in_dim(a, width - SPAN, width, axis=a.ndim - 2))
-    lats = range(lat_count)
-    left = lax.ppermute(tail, ALL, [(at(i, k), at(i + 1, k)) for i in lons for k in lats])
-    right = lax.ppermute(head, ALL, [(at(i + 1, k), at(i, k)) for i in lons for k in lats])
-    return down, cross, bottom, left, right
-
-
-def summed(keep, send):
-    core = lax.axis_index("core")
-    swap = [(0, 1), (1, 0)]
-    total = keep + lax.ppermute(send, "core", swap).astype(jnp.float32)
-    planes = lax.axis_size(PLANE)
-    rows, cols = total.shape
-    spread = lax.all_to_all(total.astype(jnp.bfloat16).reshape(planes, rows // planes, cols), PLANE, 0, 0, tiled=True)
-    part = jnp.sum(spread.astype(jnp.float32), axis=0)
-    count = lax.axis_size("z")
-    reach = 1
-    while reach < count:
-        reach *= 2
-        part = part + lax.ppermute(part, "z", [(i, i ^ (reach - 1)) for i in range(count)])
-    part = part.astype(jnp.bfloat16)
-    copies = jnp.broadcast_to(part[None], (planes,) + part.shape)
-    mine = lax.all_to_all(copies, PLANE, 0, 0, tiled=True).reshape(rows, cols)
-    other = lax.ppermute(mine, "core", swap)
-    first = jnp.where(core == 0, mine, other).astype(jnp.float32)
-    second = jnp.where(core == 0, other, mine).astype(jnp.float32)
-    return first, second
+    odd = lax.rem(lax.axis_index(("x", "yh")), 2)
+    row = lambda i: lax.dynamic_index_in_dim(fields, i, 2, keepdims=False)
+    pair = lax.ppermute(row(1 - odd), ALL, both_ways([(at(i, k), at(i, k + 1)) for i in lons for k in range(0, lat_count, 2)]))
+    between = both_ways([(at(i, k), at(i, k + 1)) for i in lons for k in range(1, lat_count - 1, 2)])
+    across = [(at(i, 0), at(i + lon_count // 2, 0)) for i in lons]
+    return pair, lax.ppermute(row(odd), ALL, between + across)
+
+
+def column_halos(fields, pair, next_pair, lon_count, lat_count):
+    width = fields.shape[3]
+    at = lambda lon, lat: (lon % lon_count) * lat_count + lat
+    odd, core = lax.rem(lax.axis_index(("x", "yh")), 2) == 1, lax.axis_index("core")
+
+    def edge(start):
+        cut = lambda a: lax.dynamic_slice_in_dim(a, start, SPAN, a.ndim - 2)
+        one, other = cut(pair), cut(next_pair)
+        top, bottom = jnp.where(odd, one, other), jnp.where(odd, other, one)
+        return jnp.concatenate([top[:, :, None], cut(fields), bottom[:, :, None]], axis=2)
+
+    reach = width - SPAN
+    places = [(i, k) for i in range(0, lon_count, 2) for k in range(lat_count)]
+    next_chip = lax.ppermute(edge(core * reach), ALL, both_ways([(at(i + 1, k), at(i + 2, k)) for i, k in places]))
+    in_chip = lax.ppermute(edge((1 - core) * reach), "core", [(0, 1), (1, 0)])
+    return in_chip, next_chip
+
+
+def folded(count, cores, reach):
+    pairs = []
+    for i in range(count):
+        for core in range(cores):
+            turn = 2 * core
+            base = (i + turn) % count
+            partner = base ^ (reach - 1 if reach == count else reach // 2)
+            pairs.append((i * cores + core, (partner - turn) % count * cores + core))
+    return pairs
 
 
 def local(features, out_grad, first_kernel, second_kernel, strides):
     slabs, rows, width, chans = features.shape
     lat_axes, lon_axes = ("x", "yh"), ("yl", "z", "core")
     lat_count, lon_count = lax.axis_size(lat_axes), lax.axis_size(lon_axes)
-    where = jnp.stack([lax.axis_index(lat_axes), lax.axis_index("core")]).astype(jnp.int32)
+    lat, core = lax.axis_index(lat_axes), lax.axis_index("core")
+    where = jnp.stack([lat, core, lax.rem(lat, 2)]).astype(jnp.int32)
     smem = pl.BlockSpec(memory_space=pltpu.SMEM)
     vmem = pl.BlockSpec(memory_space=pltpu.VMEM)
     cells = slabs * rows * width
@@ -217,8 +220,11 @@
     taps = pltpu.VMEM((9, cells, chans), jnp.bfloat16)
     params = pltpu.CompilerParams(vmem_limit_bytes=48 * 1024 * 1024)
     grads = (9 * chans, chans)
-
-    around = halos(jnp.stack([features, out_grad]), lon_count, lat_count)
+    swap = [(0, 1), (1, 0)]
+
+    fields = jnp.stack([features, out_grad])
+    around = row_halos(fields, lon_count, lat_count)
+    around += column_halos(fields, *around, lon_count, lat_count)
     keep, send, pre_grad = pl.pallas_call(
         main_kernel,
         out_shape=[
@@ -226,29 +232,48 @@
             jax.ShapeDtypeStruct(grads, jnp.bfloat16),
             jax.ShapeDtypeStruct(features.shape, jnp.bfloat16),
         ],
-        in_specs=[smem, smem] + [vmem] * 9,
+        in_specs=[smem, smem] + [vmem] * 8,
         out_specs=[vmem] * 3,
         scratch_shapes=[ext, ext, taps, taps, pltpu.VMEM((cells, chans), jnp.bfloat16)],
         compiler_params=params,
         name="main",
     )(where, strides, features, out_grad, *around, first_kernel, second_kernel)
 
-    first, second = summed(keep, send)
-
-    around = halos(pre_grad[None], lon_count, lat_count)
-    input_grad = pl.pallas_call(
-        back_kernel,
-        out_shape=jax.ShapeDtypeStruct(features.shape, jnp.bfloat16),
-        in_specs=[smem, smem] + [vmem] * 8,
-        out_specs=vmem,
-        scratch_shapes=[ext, taps],
-        compiler_params=params,
-        name="back",
-    )(where, strides, out_grad, pre_grad, *around, first_kernel)
-
+    total = keep + lax.ppermute(send, "core", swap).astype(jnp.float32)
+    planes, height, cores = lax.axis_size(PLANE), lax.axis_size("z"), lax.axis_size("core")
+    total = total.astype(jnp.bfloat16).reshape(planes, 9 * chans // planes, chans)
+    spread = lax.all_to_all(total, PLANE, 0, 0, tiled=True)
+
+    pre_field = pre_grad[None]
+    around = row_halos(pre_field, lon_count, lat_count)
+    spread, around = lax.optimization_barrier((spread, around))
+    around += column_halos(pre_field, *around, lon_count, lat_count)
+
+    part = jnp.sum(spread.astype(jnp.float32), axis=0)
+    reach = 2
+    while reach <= height:
+        part = part + lax.ppermute(part, ("z", "core"), folded(height, cores, reach))
+        if reach == 2:
+            part, around = lax.optimization_barrier((part, around))
+            input_grad = pl.pallas_call(
+                back_kernel,
+                out_shape=jax.ShapeDtypeStruct(features.shape, jnp.bfloat16),
+                in_specs=[smem, smem] + [vmem] * 7,
+                out_specs=vmem,
+                scratch_shapes=[ext, taps],
+                compiler_params=params,
+                name="back",
+            )(where, strides, out_grad, pre_grad, *around, first_kernel)
+        reach *= 2
+    part, input_grad = lax.optimization_barrier((part.astype(jnp.bfloat16), input_grad))
+
+    copies = jnp.broadcast_to(part[None], (planes,) + part.shape)
+    mine = lax.all_to_all(copies, PLANE, 0, 0, tiled=True).reshape(grads)
+    other = lax.ppermute(mine, "core", swap)
     scale = 1.0 / math.sqrt(cells * lat_count * lon_count)
-    shape = first_kernel.shape
-    return input_grad, (first * scale).reshape(shape), (second * scale).reshape(shape)
+    first = jnp.where(core == 0, mine, other).astype(jnp.float32) * scale
+    second = jnp.where(core == 0, other, mine).astype(jnp.float32) * scale
+    return input_grad, first.reshape(first_kernel.shape), second.reshape(first_kernel.shape)
 
 
 def solution(mesh):

time: 141 us -> 128 us (0.908)
  starting transfers between devices: 45.9 us -> 37.6 us
  local copies, waits for them, and re-layouts: 5.43 us -> 1.49 us
  waiting for transfers between devices: 45.5 us -> 48.1 us
    ppermute x15 -> x13, starting transfers between devices: 42 us -> 31.9 us  [the longest x2 7.25 us: row_halos(): return (pair, lax.ppermute(row(odd), ALL, between + across))]
    ppermute x15 -> x13, waiting for transfers between devices: 40.6 us -> 48 us  [the longest x2 22.2 us: row_halos(): return (pair, lax.ppermute(row(odd), ALL, between + across))]
    all_to_all x1, waiting for transfers between devices: 4.91 us -> 0.01 us  [local(): spread = lax.all_to_all(total, PLANE, 0, 0, tiled=True)]
    concatenate x4, other arithmetic: 1.98 us -> 0.06 us  [edge(): jnp.concatenate([top[:, :, None], cut(fields), bottom[:, :, None]], axis=2)]
    all_to_all x1, starting transfers between devices: 3.95 us -> 5.77 us  [local(): spread = lax.all_to_all(total, PLANE, 0, 0, tiled=True)]
    broadcast_in_dim x5 -> x1, local copies, waits for them, and re-layouts: 1.89 us -> 0.08 us  [local(): copies = jnp.broadcast_to(part[None], (planes,) + part.shape)]
  transfers between devices with their start and end apart: 16 -> 14, of which waited for: 12 -> 11; matrix products, arithmetic and copies ran while one was open for 3% -> 0% of each run, Pallas kernels for 2% -> 2%
where the time goes in v2:
time: 128 us; the launch traced here: 127 us
  waiting for transfers between devices  48.1 us (38%)
  starting transfers between devices  37.6 us (29%)
  blocking collectives  19.2 us (15%)
  Pallas kernels  11.7 us (9%)
  other arithmetic  8.61 us (7%)
  local copies, waits for them, and re-layouts  1.49 us (1%)
    ppermute x2, waiting for transfers between devices, row_halos(): return (pair, lax.ppermute(row(odd), ALL, between + across))  22.2 us
    all_to_all x1, blocking collectives, local(): mine = lax.all_to_all(copies, PLANE, 0, 0, tiled=True).reshape(grads)  19.2 us
    ppermute x3, waiting for transfers between devices, local(): lax.ppermute(part, ('z', 'core'), folded(height, cores, reach))  11.1 us
    pallas_call x1, Pallas kernels, local(): pl.pallas_call(main_kernel, out_shape=[jax.ShapeDtypeStruct(grads, jnp.fl...  9.3 us
    ppermute x2, starting transfers between devices, row_halos(): return (pair, lax.ppermute(row(odd), ALL, between + across))  7.25 us
    ppermute x2, waiting for transfers between devices, row_halos(): lax.ppermute(row(1 - odd), ALL, both_ways([(at(i, k), at(i, k + 1)) for i...  6.28 us
    all_to_all x1, starting transfers between devices, local(): spread = lax.all_to_all(total, PLANE, 0, 0, tiled=True)  5.77 us
    ppermute x2, starting transfers between devices, row_halos(): lax.ppermute(row(1 - odd), ALL, both_ways([(at(i, k), at(i, k + 1)) for i...  5.46 us
  transfers between devices with their start and end apart: 14, of which 11 were waited for; matrix products, arithmetic and copies ran while one was open for 0% of the time, Pallas kernels for 2%

profile of v2, /device:TPU:1, one launch (start us, length us, event | category | flops | bytes accessed | tf_op | source)
XLA Modules:
  0.0 127.4 jit_solution(16315340294380170583)
XLA Ops:
  0.6 0.0 copy-start.1
  0.6 0.0 copy-start.2
  0.7 0.0 copy-start.4
  0.7 0.0 copy-start
  0.7 1.3 fusion.3
  2.0 4.0 %collective-permute-start.1 = (bf16[2,2,128,256]{3,2,1,0:T(8,128)(2,1)S(1)}, bf16[2,2,128,256]{3,2,1,0:T(8,128)(2,1)S(1)}, u32[]{:S(2)}, u32[]{:S(2)}) collective-permute-start(bf16[2,2,128,256]{3,2,1,0:T(8,128)(2,1)S(1)} %get-tuple-element.37), channel_id=1, source_target_pairs={{1,2},{3,4},{5,6},{9,10},{11,12},{13,14},{17,18},{19,20},{21,22},{... | collective-permute-start | bytes 786440 | tf_op jit(solution)/shard_map/ppermute | solution.py:178
  6.0 2.7 %collective-permute-start = (bf16[2,2,128,256]{3,2,1,0:T(8,128)(2,1)S(1)}, bf16[2,2,128,256]{3,2,1,0:T(8,128)(2,1)S(1)}, u32[]{:S(2)}, u32[]{:S(2)}) collective-permute-start(bf16[2,2,128,256]{3,2,1,0:T(8,128)(2,1)S(1)} %get-tuple-element.38), channel_id=1, source_target_pairs={{0,1},{2,3},{4,5},{6,7},{8,9},{10,11},{12,13},{14,15},{16,17},{18,... | collective-permute-start | bytes 786440 | tf_op jit(solution)/shard_map/ppermute | solution.py:175
  8.7 0.0 copy-done.1
  8.7 0.0 copy-done.2
  8.7 7.7 %collective-permute-done.1.next_pair = bf16[2,2,128,256]{3,2,1,0:T(8,128)(2,1)S(1)} collective-permute-done((bf16[2,2,128,256]{3,2,1,0:T(8,128)(2,1)S(1)}, bf16[2,2,128,256]{3,2,1,0:T(8,128)(2,1)S(1)}, u32[]{:S(2)}, u32[]{:S(2)}) %collective-permute-start.1) | collective-permute-done | bytes 262176 | tf_op jit(solution)/shard_map/ppermute | solution.py:178
  16.4 5.6 %collective-permute-done.pair = bf16[2,2,128,256]{3,2,1,0:T(8,128)(2,1)S(1)} collective-permute-done((bf16[2,2,128,256]{3,2,1,0:T(8,128)(2,1)S(1)}, bf16[2,2,128,256]{3,2,1,0:T(8,128)(2,1)S(1)}, u32[]{:S(2)}, u32[]{:S(2)}) %collective-permute-start) | collective-permute-done | bytes 262176 | tf_op jit(solution)/shard_map/ppermute | solution.py:175
  22.0 1.8 %collective-permute-start.2 = (bf16[2,2,4,16,256]{4,3,2,1,0:T(8,128)(2,1)S(1)}, bf16[2,2,4,16,256]{4,3,2,1,0:T(8,128)(2,1)S(1)}, u32[]{:S(2)}, u32[]{:S(2)}) collective-permute-start(bf16[2,2,4,16,256]{4,3,2,1,0:T(8,128)(2,1)S(1)} %pad_maximum_fusion), channel_id=1, source_target_pairs={{0,8},{8,0},{1,9},{9,1},{2,10},{10,2},{3,11},{11,3},{4,12},{12,4},... | collective-permute-start | bytes 393224 | tf_op jit(solution)/shard_map/ppermute | solution.py:195
  23.9 1.6 %collective-permute-start.3 = (bf16[2,2,4,16,256]{4,3,2,1,0:T(8,128)(2,1)S(1)}, bf16[2,2,4,16,256]{4,3,2,1,0:T(8,128)(2,1)S(1)}, u32[]{:S(2)}, u32[]{:S(2)}) collective-permute-start(bf16[2,2,4,16,256]{4,3,2,1,0:T(8,128)(2,1)S(1)} %pad_maximum_fusion.1), channel_id=1, source_target_pairs={{8,16},{9,17},{10,18},{11,19},{12,20},{13,21},{14,22},{15,23},{24,... | collective-permute-start | bytes 393224 | tf_op jit(solution)/shard_map/ppermute | solution.py:194
  25.5 0.0 copy-done.4
  25.5 0.1 copy.11.strides
  25.6 0.1 pad_add_fusion.where
  25.7 0.0 collective-permute-done.2.in_chip
  25.7 2.7 %collective-permute-done.3.next_chip = bf16[2,2,4,16,256]{4,3,2,1,0:T(8,128)(2,1)S(1)} collective-permute-done((bf16[2,2,4,16,256]{4,3,2,1,0:T(8,128)(2,1)S(1)}, bf16[2,2,4,16,256]{4,3,2,1,0:T(8,128)(2,1)S(1)}, u32[]{:S(2)}, u32[]{:S(2)}) %collective-permute-start.3) | collective-permute-done | bytes 131104 | tf_op jit(solution)/shard_map/ppermute | solution.py:194
  28.4 0.0 copy-done
  28.4 0.0 copy-start.3
  28.4 1.3 copy-done.3
  29.6 9.3 %main.1 = (f32[2304,256]{1,0:T(8,128)}, bf16[2304,256]{1,0:T(8,128)(2,1)S(1)}, bf16[2,2,128,256]{3,2,1,0:T(8,128)(2,1)S(1)}) custom-call(s32[3]{0:T(128)S(1)} %pad_add_fusion.where, s32[2,16,3]{2,1,0:T(8,128)S(1)} %copy.11.strides, bf16[2,2,128,256]{3,2,1,0:T(8,128)(2,1)S(1)} %copy-done.2, bf16[2,2,128,256]{3,2,1,0:T(8,128)(2,1)S(1)} %copy-done.1, ...), custom_call_target="tpu_custom_call" | custom-call | tf_op jit(solution)/shard_map/main/pallas_call | solution.py:228
  38.9 4.1 %collective-permute-start.4 = (bf16[2304,256]{1,0:T(8,128)(2,1)S(1)}, bf16[2304,256]{1,0:T(8,128)(2,1)S(1)}, u32[]{:S(2)}, u32[]{:S(2)}) collective-permute-start(bf16[2304,256]{1,0:T(8,128)(2,1)S(1)} %get-tuple-element.17), channel_id=1, source_target_pairs={{0,8},{8,0},{1,9},{9,1},{2,10},{10,2},{3,11},{11,3},{4,12},{12,4},... | collective-permute-start | bytes 3538952 | tf_op jit(solution)/shard_map/ppermute | solution.py:242
  43.0 2.5 %collective-permute-done.4 = bf16[2304,256]{1,0:T(8,128)(2,1)S(1)} collective-permute-done((bf16[2304,256]{1,0:T(8,128)(2,1)S(1)}, bf16[2304,256]{1,0:T(8,128)(2,1)S(1)}, u32[]{:S(2)}, u32[]{:S(2)}) %collective-permute-start.4) | collective-permute-done | bytes 1179680 | tf_op jit(solution)/shard_map/ppermute | solution.py:242
  45.5 2.9 %add_convert_fusion = bf16[2304,256]{1,0:T(8,128)(2,1)} fusion(f32[2304,256]{1,0:T(8,128)} %get-tuple-element.16, bf16[2304,256]{1,0:T(8,128)(2,1)S(1)} %collective-permute-done.4), kind=kLoop, calls=%fused_computation.3 | loop fusion | flops 1769472 | bytes 4718592 | tf_op jit(solution)/shard_map/convert_element_type | solution.py:244
  48.4 5.8 %all-to-all-start = ((bf16[16,144,256]{2,1,0:T(8,128)(2,1)}), bf16[16,144,256]{2,1,0:T(8,128)(2,1)}, u32[]{:S(2)}, u32[]{:S(2)}) async-start(bf16[16,144,256]{2,1,0:T(8,128)(2,1)} %bitcast.14), calls=%async_computation | async-start | bytes 2359296 | tf_op jit(solution)/shard_map/all_to_all | solution.py:245
  54.3 3.2 %collective-permute-start.6 = (bf16[1,2,128,256]{3,2,1,0:T(8,128)(2,1)S(1)}, bf16[1,2,128,256]{3,2,1,0:T(8,128)(2,1)S(1)}, u32[]{:S(2)}, u32[]{:S(2)}) collective-permute-start(bf16[1,2,128,256]{3,2,1,0:T(8,128)(2,1)S(1)} %get-tuple-element.45), channel_id=1, source_target_pairs={{1,2},{3,4},{5,6},{9,10},{11,12},{13,14},{17,18},{19,20},{21,22},{... | collective-permute-start | bytes 393224 | tf_op jit(solution)/shard_map/ppermute | solution.py:178
  57.5 2.8 %collective-permute-start.5 = (bf16[1,2,128,256]{3,2,1,0:T(8,128)(2,1)S(1)}, bf16[1,2,128,256]{3,2,1,0:T(8,128)(2,1)S(1)}, u32[]{:S(2)}, u32[]{:S(2)}) collective-permute-start(bf16[1,2,128,256]{3,2,1,0:T(8,128)(2,1)S(1)} %get-tuple-element.46), channel_id=1, source_target_pairs={{0,1},{2,3},{4,5},{6,7},{8,9},{10,11},{12,13},{14,15},{16,17},{18,... | collective-permute-start | bytes 393224 | tf_op jit(solution)/shard_map/ppermute | solution.py:175
  60.3 14.5 %collective-permute-done.6.next_pair = bf16[1,2,128,256]{3,2,1,0:T(8,128)(2,1)S(1)} collective-permute-done((bf16[1,2,128,256]{3,2,1,0:T(8,128)(2,1)S(1)}, bf16[1,2,128,256]{3,2,1,0:T(8,128)(2,1)S(1)}, u32[]{:S(2)}, u32[]{:S(2)}) %collective-permute-start.6) | collective-permute-done | bytes 131104 | tf_op jit(solution)/shard_map/ppermute | solution.py:178
  74.8 0.7 collective-permute-done.5.pair
  75.5 0.0 all-to-all-done
  75.5 1.4 %convert_reduce_fusion = f32[144,256]{1,0:T(8,128)S(1)} fusion(bf16[16,144,256]{2,1,0:T(8,128)(2,1)} %all-to-all-done), kind=kLoop, calls=%fused_computation.2 | loop fusion | flops 1142784 | bytes 1327104 | tf_op jit(solution)/shard_map/reduce_sum | solution.py:252
  77.0 2.1 %collective-permute-start.8 = (bf16[1,2,4,16,256]{4,3,2,1,0:T(8,128)(2,1)S(1)}, bf16[1,2,4,16,256]{4,3,2,1,0:T(8,128)(2,1)S(1)}, u32[]{:S(2)}, u32[]{:S(2)}) collective-permute-start(bf16[1,2,4,16,256]{4,3,2,1,0:T(8,128)(2,1)S(1)} %pad_maximum_fusion.2), channel_id=1, source_target_pairs={{0,8},{8,0},{1,9},{9,1},{2,10},{10,2},{3,11},{11,3},{4,12},{12,4},... | collective-permute-start | bytes 196616 | tf_op jit(solution)/shard_map/ppermute | solution.py:195
  79.0 0.0 collective-permute-start.7
  79.1 1.8 %collective-permute-start.9 = (bf16[1,2,4,16,256]{4,3,2,1,0:T(8,128)(2,1)S(1)}, bf16[1,2,4,16,256]{4,3,2,1,0:T(8,128)(2,1)S(1)}, u32[]{:S(2)}, u32[]{:S(2)}) collective-permute-start(bf16[1,2,4,16,256]{4,3,2,1,0:T(8,128)(2,1)S(1)} %pad_maximum_fusion.3), channel_id=1, source_target_pairs={{8,16},{9,17},{10,18},{11,19},{12,20},{13,21},{14,22},{15,23},{24,... | collective-permute-start | bytes 196616 | tf_op jit(solution)/shard_map/ppermute | solution.py:194
  80.9 3.6 %collective-permute-done.7 = f32[144,256]{1,0:T(8,128)S(1)} collective-permute-done((f32[144,256]{1,0:T(8,128)S(1)}, f32[144,256]{1,0:T(8,128)S(1)}, u32[]{:S(2)}, u32[]{:S(2)}) %collective-permute-start.7) | collective-permute-done | bytes 147488 | tf_op jit(solution)/shard_map/ppermute | solution.py:255
  84.5 0.0 collective-permute-done.8.in_chip
  84.5 0.9 collective-permute-done.9.next_chip
  85.3 2.2 %collective-permute-start.10 = (f32[144,256]{1,0:T(8,128)S(1)}, f32[144,256]{1,0:T(8,128)S(1)}, u32[]{:S(2)}, u32[]{:S(2)}) collective-permute-start(f32[144,256]{1,0:T(8,128)S(1)} %add.52), channel_id=1, source_target_pairs={{0,32},{8,104},{16,48},{24,120},{32,0},{40,72},{48,16},{56,88},{64... | collective-permute-start | bytes 442376 | tf_op jit(solution)/shard_map/ppermute | solution.py:255
  87.6 4.0 %collective-permute-done.10 = f32[144,256]{1,0:T(8,128)S(1)} collective-permute-done((f32[144,256]{1,0:T(8,128)S(1)}, f32[144,256]{1,0:T(8,128)S(1)}, u32[]{:S(2)}, u32[]{:S(2)}) %collective-permute-start.10) | collective-permute-done | bytes 147488 | tf_op jit(solution)/shard_map/ppermute | solution.py:255
  91.6 0.1 collective-permute-start.11
  91.7 2.4 %back.1 = bf16[2,2,128,256]{3,2,1,0:T(8,128)(2,1)} custom-call(s32[3]{0:T(128)S(1)} %pad_add_fusion.where, s32[2,16,3]{2,1,0:T(8,128)S(1)} %copy.11.strides, bf16[2,2,128,256]{3,2,1,0:T(8,128)(2,1)S(1)} %copy-done.1, bf16[2,2,128,256]{3,2,1,0:T(8,128)(2,1)S(1)} %get-tuple-element.18.pre, bf16[1,2,128,256]{3,2,1,0:T(8,128)(2,1)S(1)} %collective-permute-done.5.pair, ...), custom_call_target="tpu_custom_call" | custom-call | tf_op jit(solution)/shard_map/back/pallas_call | solution.py:258
  94.0 3.5 %collective-permute-done.11 = f32[144,256]{1,0:T(8,128)S(1)} collective-permute-done((f32[144,256]{1,0:T(8,128)S(1)}, f32[144,256]{1,0:T(8,128)S(1)}, u32[]{:S(2)}, u32[]{:S(2)}) %collective-permute-start.11) | collective-permute-done | bytes 147488 | tf_op jit(solution)/shard_map/ppermute | solution.py:255
  97.6 0.1 broadcast_in_dim.39
  97.7 19.2 %all_to_all.10 = bf16[16,144,256]{2,1,0:T(8,128)(2,1)S(1)} all-to-all(bf16[16,144,256]{2,1,0:T(8,128)(2,1)S(1)} %broadcast_in_dim.39), channel_id=1, replica_groups=mesh['yl'=2,'z'=8,'core'=2,'x'=4,'yh'=2] {'x','yh','yl'}, dimensions={0} | all-to-all | bytes 2359296 | tf_op jit(solution)/shard_map/all_to_all | solution.py:271
  116.8 5.4 %collective-permute-start.12 = (bf16[2304,256]{1,0:T(8,128)(2,1)S(1)}, bf16[2304,256]{1,0:T(8,128)(2,1)S(1)}, u32[]{:S(2)}, u32[]{:S(2)}) collective-permute-start(bf16[2304,256]{1,0:T(8,128)(2,1)S(1)} %bitcast.55), channel_id=1, source_target_pairs={{0,8},{8,0},{1,9},{9,1},{2,10},{10,2},{3,11},{11,3},{4,12},{12,4},... | collective-permute-start | bytes 3538952 | tf_op jit(solution)/shard_map/ppermute | solution.py:272
  122.2 2.5 %collective-permute-done.12 = bf16[2304,256]{1,0:T(8,128)(2,1)S(1)} collective-permute-done((bf16[2304,256]{1,0:T(8,128)(2,1)S(1)}, bf16[2304,256]{1,0:T(8,128)(2,1)S(1)}, u32[]{:S(2)}, u32[]{:S(2)}) %collective-permute-start.12) | collective-permute-done | bytes 1179680 | tf_op jit(solution)/shard_map/ppermute | solution.py:272
  124.7 2.7 %convert_multiply_fusion = (f32[2304,256]{1,0:T(8,128)}, f32[2304,256]{1,0:T(8,128)}) fusion(bf16[2304,256]{1,0:T(8,128)(2,1)S(1)} %collective-permute-done.12, pred[]{:T(512)S(6)} %eq.9, bf16[16,144,256]{2,1,0:T(8,128)(2,1)S(1)} %all_to_all.10), kind=kLoop, calls=%fused_computation | loop fusion | flops 3538944 | bytes 7077889 | tf_op jit(solution)/shard_map/mul | solution.py:275
  (12 shorter events, 0.2 us)
Async XLA Ops:
  0.6 8.1 %copy-start.1 = (bf16[2,2,128,256]{3,2,1,0:T(8,128)(2,1)S(1)}, bf16[2,2,128,256]{3,2,1,0:T(8,128)(2,1)}, u32[]{:S(2)}) copy-start(bf16[2,2,128,256]{3,2,1,0:T(8,128)(2,1)} %grad.3) | copy-start | bytes 786436
  0.6 8.0 %copy-start.2 = (bf16[2,2,128,256]{3,2,1,0:T(8,128)(2,1)S(1)}, bf16[2,2,128,256]{3,2,1,0:T(8,128)(2,1)}, u32[]{:S(2)}) copy-start(bf16[2,2,128,256]{3,2,1,0:T(8,128)(2,1)} %feat.1) | copy-start | bytes 786436
  0.7 24.9 %copy-start.4 = (s32[2,16,3]{1,0,2:T(2,128)S(1)}, s32[2,16,3]{1,0,2:T(2,128)}, u32[]{:S(2)}) copy-start(s32[2,16,3]{1,0,2:T(2,128)} %param.9) | copy-start | bytes 1156
  0.7 27.7 %copy-start = (bf16[3,3,256,256]{3,2,1,0:T(8,128)(2,1)S(1)}, bf16[3,3,256,256]{3,2,1,0:T(8,128)(2,1)}, u32[]{:S(2)}) copy-start(bf16[3,3,256,256]{3,2,1,0:T(8,128)(2,1)} %first_kernel.3) | copy-start | bytes 3538948
  2.0 14.4 %collective-permute-start.1 = (bf16[2,2,128,256]{3,2,1,0:T(8,128)(2,1)S(1)}, bf16[2,2,128,256]{3,2,1,0:T(8,128)(2,1)S(1)}, u32[]{:S(2)}, u32[]{:S(2)}) collective-permute-start(bf16[2,2,128,256]{3,2,1,0:T(8,128)(2,1)S(1)} %get-tuple-element.37), channel_id=1, source_target_pairs={{1,2},{3,4},{5,6},{9,10},{11,12},{13,14},{17,18},{19,20},{21,22},{... | collective-permute-start | bytes 786440 | tf_op jit(solution)/shard_map/ppermute | solution.py:178
  6.0 16.0 %collective-permute-start = (bf16[2,2,128,256]{3,2,1,0:T(8,128)(2,1)S(1)}, bf16[2,2,128,256]{3,2,1,0:T(8,128)(2,1)S(1)}, u32[]{:S(2)}, u32[]{:S(2)}) collective-permute-start(bf16[2,2,128,256]{3,2,1,0:T(8,128)(2,1)S(1)} %get-tuple-element.38), channel_id=1, source_target_pairs={{0,1},{2,3},{4,5},{6,7},{8,9},{10,11},{12,13},{14,15},{16,17},{18,... | collective-permute-start | bytes 786440 | tf_op jit(solution)/shard_map/ppermute | solution.py:175
  22.0 3.6 %collective-permute-start.2 = (bf16[2,2,4,16,256]{4,3,2,1,0:T(8,128)(2,1)S(1)}, bf16[2,2,4,16,256]{4,3,2,1,0:T(8,128)(2,1)S(1)}, u32[]{:S(2)}, u32[]{:S(2)}) collective-permute-start(bf16[2,2,4,16,256]{4,3,2,1,0:T(8,128)(2,1)S(1)} %pad_maximum_fusion), channel_id=1, source_target_pairs={{0,8},{8,0},{1,9},{9,1},{2,10},{10,2},{3,11},{11,3},{4,12},{12,4},... | collective-permute-start | bytes 393224 | tf_op jit(solution)/shard_map/ppermute | solution.py:195
  23.9 4.5 %collective-permute-start.3 = (bf16[2,2,4,16,256]{4,3,2,1,0:T(8,128)(2,1)S(1)}, bf16[2,2,4,16,256]{4,3,2,1,0:T(8,128)(2,1)S(1)}, u32[]{:S(2)}, u32[]{:S(2)}) collective-permute-start(bf16[2,2,4,16,256]{4,3,2,1,0:T(8,128)(2,1)S(1)} %pad_maximum_fusion.1), channel_id=1, source_target_pairs={{8,16},{9,17},{10,18},{11,19},{12,20},{13,21},{14,22},{15,23},{24,... | collective-permute-start | bytes 393224 | tf_op jit(solution)/shard_map/ppermute | solution.py:194
  28.4 1.3 copy-start.3
  38.9 6.6 %collective-permute-start.4 = (bf16[2304,256]{1,0:T(8,128)(2,1)S(1)}, bf16[2304,256]{1,0:T(8,128)(2,1)S(1)}, u32[]{:S(2)}, u32[]{:S(2)}) collective-permute-start(bf16[2304,256]{1,0:T(8,128)(2,1)S(1)} %get-tuple-element.17), channel_id=1, source_target_pairs={{0,8},{8,0},{1,9},{9,1},{2,10},{10,2},{3,11},{11,3},{4,12},{12,4},... | collective-permute-start | bytes 3538952 | tf_op jit(solution)/shard_map/ppermute | solution.py:242
  48.4 27.0 %all-to-all-start = ((bf16[16,144,256]{2,1,0:T(8,128)(2,1)}), bf16[16,144,256]{2,1,0:T(8,128)(2,1)}, u32[]{:S(2)}, u32[]{:S(2)}) async-start(bf16[16,144,256]{2,1,0:T(8,128)(2,1)} %bitcast.14), calls=%async_computation | async-start | bytes 2359296 | tf_op jit(solution)/shard_map/all_to_all | solution.py:245
  54.3 20.6 %collective-permute-start.6 = (bf16[1,2,128,256]{3,2,1,0:T(8,128)(2,1)S(1)}, bf16[1,2,128,256]{3,2,1,0:T(8,128)(2,1)S(1)}, u32[]{:S(2)}, u32[]{:S(2)}) collective-permute-start(bf16[1,2,128,256]{3,2,1,0:T(8,128)(2,1)S(1)} %get-tuple-element.45), channel_id=1, source_target_pairs={{1,2},{3,4},{5,6},{9,10},{11,12},{13,14},{17,18},{19,20},{21,22},{... | collective-permute-start | bytes 393224 | tf_op jit(solution)/shard_map/ppermute | solution.py:178
  57.5 18.0 %collective-permute-start.5 = (bf16[1,2,128,256]{3,2,1,0:T(8,128)(2,1)S(1)}, bf16[1,2,128,256]{3,2,1,0:T(8,128)(2,1)S(1)}, u32[]{:S(2)}, u32[]{:S(2)}) collective-permute-start(bf16[1,2,128,256]{3,2,1,0:T(8,128)(2,1)S(1)} %get-tuple-element.46), channel_id=1, source_target_pairs={{0,1},{2,3},{4,5},{6,7},{8,9},{10,11},{12,13},{14,15},{16,17},{18,... | collective-permute-start | bytes 393224 | tf_op jit(solution)/shard_map/ppermute | solution.py:175
  77.0 7.5 %collective-permute-start.8 = (bf16[1,2,4,16,256]{4,3,2,1,0:T(8,128)(2,1)S(1)}, bf16[1,2,4,16,256]{4,3,2,1,0:T(8,128)(2,1)S(1)}, u32[]{:S(2)}, u32[]{:S(2)}) collective-permute-start(bf16[1,2,4,16,256]{4,3,2,1,0:T(8,128)(2,1)S(1)} %pad_maximum_fusion.2), channel_id=1, source_target_pairs={{0,8},{8,0},{1,9},{9,1},{2,10},{10,2},{3,11},{11,3},{4,12},{12,4},... | collective-permute-start | bytes 196616 | tf_op jit(solution)/shard_map/ppermute | solution.py:195
  79.0 5.4 %collective-permute-start.7 = (f32[144,256]{1,0:T(8,128)S(1)}, f32[144,256]{1,0:T(8,128)S(1)}, u32[]{:S(2)}, u32[]{:S(2)}) collective-permute-start(f32[144,256]{1,0:T(8,128)S(1)} %convert_reduce_fusion), channel_id=1, source_target_pairs={{0,16},{8,24},{16,0},{24,8},{32,48},{40,56},{48,32},{56,40},{64,80... | collective-permute-start | bytes 442376 | tf_op jit(solution)/shard_map/ppermute | solution.py:255
  79.1 6.3 %collective-permute-start.9 = (bf16[1,2,4,16,256]{4,3,2,1,0:T(8,128)(2,1)S(1)}, bf16[1,2,4,16,256]{4,3,2,1,0:T(8,128)(2,1)S(1)}, u32[]{:S(2)}, u32[]{:S(2)}) collective-permute-start(bf16[1,2,4,16,256]{4,3,2,1,0:T(8,128)(2,1)S(1)} %pad_maximum_fusion.3), channel_id=1, source_target_pairs={{8,16},{9,17},{10,18},{11,19},{12,20},{13,21},{14,22},{15,23},{24,... | collective-permute-start | bytes 196616 | tf_op jit(solution)/shard_map/ppermute | solution.py:194
  85.3 6.2 %collective-permute-start.10 = (f32[144,256]{1,0:T(8,128)S(1)}, f32[144,256]{1,0:T(8,128)S(1)}, u32[]{:S(2)}, u32[]{:S(2)}) collective-permute-start(f32[144,256]{1,0:T(8,128)S(1)} %add.52), channel_id=1, source_target_pairs={{0,32},{8,104},{16,48},{24,120},{32,0},{40,72},{48,16},{56,88},{64... | collective-permute-start | bytes 442376 | tf_op jit(solution)/shard_map/ppermute | solution.py:255
  91.6 6.0 %collective-permute-start.11 = (f32[144,256]{1,0:T(8,128)S(1)}, f32[144,256]{1,0:T(8,128)S(1)}, u32[]{:S(2)}, u32[]{:S(2)}) collective-permute-start(f32[144,256]{1,0:T(8,128)S(1)} %add.53), channel_id=1, source_target_pairs={{0,112},{8,56},{16,96},{24,40},{32,80},{40,24},{48,64},{56,8},{64,... | collective-permute-start | bytes 442376 | tf_op jit(solution)/shard_map/ppermute | solution.py:255
  116.8 7.9 %collective-permute-start.12 = (bf16[2304,256]{1,0:T(8,128)(2,1)S(1)}, bf16[2304,256]{1,0:T(8,128)(2,1)S(1)}, u32[]{:S(2)}, u32[]{:S(2)}) collective-permute-start(bf16[2304,256]{1,0:T(8,128)(2,1)S(1)} %bitcast.55), channel_id=1, source_target_pairs={{0,8},{8,0},{1,9},{9,1},{2,10},{10,2},{3,11},{11,3},{4,12},{12,4},... | collective-permute-start | bytes 3538952 | tf_op jit(solution)/shard_map/ppermute | solution.py:272

commit v3 on v2

--- a/solution.py
+++ b/solution.py
@@ -90,7 +90,7 @@
 
 
 def main_kernel(where, strides, feat, grad, pair, next_pair, in_chip, next_chip, first_kernel, second_kernel,
-                keep, send, pre_grad, ext_f, ext_g, taps_f, taps_g, act):
+                keep, send, pre_grad, ext_f, ext_g, taps_f, taps_g, act, sums):
     lat, core = where[0], where[1]
     mirror = lat == 0
     width = feat.shape[2]
@@ -126,28 +126,22 @@
 
     def place(value, k, col, owner):
         at = (k * 3 + col) * 256
-
-        @pl.when(core == owner)
-        def _():
-            keep[at : at + 256] = value
-
-        @pl.when(core != owner)
-        def _():
-            send[at : at + 256] = value.astype(jnp.bfloat16)
-
-    activated = act[...]
+        sums[jnp.where(core == owner, 0, 1), at : at + 256] = value
+
+    turned = act[...].T
     for col in range(3):
-        edge = dot(activated[:half], taps_g[col, :half], TN)
-        upper = dot(activated[half:], taps_g[col, half:], TN)
-        lower = dot(activated, taps_g[6 + col], TN)
-        place(dot(activated, taps_g[3 + col], TN), 1, col, 1)
+        edge = dot(turned[:, :half], taps_g[col, :half], NN)
+        upper = dot(turned[:, half:], taps_g[col, half:], NN)
+        lower = dot(turned, taps_g[6 + col], NN)
+        place(dot(turned, taps_g[3 + col], NN), 1, col, 1)
         place(lower + jnp.where(mirror, edge, 0.0), 0, col, 1)
         place(upper + jnp.where(mirror, 0.0, edge), 2, col, 1)
-    cells = [pre_grad[s, row] for row in range(2) for s in range(2)]
-    pre_all = jnp.concatenate(cells, axis=0)
+    pre_all = jnp.concatenate([pre_grad[s, row] for row in range(2) for s in range(2)], axis=0)
     for k in range(3):
         for col in range(3):
             place(dot(taps_f[k * 3 + col], pre_all, TN), k, col, 0)
+    keep[...] = sums[0]
+    send[...] = sums[1].astype(jnp.bfloat16)
 
 
 def back_kernel(where, strides, grad, pre, pair, next_pair, in_chip, next_chip, first_kernel, out, ext, taps):
@@ -234,7 +228,7 @@
         ],
         in_specs=[smem, smem] + [vmem] * 8,
         out_specs=[vmem] * 3,
-        scratch_shapes=[ext, ext, taps, taps, pltpu.VMEM((cells, chans), jnp.bfloat16)],
+        scratch_shapes=[ext, ext, taps, taps, pltpu.VMEM((cells, chans), jnp.bfloat16), pltpu.VMEM((2,) + grads, jnp.float32)],
         compiler_params=params,
         name="main",
     )(where, strides, features, out_grad, *around, first_kernel, second_kernel)
@@ -244,31 +238,31 @@
     total = total.astype(jnp.bfloat16).reshape(planes, 9 * chans // planes, chans)
     spread = lax.all_to_all(total, PLANE, 0, 0, tiled=True)
 
+    spread, pre_grad = lax.optimization_barrier((spread, pre_grad))
     pre_field = pre_grad[None]
-    around = row_halos(pre_field, lon_count, lat_count)
-    spread, around = lax.optimization_barrier((spread, around))
-    around += column_halos(pre_field, *around, lon_count, lat_count)
-
+    pair, next_pair = row_halos(pre_field, lon_count, lat_count)
     part = jnp.sum(spread.astype(jnp.float32), axis=0)
     reach = 2
     while reach <= height:
         part = part + lax.ppermute(part, ("z", "core"), folded(height, cores, reach))
-        if reach == 2:
-            part, around = lax.optimization_barrier((part, around))
-            input_grad = pl.pallas_call(
-                back_kernel,
-                out_shape=jax.ShapeDtypeStruct(features.shape, jnp.bfloat16),
-                in_specs=[smem, smem] + [vmem] * 7,
-                out_specs=vmem,
-                scratch_shapes=[ext, taps],
-                compiler_params=params,
-                name="back",
-            )(where, strides, out_grad, pre_grad, *around, first_kernel)
         reach *= 2
-    part, input_grad = lax.optimization_barrier((part.astype(jnp.bfloat16), input_grad))
+        if reach == height:
+            part, pair = lax.optimization_barrier((part, pair))
+    part, next_pair = lax.optimization_barrier((part.astype(jnp.bfloat16), next_pair))
+    around = (pair, next_pair) + column_halos(pre_field, pair, next_pair, lon_count, lat_count)
+    input_grad = pl.pallas_call(
+        back_kernel,
+        out_shape=jax.ShapeDtypeStruct(features.shape, jnp.bfloat16),
+        in_specs=[smem, smem] + [vmem] * 7,
+        out_specs=vmem,
+        scratch_shapes=[ext, taps],
+        compiler_params=params,
+        name="back",
+    )(where, strides, out_grad, pre_grad, *around, first_kernel)
 
     copies = jnp.broadcast_to(part[None], (planes,) + part.shape)
     mine = lax.all_to_all(copies, PLANE, 0, 0, tiled=True).reshape(grads)
+    mine, input_grad = lax.optimization_barrier((mine, input_grad))
     other = lax.ppermute(mine, "core", swap)
     scale = 1.0 / math.sqrt(cells * lat_count * lon_count)
     first = jnp.where(core == 0, mine, other).astype(jnp.float32) * scale

time: 128 us -> 121 us (0.945)
  waiting for transfers between devices: 48.1 us -> 40.5 us
  blocking collectives: 19.2 us -> 23.1 us
  Pallas kernels: 11.7 us -> 8.42 us
    ppermute x2, waiting for transfers between devices: 22.2 us -> 8.84 us  [row_halos(): return (pair, lax.ppermute(row(odd), ALL, between + across))]
    all_to_all x1, blocking collectives: 19.2 us -> 23.1 us  [local(): spread = lax.all_to_all(total, PLANE, 0, 0, tiled=True)]
    pallas_call x1, Pallas kernels: 9.3 us -> 6.06 us  [local(): pl.pallas_call(main_kernel, out_shape=[jax.ShapeDtypeStruct(grads, jnp.fl...]
    ppermute x2, starting transfers between devices: 3.91 us -> 7.07 us  [column_halos(): in_chip = lax.ppermute(edge((1 - core) * reach), 'core', [(0, 1), (1, 0)])]
    ppermute x2, waiting for transfers between devices: 6.28 us -> 8.98 us  [row_halos(): lax.ppermute(row(1 - odd), ALL, both_ways([(at(i, k), at(i, k + 1)) for i...]
    ppermute x2, waiting for transfers between devices: 3.53 us -> 5.97 us  [column_halos(): lax.ppermute(edge(core * reach), ALL, both_ways([(at(i + 1, k), at(i + 2,...]
    all_to_all x1, starting transfers between devices: 5.77 us -> 4.38 us  [local(): mine = lax.all_to_all(copies, PLANE, 0, 0, tiled=True).reshape(grads)]
    ppermute x2, starting transfers between devices: 5.46 us -> 4.13 us  [row_halos(): lax.ppermute(row(1 - odd), ALL, both_ways([(at(i, k), at(i, k + 1)) for i...]
  transfers between devices with their start and end apart: 14 -> 14, of which waited for: 11 -> 13; matrix products, arithmetic and copies ran while one was open for 0% -> 0% of each run, Pallas kernels for 2% -> 2%
where the time goes in v3:
time: 121 us
  waiting for transfers between devices  40.5 us (33%)
  starting transfers between devices  38 us (31%)
  blocking collectives  23.1 us (19%)
  Pallas kernels  8.42 us (7%)
  other arithmetic  7.51 us (6%)
  local copies, waits for them, and re-layouts  2.5 us (2%)
    all_to_all x1, blocking collectives, local(): spread = lax.all_to_all(total, PLANE, 0, 0, tiled=True)  23.1 us
    ppermute x3, waiting for transfers between devices, local(): lax.ppermute(part, ('z', 'core'), folded(height, cores, reach))  10.2 us
    ppermute x2, waiting for transfers between devices, row_halos(): lax.ppermute(row(1 - odd), ALL, both_ways([(at(i, k), at(i, k + 1)) for i...  8.98 us
    ppermute x2, waiting for transfers between devices, row_halos(): return (pair, lax.ppermute(row(odd), ALL, between + across))  8.84 us
    ppermute x2, starting transfers between devices, column_halos(): in_chip = lax.ppermute(edge((1 - core) * reach), 'core', [(0, 1), (1, 0)])  7.07 us
    ppermute x1, starting transfers between devices, local(): other = lax.ppermute(mine, 'core', swap)  6.47 us
    pallas_call x1, Pallas kernels, local(): pl.pallas_call(main_kernel, out_shape=[jax.ShapeDtypeStruct(grads, jnp.fl...  6.06 us
    ppermute x2, waiting for transfers between devices, column_halos(): lax.ppermute(edge(core * reach), ALL, both_ways([(at(i + 1, k), at(i + 2,...  5.97 us
  transfers between devices with their start and end apart: 14, of which 13 were waited for; matrix products, arithmetic and copies ran while one was open for 0% of the time, Pallas kernels for 2%

profile of v3, /device:TPU:1, one launch (start us, length us, event | category | flops | bytes accessed | tf_op | source)
XLA Modules:
  0.0 120.8 jit_solution(2666939842206007745)
XLA Ops:
  0.6 0.0 copy-start.1
  0.6 0.0 copy-start.2
  0.7 0.0 copy-start.4
  0.7 0.0 copy-start
  0.7 1.3 %fusion.3 = (bf16[2,2,128,256]{3,2,1,0:T(8,128)(2,1)S(1)}, bf16[2,2,128,256]{3,2,1,0:T(8,128)(2,1)S(1)}) fusion(s32[]{:T(128)S(6)} %select_n.79, bf16[1,2,2,128,256]{4,3,2,1,0:T(8,128)(2,1)} %bitcast.51, bf16[1,2,2,128,256]{4,3,2,1,0:T(8,128)(2,1)} %bitcast.49, s32[]{:T(128)S(6)} %select_n.78), kind=kLoop, calls=%fused_computation.15 | loop fusion | flops 262144 | bytes 1048584 | tf_op jit(solution)/shard_map/jit(dynamic_index_in_dim)/squeeze | solution.py:168
  2.0 4.0 %collective-permute-start.1 = (bf16[2,2,128,256]{3,2,1,0:T(8,128)(2,1)S(1)}, bf16[2,2,128,256]{3,2,1,0:T(8,128)(2,1)S(1)}, u32[]{:S(2)}, u32[]{:S(2)}) collective-permute-start(bf16[2,2,128,256]{3,2,1,0:T(8,128)(2,1)S(1)} %get-tuple-element.33), channel_id=1, source_target_pairs={{1,2},{3,4},{5,6},{9,10},{11,12},{13,14},{17,18},{19,20},{21,22},{... | collective-permute-start | bytes 786440 | tf_op jit(solution)/shard_map/ppermute | solution.py:172
  6.0 2.7 %collective-permute-start = (bf16[2,2,128,256]{3,2,1,0:T(8,128)(2,1)S(1)}, bf16[2,2,128,256]{3,2,1,0:T(8,128)(2,1)S(1)}, u32[]{:S(2)}, u32[]{:S(2)}) collective-permute-start(bf16[2,2,128,256]{3,2,1,0:T(8,128)(2,1)S(1)} %get-tuple-element.34), channel_id=1, source_target_pairs={{0,1},{2,3},{4,5},{6,7},{8,9},{10,11},{12,13},{14,15},{16,17},{18,... | collective-permute-start | bytes 786440 | tf_op jit(solution)/shard_map/ppermute | solution.py:169
  8.7 0.0 copy-done.1
  8.7 0.0 copy-done.2
  8.7 7.7 %collective-permute-done.1.next_pair = bf16[2,2,128,256]{3,2,1,0:T(8,128)(2,1)S(1)} collective-permute-done((bf16[2,2,128,256]{3,2,1,0:T(8,128)(2,1)S(1)}, bf16[2,2,128,256]{3,2,1,0:T(8,128)(2,1)S(1)}, u32[]{:S(2)}, u32[]{:S(2)}) %collective-permute-start.1) | collective-permute-done | bytes 262176 | tf_op jit(solution)/shard_map/ppermute | solution.py:172
  16.4 5.6 %collective-permute-done.pair = bf16[2,2,128,256]{3,2,1,0:T(8,128)(2,1)S(1)} collective-permute-done((bf16[2,2,128,256]{3,2,1,0:T(8,128)(2,1)S(1)}, bf16[2,2,128,256]{3,2,1,0:T(8,128)(2,1)S(1)}, u32[]{:S(2)}, u32[]{:S(2)}) %collective-permute-start) | collective-permute-done | bytes 262176 | tf_op jit(solution)/shard_map/ppermute | solution.py:169
  22.0 1.8 %collective-permute-start.2 = (bf16[2,2,4,16,256]{4,3,2,1,0:T(8,128)(2,1)S(1)}, bf16[2,2,4,16,256]{4,3,2,1,0:T(8,128)(2,1)S(1)}, u32[]{:S(2)}, u32[]{:S(2)}) collective-permute-start(bf16[2,2,4,16,256]{4,3,2,1,0:T(8,128)(2,1)S(1)} %pad_maximum_fusion), channel_id=1, source_target_pairs={{0,8},{8,0},{1,9},{9,1},{2,10},{10,2},{3,11},{11,3},{4,12},{12,4},... | collective-permute-start | bytes 393224 | tf_op jit(solution)/shard_map/ppermute | solution.py:189
  23.9 1.6 %collective-permute-start.3 = (bf16[2,2,4,16,256]{4,3,2,1,0:T(8,128)(2,1)S(1)}, bf16[2,2,4,16,256]{4,3,2,1,0:T(8,128)(2,1)S(1)}, u32[]{:S(2)}, u32[]{:S(2)}) collective-permute-start(bf16[2,2,4,16,256]{4,3,2,1,0:T(8,128)(2,1)S(1)} %pad_maximum_fusion.1), channel_id=1, source_target_pairs={{8,16},{9,17},{10,18},{11,19},{12,20},{13,21},{14,22},{15,23},{24,... | collective-permute-start | bytes 393224 | tf_op jit(solution)/shard_map/ppermute | solution.py:188
  25.5 0.0 copy-done.4
  25.5 0.1 copy.11.strides
  25.6 0.1 pad_add_fusion.where
  25.7 0.0 collective-permute-done.2.in_chip
  25.7 2.7 %collective-permute-done.3.next_chip = bf16[2,2,4,16,256]{4,3,2,1,0:T(8,128)(2,1)S(1)} collective-permute-done((bf16[2,2,4,16,256]{4,3,2,1,0:T(8,128)(2,1)S(1)}, bf16[2,2,4,16,256]{4,3,2,1,0:T(8,128)(2,1)S(1)}, u32[]{:S(2)}, u32[]{:S(2)}) %collective-permute-start.3) | collective-permute-done | bytes 131104 | tf_op jit(solution)/shard_map/ppermute | solution.py:188
  28.4 0.0 copy-done
  28.4 0.0 copy-start.3
  28.4 1.3 %copy-done.3 = bf16[3,3,256,256]{3,2,1,0:T(8,128)(2,1)S(1)} copy-done((bf16[3,3,256,256]{3,2,1,0:T(8,128)(2,1)S(1)}, bf16[3,3,256,256]{3,2,1,0:T(8,128)(2,1)}, u32[]{:S(2)}) %copy-start.3) | copy-done | bytes 1179672
  29.6 6.1 %main.1 = (f32[2304,256]{1,0:T(8,128)}, bf16[2304,256]{1,0:T(8,128)(2,1)S(1)}, bf16[2,2,128,256]{3,2,1,0:T(8,128)(2,1)S(1)}) custom-call(s32[3]{0:T(128)S(1)} %pad_add_fusion.where, s32[2,16,3]{2,1,0:T(8,128)S(1)} %copy.11.strides, bf16[2,2,128,256]{3,2,1,0:T(8,128)(2,1)S(1)} %copy-done.2, bf16[2,2,128,256]{3,2,1,0:T(8,128)(2,1)S(1)} %copy-done.1, ...), custom_call_target="tpu_custom_call" | custom-call | tf_op jit(solution)/shard_map/main/pallas_call | solution.py:222
  35.7 4.1 %collective-permute-start.4 = (bf16[2304,256]{1,0:T(8,128)(2,1)S(1)}, bf16[2304,256]{1,0:T(8,128)(2,1)S(1)}, u32[]{:S(2)}, u32[]{:S(2)}) collective-permute-start(bf16[2304,256]{1,0:T(8,128)(2,1)S(1)} %get-tuple-element.15), channel_id=1, source_target_pairs={{0,8},{8,0},{1,9},{9,1},{2,10},{10,2},{3,11},{11,3},{4,12},{12,4},... | collective-permute-start | bytes 3538952 | tf_op jit(solution)/shard_map/ppermute | solution.py:236
  39.8 2.5 %collective-permute-done.4 = bf16[2304,256]{1,0:T(8,128)(2,1)S(1)} collective-permute-done((bf16[2304,256]{1,0:T(8,128)(2,1)S(1)}, bf16[2304,256]{1,0:T(8,128)(2,1)S(1)}, u32[]{:S(2)}, u32[]{:S(2)}) %collective-permute-start.4) | collective-permute-done | bytes 1179680 | tf_op jit(solution)/shard_map/ppermute | solution.py:236
  42.3 1.9 %add_convert_fusion = bf16[2304,256]{1,0:T(8,128)(2,1)S(1)} fusion(f32[2304,256]{1,0:T(8,128)} %get-tuple-element.14, bf16[2304,256]{1,0:T(8,128)(2,1)S(1)} %collective-permute-done.4), kind=kLoop, calls=%fused_computation.3 | loop fusion | flops 1769472 | bytes 4718592 | tf_op jit(solution)/shard_map/convert_element_type | solution.py:238
  44.2 23.1 %all_to_all.10 = bf16[16,144,256]{2,1,0:T(8,128)(2,1)S(1)} all-to-all(bf16[16,144,256]{2,1,0:T(8,128)(2,1)S(1)} %bitcast.53), channel_id=1, replica_groups=mesh['yl'=2,'z'=8,'core'=2,'x'=4,'yh'=2] {'x','yh','yl'}, dimensions={0} | all-to-all | bytes 2359296 | tf_op jit(solution)/shard_map/all_to_all | solution.py:239
  67.4 0.2 convert_reduce_fusion
  67.5 0.1 collective-permute-start.5
  67.6 4.0 %collective-permute-done.5 = f32[144,256]{1,0:T(8,128)S(1)} collective-permute-done((f32[144,256]{1,0:T(8,128)S(1)}, f32[144,256]{1,0:T(8,128)S(1)}, u32[]{:S(2)}, u32[]{:S(2)}) %collective-permute-start.5) | collective-permute-done | bytes 147488 | tf_op jit(solution)/shard_map/ppermute | solution.py:247
  71.6 3.4 %collective-permute-start.6 = (f32[144,256]{1,0:T(8,128)S(1)}, f32[144,256]{1,0:T(8,128)S(1)}, u32[]{:S(2)}, u32[]{:S(2)}) collective-permute-start(f32[144,256]{1,0:T(8,128)S(1)} %add.52), channel_id=1, source_target_pairs={{0,32},{8,104},{16,48},{24,120},{32,0},{40,72},{48,16},{56,88},{64... | collective-permute-start | bytes 442376 | tf_op jit(solution)/shard_map/ppermute | solution.py:247
  75.0 1.4 %collective-permute-start.7 = (bf16[1,2,128,256]{3,2,1,0:T(8,128)(2,1)S(1)}, bf16[1,2,128,256]{3,2,1,0:T(8,128)(2,1)S(1)}, u32[]{:S(2)}, u32[]{:S(2)}) collective-permute-start(bf16[1,2,128,256]{3,2,1,0:T(8,128)(2,1)S(1)} %get-tuple-element.42), channel_id=1, source_target_pairs={{0,1},{2,3},{4,5},{6,7},{8,9},{10,11},{12,13},{14,15},{16,17},{18,... | collective-permute-start | bytes 393224 | tf_op jit(solution)/shard_map/ppermute | solution.py:169
  76.5 2.2 %collective-permute-done.6 = f32[144,256]{1,0:T(8,128)S(1)} collective-permute-done((f32[144,256]{1,0:T(8,128)S(1)}, f32[144,256]{1,0:T(8,128)S(1)}, u32[]{:S(2)}, u32[]{:S(2)}) %collective-permute-start.6) | collective-permute-done | bytes 147488 | tf_op jit(solution)/shard_map/ppermute | solution.py:247
  78.7 3.4 %collective-permute-done.7.pair = bf16[1,2,128,256]{3,2,1,0:T(8,128)(2,1)S(1)} collective-permute-done((bf16[1,2,128,256]{3,2,1,0:T(8,128)(2,1)S(1)}, bf16[1,2,128,256]{3,2,1,0:T(8,128)(2,1)S(1)}, u32[]{:S(2)}, u32[]{:S(2)}) %collective-permute-start.7) | collective-permute-done | bytes 131104 | tf_op jit(solution)/shard_map/ppermute | solution.py:169
  82.1 0.0 collective-permute-start.8
  82.1 1.9 %collective-permute-start.9 = (bf16[1,2,128,256]{3,2,1,0:T(8,128)(2,1)S(1)}, bf16[1,2,128,256]{3,2,1,0:T(8,128)(2,1)S(1)}, u32[]{:S(2)}, u32[]{:S(2)}) collective-permute-start(bf16[1,2,128,256]{3,2,1,0:T(8,128)(2,1)S(1)} %get-tuple-element.41), channel_id=1, source_target_pairs={{1,2},{3,4},{5,6},{9,10},{11,12},{13,14},{17,18},{19,20},{21,22},{... | collective-permute-start | bytes 393224 | tf_op jit(solution)/shard_map/ppermute | solution.py:172
  84.0 4.0 %collective-permute-done.8 = f32[144,256]{1,0:T(8,128)S(1)} collective-permute-done((f32[144,256]{1,0:T(8,128)S(1)}, f32[144,256]{1,0:T(8,128)S(1)}, u32[]{:S(2)}, u32[]{:S(2)}) %collective-permute-start.8) | collective-permute-done | bytes 147488 | tf_op jit(solution)/shard_map/ppermute | solution.py:247
  88.0 1.2 collective-permute-done.9.next_pair
  89.2 1.1 broadcast_in_dim.35
  90.3 4.4 %all-to-all-start.1 = ((bf16[16,144,256]{2,1,0:T(8,128)(2,1)}), bf16[16,144,256]{2,1,0:T(8,128)(2,1)}, u32[]{:S(2)}, u32[]{:S(2)}) async-start(bf16[16,144,256]{2,1,0:T(8,128)(2,1)} %broadcast_in_dim.35), calls=%async_computation.1 | async-start | bytes 2359296 | tf_op jit(solution)/shard_map/all_to_all | solution.py:264
  94.7 5.2 %collective-permute-start.10 = (bf16[1,2,4,16,256]{4,3,2,1,0:T(8,128)(2,1)S(1)}, bf16[1,2,4,16,256]{4,3,2,1,0:T(8,128)(2,1)S(1)}, u32[]{:S(2)}, u32[]{:S(2)}) collective-permute-start(bf16[1,2,4,16,256]{4,3,2,1,0:T(8,128)(2,1)S(1)} %pad_maximum_fusion.2), channel_id=1, source_target_pairs={{0,8},{8,0},{1,9},{9,1},{2,10},{10,2},{3,11},{11,3},{4,12},{12,4},... | collective-permute-start | bytes 196616 | tf_op jit(solution)/shard_map/ppermute | solution.py:189
  100.0 0.8 collective-permute-start.11
  100.8 0.1 collective-permute-done.10.in_chip
  100.9 3.3 %collective-permute-done.11.next_chip = bf16[1,2,4,16,256]{4,3,2,1,0:T(8,128)(2,1)S(1)} collective-permute-done((bf16[1,2,4,16,256]{4,3,2,1,0:T(8,128)(2,1)S(1)}, bf16[1,2,4,16,256]{4,3,2,1,0:T(8,128)(2,1)S(1)}, u32[]{:S(2)}, u32[]{:S(2)}) %collective-permute-start.11) | collective-permute-done | bytes 65568 | tf_op jit(solution)/shard_map/ppermute | solution.py:188
  104.2 2.4 %back.1 = bf16[2,2,128,256]{3,2,1,0:T(8,128)(2,1)} custom-call(s32[3]{0:T(128)S(1)} %pad_add_fusion.where, s32[2,16,3]{2,1,0:T(8,128)S(1)} %copy.11.strides, bf16[2,2,128,256]{3,2,1,0:T(8,128)(2,1)S(1)} %copy-done.1, bf16[2,2,128,256]{3,2,1,0:T(8,128)(2,1)S(1)} %get-tuple-element.18.pre, bf16[1,2,128,256]{3,2,1,0:T(8,128)(2,1)S(1)} %collective-permute-done.7.pair, ...), custom_call_target="tpu_custom_call" | custom-call | tf_op jit(solution)/shard_map/back/pallas_call | solution.py:253
  106.5 1.2 %all-to-all-done.1 = bf16[16,144,256]{2,1,0:T(8,128)(2,1)} async-done(((bf16[16,144,256]{2,1,0:T(8,128)(2,1)}), bf16[16,144,256]{2,1,0:T(8,128)(2,1)}, u32[]{:S(2)}, u32[]{:S(2)}) %all-to-all-start.1) | async-done | bytes 1179680 | tf_op jit(solution)/shard_map/all_to_all | solution.py:264
  107.8 6.5 %collective-permute-start.12 = (bf16[2304,256]{1,0:T(8,128)(2,1)}, bf16[2304,256]{1,0:T(8,128)(2,1)S(1)}, u32[]{:S(2)}, u32[]{:S(2)}) collective-permute-start(bf16[2304,256]{1,0:T(8,128)(2,1)} %bitcast.17), channel_id=1, source_target_pairs={{0,8},{8,0},{1,9},{9,1},{2,10},{10,2},{3,11},{11,3},{4,12},{12,4},... | collective-permute-start | bytes 3538952 | tf_op jit(solution)/shard_map/ppermute | solution.py:266
  114.2 2.7 %collective-permute-done.12 = bf16[2304,256]{1,0:T(8,128)(2,1)S(1)} collective-permute-done((bf16[2304,256]{1,0:T(8,128)(2,1)}, bf16[2304,256]{1,0:T(8,128)(2,1)S(1)}, u32[]{:S(2)}, u32[]{:S(2)}) %collective-permute-start.12) | collective-permute-done | bytes 1179680 | tf_op jit(solution)/shard_map/ppermute | solution.py:266
  116.9 3.9 %convert_multiply_fusion = (f32[2304,256]{1,0:T(8,128)}, f32[2304,256]{1,0:T(8,128)}) fusion(bf16[2304,256]{1,0:T(8,128)(2,1)S(1)} %collective-permute-done.12, bf16[2304,256]{1,0:T(8,128)(2,1)} %bitcast.17, pred[]{:T(512)S(6)} %eq.9), kind=kLoop, calls=%fused_computation | loop fusion | flops 3538944 | bytes 7077889 | tf_op jit(solution)/shard_map/mul | solution.py:269
  (12 shorter events, 0.2 us)
Async XLA Ops:
  0.6 8.1 %copy-start.1 = (bf16[2,2,128,256]{3,2,1,0:T(8,128)(2,1)S(1)}, bf16[2,2,128,256]{3,2,1,0:T(8,128)(2,1)}, u32[]{:S(2)}) copy-start(bf16[2,2,128,256]{3,2,1,0:T(8,128)(2,1)} %grad.3) | copy-start | bytes 786436
  0.6 8.0 %copy-start.2 = (bf16[2,2,128,256]{3,2,1,0:T(8,128)(2,1)S(1)}, bf16[2,2,128,256]{3,2,1,0:T(8,128)(2,1)}, u32[]{:S(2)}) copy-start(bf16[2,2,128,256]{3,2,1,0:T(8,128)(2,1)} %feat.1) | copy-start | bytes 786436
  0.7 24.9 %copy-start.4 = (s32[2,16,3]{1,0,2:T(2,128)S(1)}, s32[2,16,3]{1,0,2:T(2,128)}, u32[]{:S(2)}) copy-start(s32[2,16,3]{1,0,2:T(2,128)} %param.9) | copy-start | bytes 1156
  0.7 27.7 %copy-start = (bf16[3,3,256,256]{3,2,1,0:T(8,128)(2,1)S(1)}, bf16[3,3,256,256]{3,2,1,0:T(8,128)(2,1)}, u32[]{:S(2)}) copy-start(bf16[3,3,256,256]{3,2,1,0:T(8,128)(2,1)} %first_kernel.3) | copy-start | bytes 3538948
  2.0 14.4 %collective-permute-start.1 = (bf16[2,2,128,256]{3,2,1,0:T(8,128)(2,1)S(1)}, bf16[2,2,128,256]{3,2,1,0:T(8,128)(2,1)S(1)}, u32[]{:S(2)}, u32[]{:S(2)}) collective-permute-start(bf16[2,2,128,256]{3,2,1,0:T(8,128)(2,1)S(1)} %get-tuple-element.33), channel_id=1, source_target_pairs={{1,2},{3,4},{5,6},{9,10},{11,12},{13,14},{17,18},{19,20},{21,22},{... | collective-permute-start | bytes 786440 | tf_op jit(solution)/shard_map/ppermute | solution.py:172
  6.0 16.0 %collective-permute-start = (bf16[2,2,128,256]{3,2,1,0:T(8,128)(2,1)S(1)}, bf16[2,2,128,256]{3,2,1,0:T(8,128)(2,1)S(1)}, u32[]{:S(2)}, u32[]{:S(2)}) collective-permute-start(bf16[2,2,128,256]{3,2,1,0:T(8,128)(2,1)S(1)} %get-tuple-element.34), channel_id=1, source_target_pairs={{0,1},{2,3},{4,5},{6,7},{8,9},{10,11},{12,13},{14,15},{16,17},{18,... | collective-permute-start | bytes 786440 | tf_op jit(solution)/shard_map/ppermute | solution.py:169
  22.0 3.6 %collective-permute-start.2 = (bf16[2,2,4,16,256]{4,3,2,1,0:T(8,128)(2,1)S(1)}, bf16[2,2,4,16,256]{4,3,2,1,0:T(8,128)(2,1)S(1)}, u32[]{:S(2)}, u32[]{:S(2)}) collective-permute-start(bf16[2,2,4,16,256]{4,3,2,1,0:T(8,128)(2,1)S(1)} %pad_maximum_fusion), channel_id=1, source_target_pairs={{0,8},{8,0},{1,9},{9,1},{2,10},{10,2},{3,11},{11,3},{4,12},{12,4},... | collective-permute-start | bytes 393224 | tf_op jit(solution)/shard_map/ppermute | solution.py:189
  23.9 4.5 %collective-permute-start.3 = (bf16[2,2,4,16,256]{4,3,2,1,0:T(8,128)(2,1)S(1)}, bf16[2,2,4,16,256]{4,3,2,1,0:T(8,128)(2,1)S(1)}, u32[]{:S(2)}, u32[]{:S(2)}) collective-permute-start(bf16[2,2,4,16,256]{4,3,2,1,0:T(8,128)(2,1)S(1)} %pad_maximum_fusion.1), channel_id=1, source_target_pairs={{8,16},{9,17},{10,18},{11,19},{12,20},{13,21},{14,22},{15,23},{24,... | collective-permute-start | bytes 393224 | tf_op jit(solution)/shard_map/ppermute | solution.py:188
  28.4 1.3 %copy-start.3 = (bf16[3,3,256,256]{3,2,1,0:T(8,128)(2,1)S(1)}, bf16[3,3,256,256]{3,2,1,0:T(8,128)(2,1)}, u32[]{:S(2)}) copy-start(bf16[3,3,256,256]{3,2,1,0:T(8,128)(2,1)} %second_kernel.1) | copy-start | bytes 3538948
  35.7 6.6 %collective-permute-start.4 = (bf16[2304,256]{1,0:T(8,128)(2,1)S(1)}, bf16[2304,256]{1,0:T(8,128)(2,1)S(1)}, u32[]{:S(2)}, u32[]{:S(2)}) collective-permute-start(bf16[2304,256]{1,0:T(8,128)(2,1)S(1)} %get-tuple-element.15), channel_id=1, source_target_pairs={{0,8},{8,0},{1,9},{9,1},{2,10},{10,2},{3,11},{11,3},{4,12},{12,4},... | collective-permute-start | bytes 3538952 | tf_op jit(solution)/shard_map/ppermute | solution.py:236
  67.5 4.1 %collective-permute-start.5 = (f32[144,256]{1,0:T(8,128)S(1)}, f32[144,256]{1,0:T(8,128)S(1)}, u32[]{:S(2)}, u32[]{:S(2)}) collective-permute-start(f32[144,256]{1,0:T(8,128)S(1)} %convert_reduce_fusion), channel_id=1, source_target_pairs={{0,16},{8,24},{16,0},{24,8},{32,48},{40,56},{48,32},{56,40},{64,80... | collective-permute-start | bytes 442376 | tf_op jit(solution)/shard_map/ppermute | solution.py:247
  71.6 7.1 %collective-permute-start.6 = (f32[144,256]{1,0:T(8,128)S(1)}, f32[144,256]{1,0:T(8,128)S(1)}, u32[]{:S(2)}, u32[]{:S(2)}) collective-permute-start(f32[144,256]{1,0:T(8,128)S(1)} %add.52), channel_id=1, source_target_pairs={{0,32},{8,104},{16,48},{24,120},{32,0},{40,72},{48,16},{56,88},{64... | collective-permute-start | bytes 442376 | tf_op jit(solution)/shard_map/ppermute | solution.py:247
  75.0 7.0 %collective-permute-start.7 = (bf16[1,2,128,256]{3,2,1,0:T(8,128)(2,1)S(1)}, bf16[1,2,128,256]{3,2,1,0:T(8,128)(2,1)S(1)}, u32[]{:S(2)}, u32[]{:S(2)}) collective-permute-start(bf16[1,2,128,256]{3,2,1,0:T(8,128)(2,1)S(1)} %get-tuple-element.42), channel_id=1, source_target_pairs={{0,1},{2,3},{4,5},{6,7},{8,9},{10,11},{12,13},{14,15},{16,17},{18,... | collective-permute-start | bytes 393224 | tf_op jit(solution)/shard_map/ppermute | solution.py:169
  82.1 5.9 %collective-permute-start.8 = (f32[144,256]{1,0:T(8,128)S(1)}, f32[144,256]{1,0:T(8,128)S(1)}, u32[]{:S(2)}, u32[]{:S(2)}) collective-permute-start(f32[144,256]{1,0:T(8,128)S(1)} %add.53), channel_id=1, source_target_pairs={{0,112},{8,56},{16,96},{24,40},{32,80},{40,24},{48,64},{56,8},{64,... | collective-permute-start | bytes 442376 | tf_op jit(solution)/shard_map/ppermute | solution.py:247
  82.1 7.1 %collective-permute-start.9 = (bf16[1,2,128,256]{3,2,1,0:T(8,128)(2,1)S(1)}, bf16[1,2,128,256]{3,2,1,0:T(8,128)(2,1)S(1)}, u32[]{:S(2)}, u32[]{:S(2)}) collective-permute-start(bf16[1,2,128,256]{3,2,1,0:T(8,128)(2,1)S(1)} %get-tuple-element.41), channel_id=1, source_target_pairs={{1,2},{3,4},{5,6},{9,10},{11,12},{13,14},{17,18},{19,20},{21,22},{... | collective-permute-start | bytes 393224 | tf_op jit(solution)/shard_map/ppermute | solution.py:172
  90.3 17.5 %all-to-all-start.1 = ((bf16[16,144,256]{2,1,0:T(8,128)(2,1)}), bf16[16,144,256]{2,1,0:T(8,128)(2,1)}, u32[]{:S(2)}, u32[]{:S(2)}) async-start(bf16[16,144,256]{2,1,0:T(8,128)(2,1)} %broadcast_in_dim.35), calls=%async_computation.1 | async-start | bytes 2359296 | tf_op jit(solution)/shard_map/all_to_all | solution.py:264
  94.7 6.1 %collective-permute-start.10 = (bf16[1,2,4,16,256]{4,3,2,1,0:T(8,128)(2,1)S(1)}, bf16[1,2,4,16,256]{4,3,2,1,0:T(8,128)(2,1)S(1)}, u32[]{:S(2)}, u32[]{:S(2)}) collective-permute-start(bf16[1,2,4,16,256]{4,3,2,1,0:T(8,128)(2,1)S(1)} %pad_maximum_fusion.2), channel_id=1, source_target_pairs={{0,8},{8,0},{1,9},{9,1},{2,10},{10,2},{3,11},{11,3},{4,12},{12,4},... | collective-permute-start | bytes 196616 | tf_op jit(solution)/shard_map/ppermute | solution.py:189
  100.0 4.2 %collective-permute-start.11 = (bf16[1,2,4,16,256]{4,3,2,1,0:T(8,128)(2,1)S(1)}, bf16[1,2,4,16,256]{4,3,2,1,0:T(8,128)(2,1)S(1)}, u32[]{:S(2)}, u32[]{:S(2)}) collective-permute-start(bf16[1,2,4,16,256]{4,3,2,1,0:T(8,128)(2,1)S(1)} %pad_maximum_fusion.3), channel_id=1, source_target_pairs={{8,16},{9,17},{10,18},{11,19},{12,20},{13,21},{14,22},{15,23},{24,... | collective-permute-start | bytes 196616 | tf_op jit(solution)/shard_map/ppermute | solution.py:188
  107.8 9.2 %collective-permute-start.12 = (bf16[2304,256]{1,0:T(8,128)(2,1)}, bf16[2304,256]{1,0:T(8,128)(2,1)S(1)}, u32[]{:S(2)}, u32[]{:S(2)}) collective-permute-start(bf16[2304,256]{1,0:T(8,128)(2,1)} %bitcast.17), channel_id=1, source_target_pairs={{0,8},{8,0},{1,9},{9,1},{2,10},{10,2},{3,11},{11,3},{4,12},{12,4},... | collective-permute-start | bytes 3538952 | tf_op jit(solution)/shard_map/ppermute | solution.py:266

commit v4 on v3

--- a/solution.py
+++ b/solution.py
@@ -90,11 +90,15 @@
 
 
 def main_kernel(where, strides, feat, grad, pair, next_pair, in_chip, next_chip, first_kernel, second_kernel,
-                keep, send, pre_grad, ext_f, ext_g, taps_f, taps_g, act, sums):
+                keep, send, pre_grad, ext_f, ext_g, taps_f, taps_g, act, sums, first_held, second_held, sems):
     lat, core = where[0], where[1]
     mirror = lat == 0
     width = feat.shape[2]
     half = 2 * width
+    fetch_first = pltpu.make_async_copy(first_kernel, first_held, sems.at[0])
+    fetch_second = pltpu.make_async_copy(second_kernel, second_held, sems.at[1])
+    fetch_first.start()
+    fetch_second.start()
     halo = (pair, next_pair, in_chip, next_chip)
     fill(ext_f, 0, feat, halo, where)
     for row in range(2):
@@ -107,19 +111,21 @@
                     taps_f[k * 3 + col, at : at + width] = tap(ext_f, s, row + k, shift, width)
     fill(ext_g, 1, grad, halo, where)
     adjoint_taps(ext_g, taps_g, strides, lat, width)
+    fetch_first.wait()
+    fetch_second.wait()
 
     for row in range(2):
         at = row * half
         pre = None
         for k in range(3):
             for col in range(3):
-                term = dot(taps_f[k * 3 + col, at : at + half], first_kernel[k, col], NN)
+                term = dot(taps_f[k * 3 + col, at : at + half], first_held[k, col], NN)
                 pre = term if pre is None else pre + term
         square = pre * pre
         bend = jnp.tanh(ROOT * (pre + CUBIC * (pre * square)))
         act[at : at + half] = (0.5 * pre * (1.0 + bend)).astype(jnp.bfloat16)
         slope = 0.5 * (1.0 + bend) + 0.5 * pre * (1.0 - bend * bend) * (ROOT * (1.0 + 3.0 * CUBIC * square))
-        back = adjoint_product(taps_g, second_kernel, mirror, row, half)
+        back = adjoint_product(taps_g, second_held, mirror, row, half)
         result = (back * slope).astype(jnp.bfloat16)
         for s in range(2):
             pre_grad[s, row] = result[s * width : (s + 1) * width]
@@ -140,8 +146,10 @@
     for k in range(3):
         for col in range(3):
             place(dot(taps_f[k * 3 + col], pre_all, TN), k, col, 0)
-    keep[...] = sums[0]
+    store = pltpu.make_async_copy(sums.at[0], keep, sems.at[2])
+    store.start()
     send[...] = sums[1].astype(jnp.bfloat16)
+    store.wait()
 
 
 def back_kernel(where, strides, grad, pre, pair, next_pair, in_chip, next_chip, first_kernel, out, ext, taps):
@@ -157,6 +165,13 @@
             out[s, row] = (own + total[s * width : (s + 1) * width]).astype(jnp.bfloat16)
 
 
+def part_kernel(scale, where, mine, other, first, second):
+    own, swapped = mine[...].astype(jnp.float32) * scale, other[...].astype(jnp.float32) * scale
+    keeps = where[1] == 0
+    first[...] = jnp.where(keeps, own, swapped)
+    second[...] = jnp.where(keeps, swapped, own)
+
+
 def both_ways(pairs):
     return pairs + [(b, a) for a, b in pairs]
 
@@ -209,6 +224,7 @@
     where = jnp.stack([lat, core, lax.rem(lat, 2)]).astype(jnp.int32)
     smem = pl.BlockSpec(memory_space=pltpu.SMEM)
     vmem = pl.BlockSpec(memory_space=pltpu.VMEM)
+    anywhere = pl.BlockSpec(memory_space=pl.ANY)
     cells = slabs * rows * width
     ext = pltpu.VMEM((slabs * (rows + 2), width + 2 * SPAN + 8, chans), jnp.float32)
     taps = pltpu.VMEM((9, cells, chans), jnp.bfloat16)
@@ -226,9 +242,19 @@
             jax.ShapeDtypeStruct(grads, jnp.bfloat16),
             jax.ShapeDtypeStruct(features.shape, jnp.bfloat16),
         ],
-        in_specs=[smem, smem] + [vmem] * 8,
-        out_specs=[vmem] * 3,
-        scratch_shapes=[ext, ext, taps, taps, pltpu.VMEM((cells, chans), jnp.bfloat16), pltpu.VMEM((2,) + grads, jnp.float32)],
+        in_specs=[smem, smem] + [vmem] * 6 + [anywhere] * 2,
+        out_specs=[anywhere, vmem, vmem],
+        scratch_shapes=[
+            ext,
+            ext,
+            taps,
+            taps,
+            pltpu.VMEM((cells, chans), jnp.bfloat16),
+            pltpu.VMEM((2,) + grads, jnp.float32),
+            pltpu.VMEM(first_kernel.shape, jnp.bfloat16),
+            pltpu.VMEM(first_kernel.shape, jnp.bfloat16),
+            pltpu.SemaphoreType.DMA((3,)),
+        ],
         compiler_params=params,
         name="main",
     )(where, strides, features, out_grad, *around, first_kernel, second_kernel)
@@ -238,18 +264,17 @@
     total = total.astype(jnp.bfloat16).reshape(planes, 9 * chans // planes, chans)
     spread = lax.all_to_all(total, PLANE, 0, 0, tiled=True)
 
-    spread, pre_grad = lax.optimization_barrier((spread, pre_grad))
     pre_field = pre_grad[None]
-    pair, next_pair = row_halos(pre_field, lon_count, lat_count)
+    around = row_halos(pre_field, lon_count, lat_count)
+    spread, around = lax.optimization_barrier((spread, around))
     part = jnp.sum(spread.astype(jnp.float32), axis=0)
     reach = 2
     while reach <= height:
         part = part + lax.ppermute(part, ("z", "core"), folded(height, cores, reach))
+        if reach == height // 2:
+            part, pre_field = lax.optimization_barrier((part, pre_field))
         reach *= 2
-        if reach == height:
-            part, pair = lax.optimization_barrier((part, pair))
-    part, next_pair = lax.optimization_barrier((part.astype(jnp.bfloat16), next_pair))
-    around = (pair, next_pair) + column_halos(pre_field, pair, next_pair, lon_count, lat_count)
+    around += column_halos(pre_field, *around, lon_count, lat_count)
     input_grad = pl.pallas_call(
         back_kernel,
         out_shape=jax.ShapeDtypeStruct(features.shape, jnp.bfloat16),
@@ -260,13 +285,21 @@
         name="back",
     )(where, strides, out_grad, pre_grad, *around, first_kernel)
 
-    copies = jnp.broadcast_to(part[None], (planes,) + part.shape)
+    copies = jnp.broadcast_to(part.astype(jnp.bfloat16)[None], (planes,) + part.shape)
     mine = lax.all_to_all(copies, PLANE, 0, 0, tiled=True).reshape(grads)
     mine, input_grad = lax.optimization_barrier((mine, input_grad))
     other = lax.ppermute(mine, "core", swap)
     scale = 1.0 / math.sqrt(cells * lat_count * lon_count)
-    first = jnp.where(core == 0, mine, other).astype(jnp.float32) * scale
-    second = jnp.where(core == 0, other, mine).astype(jnp.float32) * scale
+    block = pl.BlockSpec((9 * chans // 4, chans), lambda i: (i, 0))
+    first, second = pl.pallas_call(
+        lambda *refs: part_kernel(scale, *refs),
+        grid=(4,),
+        out_shape=[jax.ShapeDtypeStruct(grads, jnp.float32)] * 2,
+        in_specs=[smem, block, block],
+        out_specs=[block, block],
+        compiler_params=params,
+        name="part",
+    )(where, mine, other)
     return input_grad, first.reshape(first_kernel.shape), second.reshape(first_kernel.shape)
 
 

time: 121 us -> 125 us (1.033)
  blocking collectives: 23.1 us -> 0 us
  waiting for transfers between devices: 40.5 us -> 55.2 us
  starting transfers between devices: 38 us -> 49.3 us
  Pallas kernels: 8.42 us -> 12.6 us
  other arithmetic: 7.51 us -> 4.61 us
    all_to_all x1 -> x0, blocking collectives: 23.1 us -> none  [local(): spread = lax.all_to_all(total, PLANE, 0, 0, tiled=True)]
    ppermute x2, waiting for transfers between devices: 8.84 us -> 22.2 us  [row_halos(): return (pair, lax.ppermute(row(odd), ALL, between + across))]
    all_to_all x0 -> x1, starting transfers between devices: none -> 5.69 us  [local(): spread = lax.all_to_all(total, PLANE, 0, 0, tiled=True)]
    mul x1 -> x0, other arithmetic: 3.91 us -> none  [local(): second = jnp.where(core == 0, other, mine).astype(jnp.float32) * scale]
    pallas_call x0 -> x1, Pallas kernels: none -> 3.19 us  [local(): pl.pallas_call(lambda *refs: part_kernel(scale, *refs), grid=(4,), out_sh...]
    ppermute x3, waiting for transfers between devices: 10.2 us -> 13.2 us  [local(): lax.ppermute(part, ('z', 'core'), folded(height, cores, reach))]
    ppermute x2, waiting for transfers between devices: 8.98 us -> 6.27 us  [row_halos(): lax.ppermute(row(1 - odd), ALL, both_ways([(at(i, k), at(i, k + 1)) for i...]
    all_to_all x1, starting transfers between devices: 4.38 us -> 6.53 us  [local(): mine = lax.all_to_all(copies, PLANE, 0, 0, tiled=True).reshape(grads)]
  transfers between devices with their start and end apart: 14 -> 15, of which waited for: 13 -> 12; matrix products, arithmetic and copies ran while one was open for 0% -> 0% of each run, Pallas kernels for 2% -> 2%
where the time goes in v4:
time: 125 us
  waiting for transfers between devices  55.2 us (44%)
  starting transfers between devices  49.3 us (39%)
  Pallas kernels  12.6 us (10%)
  other arithmetic  4.61 us (4%)
  local copies, waits for them, and re-layouts  2.51 us (2%)
    ppermute x2, waiting for transfers between devices, row_halos(): return (pair, lax.ppermute(row(odd), ALL, between + across))  22.2 us
    ppermute x3, waiting for transfers between devices, local(): lax.ppermute(part, ('z', 'core'), folded(height, cores, reach))  13.2 us
    ppermute x2, starting transfers between devices, row_halos(): return (pair, lax.ppermute(row(odd), ALL, between + across))  7.29 us
    pallas_call x1, Pallas kernels, local(): pl.pallas_call(main_kernel, out_shape=[jax.ShapeDtypeStruct(grads, jnp.fl...  7.01 us
    ppermute x1, starting transfers between devices, local(): other = lax.ppermute(mine, 'core', swap)  6.66 us
    all_to_all x1, starting transfers between devices, local(): mine = lax.all_to_all(copies, PLANE, 0, 0, tiled=True).reshape(grads)  6.53 us
    ppermute x2, waiting for transfers between devices, row_halos(): lax.ppermute(row(1 - odd), ALL, both_ways([(at(i, k), at(i, k + 1)) for i...  6.27 us
    ppermute x2, starting transfers between devices, column_halos(): in_chip = lax.ppermute(edge((1 - core) * reach), 'core', [(0, 1), (1, 0)])  6.05 us
  transfers between devices with their start and end apart: 15, of which 12 were waited for; matrix products, arithmetic and copies ran while one was open for 0% of the time, Pallas kernels for 2%

profile of v4, /device:TPU:1, one launch (start us, length us, event | category | flops | bytes accessed | tf_op | source)
XLA Modules:
  0.0 125.0 jit_solution(9473704389292354339)
XLA Ops:
  0.6 0.0 copy-start.1
  0.6 0.0 copy-start.2
  0.7 0.0 copy-start.4
  0.7 0.0 copy-start
  0.7 1.3 %fusion.3 = (bf16[2,2,128,256]{3,2,1,0:T(8,128)(2,1)S(1)}, bf16[2,2,128,256]{3,2,1,0:T(8,128)(2,1)S(1)}) fusion(s32[]{:T(128)S(6)} %select_n.67, bf16[1,2,2,128,256]{4,3,2,1,0:T(8,128)(2,1)} %bitcast.50, bf16[1,2,2,128,256]{4,3,2,1,0:T(8,128)(2,1)} %bitcast.48, s32[]{:T(128)S(6)} %select_n.66), kind=kLoop, calls=%fused_computation.13 | loop fusion | flops 262144 | bytes 1048584 | tf_op jit(solution)/shard_map/jit(dynamic_index_in_dim)/squeeze | solution.py:183
  2.0 4.0 %collective-permute-start.1 = (bf16[2,2,128,256]{3,2,1,0:T(8,128)(2,1)S(1)}, bf16[2,2,128,256]{3,2,1,0:T(8,128)(2,1)S(1)}, u32[]{:S(2)}, u32[]{:S(2)}) collective-permute-start(bf16[2,2,128,256]{3,2,1,0:T(8,128)(2,1)S(1)} %get-tuple-element.33), channel_id=1, source_target_pairs={{1,2},{3,4},{5,6},{9,10},{11,12},{13,14},{17,18},{19,20},{21,22},{... | collective-permute-start | bytes 786440 | tf_op jit(solution)/shard_map/ppermute | solution.py:187
  6.0 2.7 %collective-permute-start = (bf16[2,2,128,256]{3,2,1,0:T(8,128)(2,1)S(1)}, bf16[2,2,128,256]{3,2,1,0:T(8,128)(2,1)S(1)}, u32[]{:S(2)}, u32[]{:S(2)}) collective-permute-start(bf16[2,2,128,256]{3,2,1,0:T(8,128)(2,1)S(1)} %get-tuple-element.34), channel_id=1, source_target_pairs={{0,1},{2,3},{4,5},{6,7},{8,9},{10,11},{12,13},{14,15},{16,17},{18,... | collective-permute-start | bytes 786440 | tf_op jit(solution)/shard_map/ppermute | solution.py:184
  8.7 0.0 copy-done.1
  8.7 0.0 copy-done.2
  8.7 7.7 %collective-permute-done.1.next_pair = bf16[2,2,128,256]{3,2,1,0:T(8,128)(2,1)S(1)} collective-permute-done((bf16[2,2,128,256]{3,2,1,0:T(8,128)(2,1)S(1)}, bf16[2,2,128,256]{3,2,1,0:T(8,128)(2,1)S(1)}, u32[]{:S(2)}, u32[]{:S(2)}) %collective-permute-start.1) | collective-permute-done | bytes 262176 | tf_op jit(solution)/shard_map/ppermute | solution.py:187
  16.4 5.6 %collective-permute-done.pair = bf16[2,2,128,256]{3,2,1,0:T(8,128)(2,1)S(1)} collective-permute-done((bf16[2,2,128,256]{3,2,1,0:T(8,128)(2,1)S(1)}, bf16[2,2,128,256]{3,2,1,0:T(8,128)(2,1)S(1)}, u32[]{:S(2)}, u32[]{:S(2)}) %collective-permute-start) | collective-permute-done | bytes 262176 | tf_op jit(solution)/shard_map/ppermute | solution.py:184
  22.0 1.8 %collective-permute-start.2 = (bf16[2,2,4,16,256]{4,3,2,1,0:T(8,128)(2,1)S(1)}, bf16[2,2,4,16,256]{4,3,2,1,0:T(8,128)(2,1)S(1)}, u32[]{:S(2)}, u32[]{:S(2)}) collective-permute-start(bf16[2,2,4,16,256]{4,3,2,1,0:T(8,128)(2,1)S(1)} %pad_maximum_fusion), channel_id=1, source_target_pairs={{0,8},{8,0},{1,9},{9,1},{2,10},{10,2},{3,11},{11,3},{4,12},{12,4},... | collective-permute-start | bytes 393224 | tf_op jit(solution)/shard_map/ppermute | solution.py:204
  23.9 1.6 %collective-permute-start.3 = (bf16[2,2,4,16,256]{4,3,2,1,0:T(8,128)(2,1)S(1)}, bf16[2,2,4,16,256]{4,3,2,1,0:T(8,128)(2,1)S(1)}, u32[]{:S(2)}, u32[]{:S(2)}) collective-permute-start(bf16[2,2,4,16,256]{4,3,2,1,0:T(8,128)(2,1)S(1)} %pad_maximum_fusion.1), channel_id=1, source_target_pairs={{8,16},{9,17},{10,18},{11,19},{12,20},{13,21},{14,22},{15,23},{24,... | collective-permute-start | bytes 393224 | tf_op jit(solution)/shard_map/ppermute | solution.py:203
  25.5 0.0 copy-done.4
  25.5 0.1 copy.11.strides
  25.6 0.1 pad_add_fusion.where.refs_0_
  25.7 0.0 collective-permute-done.2.in_chip
  25.7 2.7 %collective-permute-done.3.next_chip = bf16[2,2,4,16,256]{4,3,2,1,0:T(8,128)(2,1)S(1)} collective-permute-done((bf16[2,2,4,16,256]{4,3,2,1,0:T(8,128)(2,1)S(1)}, bf16[2,2,4,16,256]{4,3,2,1,0:T(8,128)(2,1)S(1)}, u32[]{:S(2)}, u32[]{:S(2)}) %collective-permute-start.3) | collective-permute-done | bytes 131104 | tf_op jit(solution)/shard_map/ppermute | solution.py:203
  28.4 0.0 copy-done
  28.4 1.3 %copy-done.3 = bf16[3,3,256,256]{3,2,1,0:T(8,128)(2,1)S(1)} copy-done((bf16[3,3,256,256]{3,2,1,0:T(8,128)(2,1)S(1)}, bf16[3,3,256,256]{3,2,1,0:T(8,128)(2,1)}, u32[]{:S(2)}) %copy-start.3) | copy-done | bytes 1179672
  29.6 7.0 %main.1 = (f32[2304,256]{1,0:T(8,128)}, bf16[2304,256]{1,0:T(8,128)(2,1)S(1)}, bf16[2,2,128,256]{3,2,1,0:T(8,128)(2,1)S(1)}) custom-call(s32[3]{0:T(128)S(1)} %pad_add_fusion.where.refs_0_, s32[2,16,3]{2,1,0:T(8,128)S(1)} %copy.11.strides, bf16[2,2,128,256]{3,2,1,0:T(8,128)(2,1)S(1)} %copy-done.2, bf16[2,2,128,256]{3,2,1,0:T(8,128)(2,1)S(1)} %copy-done.1, ...), custom_call_target="tpu_custom_call" | custom-call | tf_op jit(solution)/shard_map/main/pallas_call | solution.py:238
  36.7 4.1 %collective-permute-start.4 = (bf16[2304,256]{1,0:T(8,128)(2,1)S(1)}, bf16[2304,256]{1,0:T(8,128)(2,1)S(1)}, u32[]{:S(2)}, u32[]{:S(2)}) collective-permute-start(bf16[2304,256]{1,0:T(8,128)(2,1)S(1)} %get-tuple-element.16), channel_id=1, source_target_pairs={{0,8},{8,0},{1,9},{9,1},{2,10},{10,2},{3,11},{11,3},{4,12},{12,4},... | collective-permute-start | bytes 3538952 | tf_op jit(solution)/shard_map/ppermute | solution.py:262
  40.8 2.5 %collective-permute-done.4 = bf16[2304,256]{1,0:T(8,128)(2,1)S(1)} collective-permute-done((bf16[2304,256]{1,0:T(8,128)(2,1)S(1)}, bf16[2304,256]{1,0:T(8,128)(2,1)S(1)}, u32[]{:S(2)}, u32[]{:S(2)}) %collective-permute-start.4) | collective-permute-done | bytes 1179680 | tf_op jit(solution)/shard_map/ppermute | solution.py:262
  43.3 2.9 %add_convert_fusion = bf16[2304,256]{1,0:T(8,128)(2,1)} fusion(f32[2304,256]{1,0:T(8,128)} %get-tuple-element.15, bf16[2304,256]{1,0:T(8,128)(2,1)S(1)} %collective-permute-done.4), kind=kLoop, calls=%fused_computation.1 | loop fusion | flops 1769472 | bytes 4718592 | tf_op jit(solution)/shard_map/convert_element_type | solution.py:264
  46.2 5.7 %all-to-all-start = ((bf16[16,144,256]{2,1,0:T(8,128)(2,1)}), bf16[16,144,256]{2,1,0:T(8,128)(2,1)S(1)}, u32[]{:S(2)}, u32[]{:S(2)}) async-start(bf16[16,144,256]{2,1,0:T(8,128)(2,1)} %bitcast.53), calls=%async_computation | async-start | bytes 2359296 | tf_op jit(solution)/shard_map/all_to_all | solution.py:265
  52.0 3.3 %collective-permute-start.6 = (bf16[1,2,128,256]{3,2,1,0:T(8,128)(2,1)S(1)}, bf16[1,2,128,256]{3,2,1,0:T(8,128)(2,1)S(1)}, u32[]{:S(2)}, u32[]{:S(2)}) collective-permute-start(bf16[1,2,128,256]{3,2,1,0:T(8,128)(2,1)S(1)} %get-tuple-element.41), channel_id=1, source_target_pairs={{1,2},{3,4},{5,6},{9,10},{11,12},{13,14},{17,18},{19,20},{21,22},{... | collective-permute-start | bytes 393224 | tf_op jit(solution)/shard_map/ppermute | solution.py:187
  55.2 2.8 %collective-permute-start.5 = (bf16[1,2,128,256]{3,2,1,0:T(8,128)(2,1)S(1)}, bf16[1,2,128,256]{3,2,1,0:T(8,128)(2,1)S(1)}, u32[]{:S(2)}, u32[]{:S(2)}) collective-permute-start(bf16[1,2,128,256]{3,2,1,0:T(8,128)(2,1)S(1)} %get-tuple-element.42), channel_id=1, source_target_pairs={{0,1},{2,3},{4,5},{6,7},{8,9},{10,11},{12,13},{14,15},{16,17},{18,... | collective-permute-start | bytes 393224 | tf_op jit(solution)/shard_map/ppermute | solution.py:184
  58.0 14.6 %collective-permute-done.6.next_pair = bf16[1,2,128,256]{3,2,1,0:T(8,128)(2,1)S(1)} collective-permute-done((bf16[1,2,128,256]{3,2,1,0:T(8,128)(2,1)S(1)}, bf16[1,2,128,256]{3,2,1,0:T(8,128)(2,1)S(1)}, u32[]{:S(2)}, u32[]{:S(2)}) %collective-permute-start.6) | collective-permute-done | bytes 131104 | tf_op jit(solution)/shard_map/ppermute | solution.py:187
  72.6 0.7 collective-permute-done.5.pair
  73.2 0.0 all-to-all-done
  73.2 0.2 convert_reduce_fusion
  73.4 0.1 collective-permute-start.7
  73.5 4.0 %collective-permute-done.7 = f32[144,256]{1,0:T(8,128)S(1)} collective-permute-done((f32[144,256]{1,0:T(8,128)S(1)}, f32[144,256]{1,0:T(8,128)S(1)}, u32[]{:S(2)}, u32[]{:S(2)}) %collective-permute-start.7) | collective-permute-done | bytes 147488 | tf_op jit(solution)/shard_map/ppermute | solution.py:273
  77.5 4.2 %collective-permute-start.8 = (f32[144,256]{1,0:T(8,128)S(1)}, f32[144,256]{1,0:T(8,128)S(1)}, u32[]{:S(2)}, u32[]{:S(2)}) collective-permute-start(f32[144,256]{1,0:T(8,128)S(1)} %add.52), channel_id=1, source_target_pairs={{0,32},{8,104},{16,48},{24,120},{32,0},{40,72},{48,16},{56,88},{64... | collective-permute-start | bytes 442376 | tf_op jit(solution)/shard_map/ppermute | solution.py:273
  81.7 3.7 %collective-permute-done.8 = f32[144,256]{1,0:T(8,128)S(1)} collective-permute-done((f32[144,256]{1,0:T(8,128)S(1)}, f32[144,256]{1,0:T(8,128)S(1)}, u32[]{:S(2)}, u32[]{:S(2)}) %collective-permute-start.8) | collective-permute-done | bytes 147488 | tf_op jit(solution)/shard_map/ppermute | solution.py:273
  85.4 0.5 collective-permute-start.9
  85.9 5.5 %collective-permute-done.9 = f32[144,256]{1,0:T(8,128)S(1)} collective-permute-done((f32[144,256]{1,0:T(8,128)S(1)}, f32[144,256]{1,0:T(8,128)S(1)}, u32[]{:S(2)}, u32[]{:S(2)}) %collective-permute-start.9) | collective-permute-done | bytes 147488 | tf_op jit(solution)/shard_map/ppermute | solution.py:273
  91.4 1.1 broadcast_in_dim.38
  92.5 6.5 %all-to-all-start.1 = ((bf16[16,144,256]{2,1,0:T(8,128)(2,1)}), bf16[16,144,256]{2,1,0:T(8,128)(2,1)S(1)}, u32[]{:S(2)}, u32[]{:S(2)}) async-start(bf16[16,144,256]{2,1,0:T(8,128)(2,1)} %broadcast_in_dim.38), calls=%async_computation.1 | async-start | bytes 2359296 | tf_op jit(solution)/shard_map/all_to_all | solution.py:289
  99.1 4.2 %collective-permute-start.10 = (bf16[1,2,4,16,256]{4,3,2,1,0:T(8,128)(2,1)S(1)}, bf16[1,2,4,16,256]{4,3,2,1,0:T(8,128)(2,1)S(1)}, u32[]{:S(2)}, u32[]{:S(2)}) collective-permute-start(bf16[1,2,4,16,256]{4,3,2,1,0:T(8,128)(2,1)S(1)} %pad_maximum_fusion.2), channel_id=1, source_target_pairs={{0,8},{8,0},{1,9},{9,1},{2,10},{10,2},{3,11},{11,3},{4,12},{12,4},... | collective-permute-start | bytes 196616 | tf_op jit(solution)/shard_map/ppermute | solution.py:204
  103.4 1.0 collective-permute-start.11
  104.4 0.0 collective-permute-done.10.in_chip
  104.4 3.0 %collective-permute-done.11.next_chip = bf16[1,2,4,16,256]{4,3,2,1,0:T(8,128)(2,1)S(1)} collective-permute-done((bf16[1,2,4,16,256]{4,3,2,1,0:T(8,128)(2,1)S(1)}, bf16[1,2,4,16,256]{4,3,2,1,0:T(8,128)(2,1)S(1)}, u32[]{:S(2)}, u32[]{:S(2)}) %collective-permute-start.11) | collective-permute-done | bytes 65568 | tf_op jit(solution)/shard_map/ppermute | solution.py:203
  107.4 2.4 %back.1 = bf16[2,2,128,256]{3,2,1,0:T(8,128)(2,1)} custom-call(s32[3]{0:T(128)S(1)} %pad_add_fusion.where.refs_0_, s32[2,16,3]{2,1,0:T(8,128)S(1)} %copy.11.strides, bf16[2,2,128,256]{3,2,1,0:T(8,128)(2,1)S(1)} %copy-done.1, bf16[2,2,128,256]{3,2,1,0:T(8,128)(2,1)S(1)} %get-tuple-element.17.pre, bf16[1,2,128,256]{3,2,1,0:T(8,128)(2,1)S(1)} %collective-permute-done.5.pair, ...), custom_call_target="tpu_custom_call" | custom-call | tf_op jit(solution)/shard_map/back/pallas_call | solution.py:278
  109.8 2.9 %all-to-all-done.1 = bf16[16,144,256]{2,1,0:T(8,128)(2,1)S(1)} async-done(((bf16[16,144,256]{2,1,0:T(8,128)(2,1)}), bf16[16,144,256]{2,1,0:T(8,128)(2,1)S(1)}, u32[]{:S(2)}, u32[]{:S(2)}) %all-to-all-start.1) | async-done | bytes 1179680 | tf_op jit(solution)/shard_map/all_to_all | solution.py:289
  112.7 6.7 %collective-permute-start.12 = (bf16[2304,256]{1,0:T(8,128)(2,1)S(1)}, bf16[2304,256]{1,0:T(8,128)(2,1)S(1)}, u32[]{:S(2)}, u32[]{:S(2)}) collective-permute-start(bf16[2304,256]{1,0:T(8,128)(2,1)S(1)} %bitcast.46), channel_id=1, source_target_pairs={{0,8},{8,0},{1,9},{9,1},{2,10},{10,2},{3,11},{11,3},{4,12},{12,4},... | collective-permute-start | bytes 3538952 | tf_op jit(solution)/shard_map/ppermute | solution.py:291
  119.3 2.5 %collective-permute-done.12.refs_2_ = bf16[2304,256]{1,0:T(8,128)(2,1)S(1)} collective-permute-done((bf16[2304,256]{1,0:T(8,128)(2,1)S(1)}, bf16[2304,256]{1,0:T(8,128)(2,1)S(1)}, u32[]{:S(2)}, u32[]{:S(2)}) %collective-permute-start.12) | collective-permute-done | bytes 1179680 | tf_op jit(solution)/shard_map/ppermute | solution.py:291
  121.8 3.2 %part.1 = (f32[2304,256]{1,0:T(8,128)}, f32[2304,256]{1,0:T(8,128)}) custom-call(s32[3]{0:T(128)S(1)} %pad_add_fusion.where.refs_0_, bf16[2304,256]{1,0:T(8,128)(2,1)S(1)} %bitcast.47, bf16[2304,256]{1,0:T(8,128)(2,1)S(1)} %collective-permute-done.12.refs_2_), custom_call_target="tpu_custom_call" | custom-call | tf_op jit(solution)/shard_map/part/pallas_call | solution.py:294
  (13 shorter events, 0.2 us)
Async XLA Ops:
  0.6 8.1 %copy-start.1 = (bf16[2,2,128,256]{3,2,1,0:T(8,128)(2,1)S(1)}, bf16[2,2,128,256]{3,2,1,0:T(8,128)(2,1)}, u32[]{:S(2)}) copy-start(bf16[2,2,128,256]{3,2,1,0:T(8,128)(2,1)} %grad.3) | copy-start | bytes 786436
  0.6 8.0 %copy-start.2 = (bf16[2,2,128,256]{3,2,1,0:T(8,128)(2,1)S(1)}, bf16[2,2,128,256]{3,2,1,0:T(8,128)(2,1)}, u32[]{:S(2)}) copy-start(bf16[2,2,128,256]{3,2,1,0:T(8,128)(2,1)} %feat.1) | copy-start | bytes 786436
  0.7 24.9 %copy-start.4 = (s32[2,16,3]{1,0,2:T(2,128)S(1)}, s32[2,16,3]{1,0,2:T(2,128)}, u32[]{:S(2)}) copy-start(s32[2,16,3]{1,0,2:T(2,128)} %param.9) | copy-start | bytes 1156
  0.7 27.7 %copy-start = (bf16[3,3,256,256]{3,2,1,0:T(8,128)(2,1)S(1)}, bf16[3,3,256,256]{3,2,1,0:T(8,128)(2,1)}, u32[]{:S(2)}) copy-start(bf16[3,3,256,256]{3,2,1,0:T(8,128)(2,1)} %first_kernel.3) | copy-start | bytes 3538948
  2.0 14.4 %collective-permute-start.1 = (bf16[2,2,128,256]{3,2,1,0:T(8,128)(2,1)S(1)}, bf16[2,2,128,256]{3,2,1,0:T(8,128)(2,1)S(1)}, u32[]{:S(2)}, u32[]{:S(2)}) collective-permute-start(bf16[2,2,128,256]{3,2,1,0:T(8,128)(2,1)S(1)} %get-tuple-element.33), channel_id=1, source_target_pairs={{1,2},{3,4},{5,6},{9,10},{11,12},{13,14},{17,18},{19,20},{21,22},{... | collective-permute-start | bytes 786440 | tf_op jit(solution)/shard_map/ppermute | solution.py:187
  6.0 16.0 %collective-permute-start = (bf16[2,2,128,256]{3,2,1,0:T(8,128)(2,1)S(1)}, bf16[2,2,128,256]{3,2,1,0:T(8,128)(2,1)S(1)}, u32[]{:S(2)}, u32[]{:S(2)}) collective-permute-start(bf16[2,2,128,256]{3,2,1,0:T(8,128)(2,1)S(1)} %get-tuple-element.34), channel_id=1, source_target_pairs={{0,1},{2,3},{4,5},{6,7},{8,9},{10,11},{12,13},{14,15},{16,17},{18,... | collective-permute-start | bytes 786440 | tf_op jit(solution)/shard_map/ppermute | solution.py:184
  22.0 3.6 %collective-permute-start.2 = (bf16[2,2,4,16,256]{4,3,2,1,0:T(8,128)(2,1)S(1)}, bf16[2,2,4,16,256]{4,3,2,1,0:T(8,128)(2,1)S(1)}, u32[]{:S(2)}, u32[]{:S(2)}) collective-permute-start(bf16[2,2,4,16,256]{4,3,2,1,0:T(8,128)(2,1)S(1)} %pad_maximum_fusion), channel_id=1, source_target_pairs={{0,8},{8,0},{1,9},{9,1},{2,10},{10,2},{3,11},{11,3},{4,12},{12,4},... | collective-permute-start | bytes 393224 | tf_op jit(solution)/shard_map/ppermute | solution.py:204
  23.9 4.5 %collective-permute-start.3 = (bf16[2,2,4,16,256]{4,3,2,1,0:T(8,128)(2,1)S(1)}, bf16[2,2,4,16,256]{4,3,2,1,0:T(8,128)(2,1)S(1)}, u32[]{:S(2)}, u32[]{:S(2)}) collective-permute-start(bf16[2,2,4,16,256]{4,3,2,1,0:T(8,128)(2,1)S(1)} %pad_maximum_fusion.1), channel_id=1, source_target_pairs={{8,16},{9,17},{10,18},{11,19},{12,20},{13,21},{14,22},{15,23},{24,... | collective-permute-start | bytes 393224 | tf_op jit(solution)/shard_map/ppermute | solution.py:203
  28.4 1.3 %copy-start.3 = (bf16[3,3,256,256]{3,2,1,0:T(8,128)(2,1)S(1)}, bf16[3,3,256,256]{3,2,1,0:T(8,128)(2,1)}, u32[]{:S(2)}) copy-start(bf16[3,3,256,256]{3,2,1,0:T(8,128)(2,1)} %second_kernel.1) | copy-start | bytes 3538948
  36.7 6.6 %collective-permute-start.4 = (bf16[2304,256]{1,0:T(8,128)(2,1)S(1)}, bf16[2304,256]{1,0:T(8,128)(2,1)S(1)}, u32[]{:S(2)}, u32[]{:S(2)}) collective-permute-start(bf16[2304,256]{1,0:T(8,128)(2,1)S(1)} %get-tuple-element.16), channel_id=1, source_target_pairs={{0,8},{8,0},{1,9},{9,1},{2,10},{10,2},{3,11},{11,3},{4,12},{12,4},... | collective-permute-start | bytes 3538952 | tf_op jit(solution)/shard_map/ppermute | solution.py:262
  46.2 27.0 %all-to-all-start = ((bf16[16,144,256]{2,1,0:T(8,128)(2,1)}), bf16[16,144,256]{2,1,0:T(8,128)(2,1)S(1)}, u32[]{:S(2)}, u32[]{:S(2)}) async-start(bf16[16,144,256]{2,1,0:T(8,128)(2,1)} %bitcast.53), calls=%async_computation | async-start | bytes 2359296 | tf_op jit(solution)/shard_map/all_to_all | solution.py:265
  52.0 20.6 %collective-permute-start.6 = (bf16[1,2,128,256]{3,2,1,0:T(8,128)(2,1)S(1)}, bf16[1,2,128,256]{3,2,1,0:T(8,128)(2,1)S(1)}, u32[]{:S(2)}, u32[]{:S(2)}) collective-permute-start(bf16[1,2,128,256]{3,2,1,0:T(8,128)(2,1)S(1)} %get-tuple-element.41), channel_id=1, source_target_pairs={{1,2},{3,4},{5,6},{9,10},{11,12},{13,14},{17,18},{19,20},{21,22},{... | collective-permute-start | bytes 393224 | tf_op jit(solution)/shard_map/ppermute | solution.py:187
  55.2 18.0 %collective-permute-start.5 = (bf16[1,2,128,256]{3,2,1,0:T(8,128)(2,1)S(1)}, bf16[1,2,128,256]{3,2,1,0:T(8,128)(2,1)S(1)}, u32[]{:S(2)}, u32[]{:S(2)}) collective-permute-start(bf16[1,2,128,256]{3,2,1,0:T(8,128)(2,1)S(1)} %get-tuple-element.42), channel_id=1, source_target_pairs={{0,1},{2,3},{4,5},{6,7},{8,9},{10,11},{12,13},{14,15},{16,17},{18,... | collective-permute-start | bytes 393224 | tf_op jit(solution)/shard_map/ppermute | solution.py:184
  73.4 4.1 %collective-permute-start.7 = (f32[144,256]{1,0:T(8,128)S(1)}, f32[144,256]{1,0:T(8,128)S(1)}, u32[]{:S(2)}, u32[]{:S(2)}) collective-permute-start(f32[144,256]{1,0:T(8,128)S(1)} %convert_reduce_fusion), channel_id=1, source_target_pairs={{0,16},{8,24},{16,0},{24,8},{32,48},{40,56},{48,32},{56,40},{64,80... | collective-permute-start | bytes 442376 | tf_op jit(solution)/shard_map/ppermute | solution.py:273
  77.5 7.9 %collective-permute-start.8 = (f32[144,256]{1,0:T(8,128)S(1)}, f32[144,256]{1,0:T(8,128)S(1)}, u32[]{:S(2)}, u32[]{:S(2)}) collective-permute-start(f32[144,256]{1,0:T(8,128)S(1)} %add.52), channel_id=1, source_target_pairs={{0,32},{8,104},{16,48},{24,120},{32,0},{40,72},{48,16},{56,88},{64... | collective-permute-start | bytes 442376 | tf_op jit(solution)/shard_map/ppermute | solution.py:273
  85.4 6.0 %collective-permute-start.9 = (f32[144,256]{1,0:T(8,128)S(1)}, f32[144,256]{1,0:T(8,128)S(1)}, u32[]{:S(2)}, u32[]{:S(2)}) collective-permute-start(f32[144,256]{1,0:T(8,128)S(1)} %add.53), channel_id=1, source_target_pairs={{0,112},{8,56},{16,96},{24,40},{32,80},{40,24},{48,64},{56,8},{64,... | collective-permute-start | bytes 442376 | tf_op jit(solution)/shard_map/ppermute | solution.py:273
  92.5 20.1 %all-to-all-start.1 = ((bf16[16,144,256]{2,1,0:T(8,128)(2,1)}), bf16[16,144,256]{2,1,0:T(8,128)(2,1)S(1)}, u32[]{:S(2)}, u32[]{:S(2)}) async-start(bf16[16,144,256]{2,1,0:T(8,128)(2,1)} %broadcast_in_dim.38), calls=%async_computation.1 | async-start | bytes 2359296 | tf_op jit(solution)/shard_map/all_to_all | solution.py:289
  99.1 5.3 %collective-permute-start.10 = (bf16[1,2,4,16,256]{4,3,2,1,0:T(8,128)(2,1)S(1)}, bf16[1,2,4,16,256]{4,3,2,1,0:T(8,128)(2,1)S(1)}, u32[]{:S(2)}, u32[]{:S(2)}) collective-permute-start(bf16[1,2,4,16,256]{4,3,2,1,0:T(8,128)(2,1)S(1)} %pad_maximum_fusion.2), channel_id=1, source_target_pairs={{0,8},{8,0},{1,9},{9,1},{2,10},{10,2},{3,11},{11,3},{4,12},{12,4},... | collective-permute-start | bytes 196616 | tf_op jit(solution)/shard_map/ppermute | solution.py:204
  103.4 4.1 %collective-permute-start.11 = (bf16[1,2,4,16,256]{4,3,2,1,0:T(8,128)(2,1)S(1)}, bf16[1,2,4,16,256]{4,3,2,1,0:T(8,128)(2,1)S(1)}, u32[]{:S(2)}, u32[]{:S(2)}) collective-permute-start(bf16[1,2,4,16,256]{4,3,2,1,0:T(8,128)(2,1)S(1)} %pad_maximum_fusion.3), channel_id=1, source_target_pairs={{8,16},{9,17},{10,18},{11,19},{12,20},{13,21},{14,22},{15,23},{24,... | collective-permute-start | bytes 196616 | tf_op jit(solution)/shard_map/ppermute | solution.py:203
  112.7 9.1 %collective-permute-start.12 = (bf16[2304,256]{1,0:T(8,128)(2,1)S(1)}, bf16[2304,256]{1,0:T(8,128)(2,1)S(1)}, u32[]{:S(2)}, u32[]{:S(2)}) collective-permute-start(bf16[2304,256]{1,0:T(8,128)(2,1)S(1)} %bitcast.46), channel_id=1, source_target_pairs={{0,8},{8,0},{1,9},{9,1},{2,10},{10,2},{3,11},{11,3},{4,12},{12,4},... | collective-permute-start | bytes 3538952 | tf_op jit(solution)/shard_map/ppermute | solution.py:291

commit v5 on v3

--- a/solution.py
+++ b/solution.py
@@ -89,37 +89,85 @@
     return total
 
 
-def main_kernel(where, strides, feat, grad, pair, next_pair, in_chip, next_chip, first_kernel, second_kernel,
-                keep, send, pre_grad, ext_f, ext_g, taps_f, taps_g, act, sums):
-    lat, core = where[0], where[1]
-    mirror = lat == 0
+OWN = ((0, 1), (0, 2), (1, 0), (1, 1))
+
+
+def stretch(place, middle, near, far, core):
+    width = middle.shape[0]
+    near, far = near.astype(jnp.float32), far.astype(jnp.float32)
+    place[:SPAN] = jnp.where(core, near, far)
+    place[SPAN : SPAN + width] = middle.astype(jnp.float32)
+    place[SPAN + width : 2 * SPAN + width] = jnp.where(core, far, near)
+
+
+def moved(ext, at, shift, width):
+    return tap(ext, at // 4, at % 4, shift, width)
+
+
+def early_kernel(where, strides, feat, grad, in_chip, next_chip, first_kernel, second_kernel,
+                 taps_f, taps_g, pre_part, back_part, ext_f, ext_g):
+    lat, core = where[0], where[1] == 1
     width = feat.shape[2]
     half = 2 * width
-    halo = (pair, next_pair, in_chip, next_chip)
-    fill(ext_f, 0, feat, halo, where)
-    for row in range(2):
-        for s in range(2):
-            at = (row * 2 + s) * width
-            for k in range(3):
-                stride = strides[s, lat * 2 + row, k]
-                for col in range(3):
-                    shift = 0 if col == 1 else (col - 1) * stride
-                    taps_f[k * 3 + col, at : at + width] = tap(ext_f, s, row + k, shift, width)
-    fill(ext_g, 1, grad, halo, where)
-    adjoint_taps(ext_g, taps_g, strides, lat, width)
-
-    for row in range(2):
-        at = row * half
-        pre = None
-        for k in range(3):
+    for field, own, ext in ((0, feat, ext_f), (1, grad, ext_g)):
+        for s in range(2):
+            for row in range(2):
+                stretch(ext.at[s * 2 + row], own[s, row], in_chip[field, s, row], next_chip[field, s, row], core)
+    for i, (row, k) in enumerate(OWN):
+        for s in range(2):
+            ahead, behind = strides[s, lat * 2 + row, k], adjoint_stride(strides, s, row, k, lat)
+            at, cells = s * 2 + row + k - 1, slice(s * width, (s + 1) * width)
             for col in range(3):
-                term = dot(taps_f[k * 3 + col, at : at + half], first_kernel[k, col], NN)
+                taps_f[i * 3 + col, cells] = moved(ext_f, at, 0 if col == 1 else (col - 1) * ahead, width)
+                taps_g[i * 3 + col, cells] = moved(ext_g, at, 0 if col == 1 else (1 - col) * behind, width)
+    for row in range(2):
+        pre, back = None, None
+        for i, (at, k) in enumerate(OWN):
+            if at != row:
+                continue
+            for col in range(3):
+                term = dot(taps_f[i * 3 + col], first_kernel[k, col], NN)
                 pre = term if pre is None else pre + term
+                term = dot(taps_g[i * 3 + col], second_kernel[2 - k, col], NT)
+                back = term if back is None else back + term
+        pre_part[row * half : (row + 1) * half] = pre
+        back_part[row * half : (row + 1) * half] = back
+
+
+def main_kernel(where, strides, own_f, own_g, pre_part, back_part, pair, next_pair, in_chip, next_chip,
+                first_kernel, second_kernel, keep, send, pre_grad, ext_f, ext_g, edge_f, edge_g, act, sums):
+    lat, core = where[0], where[1]
+    odd, second_core = where[2] == 1, core == 1
+    mirror = lat == 0
+    width = pair.shape[2]
+    half = 2 * width
+    for field, ext in ((0, ext_f), (1, ext_g)):
+        for s in range(2):
+            one, other = pair[field, s], next_pair[field, s]
+            for row in range(2):
+                middle = jnp.where(odd, one, other) if row == 0 else jnp.where(odd, other, one)
+                stretch(ext.at[s * 2 + row], middle, in_chip[field, s, row], next_chip[field, s, row], second_core)
+    for row in range(2):
+        for s in range(2):
+            ahead, behind = strides[s, lat * 2 + row, 2 * row], adjoint_stride(strides, s, row, 2 * row, lat)
+            cells = slice(s * width, (s + 1) * width)
+            for col in range(3):
+                edge_f[row * 3 + col, cells] = moved(ext_f, s * 2 + row, 0 if col == 1 else (col - 1) * ahead, width)
+                edge_g[row * 3 + col, cells] = moved(ext_g, s * 2 + row, 0 if col == 1 else (1 - col) * behind, width)
+
+    for row in range(2):
+        at = slice(row * half, (row + 1) * half)
+        pre, back = pre_part[at], back_part[at]
+        for col in range(3):
+            pre += dot(edge_f[row * 3 + col], first_kernel[2 * row, col], NN)
+            weight = second_kernel[2 - 2 * row, col]
+            if row == 0:
+                weight = jnp.where(mirror, second_kernel[0, col], weight)
+            back += dot(edge_g[row * 3 + col], weight, NT)
         square = pre * pre
         bend = jnp.tanh(ROOT * (pre + CUBIC * (pre * square)))
-        act[at : at + half] = (0.5 * pre * (1.0 + bend)).astype(jnp.bfloat16)
+        act[at] = (0.5 * pre * (1.0 + bend)).astype(jnp.bfloat16)
         slope = 0.5 * (1.0 + bend) + 0.5 * pre * (1.0 - bend * bend) * (ROOT * (1.0 + 3.0 * CUBIC * square))
-        back = adjoint_product(taps_g, second_kernel, mirror, row, half)
         result = (back * slope).astype(jnp.bfloat16)
         for s in range(2):
             pre_grad[s, row] = result[s * width : (s + 1) * width]
@@ -128,18 +176,23 @@
         at = (k * 3 + col) * 256
         sums[jnp.where(core == owner, 0, 1), at : at + 256] = value
 
+    def taps_of(own, edge, row, k, col):
+        return own[OWN.index((row, k)) * 3 + col] if (row, k) in OWN else edge[row * 3 + col]
+
     turned = act[...].T
+    above, below = turned[:, :half], turned[:, half:]
     for col in range(3):
-        edge = dot(turned[:, :half], taps_g[col, :half], NN)
-        upper = dot(turned[:, half:], taps_g[col, half:], NN)
-        lower = dot(turned, taps_g[6 + col], NN)
-        place(dot(turned, taps_g[3 + col], NN), 1, col, 1)
+        edge, upper = (dot(a, taps_of(own_g, edge_g, r, 0, col), NN) for r, a in enumerate((above, below)))
+        centre, lower = (
+            sum(dot(a, taps_of(own_g, edge_g, r, slot, col), NN) for r, a in enumerate((above, below))) for slot in (1, 2)
+        )
+        place(centre, 1, col, 1)
         place(lower + jnp.where(mirror, edge, 0.0), 0, col, 1)
         place(upper + jnp.where(mirror, 0.0, edge), 2, col, 1)
-    pre_all = jnp.concatenate([pre_grad[s, row] for row in range(2) for s in range(2)], axis=0)
+    rows = [jnp.concatenate([pre_grad[s, row] for s in range(2)], axis=0) for row in range(2)]
     for k in range(3):
         for col in range(3):
-            place(dot(taps_f[k * 3 + col], pre_all, TN), k, col, 0)
+            place(sum(dot(taps_of(own_f, edge_f, r, k, col), rows[r], TN) for r in range(2)), k, col, 0)
     keep[...] = sums[0]
     send[...] = sums[1].astype(jnp.bfloat16)
 
@@ -155,6 +208,13 @@
         for s in range(2):
             own = grad[s, row].astype(jnp.float32)
             out[s, row] = (own + total[s * width : (s + 1) * width]).astype(jnp.bfloat16)
+
+
+def part_kernel(scale, where, mine, other, first, second):
+    own, swapped = mine[...].astype(jnp.float32) * scale, other[...].astype(jnp.float32) * scale
+    keeps = where[1] == 0
+    first[...] = jnp.where(keeps, own, swapped)
+    second[...] = jnp.where(keeps, swapped, own)
 
 
 def both_ways(pairs):
@@ -172,22 +232,23 @@
     return pair, lax.ppermute(row(odd), ALL, between + across)
 
 
-def column_halos(fields, pair, next_pair, lon_count, lat_count):
-    width = fields.shape[3]
+def column_halos(parts, width, lon_count, lat_count):
     at = lambda lon, lat: (lon % lon_count) * lat_count + lat
-    odd, core = lax.rem(lax.axis_index(("x", "yh")), 2) == 1, lax.axis_index("core")
+    core = lax.axis_index("core")
 
     def edge(start):
-        cut = lambda a: lax.dynamic_slice_in_dim(a, start, SPAN, a.ndim - 2)
-        one, other = cut(pair), cut(next_pair)
-        top, bottom = jnp.where(odd, one, other), jnp.where(odd, other, one)
-        return jnp.concatenate([top[:, :, None], cut(fields), bottom[:, :, None]], axis=2)
+        return jnp.concatenate([lax.dynamic_slice_in_dim(a, start, SPAN, 3) for a in parts], axis=2)
 
     reach = width - SPAN
     places = [(i, k) for i in range(0, lon_count, 2) for k in range(lat_count)]
     next_chip = lax.ppermute(edge(core * reach), ALL, both_ways([(at(i + 1, k), at(i + 2, k)) for i, k in places]))
     in_chip = lax.ppermute(edge((1 - core) * reach), "core", [(0, 1), (1, 0)])
     return in_chip, next_chip
+
+
+def ordered(pair, next_pair):
+    odd = lax.rem(lax.axis_index(("x", "yh")), 2) == 1
+    return jnp.where(odd, pair, next_pair)[:, :, None], jnp.where(odd, next_pair, pair)[:, :, None]
 
 
 def folded(count, cores, reach):
@@ -217,8 +278,23 @@
     swap = [(0, 1), (1, 0)]
 
     fields = jnp.stack([features, out_grad])
-    around = row_halos(fields, lon_count, lat_count)
-    around += column_halos(fields, *around, lon_count, lat_count)
+    rows_around = row_halos(fields, lon_count, lat_count)
+    own_columns = column_halos([fields], width, lon_count, lat_count)
+    ext_rows = pltpu.VMEM((2 * slabs, width + 2 * SPAN + 8, chans), jnp.float32)
+    half = slabs * width
+    early = pl.pallas_call(
+        early_kernel,
+        out_shape=[jax.ShapeDtypeStruct((3 * len(OWN), half, chans), jnp.bfloat16)] * 2
+        + [jax.ShapeDtypeStruct((cells, chans), jnp.float32)] * 2,
+        in_specs=[smem, smem] + [vmem] * 6,
+        out_specs=[vmem] * 4,
+        scratch_shapes=[ext_rows, ext_rows],
+        compiler_params=params,
+        name="early",
+    )(where, strides, features, out_grad, *own_columns, first_kernel, second_kernel)
+    early, rows_around = lax.optimization_barrier((early, rows_around))
+    corners = column_halos(ordered(*rows_around), width, lon_count, lat_count)
+    edge = pltpu.VMEM((6, half, chans), jnp.bfloat16)
     keep, send, pre_grad = pl.pallas_call(
         main_kernel,
         out_shape=[
@@ -226,12 +302,19 @@
             jax.ShapeDtypeStruct(grads, jnp.bfloat16),
             jax.ShapeDtypeStruct(features.shape, jnp.bfloat16),
         ],
-        in_specs=[smem, smem] + [vmem] * 8,
+        in_specs=[smem, smem] + [vmem] * 10,
         out_specs=[vmem] * 3,
-        scratch_shapes=[ext, ext, taps, taps, pltpu.VMEM((cells, chans), jnp.bfloat16), pltpu.VMEM((2,) + grads, jnp.float32)],
+        scratch_shapes=[
+            ext_rows,
+            ext_rows,
+            edge,
+            edge,
+            pltpu.VMEM((cells, chans), jnp.bfloat16),
+            pltpu.VMEM((2,) + grads, jnp.float32),
+        ],
         compiler_params=params,
         name="main",
-    )(where, strides, features, out_grad, *around, first_kernel, second_kernel)
+    )(where, strides, *early, *rows_around, *corners, first_kernel, second_kernel)
 
     total = keep + lax.ppermute(send, "core", swap).astype(jnp.float32)
     planes, height, cores = lax.axis_size(PLANE), lax.axis_size("z"), lax.axis_size("core")
@@ -249,7 +332,8 @@
         if reach == height:
             part, pair = lax.optimization_barrier((part, pair))
     part, next_pair = lax.optimization_barrier((part.astype(jnp.bfloat16), next_pair))
-    around = (pair, next_pair) + column_halos(pre_field, pair, next_pair, lon_count, lat_count)
+    above, below = ordered(pair, next_pair)
+    around = (pair, next_pair) + column_halos([above, pre_field, below], width, lon_count, lat_count)
     input_grad = pl.pallas_call(
         back_kernel,
         out_shape=jax.ShapeDtypeStruct(features.shape, jnp.bfloat16),
@@ -265,8 +349,16 @@
     mine, input_grad = lax.optimization_barrier((mine, input_grad))
     other = lax.ppermute(mine, "core", swap)
     scale = 1.0 / math.sqrt(cells * lat_count * lon_count)
-    first = jnp.where(core == 0, mine, other).astype(jnp.float32) * scale
-    second = jnp.where(core == 0, other, mine).astype(jnp.float32) * scale
+    block = pl.BlockSpec((9 * chans // 4, chans), lambda i: (i, 0))
+    first, second = pl.pallas_call(
+        lambda *refs: part_kernel(scale, *refs),
+        grid=(4,),
+        out_shape=[jax.ShapeDtypeStruct(grads, jnp.float32)] * 2,
+        in_specs=[smem, block, block],
+        out_specs=[block, block],
+        compiler_params=params,
+        name="part",
+    )(where, mine, other)
     return input_grad, first.reshape(first_kernel.shape), second.reshape(first_kernel.shape)
 
 

time: 121 us -> 119 us (0.983)
  waiting for transfers between devices: 40.5 us -> 29.4 us
  Pallas kernels: 8.42 us -> 15.1 us
  starting transfers between devices: 38 us -> 43.1 us
  other arithmetic: 7.51 us -> 3.67 us
  local copies, waits for them, and re-layouts: 2.5 us -> 3.73 us
    ppermute x2, waiting for transfers between devices: 8.84 us -> 1.4 us  [row_halos(): return (pair, lax.ppermute(row(odd), ALL, between + across))]
    pallas_call x0 -> x2, Pallas kernels: none -> 6.2 us  [the longest x1 3.19 us: local(): pl.pallas_call(lambda *refs: part_kernel(scale, *refs), grid=(4,), out_sh...]
    ppermute x2, waiting for transfers between devices: 8.98 us -> 4.05 us  [row_halos(): lax.ppermute(row(1 - odd), ALL, both_ways([(at(i, k), at(i, k + 1)) for i...]
    ppermute x2 -> x3, starting transfers between devices: 7.07 us -> 11.1 us  [column_halos(): in_chip = lax.ppermute(edge((1 - core) * reach), 'core', [(0, 1), (1, 0)])]
    mul x1 -> x0, other arithmetic: 3.91 us -> none  [local(): second = jnp.where(core == 0, other, mine).astype(jnp.float32) * scale]
    ppermute x2 -> x3, starting transfers between devices: 2.43 us -> 4.19 us  [column_halos(): lax.ppermute(edge(core * reach), ALL, both_ways([(at(i + 1, k), at(i + 2,...]
    unnamed x11 -> x13, local copies, waits for them, and re-layouts: 1.38 us -> 2.57 us
    ppermute x2 -> x3, waiting for transfers between devices: 5.97 us -> 6.03 us  [column_halos(): lax.ppermute(edge(core * reach), ALL, both_ways([(at(i + 1, k), at(i + 2,...]
  transfers between devices with their start and end apart: 14 -> 16, of which waited for: 13 -> 13; matrix products, arithmetic and copies ran while one was open for 0% -> 0% of each run, Pallas kernels for 2% -> 5%
where the time goes in v5:
time: 119 us
  starting transfers between devices  43.1 us (36%)
  waiting for transfers between devices  29.4 us (25%)
  blocking collectives  23.1 us (19%)
  Pallas kernels  15.1 us (13%)
  local copies, waits for them, and re-layouts  3.73 us (3%)
  other arithmetic  3.67 us (3%)
    all_to_all x1, blocking collectives, local(): spread = lax.all_to_all(total, PLANE, 0, 0, tiled=True)  23.1 us
    ppermute x3, starting transfers between devices, column_halos(): in_chip = lax.ppermute(edge((1 - core) * reach), 'core', [(0, 1), (1, 0)])  11.1 us
    ppermute x3, waiting for transfers between devices, local(): lax.ppermute(part, ('z', 'core'), folded(height, cores, reach))  10.1 us
    pallas_call x1, Pallas kernels, local(): pl.pallas_call(main_kernel, out_shape=[jax.ShapeDtypeStruct(grads, jnp.fl...  6.53 us
    ppermute x1, starting transfers between devices, local(): other = lax.ppermute(mine, 'core', swap)  6.17 us
    ppermute x3, waiting for transfers between devices, column_halos(): lax.ppermute(edge(core * reach), ALL, both_ways([(at(i + 1, k), at(i + 2,...  6.03 us
    ppermute x2, starting transfers between devices, row_halos(): return (pair, lax.ppermute(row(odd), ALL, between + across))  5.94 us
    ppermute x3, starting transfers between devices, column_halos(): lax.ppermute(edge(core * reach), ALL, both_ways([(at(i + 1, k), at(i + 2,...  4.19 us
  transfers between devices with their start and end apart: 16, of which 13 were waited for; matrix products, arithmetic and copies ran while one was open for 0% of the time, Pallas kernels for 5%

profile of v5, /device:TPU:1, one launch (start us, length us, event | category | flops | bytes accessed | tf_op | source)
XLA Modules:
  0.0 118.9 jit_solution(13684745532435568323)
XLA Ops:
  0.6 0.0 copy-start.2
  0.6 0.0 copy-start.3
  0.7 1.3 %fusion.1 = (bf16[2,2,128,256]{3,2,1,0:T(8,128)(2,1)S(1)}, bf16[2,2,128,256]{3,2,1,0:T(8,128)(2,1)S(1)}) fusion(s32[]{:T(128)S(6)} %select_n.53, bf16[1,2,2,128,256]{4,3,2,1,0:T(8,128)(2,1)} %bitcast.41, bf16[1,2,2,128,256]{4,3,2,1,0:T(8,128)(2,1)} %bitcast.39, s32[]{:T(128)S(6)} %select_n.52), kind=kLoop, calls=%fused_computation.11 | loop fusion | flops 262144 | bytes 1048584 | tf_op jit(solution)/shard_map/jit(dynamic_index_in_dim)/squeeze | solution.py:228
  2.0 4.0 %collective-permute-start.3 = (bf16[2,2,128,256]{3,2,1,0:T(8,128)(2,1)S(1)}, bf16[2,2,128,256]{3,2,1,0:T(8,128)(2,1)S(1)}, u32[]{:S(2)}, u32[]{:S(2)}) collective-permute-start(bf16[2,2,128,256]{3,2,1,0:T(8,128)(2,1)S(1)} %get-tuple-element.51), channel_id=1, source_target_pairs={{1,2},{3,4},{5,6},{9,10},{11,12},{13,14},{17,18},{19,20},{21,22},{... | collective-permute-start | bytes 786440 | tf_op jit(solution)/shard_map/ppermute | solution.py:232
  6.0 2.7 %collective-permute-start.2 = (bf16[2,2,128,256]{3,2,1,0:T(8,128)(2,1)S(1)}, bf16[2,2,128,256]{3,2,1,0:T(8,128)(2,1)S(1)}, u32[]{:S(2)}, u32[]{:S(2)}) collective-permute-start(bf16[2,2,128,256]{3,2,1,0:T(8,128)(2,1)S(1)} %get-tuple-element.52), channel_id=1, source_target_pairs={{0,1},{2,3},{4,5},{6,7},{8,9},{10,11},{12,13},{14,15},{16,17},{18,... | collective-permute-start | bytes 786440 | tf_op jit(solution)/shard_map/ppermute | solution.py:229
  8.7 0.0 copy-done.2
  8.7 2.8 %collective-permute-start.1 = (bf16[2,2,2,16,256]{4,3,2,1,0:T(8,128)(2,1)S(1)}, bf16[2,2,2,16,256]{4,3,2,1,0:T(8,128)(2,1)S(1)}, u32[]{:S(2)}, u32[]{:S(2)}) collective-permute-start(bf16[2,2,2,16,256]{4,3,2,1,0:T(8,128)(2,1)S(1)} %get-tuple-element.53), channel_id=1, source_target_pairs={{8,16},{9,17},{10,18},{11,19},{12,20},{13,21},{14,22},{15,23},{24,... | collective-permute-start | bytes 196616 | tf_op jit(solution)/shard_map/ppermute | solution.py:244
  11.5 4.2 %collective-permute-start = (bf16[2,2,2,16,256]{4,3,2,1,0:T(8,128)(2,1)S(1)}, bf16[2,2,2,16,256]{4,3,2,1,0:T(8,128)(2,1)S(1)}, u32[]{:S(2)}, u32[]{:S(2)}) collective-permute-start(bf16[2,2,2,16,256]{4,3,2,1,0:T(8,128)(2,1)S(1)} %get-tuple-element.54), channel_id=1, source_target_pairs={{0,8},{8,0},{1,9},{9,1},{2,10},{10,2},{3,11},{11,3},{4,12},{12,4},... | collective-permute-start | bytes 196616 | tf_op jit(solution)/shard_map/ppermute | solution.py:245
  15.8 0.1 copy.9.strides
  15.9 0.1 pad_add_fusion.where.refs_0_
  15.9 0.0 collective-permute-done.1.next_chip
  15.9 0.7 collective-permute-done.in_chip
  16.7 1.3 %copy-done.1 = bf16[3,3,256,256]{3,2,1,0:T(8,128)(2,1)S(1)} copy-done((bf16[3,3,256,256]{3,2,1,0:T(8,128)(2,1)S(1)}, bf16[3,3,256,256]{3,2,1,0:T(8,128)(2,1)}, u32[]{:S(2)}) %copy-start.1) | copy-done | bytes 1179672
  18.0 3.0 %early.1 = (bf16[12,256,256]{2,1,0:T(8,128)(2,1)S(1)}, bf16[12,256,256]{2,1,0:T(8,128)(2,1)}, f32[512,256]{1,0:T(8,128)S(1)}, f32[512,256]{1,0:T(8,128)S(1)}) custom-call(s32[3]{0:T(128)S(1)} %pad_add_fusion.where.refs_0_, s32[2,16,3]{2,1,0:T(8,128)S(1)} %copy.9.strides, bf16[2,2,128,256]{3,2,1,0:T(8,128)(2,1)S(1)} %copy-done.3, ...), custom_call_target="tpu_custom_call" | custom-call | tf_op jit(solution)/shard_map/early/pallas_call | solution.py:285
  21.0 1.2 copy-done.4
  22.2 0.0 collective-permute-done.3.next_pair
  22.2 0.5 collective-permute-done.2.pair
  22.8 1.8 %collective-permute-start.4 = (bf16[2,2,2,16,256]{4,3,2,1,0:T(8,128)(2,1)S(1)}, bf16[2,2,2,16,256]{4,3,2,1,0:T(8,128)(2,1)S(1)}, u32[]{:S(2)}, u32[]{:S(2)}) collective-permute-start(bf16[2,2,2,16,256]{4,3,2,1,0:T(8,128)(2,1)S(1)} %pad_maximum_fusion), channel_id=1, source_target_pairs={{0,8},{8,0},{1,9},{9,1},{2,10},{10,2},{3,11},{11,3},{4,12},{12,4},... | collective-permute-start | bytes 196616 | tf_op jit(solution)/shard_map/ppermute | solution.py:245
  24.6 0.9 collective-permute-start.5
  25.5 0.0 collective-permute-done.4.in_chip
  25.5 2.8 %collective-permute-done.5.next_chip = bf16[2,2,2,16,256]{4,3,2,1,0:T(8,128)(2,1)S(1)} collective-permute-done((bf16[2,2,2,16,256]{4,3,2,1,0:T(8,128)(2,1)S(1)}, bf16[2,2,2,16,256]{4,3,2,1,0:T(8,128)(2,1)S(1)}, u32[]{:S(2)}, u32[]{:S(2)}) %collective-permute-start.5) | collective-permute-done | bytes 65568 | tf_op jit(solution)/shard_map/ppermute | solution.py:244
  28.4 6.5 %main.1 = (f32[2304,256]{1,0:T(8,128)}, bf16[2304,256]{1,0:T(8,128)(2,1)S(1)}, bf16[2,2,128,256]{3,2,1,0:T(8,128)(2,1)S(1)}) custom-call(s32[3]{0:T(128)S(1)} %pad_add_fusion.where.refs_0_, s32[2,16,3]{2,1,0:T(8,128)S(1)} %copy.9.strides, bf16[12,256,256]{2,1,0:T(8,128)(2,1)} %copy-done.4, bf16[12,256,256]{2,1,0:T(8,128)(2,1)} %get-tuple-element.31.own_g, ...), custom_call_target="tpu_custom_call" | custom-call | tf_op jit(solution)/shard_map/main/pallas_call | solution.py:298
  34.9 4.1 %collective-permute-start.6 = (bf16[2304,256]{1,0:T(8,128)(2,1)S(1)}, bf16[2304,256]{1,0:T(8,128)(2,1)S(1)}, u32[]{:S(2)}, u32[]{:S(2)}) collective-permute-start(bf16[2304,256]{1,0:T(8,128)(2,1)S(1)} %get-tuple-element.37), channel_id=1, source_target_pairs={{0,8},{8,0},{1,9},{9,1},{2,10},{10,2},{3,11},{11,3},{4,12},{12,4},... | collective-permute-start | bytes 3538952 | tf_op jit(solution)/shard_map/ppermute | solution.py:319
  39.1 2.5 %collective-permute-done.6 = bf16[2304,256]{1,0:T(8,128)(2,1)S(1)} collective-permute-done((bf16[2304,256]{1,0:T(8,128)(2,1)S(1)}, bf16[2304,256]{1,0:T(8,128)(2,1)S(1)}, u32[]{:S(2)}, u32[]{:S(2)}) %collective-permute-start.6) | collective-permute-done | bytes 1179680 | tf_op jit(solution)/shard_map/ppermute | solution.py:319
  41.5 2.0 %add_convert_fusion = bf16[2304,256]{1,0:T(8,128)(2,1)S(1)} fusion(f32[2304,256]{1,0:T(8,128)} %get-tuple-element.36, bf16[2304,256]{1,0:T(8,128)(2,1)S(1)} %collective-permute-done.6), kind=kLoop, calls=%fused_computation.1 | loop fusion | flops 1769472 | bytes 4718592 | tf_op jit(solution)/shard_map/convert_element_type | solution.py:321
  43.5 23.1 %all_to_all.10 = bf16[16,144,256]{2,1,0:T(8,128)(2,1)S(1)} all-to-all(bf16[16,144,256]{2,1,0:T(8,128)(2,1)S(1)} %bitcast.43), channel_id=1, replica_groups=mesh['yl'=2,'z'=8,'core'=2,'x'=4,'yh'=2] {'x','yh','yl'}, dimensions={0} | all-to-all | bytes 2359296 | tf_op jit(solution)/shard_map/all_to_all | solution.py:322
  66.6 0.2 convert_reduce_fusion
  66.8 0.1 collective-permute-start.7
  66.9 4.0 %collective-permute-done.7 = f32[144,256]{1,0:T(8,128)S(1)} collective-permute-done((f32[144,256]{1,0:T(8,128)S(1)}, f32[144,256]{1,0:T(8,128)S(1)}, u32[]{:S(2)}, u32[]{:S(2)}) %collective-permute-start.7) | collective-permute-done | bytes 147488 | tf_op jit(solution)/shard_map/ppermute | solution.py:330
  70.9 3.4 %collective-permute-start.8 = (f32[144,256]{1,0:T(8,128)S(1)}, f32[144,256]{1,0:T(8,128)S(1)}, u32[]{:S(2)}, u32[]{:S(2)}) collective-permute-start(f32[144,256]{1,0:T(8,128)S(1)} %add.52), channel_id=1, source_target_pairs={{0,32},{8,104},{16,48},{24,120},{32,0},{40,72},{48,16},{56,88},{64... | collective-permute-start | bytes 442376 | tf_op jit(solution)/shard_map/ppermute | solution.py:330
  74.3 1.4 %collective-permute-start.9 = (bf16[1,2,128,256]{3,2,1,0:T(8,128)(2,1)S(1)}, bf16[1,2,128,256]{3,2,1,0:T(8,128)(2,1)S(1)}, u32[]{:S(2)}, u32[]{:S(2)}) collective-permute-start(bf16[1,2,128,256]{3,2,1,0:T(8,128)(2,1)S(1)} %get-tuple-element.60), channel_id=1, source_target_pairs={{0,1},{2,3},{4,5},{6,7},{8,9},{10,11},{12,13},{14,15},{16,17},{18,... | collective-permute-start | bytes 393224 | tf_op jit(solution)/shard_map/ppermute | solution.py:229
  75.7 2.0 %collective-permute-done.8 = f32[144,256]{1,0:T(8,128)S(1)} collective-permute-done((f32[144,256]{1,0:T(8,128)S(1)}, f32[144,256]{1,0:T(8,128)S(1)}, u32[]{:S(2)}, u32[]{:S(2)}) %collective-permute-start.8) | collective-permute-done | bytes 147488 | tf_op jit(solution)/shard_map/ppermute | solution.py:330
  77.8 3.5 %collective-permute-done.9.pair = bf16[1,2,128,256]{3,2,1,0:T(8,128)(2,1)S(1)} collective-permute-done((bf16[1,2,128,256]{3,2,1,0:T(8,128)(2,1)S(1)}, bf16[1,2,128,256]{3,2,1,0:T(8,128)(2,1)S(1)}, u32[]{:S(2)}, u32[]{:S(2)}) %collective-permute-start.9) | collective-permute-done | bytes 131104 | tf_op jit(solution)/shard_map/ppermute | solution.py:229
  81.3 0.0 collective-permute-start.10
  81.3 1.9 %collective-permute-start.11 = (bf16[1,2,128,256]{3,2,1,0:T(8,128)(2,1)S(1)}, bf16[1,2,128,256]{3,2,1,0:T(8,128)(2,1)S(1)}, u32[]{:S(2)}, u32[]{:S(2)}) collective-permute-start(bf16[1,2,128,256]{3,2,1,0:T(8,128)(2,1)S(1)} %get-tuple-element.59), channel_id=1, source_target_pairs={{1,2},{3,4},{5,6},{9,10},{11,12},{13,14},{17,18},{19,20},{21,22},{... | collective-permute-start | bytes 393224 | tf_op jit(solution)/shard_map/ppermute | solution.py:232
  83.2 4.1 %collective-permute-done.10 = f32[144,256]{1,0:T(8,128)S(1)} collective-permute-done((f32[144,256]{1,0:T(8,128)S(1)}, f32[144,256]{1,0:T(8,128)S(1)}, u32[]{:S(2)}, u32[]{:S(2)}) %collective-permute-start.10) | collective-permute-done | bytes 147488 | tf_op jit(solution)/shard_map/ppermute | solution.py:330
  87.3 1.4 %collective-permute-done.11.next_pair = bf16[1,2,128,256]{3,2,1,0:T(8,128)(2,1)S(1)} collective-permute-done((bf16[1,2,128,256]{3,2,1,0:T(8,128)(2,1)S(1)}, bf16[1,2,128,256]{3,2,1,0:T(8,128)(2,1)S(1)}, u32[]{:S(2)}, u32[]{:S(2)}) %collective-permute-start.11) | collective-permute-done | bytes 131104 | tf_op jit(solution)/shard_map/ppermute | solution.py:232
  88.7 1.1 broadcast_in_dim.2
  89.8 3.9 %all-to-all-start.1 = ((bf16[16,144,256]{2,1,0:T(8,128)(2,1)}), bf16[16,144,256]{2,1,0:T(8,128)(2,1)S(1)}, u32[]{:S(2)}, u32[]{:S(2)}) async-start(bf16[16,144,256]{2,1,0:T(8,128)(2,1)} %broadcast_in_dim.2), calls=%async_computation.1 | async-start | bytes 2359296 | tf_op jit(solution)/shard_map/all_to_all | solution.py:348
  93.8 5.1 %collective-permute-start.12 = (bf16[1,2,4,16,256]{4,3,2,1,0:T(8,128)(2,1)S(1)}, bf16[1,2,4,16,256]{4,3,2,1,0:T(8,128)(2,1)S(1)}, u32[]{:S(2)}, u32[]{:S(2)}) collective-permute-start(bf16[1,2,4,16,256]{4,3,2,1,0:T(8,128)(2,1)S(1)} %pad_maximum_fusion.2), channel_id=1, source_target_pairs={{0,8},{8,0},{1,9},{9,1},{2,10},{10,2},{3,11},{11,3},{4,12},{12,4},... | collective-permute-start | bytes 196616 | tf_op jit(solution)/shard_map/ppermute | solution.py:245
  98.9 0.4 collective-permute-start.13
  99.3 0.5 collective-permute-done.12.in_chip
  99.8 3.2 %collective-permute-done.13.next_chip = bf16[1,2,4,16,256]{4,3,2,1,0:T(8,128)(2,1)S(1)} collective-permute-done((bf16[1,2,4,16,256]{4,3,2,1,0:T(8,128)(2,1)S(1)}, bf16[1,2,4,16,256]{4,3,2,1,0:T(8,128)(2,1)S(1)}, u32[]{:S(2)}, u32[]{:S(2)}) %collective-permute-start.13) | collective-permute-done | bytes 65568 | tf_op jit(solution)/shard_map/ppermute | solution.py:244
  103.0 2.4 %back.1 = bf16[2,2,128,256]{3,2,1,0:T(8,128)(2,1)} custom-call(s32[3]{0:T(128)S(1)} %pad_add_fusion.where.refs_0_, s32[2,16,3]{2,1,0:T(8,128)S(1)} %copy.9.strides, bf16[2,2,128,256]{3,2,1,0:T(8,128)(2,1)S(1)} %copy-done.2, bf16[2,2,128,256]{3,2,1,0:T(8,128)(2,1)S(1)} %get-tuple-element.40.pre, bf16[1,2,128,256]{3,2,1,0:T(8,128)(2,1)S(1)} %collective-permute-done.9.pair, ...), custom_call_target="tpu_custom_call" | custom-call | tf_op jit(solution)/shard_map/back/pallas_call | solution.py:337
  105.4 1.7 %all-to-all-done.1 = bf16[16,144,256]{2,1,0:T(8,128)(2,1)S(1)} async-done(((bf16[16,144,256]{2,1,0:T(8,128)(2,1)}), bf16[16,144,256]{2,1,0:T(8,128)(2,1)S(1)}, u32[]{:S(2)}, u32[]{:S(2)}) %all-to-all-start.1) | async-done | bytes 1179680 | tf_op jit(solution)/shard_map/all_to_all | solution.py:348
  107.1 6.2 %collective-permute-start.14 = (bf16[2304,256]{1,0:T(8,128)(2,1)S(1)}, bf16[2304,256]{1,0:T(8,128)(2,1)S(1)}, u32[]{:S(2)}, u32[]{:S(2)}) collective-permute-start(bf16[2304,256]{1,0:T(8,128)(2,1)S(1)} %bitcast.37), channel_id=1, source_target_pairs={{0,8},{8,0},{1,9},{9,1},{2,10},{10,2},{3,11},{11,3},{4,12},{12,4},... | collective-permute-start | bytes 3538952 | tf_op jit(solution)/shard_map/ppermute | solution.py:350
  113.2 2.5 %collective-permute-done.14.refs_2_ = bf16[2304,256]{1,0:T(8,128)(2,1)S(1)} collective-permute-done((bf16[2304,256]{1,0:T(8,128)(2,1)S(1)}, bf16[2304,256]{1,0:T(8,128)(2,1)S(1)}, u32[]{:S(2)}, u32[]{:S(2)}) %collective-permute-start.14) | collective-permute-done | bytes 1179680 | tf_op jit(solution)/shard_map/ppermute | solution.py:350
  115.7 3.2 %part.1 = (f32[2304,256]{1,0:T(8,128)}, f32[2304,256]{1,0:T(8,128)}) custom-call(s32[3]{0:T(128)S(1)} %pad_add_fusion.where.refs_0_, bf16[2304,256]{1,0:T(8,128)(2,1)S(1)} %bitcast.38, bf16[2304,256]{1,0:T(8,128)(2,1)S(1)} %collective-permute-done.14.refs_2_), custom_call_target="tpu_custom_call" | custom-call | tf_op jit(solution)/shard_map/part/pallas_call | solution.py:353
  (22 shorter events, 0.3 us)
Async XLA Ops:
  0.6 8.1 %copy-start.2 = (bf16[2,2,128,256]{3,2,1,0:T(8,128)(2,1)S(1)}, bf16[2,2,128,256]{3,2,1,0:T(8,128)(2,1)}, u32[]{:S(2)}) copy-start(bf16[2,2,128,256]{3,2,1,0:T(8,128)(2,1)} %grad.3) | copy-start | bytes 786436
  0.6 8.0 %copy-start.3 = (bf16[2,2,128,256]{3,2,1,0:T(8,128)(2,1)S(1)}, bf16[2,2,128,256]{3,2,1,0:T(8,128)(2,1)}, u32[]{:S(2)}) copy-start(bf16[2,2,128,256]{3,2,1,0:T(8,128)(2,1)} %feat.1) | copy-start | bytes 786436
  0.7 15.1 %copy-start.5 = (s32[2,16,3]{1,0,2:T(2,128)S(1)}, s32[2,16,3]{1,0,2:T(2,128)}, u32[]{:S(2)}) copy-start(s32[2,16,3]{1,0,2:T(2,128)} %param.9) | copy-start | bytes 1156
  0.7 16.0 %copy-start = (bf16[3,3,256,256]{3,2,1,0:T(8,128)(2,1)S(1)}, bf16[3,3,256,256]{3,2,1,0:T(8,128)(2,1)}, u32[]{:S(2)}) copy-start(bf16[3,3,256,256]{3,2,1,0:T(8,128)(2,1)} %first_kernel.5) | copy-start | bytes 3538948
  2.0 20.2 %collective-permute-start.3 = (bf16[2,2,128,256]{3,2,1,0:T(8,128)(2,1)S(1)}, bf16[2,2,128,256]{3,2,1,0:T(8,128)(2,1)S(1)}, u32[]{:S(2)}, u32[]{:S(2)}) collective-permute-start(bf16[2,2,128,256]{3,2,1,0:T(8,128)(2,1)S(1)} %get-tuple-element.51), channel_id=1, source_target_pairs={{1,2},{3,4},{5,6},{9,10},{11,12},{13,14},{17,18},{19,20},{21,22},{... | collective-permute-start | bytes 786440 | tf_op jit(solution)/shard_map/ppermute | solution.py:232
  6.0 16.7 %collective-permute-start.2 = (bf16[2,2,128,256]{3,2,1,0:T(8,128)(2,1)S(1)}, bf16[2,2,128,256]{3,2,1,0:T(8,128)(2,1)S(1)}, u32[]{:S(2)}, u32[]{:S(2)}) collective-permute-start(bf16[2,2,128,256]{3,2,1,0:T(8,128)(2,1)S(1)} %get-tuple-element.52), channel_id=1, source_target_pairs={{0,1},{2,3},{4,5},{6,7},{8,9},{10,11},{12,13},{14,15},{16,17},{18,... | collective-permute-start | bytes 786440 | tf_op jit(solution)/shard_map/ppermute | solution.py:229
  8.7 7.2 %collective-permute-start.1 = (bf16[2,2,2,16,256]{4,3,2,1,0:T(8,128)(2,1)S(1)}, bf16[2,2,2,16,256]{4,3,2,1,0:T(8,128)(2,1)S(1)}, u32[]{:S(2)}, u32[]{:S(2)}) collective-permute-start(bf16[2,2,2,16,256]{4,3,2,1,0:T(8,128)(2,1)S(1)} %get-tuple-element.53), channel_id=1, source_target_pairs={{8,16},{9,17},{10,18},{11,19},{12,20},{13,21},{14,22},{15,23},{24,... | collective-permute-start | bytes 196616 | tf_op jit(solution)/shard_map/ppermute | solution.py:244
  11.5 5.1 %collective-permute-start = (bf16[2,2,2,16,256]{4,3,2,1,0:T(8,128)(2,1)S(1)}, bf16[2,2,2,16,256]{4,3,2,1,0:T(8,128)(2,1)S(1)}, u32[]{:S(2)}, u32[]{:S(2)}) collective-permute-start(bf16[2,2,2,16,256]{4,3,2,1,0:T(8,128)(2,1)S(1)} %get-tuple-element.54), channel_id=1, source_target_pairs={{0,8},{8,0},{1,9},{9,1},{2,10},{10,2},{3,11},{11,3},{4,12},{12,4},... | collective-permute-start | bytes 196616 | tf_op jit(solution)/shard_map/ppermute | solution.py:245
  16.7 1.3 %copy-start.1 = (bf16[3,3,256,256]{3,2,1,0:T(8,128)(2,1)S(1)}, bf16[3,3,256,256]{3,2,1,0:T(8,128)(2,1)}, u32[]{:S(2)}) copy-start(bf16[3,3,256,256]{3,2,1,0:T(8,128)(2,1)} %second_kernel.3) | copy-start | bytes 3538948
  21.0 1.2 %copy-start.4 = (bf16[12,256,256]{2,1,0:T(8,128)(2,1)}, bf16[12,256,256]{2,1,0:T(8,128)(2,1)S(1)}, u32[]{:S(2)}) copy-start(bf16[12,256,256]{2,1,0:T(8,128)(2,1)S(1)} %get-tuple-element.30.own_f) | copy-start | bytes 4718596
  22.8 2.8 %collective-permute-start.4 = (bf16[2,2,2,16,256]{4,3,2,1,0:T(8,128)(2,1)S(1)}, bf16[2,2,2,16,256]{4,3,2,1,0:T(8,128)(2,1)S(1)}, u32[]{:S(2)}, u32[]{:S(2)}) collective-permute-start(bf16[2,2,2,16,256]{4,3,2,1,0:T(8,128)(2,1)S(1)} %pad_maximum_fusion), channel_id=1, source_target_pairs={{0,8},{8,0},{1,9},{9,1},{2,10},{10,2},{3,11},{11,3},{4,12},{12,4},... | collective-permute-start | bytes 196616 | tf_op jit(solution)/shard_map/ppermute | solution.py:245
  24.6 3.8 %collective-permute-start.5 = (bf16[2,2,2,16,256]{4,3,2,1,0:T(8,128)(2,1)S(1)}, bf16[2,2,2,16,256]{4,3,2,1,0:T(8,128)(2,1)S(1)}, u32[]{:S(2)}, u32[]{:S(2)}) collective-permute-start(bf16[2,2,2,16,256]{4,3,2,1,0:T(8,128)(2,1)S(1)} %pad_maximum_fusion.1), channel_id=1, source_target_pairs={{8,16},{9,17},{10,18},{11,19},{12,20},{13,21},{14,22},{15,23},{24,... | collective-permute-start | bytes 196616 | tf_op jit(solution)/shard_map/ppermute | solution.py:244
  34.9 6.6 %collective-permute-start.6 = (bf16[2304,256]{1,0:T(8,128)(2,1)S(1)}, bf16[2304,256]{1,0:T(8,128)(2,1)S(1)}, u32[]{:S(2)}, u32[]{:S(2)}) collective-permute-start(bf16[2304,256]{1,0:T(8,128)(2,1)S(1)} %get-tuple-element.37), channel_id=1, source_target_pairs={{0,8},{8,0},{1,9},{9,1},{2,10},{10,2},{3,11},{11,3},{4,12},{12,4},... | collective-permute-start | bytes 3538952 | tf_op jit(solution)/shard_map/ppermute | solution.py:319
  66.8 4.1 %collective-permute-start.7 = (f32[144,256]{1,0:T(8,128)S(1)}, f32[144,256]{1,0:T(8,128)S(1)}, u32[]{:S(2)}, u32[]{:S(2)}) collective-permute-start(f32[144,256]{1,0:T(8,128)S(1)} %convert_reduce_fusion), channel_id=1, source_target_pairs={{0,16},{8,24},{16,0},{24,8},{32,48},{40,56},{48,32},{56,40},{64,80... | collective-permute-start | bytes 442376 | tf_op jit(solution)/shard_map/ppermute | solution.py:330
  70.9 6.9 %collective-permute-start.8 = (f32[144,256]{1,0:T(8,128)S(1)}, f32[144,256]{1,0:T(8,128)S(1)}, u32[]{:S(2)}, u32[]{:S(2)}) collective-permute-start(f32[144,256]{1,0:T(8,128)S(1)} %add.52), channel_id=1, source_target_pairs={{0,32},{8,104},{16,48},{24,120},{32,0},{40,72},{48,16},{56,88},{64... | collective-permute-start | bytes 442376 | tf_op jit(solution)/shard_map/ppermute | solution.py:330
  74.3 7.0 %collective-permute-start.9 = (bf16[1,2,128,256]{3,2,1,0:T(8,128)(2,1)S(1)}, bf16[1,2,128,256]{3,2,1,0:T(8,128)(2,1)S(1)}, u32[]{:S(2)}, u32[]{:S(2)}) collective-permute-start(bf16[1,2,128,256]{3,2,1,0:T(8,128)(2,1)S(1)} %get-tuple-element.60), channel_id=1, source_target_pairs={{0,1},{2,3},{4,5},{6,7},{8,9},{10,11},{12,13},{14,15},{16,17},{18,... | collective-permute-start | bytes 393224 | tf_op jit(solution)/shard_map/ppermute | solution.py:229
  81.3 6.0 %collective-permute-start.10 = (f32[144,256]{1,0:T(8,128)S(1)}, f32[144,256]{1,0:T(8,128)S(1)}, u32[]{:S(2)}, u32[]{:S(2)}) collective-permute-start(f32[144,256]{1,0:T(8,128)S(1)} %add.53), channel_id=1, source_target_pairs={{0,112},{8,56},{16,96},{24,40},{32,80},{40,24},{48,64},{56,8},{64,... | collective-permute-start | bytes 442376 | tf_op jit(solution)/shard_map/ppermute | solution.py:330
  81.3 7.4 %collective-permute-start.11 = (bf16[1,2,128,256]{3,2,1,0:T(8,128)(2,1)S(1)}, bf16[1,2,128,256]{3,2,1,0:T(8,128)(2,1)S(1)}, u32[]{:S(2)}, u32[]{:S(2)}) collective-permute-start(bf16[1,2,128,256]{3,2,1,0:T(8,128)(2,1)S(1)} %get-tuple-element.59), channel_id=1, source_target_pairs={{1,2},{3,4},{5,6},{9,10},{11,12},{13,14},{17,18},{19,20},{21,22},{... | collective-permute-start | bytes 393224 | tf_op jit(solution)/shard_map/ppermute | solution.py:232
  89.8 17.3 %all-to-all-start.1 = ((bf16[16,144,256]{2,1,0:T(8,128)(2,1)}), bf16[16,144,256]{2,1,0:T(8,128)(2,1)S(1)}, u32[]{:S(2)}, u32[]{:S(2)}) async-start(bf16[16,144,256]{2,1,0:T(8,128)(2,1)} %broadcast_in_dim.2), calls=%async_computation.1 | async-start | bytes 2359296 | tf_op jit(solution)/shard_map/all_to_all | solution.py:348
  93.8 6.0 %collective-permute-start.12 = (bf16[1,2,4,16,256]{4,3,2,1,0:T(8,128)(2,1)S(1)}, bf16[1,2,4,16,256]{4,3,2,1,0:T(8,128)(2,1)S(1)}, u32[]{:S(2)}, u32[]{:S(2)}) collective-permute-start(bf16[1,2,4,16,256]{4,3,2,1,0:T(8,128)(2,1)S(1)} %pad_maximum_fusion.2), channel_id=1, source_target_pairs={{0,8},{8,0},{1,9},{9,1},{2,10},{10,2},{3,11},{11,3},{4,12},{12,4},... | collective-permute-start | bytes 196616 | tf_op jit(solution)/shard_map/ppermute | solution.py:245
  98.9 4.1 %collective-permute-start.13 = (bf16[1,2,4,16,256]{4,3,2,1,0:T(8,128)(2,1)S(1)}, bf16[1,2,4,16,256]{4,3,2,1,0:T(8,128)(2,1)S(1)}, u32[]{:S(2)}, u32[]{:S(2)}) collective-permute-start(bf16[1,2,4,16,256]{4,3,2,1,0:T(8,128)(2,1)S(1)} %pad_maximum_fusion.3), channel_id=1, source_target_pairs={{8,16},{9,17},{10,18},{11,19},{12,20},{13,21},{14,22},{15,23},{24,... | collective-permute-start | bytes 196616 | tf_op jit(solution)/shard_map/ppermute | solution.py:244
  107.1 8.6 %collective-permute-start.14 = (bf16[2304,256]{1,0:T(8,128)(2,1)S(1)}, bf16[2304,256]{1,0:T(8,128)(2,1)S(1)}, u32[]{:S(2)}, u32[]{:S(2)}) collective-permute-start(bf16[2304,256]{1,0:T(8,128)(2,1)S(1)} %bitcast.37), channel_id=1, source_target_pairs={{0,8},{8,0},{1,9},{9,1},{2,10},{10,2},{3,11},{11,3},{4,12},{12,4},... | collective-permute-start | bytes 3538952 | tf_op jit(solution)/shard_map/ppermute | solution.py:350

commit v6 on v5

--- a/solution.py
+++ b/solution.py
@@ -210,11 +210,21 @@
             out[s, row] = (own + total[s * width : (s + 1) * width]).astype(jnp.bfloat16)
 
 
-def part_kernel(scale, where, mine, other, first, second):
-    own, swapped = mine[...].astype(jnp.float32) * scale, other[...].astype(jnp.float32) * scale
+def part_kernel(scale, where, mine, other, first, second, held, sems):
     keeps = where[1] == 0
-    first[...] = jnp.where(keeps, own, swapped)
-    second[...] = jnp.where(keeps, swapped, own)
+    count = sems.shape[1]
+    step = mine.shape[0] // count
+    stores = []
+    for i in range(count):
+        rows = pl.ds(i * step, step)
+        own, swapped = mine[rows].astype(jnp.float32) * scale, other[rows].astype(jnp.float32) * scale
+        held[0, rows] = jnp.where(keeps, own, swapped)
+        held[1, rows] = jnp.where(keeps, swapped, own)
+        for j, out in enumerate((first, second)):
+            stores.append(pltpu.make_async_copy(held.at[j, rows], out.at[rows], sems.at[j, i]))
+            stores[-1].start()
+    for store in stores:
+        store.wait()
 
 
 def both_ways(pairs):
@@ -270,10 +280,11 @@
     where = jnp.stack([lat, core, lax.rem(lat, 2)]).astype(jnp.int32)
     smem = pl.BlockSpec(memory_space=pltpu.SMEM)
     vmem = pl.BlockSpec(memory_space=pltpu.VMEM)
+    anywhere = pl.BlockSpec(memory_space=pl.ANY)
     cells = slabs * rows * width
     ext = pltpu.VMEM((slabs * (rows + 2), width + 2 * SPAN + 8, chans), jnp.float32)
     taps = pltpu.VMEM((9, cells, chans), jnp.bfloat16)
-    params = pltpu.CompilerParams(vmem_limit_bytes=48 * 1024 * 1024)
+    params = pltpu.CompilerParams(vmem_limit_bytes=24 * 1024 * 1024)
     grads = (9 * chans, chans)
     swap = [(0, 1), (1, 0)]
 
@@ -349,13 +360,12 @@
     mine, input_grad = lax.optimization_barrier((mine, input_grad))
     other = lax.ppermute(mine, "core", swap)
     scale = 1.0 / math.sqrt(cells * lat_count * lon_count)
-    block = pl.BlockSpec((9 * chans // 4, chans), lambda i: (i, 0))
     first, second = pl.pallas_call(
         lambda *refs: part_kernel(scale, *refs),
-        grid=(4,),
         out_shape=[jax.ShapeDtypeStruct(grads, jnp.float32)] * 2,
-        in_specs=[smem, block, block],
-        out_specs=[block, block],
+        in_specs=[smem, vmem, vmem],
+        out_specs=[anywhere] * 2,
+        scratch_shapes=[pltpu.VMEM((2,) + grads, jnp.float32), pltpu.SemaphoreType.DMA((2, 9))],
         compiler_params=params,
         name="part",
     )(where, mine, other)

time: 119 us -> 115 us (0.966)
  Pallas kernels: 15.1 us -> 11.4 us
  waiting for transfers between devices: 29.4 us -> 31.5 us
  other arithmetic: 3.67 us -> 2.09 us
  local copies, waits for them, and re-layouts: 3.73 us -> 2.54 us
    pallas_call x1, Pallas kernels: 6.53 us -> 4.05 us  [local(): pl.pallas_call(main_kernel, out_shape=[jax.ShapeDtypeStruct(grads, jnp.fl...]
    ppermute x2, waiting for transfers between devices: 4.05 us -> 6.2 us  [row_halos(): lax.ppermute(row(1 - odd), ALL, both_ways([(at(i, k), at(i, k + 1)) for i...]
    convert_element_type x1, other arithmetic: 2 us -> 0.42 us  [local(): total.astype(jnp.bfloat16).reshape(planes, 9 * chans // planes, chans)]
    unnamed x13 -> x11, local copies, waits for them, and re-layouts: 2.57 us -> 1.38 us
  transfers between devices with their start and end apart: 16 -> 16, of which waited for: 13 -> 13; matrix products, arithmetic and copies ran while one was open for 0% -> 0% of each run, Pallas kernels for 5% -> 4%
where the time goes in v6:
time: 115 us
  starting transfers between devices  43.2 us (38%)
  waiting for transfers between devices  31.5 us (27%)
  blocking collectives  23.1 us (20%)
  Pallas kernels  11.4 us (10%)
  local copies, waits for them, and re-layouts  2.54 us (2%)
  other arithmetic  2.09 us (2%)
    all_to_all x1, blocking collectives, local(): spread = lax.all_to_all(total, PLANE, 0, 0, tiled=True)  23.1 us
    ppermute x3, starting transfers between devices, column_halos(): in_chip = lax.ppermute(edge((1 - core) * reach), 'core', [(0, 1), (1, 0)])  11.1 us
    ppermute x3, waiting for transfers between devices, local(): lax.ppermute(part, ('z', 'core'), folded(height, cores, reach))  10.1 us
    ppermute x2, waiting for transfers between devices, row_halos(): lax.ppermute(row(1 - odd), ALL, both_ways([(at(i, k), at(i, k + 1)) for i...  6.2 us
    ppermute x1, starting transfers between devices, local(): other = lax.ppermute(mine, 'core', swap)  6.17 us
    ppermute x3, waiting for transfers between devices, column_halos(): lax.ppermute(edge(core * reach), ALL, both_ways([(at(i + 1, k), at(i + 2,...  6.03 us
    ppermute x2, starting transfers between devices, row_halos(): return (pair, lax.ppermute(row(odd), ALL, between + across))  5.94 us
    ppermute x1, starting transfers between devices, local(): total = keep + lax.ppermute(send, 'core', swap).astype(jnp.float32)  4.23 us
  transfers between devices with their start and end apart: 16, of which 13 were waited for; matrix products, arithmetic and copies ran while one was open for 0% of the time, Pallas kernels for 4%

profile of v6, /device:TPU:1, one launch (start us, length us, event | category | flops | bytes accessed | tf_op | source)
XLA Modules:
  0.0 114.7 jit_solution(17805805335702525315)
XLA Ops:
  0.6 0.0 copy-start.2
  0.6 0.0 copy-start.3
  0.7 1.3 %fusion.1 = (bf16[2,2,128,256]{3,2,1,0:T(8,128)(2,1)S(1)}, bf16[2,2,128,256]{3,2,1,0:T(8,128)(2,1)S(1)}) fusion(s32[]{:T(128)S(6)} %select_n.53, bf16[1,2,2,128,256]{4,3,2,1,0:T(8,128)(2,1)} %bitcast.41, bf16[1,2,2,128,256]{4,3,2,1,0:T(8,128)(2,1)} %bitcast.39, s32[]{:T(128)S(6)} %select_n.52), kind=kLoop, calls=%fused_computation.11 | loop fusion | flops 262144 | bytes 1048584 | tf_op jit(solution)/shard_map/jit(dynamic_index_in_dim)/squeeze | solution.py:238
  2.0 4.0 %collective-permute-start.3 = (bf16[2,2,128,256]{3,2,1,0:T(8,128)(2,1)S(1)}, bf16[2,2,128,256]{3,2,1,0:T(8,128)(2,1)S(1)}, u32[]{:S(2)}, u32[]{:S(2)}) collective-permute-start(bf16[2,2,128,256]{3,2,1,0:T(8,128)(2,1)S(1)} %get-tuple-element.51), channel_id=1, source_target_pairs={{1,2},{3,4},{5,6},{9,10},{11,12},{13,14},{17,18},{19,20},{21,22},{... | collective-permute-start | bytes 786440 | tf_op jit(solution)/shard_map/ppermute | solution.py:242
  6.0 2.7 %collective-permute-start.2 = (bf16[2,2,128,256]{3,2,1,0:T(8,128)(2,1)S(1)}, bf16[2,2,128,256]{3,2,1,0:T(8,128)(2,1)S(1)}, u32[]{:S(2)}, u32[]{:S(2)}) collective-permute-start(bf16[2,2,128,256]{3,2,1,0:T(8,128)(2,1)S(1)} %get-tuple-element.52), channel_id=1, source_target_pairs={{0,1},{2,3},{4,5},{6,7},{8,9},{10,11},{12,13},{14,15},{16,17},{18,... | collective-permute-start | bytes 786440 | tf_op jit(solution)/shard_map/ppermute | solution.py:239
  8.7 0.0 copy-done.3
  8.7 2.8 %collective-permute-start.1 = (bf16[2,2,2,16,256]{4,3,2,1,0:T(8,128)(2,1)S(1)}, bf16[2,2,2,16,256]{4,3,2,1,0:T(8,128)(2,1)S(1)}, u32[]{:S(2)}, u32[]{:S(2)}) collective-permute-start(bf16[2,2,2,16,256]{4,3,2,1,0:T(8,128)(2,1)S(1)} %get-tuple-element.53), channel_id=1, source_target_pairs={{8,16},{9,17},{10,18},{11,19},{12,20},{13,21},{14,22},{15,23},{24,... | collective-permute-start | bytes 196616 | tf_op jit(solution)/shard_map/ppermute | solution.py:254
  11.5 4.2 %collective-permute-start = (bf16[2,2,2,16,256]{4,3,2,1,0:T(8,128)(2,1)S(1)}, bf16[2,2,2,16,256]{4,3,2,1,0:T(8,128)(2,1)S(1)}, u32[]{:S(2)}, u32[]{:S(2)}) collective-permute-start(bf16[2,2,2,16,256]{4,3,2,1,0:T(8,128)(2,1)S(1)} %get-tuple-element.54), channel_id=1, source_target_pairs={{0,8},{8,0},{1,9},{9,1},{2,10},{10,2},{3,11},{11,3},{4,12},{12,4},... | collective-permute-start | bytes 196616 | tf_op jit(solution)/shard_map/ppermute | solution.py:255
  15.8 0.0 copy-done.4
  15.8 0.1 copy.9.strides
  15.9 0.1 pad_add_fusion.where.refs_0_
  15.9 0.0 collective-permute-done.1.next_chip
  15.9 0.7 collective-permute-done.in_chip
  16.7 1.3 %copy-done.1 = bf16[3,3,256,256]{3,2,1,0:T(8,128)(2,1)S(1)} copy-done((bf16[3,3,256,256]{3,2,1,0:T(8,128)(2,1)S(1)}, bf16[3,3,256,256]{3,2,1,0:T(8,128)(2,1)}, u32[]{:S(2)}) %copy-start.1) | copy-done | bytes 1179672
  18.0 2.0 %early.1 = (bf16[12,256,256]{2,1,0:T(8,128)(2,1)S(1)}, bf16[12,256,256]{2,1,0:T(8,128)(2,1)S(1)}, f32[512,256]{1,0:T(8,128)S(1)}, f32[512,256]{1,0:T(8,128)S(1)}) custom-call(s32[3]{0:T(128)S(1)} %pad_add_fusion.where.refs_0_, s32[2,16,3]{2,1,0:T(8,128)S(1)} %copy.9.strides, bf16[2,2,128,256]{3,2,1,0:T(8,128)(2,1)S(1)} %copy-done.3, ...), custom_call_target="tpu_custom_call" | custom-call | tf_op jit(solution)/shard_map/early/pallas_call | solution.py:296
  20.0 0.0 collective-permute-done.3.next_pair
  20.0 2.7 %collective-permute-done.2.pair = bf16[2,2,128,256]{3,2,1,0:T(8,128)(2,1)S(1)} collective-permute-done((bf16[2,2,128,256]{3,2,1,0:T(8,128)(2,1)S(1)}, bf16[2,2,128,256]{3,2,1,0:T(8,128)(2,1)S(1)}, u32[]{:S(2)}, u32[]{:S(2)}) %collective-permute-start.2) | collective-permute-done | bytes 262176 | tf_op jit(solution)/shard_map/ppermute | solution.py:239
  22.8 1.8 %collective-permute-start.4 = (bf16[2,2,2,16,256]{4,3,2,1,0:T(8,128)(2,1)S(1)}, bf16[2,2,2,16,256]{4,3,2,1,0:T(8,128)(2,1)S(1)}, u32[]{:S(2)}, u32[]{:S(2)}) collective-permute-start(bf16[2,2,2,16,256]{4,3,2,1,0:T(8,128)(2,1)S(1)} %pad_maximum_fusion), channel_id=1, source_target_pairs={{0,8},{8,0},{1,9},{9,1},{2,10},{10,2},{3,11},{11,3},{4,12},{12,4},... | collective-permute-start | bytes 196616 | tf_op jit(solution)/shard_map/ppermute | solution.py:255
  24.6 0.9 collective-permute-start.5
  25.5 0.0 collective-permute-done.4.in_chip
  25.5 2.8 %collective-permute-done.5.next_chip = bf16[2,2,2,16,256]{4,3,2,1,0:T(8,128)(2,1)S(1)} collective-permute-done((bf16[2,2,2,16,256]{4,3,2,1,0:T(8,128)(2,1)S(1)}, bf16[2,2,2,16,256]{4,3,2,1,0:T(8,128)(2,1)S(1)}, u32[]{:S(2)}, u32[]{:S(2)}) %collective-permute-start.5) | collective-permute-done | bytes 65568 | tf_op jit(solution)/shard_map/ppermute | solution.py:254
  28.4 4.1 %main.1 = (f32[2304,256]{1,0:T(8,128)S(1)}, bf16[2304,256]{1,0:T(8,128)(2,1)S(1)}, bf16[2,2,128,256]{3,2,1,0:T(8,128)(2,1)S(1)}) custom-call(s32[3]{0:T(128)S(1)} %pad_add_fusion.where.refs_0_, s32[2,16,3]{2,1,0:T(8,128)S(1)} %copy.9.strides, bf16[12,256,256]{2,1,0:T(8,128)(2,1)S(1)} %get-tuple-element.30.own_f, ...), custom_call_target="tpu_custom_call" | custom-call | tf_op jit(solution)/shard_map/main/pallas_call | solution.py:309
  32.5 4.2 %collective-permute-start.6 = (bf16[2304,256]{1,0:T(8,128)(2,1)S(1)}, bf16[2304,256]{1,0:T(8,128)(2,1)S(1)}, u32[]{:S(2)}, u32[]{:S(2)}) collective-permute-start(bf16[2304,256]{1,0:T(8,128)(2,1)S(1)} %get-tuple-element.37), channel_id=1, source_target_pairs={{0,8},{8,0},{1,9},{9,1},{2,10},{10,2},{3,11},{11,3},{4,12},{12,4},... | collective-permute-start | bytes 3538952 | tf_op jit(solution)/shard_map/ppermute | solution.py:330
  36.7 2.5 %collective-permute-done.6 = bf16[2304,256]{1,0:T(8,128)(2,1)S(1)} collective-permute-done((bf16[2304,256]{1,0:T(8,128)(2,1)S(1)}, bf16[2304,256]{1,0:T(8,128)(2,1)S(1)}, u32[]{:S(2)}, u32[]{:S(2)}) %collective-permute-start.6) | collective-permute-done | bytes 1179680 | tf_op jit(solution)/shard_map/ppermute | solution.py:330
  39.2 0.4 add_convert_fusion
  39.6 23.1 %all_to_all.10 = bf16[16,144,256]{2,1,0:T(8,128)(2,1)S(1)} all-to-all(bf16[16,144,256]{2,1,0:T(8,128)(2,1)S(1)} %bitcast.43), channel_id=1, replica_groups=mesh['yl'=2,'z'=8,'core'=2,'x'=4,'yh'=2] {'x','yh','yl'}, dimensions={0} | all-to-all | bytes 2359296 | tf_op jit(solution)/shard_map/all_to_all | solution.py:333
  62.7 0.2 convert_reduce_fusion
  62.8 0.1 collective-permute-start.7
  62.9 4.0 %collective-permute-done.7 = f32[144,256]{1,0:T(8,128)S(1)} collective-permute-done((f32[144,256]{1,0:T(8,128)S(1)}, f32[144,256]{1,0:T(8,128)S(1)}, u32[]{:S(2)}, u32[]{:S(2)}) %collective-permute-start.7) | collective-permute-done | bytes 147488 | tf_op jit(solution)/shard_map/ppermute | solution.py:341
  66.9 3.4 %collective-permute-start.8 = (f32[144,256]{1,0:T(8,128)S(1)}, f32[144,256]{1,0:T(8,128)S(1)}, u32[]{:S(2)}, u32[]{:S(2)}) collective-permute-start(f32[144,256]{1,0:T(8,128)S(1)} %add.52), channel_id=1, source_target_pairs={{0,32},{8,104},{16,48},{24,120},{32,0},{40,72},{48,16},{56,88},{64... | collective-permute-start | bytes 442376 | tf_op jit(solution)/shard_map/ppermute | solution.py:341
  70.3 1.4 %collective-permute-start.9 = (bf16[1,2,128,256]{3,2,1,0:T(8,128)(2,1)S(1)}, bf16[1,2,128,256]{3,2,1,0:T(8,128)(2,1)S(1)}, u32[]{:S(2)}, u32[]{:S(2)}) collective-permute-start(bf16[1,2,128,256]{3,2,1,0:T(8,128)(2,1)S(1)} %get-tuple-element.60), channel_id=1, source_target_pairs={{0,1},{2,3},{4,5},{6,7},{8,9},{10,11},{12,13},{14,15},{16,17},{18,... | collective-permute-start | bytes 393224 | tf_op jit(solution)/shard_map/ppermute | solution.py:239
  71.8 2.0 %collective-permute-done.8 = f32[144,256]{1,0:T(8,128)S(1)} collective-permute-done((f32[144,256]{1,0:T(8,128)S(1)}, f32[144,256]{1,0:T(8,128)S(1)}, u32[]{:S(2)}, u32[]{:S(2)}) %collective-permute-start.8) | collective-permute-done | bytes 147488 | tf_op jit(solution)/shard_map/ppermute | solution.py:341
  73.8 3.5 %collective-permute-done.9.pair = bf16[1,2,128,256]{3,2,1,0:T(8,128)(2,1)S(1)} collective-permute-done((bf16[1,2,128,256]{3,2,1,0:T(8,128)(2,1)S(1)}, bf16[1,2,128,256]{3,2,1,0:T(8,128)(2,1)S(1)}, u32[]{:S(2)}, u32[]{:S(2)}) %collective-permute-start.9) | collective-permute-done | bytes 131104 | tf_op jit(solution)/shard_map/ppermute | solution.py:239
  77.3 0.0 collective-permute-start.10
  77.3 1.9 %collective-permute-start.11 = (bf16[1,2,128,256]{3,2,1,0:T(8,128)(2,1)S(1)}, bf16[1,2,128,256]{3,2,1,0:T(8,128)(2,1)S(1)}, u32[]{:S(2)}, u32[]{:S(2)}) collective-permute-start(bf16[1,2,128,256]{3,2,1,0:T(8,128)(2,1)S(1)} %get-tuple-element.59), channel_id=1, source_target_pairs={{1,2},{3,4},{5,6},{9,10},{11,12},{13,14},{17,18},{19,20},{21,22},{... | collective-permute-start | bytes 393224 | tf_op jit(solution)/shard_map/ppermute | solution.py:242
  79.3 4.1 %collective-permute-done.10 = f32[144,256]{1,0:T(8,128)S(1)} collective-permute-done((f32[144,256]{1,0:T(8,128)S(1)}, f32[144,256]{1,0:T(8,128)S(1)}, u32[]{:S(2)}, u32[]{:S(2)}) %collective-permute-start.10) | collective-permute-done | bytes 147488 | tf_op jit(solution)/shard_map/ppermute | solution.py:341
  83.3 1.4 %collective-permute-done.11.next_pair = bf16[1,2,128,256]{3,2,1,0:T(8,128)(2,1)S(1)} collective-permute-done((bf16[1,2,128,256]{3,2,1,0:T(8,128)(2,1)S(1)}, bf16[1,2,128,256]{3,2,1,0:T(8,128)(2,1)S(1)}, u32[]{:S(2)}, u32[]{:S(2)}) %collective-permute-start.11) | collective-permute-done | bytes 131104 | tf_op jit(solution)/shard_map/ppermute | solution.py:242
  84.7 1.1 broadcast_in_dim.2
  85.8 3.9 %all-to-all-start.1 = ((bf16[16,144,256]{2,1,0:T(8,128)(2,1)}), bf16[16,144,256]{2,1,0:T(8,128)(2,1)S(1)}, u32[]{:S(2)}, u32[]{:S(2)}) async-start(bf16[16,144,256]{2,1,0:T(8,128)(2,1)} %broadcast_in_dim.2), calls=%async_computation.1 | async-start | bytes 2359296 | tf_op jit(solution)/shard_map/all_to_all | solution.py:359
  89.8 5.1 %collective-permute-start.12 = (bf16[1,2,4,16,256]{4,3,2,1,0:T(8,128)(2,1)S(1)}, bf16[1,2,4,16,256]{4,3,2,1,0:T(8,128)(2,1)S(1)}, u32[]{:S(2)}, u32[]{:S(2)}) collective-permute-start(bf16[1,2,4,16,256]{4,3,2,1,0:T(8,128)(2,1)S(1)} %pad_maximum_fusion.2), channel_id=1, source_target_pairs={{0,8},{8,0},{1,9},{9,1},{2,10},{10,2},{3,11},{11,3},{4,12},{12,4},... | collective-permute-start | bytes 196616 | tf_op jit(solution)/shard_map/ppermute | solution.py:255
  94.9 0.4 collective-permute-start.13
  95.4 0.5 collective-permute-done.12.in_chip
  95.8 3.2 %collective-permute-done.13.next_chip = bf16[1,2,4,16,256]{4,3,2,1,0:T(8,128)(2,1)S(1)} collective-permute-done((bf16[1,2,4,16,256]{4,3,2,1,0:T(8,128)(2,1)S(1)}, bf16[1,2,4,16,256]{4,3,2,1,0:T(8,128)(2,1)S(1)}, u32[]{:S(2)}, u32[]{:S(2)}) %collective-permute-start.13) | collective-permute-done | bytes 65568 | tf_op jit(solution)/shard_map/ppermute | solution.py:254
  99.0 2.4 %back.1 = bf16[2,2,128,256]{3,2,1,0:T(8,128)(2,1)} custom-call(s32[3]{0:T(128)S(1)} %pad_add_fusion.where.refs_0_, s32[2,16,3]{2,1,0:T(8,128)S(1)} %copy.9.strides, bf16[2,2,128,256]{3,2,1,0:T(8,128)(2,1)S(1)} %copy-done.2, bf16[2,2,128,256]{3,2,1,0:T(8,128)(2,1)S(1)} %get-tuple-element.40.pre, bf16[1,2,128,256]{3,2,1,0:T(8,128)(2,1)S(1)} %collective-permute-done.9.pair, ...), custom_call_target="tpu_custom_call" | custom-call | tf_op jit(solution)/shard_map/back/pallas_call | solution.py:348
  101.4 1.7 %all-to-all-done.1 = bf16[16,144,256]{2,1,0:T(8,128)(2,1)S(1)} async-done(((bf16[16,144,256]{2,1,0:T(8,128)(2,1)}), bf16[16,144,256]{2,1,0:T(8,128)(2,1)S(1)}, u32[]{:S(2)}, u32[]{:S(2)}) %all-to-all-start.1) | async-done | bytes 1179680 | tf_op jit(solution)/shard_map/all_to_all | solution.py:359
  103.1 6.2 %collective-permute-start.14 = (bf16[2304,256]{1,0:T(8,128)(2,1)S(1)}, bf16[2304,256]{1,0:T(8,128)(2,1)S(1)}, u32[]{:S(2)}, u32[]{:S(2)}) collective-permute-start(bf16[2304,256]{1,0:T(8,128)(2,1)S(1)} %bitcast.37), channel_id=1, source_target_pairs={{0,8},{8,0},{1,9},{9,1},{2,10},{10,2},{3,11},{11,3},{4,12},{12,4},... | collective-permute-start | bytes 3538952 | tf_op jit(solution)/shard_map/ppermute | solution.py:361
  109.3 2.5 %collective-permute-done.14.refs_2_ = bf16[2304,256]{1,0:T(8,128)(2,1)S(1)} collective-permute-done((bf16[2304,256]{1,0:T(8,128)(2,1)S(1)}, bf16[2304,256]{1,0:T(8,128)(2,1)S(1)}, u32[]{:S(2)}, u32[]{:S(2)}) %collective-permute-start.14) | collective-permute-done | bytes 1179680 | tf_op jit(solution)/shard_map/ppermute | solution.py:361
  111.7 2.9 %part.1 = (f32[2304,256]{1,0:T(8,128)}, f32[2304,256]{1,0:T(8,128)}) custom-call(s32[3]{0:T(128)S(1)} %pad_add_fusion.where.refs_0_, bf16[2304,256]{1,0:T(8,128)(2,1)S(1)} %bitcast.38, bf16[2304,256]{1,0:T(8,128)(2,1)S(1)} %collective-permute-done.14.refs_2_), custom_call_target="tpu_custom_call" | custom-call | tf_op jit(solution)/shard_map/part/pallas_call | solution.py:363
  (20 shorter events, 0.3 us)
Async XLA Ops:
  0.6 8.1 %copy-start.2 = (bf16[2,2,128,256]{3,2,1,0:T(8,128)(2,1)S(1)}, bf16[2,2,128,256]{3,2,1,0:T(8,128)(2,1)}, u32[]{:S(2)}) copy-start(bf16[2,2,128,256]{3,2,1,0:T(8,128)(2,1)} %grad.3) | copy-start | bytes 786436
  0.6 8.0 %copy-start.3 = (bf16[2,2,128,256]{3,2,1,0:T(8,128)(2,1)S(1)}, bf16[2,2,128,256]{3,2,1,0:T(8,128)(2,1)}, u32[]{:S(2)}) copy-start(bf16[2,2,128,256]{3,2,1,0:T(8,128)(2,1)} %feat.1) | copy-start | bytes 786436
  0.7 15.1 %copy-start.4 = (s32[2,16,3]{1,0,2:T(2,128)S(1)}, s32[2,16,3]{1,0,2:T(2,128)}, u32[]{:S(2)}) copy-start(s32[2,16,3]{1,0,2:T(2,128)} %param.9) | copy-start | bytes 1156
  0.7 16.0 %copy-start = (bf16[3,3,256,256]{3,2,1,0:T(8,128)(2,1)S(1)}, bf16[3,3,256,256]{3,2,1,0:T(8,128)(2,1)}, u32[]{:S(2)}) copy-start(bf16[3,3,256,256]{3,2,1,0:T(8,128)(2,1)} %first_kernel.5) | copy-start | bytes 3538948
  2.0 18.0 %collective-permute-start.3 = (bf16[2,2,128,256]{3,2,1,0:T(8,128)(2,1)S(1)}, bf16[2,2,128,256]{3,2,1,0:T(8,128)(2,1)S(1)}, u32[]{:S(2)}, u32[]{:S(2)}) collective-permute-start(bf16[2,2,128,256]{3,2,1,0:T(8,128)(2,1)S(1)} %get-tuple-element.51), channel_id=1, source_target_pairs={{1,2},{3,4},{5,6},{9,10},{11,12},{13,14},{17,18},{19,20},{21,22},{... | collective-permute-start | bytes 786440 | tf_op jit(solution)/shard_map/ppermute | solution.py:242
  6.0 16.7 %collective-permute-start.2 = (bf16[2,2,128,256]{3,2,1,0:T(8,128)(2,1)S(1)}, bf16[2,2,128,256]{3,2,1,0:T(8,128)(2,1)S(1)}, u32[]{:S(2)}, u32[]{:S(2)}) collective-permute-start(bf16[2,2,128,256]{3,2,1,0:T(8,128)(2,1)S(1)} %get-tuple-element.52), channel_id=1, source_target_pairs={{0,1},{2,3},{4,5},{6,7},{8,9},{10,11},{12,13},{14,15},{16,17},{18,... | collective-permute-start | bytes 786440 | tf_op jit(solution)/shard_map/ppermute | solution.py:239
  8.7 7.2 %collective-permute-start.1 = (bf16[2,2,2,16,256]{4,3,2,1,0:T(8,128)(2,1)S(1)}, bf16[2,2,2,16,256]{4,3,2,1,0:T(8,128)(2,1)S(1)}, u32[]{:S(2)}, u32[]{:S(2)}) collective-permute-start(bf16[2,2,2,16,256]{4,3,2,1,0:T(8,128)(2,1)S(1)} %get-tuple-element.53), channel_id=1, source_target_pairs={{8,16},{9,17},{10,18},{11,19},{12,20},{13,21},{14,22},{15,23},{24,... | collective-permute-start | bytes 196616 | tf_op jit(solution)/shard_map/ppermute | solution.py:254
  11.5 5.1 %collective-permute-start = (bf16[2,2,2,16,256]{4,3,2,1,0:T(8,128)(2,1)S(1)}, bf16[2,2,2,16,256]{4,3,2,1,0:T(8,128)(2,1)S(1)}, u32[]{:S(2)}, u32[]{:S(2)}) collective-permute-start(bf16[2,2,2,16,256]{4,3,2,1,0:T(8,128)(2,1)S(1)} %get-tuple-element.54), channel_id=1, source_target_pairs={{0,8},{8,0},{1,9},{9,1},{2,10},{10,2},{3,11},{11,3},{4,12},{12,4},... | collective-permute-start | bytes 196616 | tf_op jit(solution)/shard_map/ppermute | solution.py:255
  16.7 1.3 %copy-start.1 = (bf16[3,3,256,256]{3,2,1,0:T(8,128)(2,1)S(1)}, bf16[3,3,256,256]{3,2,1,0:T(8,128)(2,1)}, u32[]{:S(2)}) copy-start(bf16[3,3,256,256]{3,2,1,0:T(8,128)(2,1)} %second_kernel.3) | copy-start | bytes 3538948
  22.8 2.8 %collective-permute-start.4 = (bf16[2,2,2,16,256]{4,3,2,1,0:T(8,128)(2,1)S(1)}, bf16[2,2,2,16,256]{4,3,2,1,0:T(8,128)(2,1)S(1)}, u32[]{:S(2)}, u32[]{:S(2)}) collective-permute-start(bf16[2,2,2,16,256]{4,3,2,1,0:T(8,128)(2,1)S(1)} %pad_maximum_fusion), channel_id=1, source_target_pairs={{0,8},{8,0},{1,9},{9,1},{2,10},{10,2},{3,11},{11,3},{4,12},{12,4},... | collective-permute-start | bytes 196616 | tf_op jit(solution)/shard_map/ppermute | solution.py:255
  24.6 3.8 %collective-permute-start.5 = (bf16[2,2,2,16,256]{4,3,2,1,0:T(8,128)(2,1)S(1)}, bf16[2,2,2,16,256]{4,3,2,1,0:T(8,128)(2,1)S(1)}, u32[]{:S(2)}, u32[]{:S(2)}) collective-permute-start(bf16[2,2,2,16,256]{4,3,2,1,0:T(8,128)(2,1)S(1)} %pad_maximum_fusion.1), channel_id=1, source_target_pairs={{8,16},{9,17},{10,18},{11,19},{12,20},{13,21},{14,22},{15,23},{24,... | collective-permute-start | bytes 196616 | tf_op jit(solution)/shard_map/ppermute | solution.py:254
  32.5 6.7 %collective-permute-start.6 = (bf16[2304,256]{1,0:T(8,128)(2,1)S(1)}, bf16[2304,256]{1,0:T(8,128)(2,1)S(1)}, u32[]{:S(2)}, u32[]{:S(2)}) collective-permute-start(bf16[2304,256]{1,0:T(8,128)(2,1)S(1)} %get-tuple-element.37), channel_id=1, source_target_pairs={{0,8},{8,0},{1,9},{9,1},{2,10},{10,2},{3,11},{11,3},{4,12},{12,4},... | collective-permute-start | bytes 3538952 | tf_op jit(solution)/shard_map/ppermute | solution.py:330
  62.8 4.1 %collective-permute-start.7 = (f32[144,256]{1,0:T(8,128)S(1)}, f32[144,256]{1,0:T(8,128)S(1)}, u32[]{:S(2)}, u32[]{:S(2)}) collective-permute-start(f32[144,256]{1,0:T(8,128)S(1)} %convert_reduce_fusion), channel_id=1, source_target_pairs={{0,16},{8,24},{16,0},{24,8},{32,48},{40,56},{48,32},{56,40},{64,80... | collective-permute-start | bytes 442376 | tf_op jit(solution)/shard_map/ppermute | solution.py:341
  66.9 6.9 %collective-permute-start.8 = (f32[144,256]{1,0:T(8,128)S(1)}, f32[144,256]{1,0:T(8,128)S(1)}, u32[]{:S(2)}, u32[]{:S(2)}) collective-permute-start(f32[144,256]{1,0:T(8,128)S(1)} %add.52), channel_id=1, source_target_pairs={{0,32},{8,104},{16,48},{24,120},{32,0},{40,72},{48,16},{56,88},{64... | collective-permute-start | bytes 442376 | tf_op jit(solution)/shard_map/ppermute | solution.py:341
  70.3 7.0 %collective-permute-start.9 = (bf16[1,2,128,256]{3,2,1,0:T(8,128)(2,1)S(1)}, bf16[1,2,128,256]{3,2,1,0:T(8,128)(2,1)S(1)}, u32[]{:S(2)}, u32[]{:S(2)}) collective-permute-start(bf16[1,2,128,256]{3,2,1,0:T(8,128)(2,1)S(1)} %get-tuple-element.60), channel_id=1, source_target_pairs={{0,1},{2,3},{4,5},{6,7},{8,9},{10,11},{12,13},{14,15},{16,17},{18,... | collective-permute-start | bytes 393224 | tf_op jit(solution)/shard_map/ppermute | solution.py:239
  77.3 6.0 %collective-permute-start.10 = (f32[144,256]{1,0:T(8,128)S(1)}, f32[144,256]{1,0:T(8,128)S(1)}, u32[]{:S(2)}, u32[]{:S(2)}) collective-permute-start(f32[144,256]{1,0:T(8,128)S(1)} %add.53), channel_id=1, source_target_pairs={{0,112},{8,56},{16,96},{24,40},{32,80},{40,24},{48,64},{56,8},{64,... | collective-permute-start | bytes 442376 | tf_op jit(solution)/shard_map/ppermute | solution.py:341
  77.3 7.4 %collective-permute-start.11 = (bf16[1,2,128,256]{3,2,1,0:T(8,128)(2,1)S(1)}, bf16[1,2,128,256]{3,2,1,0:T(8,128)(2,1)S(1)}, u32[]{:S(2)}, u32[]{:S(2)}) collective-permute-start(bf16[1,2,128,256]{3,2,1,0:T(8,128)(2,1)S(1)} %get-tuple-element.59), channel_id=1, source_target_pairs={{1,2},{3,4},{5,6},{9,10},{11,12},{13,14},{17,18},{19,20},{21,22},{... | collective-permute-start | bytes 393224 | tf_op jit(solution)/shard_map/ppermute | solution.py:242
  85.8 17.3 %all-to-all-start.1 = ((bf16[16,144,256]{2,1,0:T(8,128)(2,1)}), bf16[16,144,256]{2,1,0:T(8,128)(2,1)S(1)}, u32[]{:S(2)}, u32[]{:S(2)}) async-start(bf16[16,144,256]{2,1,0:T(8,128)(2,1)} %broadcast_in_dim.2), calls=%async_computation.1 | async-start | bytes 2359296 | tf_op jit(solution)/shard_map/all_to_all | solution.py:359
  89.8 6.0 %collective-permute-start.12 = (bf16[1,2,4,16,256]{4,3,2,1,0:T(8,128)(2,1)S(1)}, bf16[1,2,4,16,256]{4,3,2,1,0:T(8,128)(2,1)S(1)}, u32[]{:S(2)}, u32[]{:S(2)}) collective-permute-start(bf16[1,2,4,16,256]{4,3,2,1,0:T(8,128)(2,1)S(1)} %pad_maximum_fusion.2), channel_id=1, source_target_pairs={{0,8},{8,0},{1,9},{9,1},{2,10},{10,2},{3,11},{11,3},{4,12},{12,4},... | collective-permute-start | bytes 196616 | tf_op jit(solution)/shard_map/ppermute | solution.py:255
  94.9 4.1 %collective-permute-start.13 = (bf16[1,2,4,16,256]{4,3,2,1,0:T(8,128)(2,1)S(1)}, bf16[1,2,4,16,256]{4,3,2,1,0:T(8,128)(2,1)S(1)}, u32[]{:S(2)}, u32[]{:S(2)}) collective-permute-start(bf16[1,2,4,16,256]{4,3,2,1,0:T(8,128)(2,1)S(1)} %pad_maximum_fusion.3), channel_id=1, source_target_pairs={{8,16},{9,17},{10,18},{11,19},{12,20},{13,21},{14,22},{15,23},{24,... | collective-permute-start | bytes 196616 | tf_op jit(solution)/shard_map/ppermute | solution.py:254
  103.1 8.6 %collective-permute-start.14 = (bf16[2304,256]{1,0:T(8,128)(2,1)S(1)}, bf16[2304,256]{1,0:T(8,128)(2,1)S(1)}, u32[]{:S(2)}, u32[]{:S(2)}) collective-permute-start(bf16[2304,256]{1,0:T(8,128)(2,1)S(1)} %bitcast.37), channel_id=1, source_target_pairs={{0,8},{8,0},{1,9},{9,1},{2,10},{10,2},{3,11},{11,3},{4,12},{12,4},... | collective-permute-start | bytes 3538952 | tf_op jit(solution)/shard_map/ppermute | solution.py:361

commit v7 on v5

--- a/solution.py
+++ b/solution.py
@@ -210,11 +210,33 @@
             out[s, row] = (own + total[s * width : (s + 1) * width]).astype(jnp.bfloat16)
 
 
-def part_kernel(scale, where, mine, other, first, second):
-    own, swapped = mine[...].astype(jnp.float32) * scale, other[...].astype(jnp.float32) * scale
-    keeps = where[1] == 0
-    first[...] = jnp.where(keeps, own, swapped)
-    second[...] = jnp.where(keeps, swapped, own)
+def part_kernel(scale, owner, where, given, *refs):
+    first, second, held, sems = refs[-4:]
+    count = sems.shape[0]
+    step = given.shape[0] // count
+    rows = [pl.ds(i * step, step) for i in range(count)]
+    to_first = where[1] == owner
+
+    def every(act_on):
+        for i, at in enumerate(rows):
+            act_on(i, at)
+
+    def write(out):
+        def one(i, at):
+            held[at] = given[at].astype(jnp.float32) * scale
+            pltpu.make_async_copy(held.at[at], out.at[at], sems.at[i]).start()
+
+        every(one)
+        every(lambda i, at: pltpu.make_async_copy(held.at[at], out.at[at], sems.at[i]).wait())
+
+    pl.when(to_first)(lambda: write(first))
+    pl.when(jnp.logical_not(to_first))(lambda: write(second))
+
+
+def copies_kernel(part, got, out):
+    value = (part[...] + got[...]).astype(jnp.bfloat16)
+    for i in range(out.shape[0]):
+        out[i] = value
 
 
 def both_ways(pairs):
@@ -270,10 +292,11 @@
     where = jnp.stack([lat, core, lax.rem(lat, 2)]).astype(jnp.int32)
     smem = pl.BlockSpec(memory_space=pltpu.SMEM)
     vmem = pl.BlockSpec(memory_space=pltpu.VMEM)
+    anywhere = pl.BlockSpec(memory_space=pl.ANY)
     cells = slabs * rows * width
     ext = pltpu.VMEM((slabs * (rows + 2), width + 2 * SPAN + 8, chans), jnp.float32)
     taps = pltpu.VMEM((9, cells, chans), jnp.bfloat16)
-    params = pltpu.CompilerParams(vmem_limit_bytes=48 * 1024 * 1024)
+    params = pltpu.CompilerParams(vmem_limit_bytes=24 * 1024 * 1024)
     grads = (9 * chans, chans)
     swap = [(0, 1), (1, 0)]
 
@@ -327,11 +350,13 @@
     part = jnp.sum(spread.astype(jnp.float32), axis=0)
     reach = 2
     while reach <= height:
-        part = part + lax.ppermute(part, ("z", "core"), folded(height, cores, reach))
+        got = lax.ppermute(part, ("z", "core"), folded(height, cores, reach))
+        if reach < height:
+            part = part + got
         reach *= 2
         if reach == height:
             part, pair = lax.optimization_barrier((part, pair))
-    part, next_pair = lax.optimization_barrier((part.astype(jnp.bfloat16), next_pair))
+    got, next_pair = lax.optimization_barrier((got, next_pair))
     above, below = ordered(pair, next_pair)
     around = (pair, next_pair) + column_halos([above, pre_field, below], width, lon_count, lat_count)
     input_grad = pl.pallas_call(
@@ -344,21 +369,39 @@
         name="back",
     )(where, strides, out_grad, pre_grad, *around, first_kernel)
 
-    copies = jnp.broadcast_to(part[None], (planes,) + part.shape)
+    copies = pl.pallas_call(
+        copies_kernel,
+        out_shape=jax.ShapeDtypeStruct((planes,) + part.shape, jnp.bfloat16),
+        in_specs=[vmem] * 2,
+        out_specs=vmem,
+        compiler_params=params,
+        name="copies",
+    )(part, got)
     mine = lax.all_to_all(copies, PLANE, 0, 0, tiled=True).reshape(grads)
     mine, input_grad = lax.optimization_barrier((mine, input_grad))
     other = lax.ppermute(mine, "core", swap)
     scale = 1.0 / math.sqrt(cells * lat_count * lon_count)
-    block = pl.BlockSpec((9 * chans // 4, chans), lambda i: (i, 0))
+    wide = [jax.ShapeDtypeStruct(grads, jnp.float32)] * 2
+    scratch = [pltpu.VMEM(grads, jnp.float32), pltpu.SemaphoreType.DMA((6,))]
+    sides = pl.pallas_call(
+        lambda *refs: part_kernel(scale, 0, *refs),
+        out_shape=wide,
+        in_specs=[smem, vmem],
+        out_specs=[anywhere] * 2,
+        scratch_shapes=scratch,
+        compiler_params=params,
+        name="own_part",
+    )(where, mine)
     first, second = pl.pallas_call(
-        lambda *refs: part_kernel(scale, *refs),
-        grid=(4,),
-        out_shape=[jax.ShapeDtypeStruct(grads, jnp.float32)] * 2,
-        in_specs=[smem, block, block],
-        out_specs=[block, block],
-        compiler_params=params,
-        name="part",
-    )(where, mine, other)
+        lambda *refs: part_kernel(scale, 1, *refs),
+        out_shape=wide,
+        in_specs=[smem, vmem, anywhere, anywhere],
+        out_specs=[anywhere] * 2,
+        scratch_shapes=scratch,
+        input_output_aliases={2: 0, 3: 1},
+        compiler_params=params,
+        name="other_part",
+    )(where, other, *sides)
     return input_grad, first.reshape(first_kernel.shape), second.reshape(first_kernel.shape)
 
 

time: 119 us -> 114 us (0.958)
  local copies, waits for them, and re-layouts: 3.73 us -> 1.45 us
  other arithmetic: 3.67 us -> 1.95 us
  Pallas kernels: 15.1 us -> 13.5 us
    ppermute x3, waiting for transfers between devices: 10.1 us -> 5.92 us  [local(): got = lax.ppermute(part, ('z', 'core'), folded(height, cores, reach))]
    ppermute x2, waiting for transfers between devices: 1.4 us -> 5.49 us  [row_halos(): return (pair, lax.ppermute(row(odd), ALL, between + across))]
    pallas_call x1, Pallas kernels: 6.53 us -> 4.03 us  [local(): pl.pallas_call(main_kernel, out_shape=[jax.ShapeDtypeStruct(grads, jnp.fl...]
    ppermute x2, waiting for transfers between devices: 4.05 us -> 6.37 us  [row_halos(): lax.ppermute(row(1 - odd), ALL, both_ways([(at(i, k), at(i, k + 1)) for i...]
    ppermute x1, waiting for transfers between devices: 2.47 us -> 0.44 us  [local(): other = lax.ppermute(mine, 'core', swap)]
    pallas_call x1 -> x3, Pallas kernels: 3.19 us -> 5.13 us  [the longest x1 2.02 us: local(): pl.pallas_call(lambda *refs: part_kernel(scale, 0, *refs), out_shape=wide...]
    convert_element_type x1, other arithmetic: 2 us -> 0.3 us  [local(): total.astype(jnp.bfloat16).reshape(planes, 9 * chans // planes, chans)]
    unnamed x13 -> x11, local copies, waits for them, and re-layouts: 2.57 us -> 1.38 us
  transfers between devices with their start and end apart: 16 -> 16, of which waited for: 13 -> 12; matrix products, arithmetic and copies ran while one was open for 0% -> 0% of each run, Pallas kernels for 5% -> 6%
where the time goes in v7:
time: 114 us
  starting transfers between devices  43.2 us (38%)
  waiting for transfers between devices  29.6 us (26%)
  blocking collectives  23.1 us (20%)
  Pallas kernels  13.5 us (12%)
  other arithmetic  1.95 us (2%)
  local copies, waits for them, and re-layouts  1.45 us (1%)
    all_to_all x1, blocking collectives, local(): spread = lax.all_to_all(total, PLANE, 0, 0, tiled=True)  23.1 us
    ppermute x3, starting transfers between devices, column_halos(): in_chip = lax.ppermute(edge((1 - core) * reach), 'core', [(0, 1), (1, 0)])  11.1 us
    ppermute x2, waiting for transfers between devices, row_halos(): lax.ppermute(row(1 - odd), ALL, both_ways([(at(i, k), at(i, k + 1)) for i...  6.37 us
    ppermute x1, starting transfers between devices, local(): other = lax.ppermute(mine, 'core', swap)  6.18 us
    ppermute x3, waiting for transfers between devices, column_halos(): lax.ppermute(edge(core * reach), ALL, both_ways([(at(i + 1, k), at(i + 2,...  6.03 us
    ppermute x2, starting transfers between devices, row_halos(): return (pair, lax.ppermute(row(odd), ALL, between + across))  5.94 us
    ppermute x3, waiting for transfers between devices, local(): got = lax.ppermute(part, ('z', 'core'), folded(height, cores, reach))  5.92 us
    ppermute x2, waiting for transfers between devices, row_halos(): return (pair, lax.ppermute(row(odd), ALL, between + across))  5.49 us
  transfers between devices with their start and end apart: 16, of which 12 were waited for; matrix products, arithmetic and copies ran while one was open for 0% of the time, Pallas kernels for 6%

profile of v7, /device:TPU:1, one launch (start us, length us, event | category | flops | bytes accessed | tf_op | source)
XLA Modules:
  0.0 113.6 jit_solution(7766163507361456977)
XLA Ops:
  0.6 0.0 copy-start.2
  0.6 0.0 copy-start.3
  0.7 1.3 %fusion.1 = (bf16[2,2,128,256]{3,2,1,0:T(8,128)(2,1)S(1)}, bf16[2,2,128,256]{3,2,1,0:T(8,128)(2,1)S(1)}) fusion(s32[]{:T(128)S(6)} %select_n.53, bf16[1,2,2,128,256]{4,3,2,1,0:T(8,128)(2,1)} %bitcast.41, bf16[1,2,2,128,256]{4,3,2,1,0:T(8,128)(2,1)} %bitcast.39, s32[]{:T(128)S(6)} %select_n.52), kind=kLoop, calls=%fused_computation.11 | loop fusion | flops 262144 | bytes 1048584 | tf_op jit(solution)/shard_map/jit(dynamic_index_in_dim)/squeeze | solution.py:250
  2.0 4.0 %collective-permute-start.3 = (bf16[2,2,128,256]{3,2,1,0:T(8,128)(2,1)S(1)}, bf16[2,2,128,256]{3,2,1,0:T(8,128)(2,1)S(1)}, u32[]{:S(2)}, u32[]{:S(2)}) collective-permute-start(bf16[2,2,128,256]{3,2,1,0:T(8,128)(2,1)S(1)} %get-tuple-element.55), channel_id=1, source_target_pairs={{1,2},{3,4},{5,6},{9,10},{11,12},{13,14},{17,18},{19,20},{21,22},{... | collective-permute-start | bytes 786440 | tf_op jit(solution)/shard_map/ppermute | solution.py:254
  6.0 2.7 %collective-permute-start.2 = (bf16[2,2,128,256]{3,2,1,0:T(8,128)(2,1)S(1)}, bf16[2,2,128,256]{3,2,1,0:T(8,128)(2,1)S(1)}, u32[]{:S(2)}, u32[]{:S(2)}) collective-permute-start(bf16[2,2,128,256]{3,2,1,0:T(8,128)(2,1)S(1)} %get-tuple-element.56), channel_id=1, source_target_pairs={{0,1},{2,3},{4,5},{6,7},{8,9},{10,11},{12,13},{14,15},{16,17},{18,... | collective-permute-start | bytes 786440 | tf_op jit(solution)/shard_map/ppermute | solution.py:251
  8.7 2.8 %collective-permute-start.1 = (bf16[2,2,2,16,256]{4,3,2,1,0:T(8,128)(2,1)S(1)}, bf16[2,2,2,16,256]{4,3,2,1,0:T(8,128)(2,1)S(1)}, u32[]{:S(2)}, u32[]{:S(2)}) collective-permute-start(bf16[2,2,2,16,256]{4,3,2,1,0:T(8,128)(2,1)S(1)} %get-tuple-element.57), channel_id=1, source_target_pairs={{8,16},{9,17},{10,18},{11,19},{12,20},{13,21},{14,22},{15,23},{24,... | collective-permute-start | bytes 196616 | tf_op jit(solution)/shard_map/ppermute | solution.py:266
  11.5 4.2 %collective-permute-start = (bf16[2,2,2,16,256]{4,3,2,1,0:T(8,128)(2,1)S(1)}, bf16[2,2,2,16,256]{4,3,2,1,0:T(8,128)(2,1)S(1)}, u32[]{:S(2)}, u32[]{:S(2)}) collective-permute-start(bf16[2,2,2,16,256]{4,3,2,1,0:T(8,128)(2,1)S(1)} %get-tuple-element.58), channel_id=1, source_target_pairs={{0,8},{8,0},{1,9},{9,1},{2,10},{10,2},{3,11},{11,3},{4,12},{12,4},... | collective-permute-start | bytes 196616 | tf_op jit(solution)/shard_map/ppermute | solution.py:267
  15.8 0.1 copy.11.strides
  15.9 0.1 pad_add_fusion.where.refs_0_
  15.9 0.0 collective-permute-done.1.next_chip
  15.9 0.7 collective-permute-done.in_chip
  16.7 0.0 copy-done
  16.7 1.3 %copy-done.1 = bf16[3,3,256,256]{3,2,1,0:T(8,128)(2,1)S(1)} copy-done((bf16[3,3,256,256]{3,2,1,0:T(8,128)(2,1)S(1)}, bf16[3,3,256,256]{3,2,1,0:T(8,128)(2,1)}, u32[]{:S(2)}) %copy-start.1) | copy-done | bytes 1179672
  18.0 2.0 %early.1 = (bf16[12,256,256]{2,1,0:T(8,128)(2,1)S(1)}, bf16[12,256,256]{2,1,0:T(8,128)(2,1)S(1)}, f32[512,256]{1,0:T(8,128)S(1)}, f32[512,256]{1,0:T(8,128)S(1)}) custom-call(s32[3]{0:T(128)S(1)} %pad_add_fusion.where.refs_0_, s32[2,16,3]{2,1,0:T(8,128)S(1)} %copy.11.strides, bf16[2,2,128,256]{3,2,1,0:T(8,128)(2,1)S(1)} %copy-done.3, ...), custom_call_target="tpu_custom_call" | custom-call | tf_op jit(solution)/shard_map/early/pallas_call | solution.py:308
  19.9 0.0 collective-permute-done.3.next_pair
  19.9 2.7 %collective-permute-done.2.pair = bf16[2,2,128,256]{3,2,1,0:T(8,128)(2,1)S(1)} collective-permute-done((bf16[2,2,128,256]{3,2,1,0:T(8,128)(2,1)S(1)}, bf16[2,2,128,256]{3,2,1,0:T(8,128)(2,1)S(1)}, u32[]{:S(2)}, u32[]{:S(2)}) %collective-permute-start.2) | collective-permute-done | bytes 262176 | tf_op jit(solution)/shard_map/ppermute | solution.py:251
  22.8 1.8 %collective-permute-start.4 = (bf16[2,2,2,16,256]{4,3,2,1,0:T(8,128)(2,1)S(1)}, bf16[2,2,2,16,256]{4,3,2,1,0:T(8,128)(2,1)S(1)}, u32[]{:S(2)}, u32[]{:S(2)}) collective-permute-start(bf16[2,2,2,16,256]{4,3,2,1,0:T(8,128)(2,1)S(1)} %pad_maximum_fusion), channel_id=1, source_target_pairs={{0,8},{8,0},{1,9},{9,1},{2,10},{10,2},{3,11},{11,3},{4,12},{12,4},... | collective-permute-start | bytes 196616 | tf_op jit(solution)/shard_map/ppermute | solution.py:267
  24.6 0.9 collective-permute-start.5
  25.5 0.0 collective-permute-done.4.in_chip
  25.5 2.8 %collective-permute-done.5.next_chip = bf16[2,2,2,16,256]{4,3,2,1,0:T(8,128)(2,1)S(1)} collective-permute-done((bf16[2,2,2,16,256]{4,3,2,1,0:T(8,128)(2,1)S(1)}, bf16[2,2,2,16,256]{4,3,2,1,0:T(8,128)(2,1)S(1)}, u32[]{:S(2)}, u32[]{:S(2)}) %collective-permute-start.5) | collective-permute-done | bytes 65568 | tf_op jit(solution)/shard_map/ppermute | solution.py:266
  28.4 4.0 %main.1 = (f32[2304,256]{1,0:T(8,128)S(1)}, bf16[2304,256]{1,0:T(8,128)(2,1)S(1)}, bf16[2,2,128,256]{3,2,1,0:T(8,128)(2,1)S(1)}) custom-call(s32[3]{0:T(128)S(1)} %pad_add_fusion.where.refs_0_, s32[2,16,3]{2,1,0:T(8,128)S(1)} %copy.11.strides, bf16[12,256,256]{2,1,0:T(8,128)(2,1)S(1)} %get-tuple-element.32.own_f, ...), custom_call_target="tpu_custom_call" | custom-call | tf_op jit(solution)/shard_map/main/pallas_call | solution.py:321
  32.4 4.2 %collective-permute-start.6 = (bf16[2304,256]{1,0:T(8,128)(2,1)S(1)}, bf16[2304,256]{1,0:T(8,128)(2,1)S(1)}, u32[]{:S(2)}, u32[]{:S(2)}) collective-permute-start(bf16[2304,256]{1,0:T(8,128)(2,1)S(1)} %get-tuple-element.39), channel_id=1, source_target_pairs={{0,8},{8,0},{1,9},{9,1},{2,10},{10,2},{3,11},{11,3},{4,12},{12,4},... | collective-permute-start | bytes 3538952 | tf_op jit(solution)/shard_map/ppermute | solution.py:342
  36.7 2.5 %collective-permute-done.6 = bf16[2304,256]{1,0:T(8,128)(2,1)S(1)} collective-permute-done((bf16[2304,256]{1,0:T(8,128)(2,1)S(1)}, bf16[2304,256]{1,0:T(8,128)(2,1)S(1)}, u32[]{:S(2)}, u32[]{:S(2)}) %collective-permute-start.6) | collective-permute-done | bytes 1179680 | tf_op jit(solution)/shard_map/ppermute | solution.py:342
  39.1 0.3 add_convert_fusion
  39.4 23.1 %all_to_all.10 = bf16[16,144,256]{2,1,0:T(8,128)(2,1)S(1)} all-to-all(bf16[16,144,256]{2,1,0:T(8,128)(2,1)S(1)} %bitcast.43), channel_id=1, replica_groups=mesh['yl'=2,'z'=8,'core'=2,'x'=4,'yh'=2] {'x','yh','yl'}, dimensions={0} | all-to-all | bytes 2359296 | tf_op jit(solution)/shard_map/all_to_all | solution.py:345
  62.5 0.2 convert_reduce_fusion
  62.7 0.1 collective-permute-start.7
  62.8 4.0 %collective-permute-done.7 = f32[144,256]{1,0:T(8,128)S(1)} collective-permute-done((f32[144,256]{1,0:T(8,128)S(1)}, f32[144,256]{1,0:T(8,128)S(1)}, u32[]{:S(2)}, u32[]{:S(2)}) %collective-permute-start.7) | collective-permute-done | bytes 147488 | tf_op jit(solution)/shard_map/ppermute | solution.py:353
  66.8 3.4 %collective-permute-start.8 = (f32[144,256]{1,0:T(8,128)S(1)}, f32[144,256]{1,0:T(8,128)S(1)}, u32[]{:S(2)}, u32[]{:S(2)}) collective-permute-start(f32[144,256]{1,0:T(8,128)S(1)} %add.49), channel_id=1, source_target_pairs={{0,32},{8,104},{16,48},{24,120},{32,0},{40,72},{48,16},{56,88},{64... | collective-permute-start | bytes 442376 | tf_op jit(solution)/shard_map/ppermute | solution.py:353
  70.2 1.4 %collective-permute-start.9 = (bf16[1,2,128,256]{3,2,1,0:T(8,128)(2,1)S(1)}, bf16[1,2,128,256]{3,2,1,0:T(8,128)(2,1)S(1)}, u32[]{:S(2)}, u32[]{:S(2)}) collective-permute-start(bf16[1,2,128,256]{3,2,1,0:T(8,128)(2,1)S(1)} %get-tuple-element.64), channel_id=1, source_target_pairs={{0,1},{2,3},{4,5},{6,7},{8,9},{10,11},{12,13},{14,15},{16,17},{18,... | collective-permute-start | bytes 393224 | tf_op jit(solution)/shard_map/ppermute | solution.py:251
  71.6 1.9 %collective-permute-done.8 = f32[144,256]{1,0:T(8,128)S(1)} collective-permute-done((f32[144,256]{1,0:T(8,128)S(1)}, f32[144,256]{1,0:T(8,128)S(1)}, u32[]{:S(2)}, u32[]{:S(2)}) %collective-permute-start.8) | collective-permute-done | bytes 147488 | tf_op jit(solution)/shard_map/ppermute | solution.py:353
  73.6 3.6 %collective-permute-done.9.pair = bf16[1,2,128,256]{3,2,1,0:T(8,128)(2,1)S(1)} collective-permute-done((bf16[1,2,128,256]{3,2,1,0:T(8,128)(2,1)S(1)}, bf16[1,2,128,256]{3,2,1,0:T(8,128)(2,1)S(1)}, u32[]{:S(2)}, u32[]{:S(2)}) %collective-permute-start.9) | collective-permute-done | bytes 131104 | tf_op jit(solution)/shard_map/ppermute | solution.py:251
  77.2 0.0 collective-permute-start.10
  77.2 1.9 %collective-permute-start.11 = (bf16[1,2,128,256]{3,2,1,0:T(8,128)(2,1)S(1)}, bf16[1,2,128,256]{3,2,1,0:T(8,128)(2,1)S(1)}, u32[]{:S(2)}, u32[]{:S(2)}) collective-permute-start(bf16[1,2,128,256]{3,2,1,0:T(8,128)(2,1)S(1)} %get-tuple-element.63), channel_id=1, source_target_pairs={{1,2},{3,4},{5,6},{9,10},{11,12},{13,14},{17,18},{19,20},{21,22},{... | collective-permute-start | bytes 393224 | tf_op jit(solution)/shard_map/ppermute | solution.py:254
  79.1 5.5 %collective-permute-done.11.next_pair = bf16[1,2,128,256]{3,2,1,0:T(8,128)(2,1)S(1)} collective-permute-done((bf16[1,2,128,256]{3,2,1,0:T(8,128)(2,1)S(1)}, bf16[1,2,128,256]{3,2,1,0:T(8,128)(2,1)S(1)}, u32[]{:S(2)}, u32[]{:S(2)}) %collective-permute-start.11) | collective-permute-done | bytes 131104 | tf_op jit(solution)/shard_map/ppermute | solution.py:254
  84.6 0.0 collective-permute-done.10.got
  84.6 1.1 copies.1
  85.7 3.9 %all-to-all-start.1 = ((bf16[16,144,256]{2,1,0:T(8,128)(2,1)}), bf16[16,144,256]{2,1,0:T(8,128)(2,1)S(1)}, u32[]{:S(2)}, u32[]{:S(2)}) async-start(bf16[16,144,256]{2,1,0:T(8,128)(2,1)} %copies.1), calls=%async_computation.1 | async-start | bytes 2359296 | tf_op jit(solution)/shard_map/all_to_all | solution.py:380
  89.7 5.1 %collective-permute-start.12 = (bf16[1,2,4,16,256]{4,3,2,1,0:T(8,128)(2,1)S(1)}, bf16[1,2,4,16,256]{4,3,2,1,0:T(8,128)(2,1)S(1)}, u32[]{:S(2)}, u32[]{:S(2)}) collective-permute-start(bf16[1,2,4,16,256]{4,3,2,1,0:T(8,128)(2,1)S(1)} %pad_maximum_fusion.2), channel_id=1, source_target_pairs={{0,8},{8,0},{1,9},{9,1},{2,10},{10,2},{3,11},{11,3},{4,12},{12,4},... | collective-permute-start | bytes 196616 | tf_op jit(solution)/shard_map/ppermute | solution.py:267
  94.8 0.4 collective-permute-start.13
  95.3 0.5 collective-permute-done.12.in_chip
  95.7 3.2 %collective-permute-done.13.next_chip = bf16[1,2,4,16,256]{4,3,2,1,0:T(8,128)(2,1)S(1)} collective-permute-done((bf16[1,2,4,16,256]{4,3,2,1,0:T(8,128)(2,1)S(1)}, bf16[1,2,4,16,256]{4,3,2,1,0:T(8,128)(2,1)S(1)}, u32[]{:S(2)}, u32[]{:S(2)}) %collective-permute-start.13) | collective-permute-done | bytes 65568 | tf_op jit(solution)/shard_map/ppermute | solution.py:266
  98.9 2.4 %back.1 = bf16[2,2,128,256]{3,2,1,0:T(8,128)(2,1)} custom-call(s32[3]{0:T(128)S(1)} %pad_add_fusion.where.refs_0_, s32[2,16,3]{2,1,0:T(8,128)S(1)} %copy.11.strides, bf16[2,2,128,256]{3,2,1,0:T(8,128)(2,1)S(1)} %copy-done.2, bf16[2,2,128,256]{3,2,1,0:T(8,128)(2,1)S(1)} %get-tuple-element.42.pre, bf16[1,2,128,256]{3,2,1,0:T(8,128)(2,1)S(1)} %collective-permute-done.9.pair, ...), custom_call_target="tpu_custom_call" | custom-call | tf_op jit(solution)/shard_map/back/pallas_call | solution.py:362
  101.3 1.7 %all-to-all-done.1 = bf16[16,144,256]{2,1,0:T(8,128)(2,1)S(1)} async-done(((bf16[16,144,256]{2,1,0:T(8,128)(2,1)}), bf16[16,144,256]{2,1,0:T(8,128)(2,1)S(1)}, u32[]{:S(2)}, u32[]{:S(2)}) %all-to-all-start.1) | async-done | bytes 1179680 | tf_op jit(solution)/shard_map/all_to_all | solution.py:380
  103.0 6.2 %collective-permute-start.14 = (bf16[2304,256]{1,0:T(8,128)(2,1)S(1)}, bf16[2304,256]{1,0:T(8,128)(2,1)S(1)}, u32[]{:S(2)}, u32[]{:S(2)}) collective-permute-start(bf16[2304,256]{1,0:T(8,128)(2,1)S(1)} %bitcast.37), channel_id=1, source_target_pairs={{0,8},{8,0},{1,9},{9,1},{2,10},{10,2},{3,11},{11,3},{4,12},{12,4},... | collective-permute-start | bytes 3538952 | tf_op jit(solution)/shard_map/ppermute | solution.py:382
  109.1 2.0 %own_part.1 = (f32[2304,256]{1,0:T(8,128)}, f32[2304,256]{1,0:T(8,128)}) custom-call(s32[3]{0:T(128)S(1)} %pad_add_fusion.where.refs_0_, bf16[2304,256]{1,0:T(8,128)(2,1)S(1)} %bitcast.38), custom_call_target="tpu_custom_call" | custom-call | tf_op jit(solution)/shard_map/own_part/pallas_call | solution.py:386
  111.2 0.4 collective-permute-done.14.refs_1_
  111.6 2.0 %other_part.1 = (f32[2304,256]{1,0:T(8,128)}, f32[2304,256]{1,0:T(8,128)}) custom-call(s32[3]{0:T(128)S(1)} %pad_add_fusion.where.refs_0_, bf16[2304,256]{1,0:T(8,128)(2,1)S(1)} %collective-permute-done.14.refs_1_, f32[2304,256]{1,0:T(8,128)} %get-tuple-element.49.refs_2_, ...), custom_call_target="tpu_custom_call", output_to_operand_aliasing={{0}: (2, {}), {1}: (3, {})} | custom-call | tf_op jit(solution)/shard_map/other_part/pallas_call | solution.py:395
  (20 shorter events, 0.2 us)
Async XLA Ops:
  0.6 8.1 %copy-start.2 = (bf16[2,2,128,256]{3,2,1,0:T(8,128)(2,1)S(1)}, bf16[2,2,128,256]{3,2,1,0:T(8,128)(2,1)}, u32[]{:S(2)}) copy-start(bf16[2,2,128,256]{3,2,1,0:T(8,128)(2,1)} %grad.3) | copy-start | bytes 786436
  0.6 8.0 %copy-start.3 = (bf16[2,2,128,256]{3,2,1,0:T(8,128)(2,1)S(1)}, bf16[2,2,128,256]{3,2,1,0:T(8,128)(2,1)}, u32[]{:S(2)}) copy-start(bf16[2,2,128,256]{3,2,1,0:T(8,128)(2,1)} %feat.1) | copy-start | bytes 786436
  0.7 15.1 %copy-start.4 = (s32[2,16,3]{1,0,2:T(2,128)S(1)}, s32[2,16,3]{1,0,2:T(2,128)}, u32[]{:S(2)}) copy-start(s32[2,16,3]{1,0,2:T(2,128)} %param.9) | copy-start | bytes 1156
  0.7 16.0 %copy-start = (bf16[3,3,256,256]{3,2,1,0:T(8,128)(2,1)S(1)}, bf16[3,3,256,256]{3,2,1,0:T(8,128)(2,1)}, u32[]{:S(2)}) copy-start(bf16[3,3,256,256]{3,2,1,0:T(8,128)(2,1)} %first_kernel.5) | copy-start | bytes 3538948
  2.0 18.0 %collective-permute-start.3 = (bf16[2,2,128,256]{3,2,1,0:T(8,128)(2,1)S(1)}, bf16[2,2,128,256]{3,2,1,0:T(8,128)(2,1)S(1)}, u32[]{:S(2)}, u32[]{:S(2)}) collective-permute-start(bf16[2,2,128,256]{3,2,1,0:T(8,128)(2,1)S(1)} %get-tuple-element.55), channel_id=1, source_target_pairs={{1,2},{3,4},{5,6},{9,10},{11,12},{13,14},{17,18},{19,20},{21,22},{... | collective-permute-start | bytes 786440 | tf_op jit(solution)/shard_map/ppermute | solution.py:254
  6.0 16.7 %collective-permute-start.2 = (bf16[2,2,128,256]{3,2,1,0:T(8,128)(2,1)S(1)}, bf16[2,2,128,256]{3,2,1,0:T(8,128)(2,1)S(1)}, u32[]{:S(2)}, u32[]{:S(2)}) collective-permute-start(bf16[2,2,128,256]{3,2,1,0:T(8,128)(2,1)S(1)} %get-tuple-element.56), channel_id=1, source_target_pairs={{0,1},{2,3},{4,5},{6,7},{8,9},{10,11},{12,13},{14,15},{16,17},{18,... | collective-permute-start | bytes 786440 | tf_op jit(solution)/shard_map/ppermute | solution.py:251
  8.7 7.2 %collective-permute-start.1 = (bf16[2,2,2,16,256]{4,3,2,1,0:T(8,128)(2,1)S(1)}, bf16[2,2,2,16,256]{4,3,2,1,0:T(8,128)(2,1)S(1)}, u32[]{:S(2)}, u32[]{:S(2)}) collective-permute-start(bf16[2,2,2,16,256]{4,3,2,1,0:T(8,128)(2,1)S(1)} %get-tuple-element.57), channel_id=1, source_target_pairs={{8,16},{9,17},{10,18},{11,19},{12,20},{13,21},{14,22},{15,23},{24,... | collective-permute-start | bytes 196616 | tf_op jit(solution)/shard_map/ppermute | solution.py:266
  11.5 5.1 %collective-permute-start = (bf16[2,2,2,16,256]{4,3,2,1,0:T(8,128)(2,1)S(1)}, bf16[2,2,2,16,256]{4,3,2,1,0:T(8,128)(2,1)S(1)}, u32[]{:S(2)}, u32[]{:S(2)}) collective-permute-start(bf16[2,2,2,16,256]{4,3,2,1,0:T(8,128)(2,1)S(1)} %get-tuple-element.58), channel_id=1, source_target_pairs={{0,8},{8,0},{1,9},{9,1},{2,10},{10,2},{3,11},{11,3},{4,12},{12,4},... | collective-permute-start | bytes 196616 | tf_op jit(solution)/shard_map/ppermute | solution.py:267
  16.7 1.3 %copy-start.1 = (bf16[3,3,256,256]{3,2,1,0:T(8,128)(2,1)S(1)}, bf16[3,3,256,256]{3,2,1,0:T(8,128)(2,1)}, u32[]{:S(2)}) copy-start(bf16[3,3,256,256]{3,2,1,0:T(8,128)(2,1)} %second_kernel.3) | copy-start | bytes 3538948
  22.8 2.8 %collective-permute-start.4 = (bf16[2,2,2,16,256]{4,3,2,1,0:T(8,128)(2,1)S(1)}, bf16[2,2,2,16,256]{4,3,2,1,0:T(8,128)(2,1)S(1)}, u32[]{:S(2)}, u32[]{:S(2)}) collective-permute-start(bf16[2,2,2,16,256]{4,3,2,1,0:T(8,128)(2,1)S(1)} %pad_maximum_fusion), channel_id=1, source_target_pairs={{0,8},{8,0},{1,9},{9,1},{2,10},{10,2},{3,11},{11,3},{4,12},{12,4},... | collective-permute-start | bytes 196616 | tf_op jit(solution)/shard_map/ppermute | solution.py:267
  24.6 3.8 %collective-permute-start.5 = (bf16[2,2,2,16,256]{4,3,2,1,0:T(8,128)(2,1)S(1)}, bf16[2,2,2,16,256]{4,3,2,1,0:T(8,128)(2,1)S(1)}, u32[]{:S(2)}, u32[]{:S(2)}) collective-permute-start(bf16[2,2,2,16,256]{4,3,2,1,0:T(8,128)(2,1)S(1)} %pad_maximum_fusion.1), channel_id=1, source_target_pairs={{8,16},{9,17},{10,18},{11,19},{12,20},{13,21},{14,22},{15,23},{24,... | collective-permute-start | bytes 196616 | tf_op jit(solution)/shard_map/ppermute | solution.py:266
  32.4 6.7 %collective-permute-start.6 = (bf16[2304,256]{1,0:T(8,128)(2,1)S(1)}, bf16[2304,256]{1,0:T(8,128)(2,1)S(1)}, u32[]{:S(2)}, u32[]{:S(2)}) collective-permute-start(bf16[2304,256]{1,0:T(8,128)(2,1)S(1)} %get-tuple-element.39), channel_id=1, source_target_pairs={{0,8},{8,0},{1,9},{9,1},{2,10},{10,2},{3,11},{11,3},{4,12},{12,4},... | collective-permute-start | bytes 3538952 | tf_op jit(solution)/shard_map/ppermute | solution.py:342
  62.7 4.1 %collective-permute-start.7 = (f32[144,256]{1,0:T(8,128)S(1)}, f32[144,256]{1,0:T(8,128)S(1)}, u32[]{:S(2)}, u32[]{:S(2)}) collective-permute-start(f32[144,256]{1,0:T(8,128)S(1)} %convert_reduce_fusion), channel_id=1, source_target_pairs={{0,16},{8,24},{16,0},{24,8},{32,48},{40,56},{48,32},{56,40},{64,80... | collective-permute-start | bytes 442376 | tf_op jit(solution)/shard_map/ppermute | solution.py:353
  66.8 6.8 %collective-permute-start.8 = (f32[144,256]{1,0:T(8,128)S(1)}, f32[144,256]{1,0:T(8,128)S(1)}, u32[]{:S(2)}, u32[]{:S(2)}) collective-permute-start(f32[144,256]{1,0:T(8,128)S(1)} %add.49), channel_id=1, source_target_pairs={{0,32},{8,104},{16,48},{24,120},{32,0},{40,72},{48,16},{56,88},{64... | collective-permute-start | bytes 442376 | tf_op jit(solution)/shard_map/ppermute | solution.py:353
  70.2 7.0 %collective-permute-start.9 = (bf16[1,2,128,256]{3,2,1,0:T(8,128)(2,1)S(1)}, bf16[1,2,128,256]{3,2,1,0:T(8,128)(2,1)S(1)}, u32[]{:S(2)}, u32[]{:S(2)}) collective-permute-start(bf16[1,2,128,256]{3,2,1,0:T(8,128)(2,1)S(1)} %get-tuple-element.64), channel_id=1, source_target_pairs={{0,1},{2,3},{4,5},{6,7},{8,9},{10,11},{12,13},{14,15},{16,17},{18,... | collective-permute-start | bytes 393224 | tf_op jit(solution)/shard_map/ppermute | solution.py:251
  77.2 7.4 %collective-permute-start.10 = (f32[144,256]{1,0:T(8,128)S(1)}, f32[144,256]{1,0:T(8,128)S(1)}, u32[]{:S(2)}, u32[]{:S(2)}) collective-permute-start(f32[144,256]{1,0:T(8,128)S(1)} %add.50.part), channel_id=1, source_target_pairs={{0,112},{8,56},{16,96},{24,40},{32,80},{40,24},{48,64},{56,8},{64,... | collective-permute-start | bytes 442376 | tf_op jit(solution)/shard_map/ppermute | solution.py:353
  77.2 7.4 %collective-permute-start.11 = (bf16[1,2,128,256]{3,2,1,0:T(8,128)(2,1)S(1)}, bf16[1,2,128,256]{3,2,1,0:T(8,128)(2,1)S(1)}, u32[]{:S(2)}, u32[]{:S(2)}) collective-permute-start(bf16[1,2,128,256]{3,2,1,0:T(8,128)(2,1)S(1)} %get-tuple-element.63), channel_id=1, source_target_pairs={{1,2},{3,4},{5,6},{9,10},{11,12},{13,14},{17,18},{19,20},{21,22},{... | collective-permute-start | bytes 393224 | tf_op jit(solution)/shard_map/ppermute | solution.py:254
  85.7 17.2 %all-to-all-start.1 = ((bf16[16,144,256]{2,1,0:T(8,128)(2,1)}), bf16[16,144,256]{2,1,0:T(8,128)(2,1)S(1)}, u32[]{:S(2)}, u32[]{:S(2)}) async-start(bf16[16,144,256]{2,1,0:T(8,128)(2,1)} %copies.1), calls=%async_computation.1 | async-start | bytes 2359296 | tf_op jit(solution)/shard_map/all_to_all | solution.py:380
  89.7 6.0 %collective-permute-start.12 = (bf16[1,2,4,16,256]{4,3,2,1,0:T(8,128)(2,1)S(1)}, bf16[1,2,4,16,256]{4,3,2,1,0:T(8,128)(2,1)S(1)}, u32[]{:S(2)}, u32[]{:S(2)}) collective-permute-start(bf16[1,2,4,16,256]{4,3,2,1,0:T(8,128)(2,1)S(1)} %pad_maximum_fusion.2), channel_id=1, source_target_pairs={{0,8},{8,0},{1,9},{9,1},{2,10},{10,2},{3,11},{11,3},{4,12},{12,4},... | collective-permute-start | bytes 196616 | tf_op jit(solution)/shard_map/ppermute | solution.py:267
  94.8 4.1 %collective-permute-start.13 = (bf16[1,2,4,16,256]{4,3,2,1,0:T(8,128)(2,1)S(1)}, bf16[1,2,4,16,256]{4,3,2,1,0:T(8,128)(2,1)S(1)}, u32[]{:S(2)}, u32[]{:S(2)}) collective-permute-start(bf16[1,2,4,16,256]{4,3,2,1,0:T(8,128)(2,1)S(1)} %pad_maximum_fusion.3), channel_id=1, source_target_pairs={{8,16},{9,17},{10,18},{11,19},{12,20},{13,21},{14,22},{15,23},{24,... | collective-permute-start | bytes 196616 | tf_op jit(solution)/shard_map/ppermute | solution.py:266
  103.0 8.7 %collective-permute-start.14 = (bf16[2304,256]{1,0:T(8,128)(2,1)S(1)}, bf16[2304,256]{1,0:T(8,128)(2,1)S(1)}, u32[]{:S(2)}, u32[]{:S(2)}) collective-permute-start(bf16[2304,256]{1,0:T(8,128)(2,1)S(1)} %bitcast.37), channel_id=1, source_target_pairs={{0,8},{8,0},{1,9},{9,1},{2,10},{10,2},{3,11},{11,3},{4,12},{12,4},... | collective-permute-start | bytes 3538952 | tf_op jit(solution)/shard_map/ppermute | solution.py:382

commit v8 on v7

--- a/solution.py
+++ b/solution.py
@@ -342,11 +342,12 @@
     total = keep + lax.ppermute(send, "core", swap).astype(jnp.float32)
     planes, height, cores = lax.axis_size(PLANE), lax.axis_size("z"), lax.axis_size("core")
     total = total.astype(jnp.bfloat16).reshape(planes, 9 * chans // planes, chans)
-    spread = lax.all_to_all(total, PLANE, 0, 0, tiled=True)
-
-    spread, pre_grad = lax.optimization_barrier((spread, pre_grad))
     pre_field = pre_grad[None]
     pair, next_pair = row_halos(pre_field, lon_count, lat_count)
+    total, pair = lax.optimization_barrier((total, pair))
+    spread = lax.all_to_all(total, PLANE, 0, 0, tiled=True)
+
+    spread, next_pair = lax.optimization_barrier((spread, next_pair))
     part = jnp.sum(spread.astype(jnp.float32), axis=0)
     reach = 2
     while reach <= height:
@@ -354,9 +355,7 @@
         if reach < height:
             part = part + got
         reach *= 2
-        if reach == height:
-            part, pair = lax.optimization_barrier((part, pair))
-    got, next_pair = lax.optimization_barrier((got, next_pair))
+    got, pair, pre_field = lax.optimization_barrier((got, pair, pre_field))
     above, below = ordered(pair, next_pair)
     around = (pair, next_pair) + column_halos([above, pre_field, below], width, lon_count, lat_count)
     input_grad = pl.pallas_call(

time: 114 us -> 117 us (1.026)
  blocking collectives: 23.1 us -> 0 us
  waiting for transfers between devices: 29.6 us -> 45 us
  starting transfers between devices: 43.2 us -> 52.1 us
  other arithmetic: 1.95 us -> 3.12 us
    all_to_all x1 -> x0, blocking collectives: 23.1 us -> none  [local(): spread = lax.all_to_all(total, PLANE, 0, 0, tiled=True)]
    ppermute x2, waiting for transfers between devices: 5.49 us -> 16.7 us  [row_halos(): return (pair, lax.ppermute(row(odd), ALL, between + across))]
    ppermute x3, waiting for transfers between devices: 5.92 us -> 15.3 us  [local(): got = lax.ppermute(part, ('z', 'core'), folded(height, cores, reach))]
    all_to_all x0 -> x1, starting transfers between devices: none -> 4.14 us  [local(): spread = lax.all_to_all(total, PLANE, 0, 0, tiled=True)]
    ppermute x2, starting transfers between devices: 4.13 us -> 7.09 us  [row_halos(): lax.ppermute(row(1 - odd), ALL, both_ways([(at(i, k), at(i, k + 1)) for i...]
    ppermute x1, waiting for transfers between devices: 2.47 us -> 0.01 us  [local(): total = keep + lax.ppermute(send, 'core', swap).astype(jnp.float32)]
    ppermute x3, starting transfers between devices: 3.47 us -> 1.08 us  [local(): got = lax.ppermute(part, ('z', 'core'), folded(height, cores, reach))]
    ppermute x3, starting transfers between devices: 11.1 us -> 13.5 us  [column_halos(): in_chip = lax.ppermute(edge((1 - core) * reach), 'core', [(0, 1), (1, 0)])]
  transfers between devices with their start and end apart: 16 -> 17, of which waited for: 12 -> 11; matrix products, arithmetic and copies ran while one was open for 0% -> 2% of each run, Pallas kernels for 6% -> 6%
where the time goes in v8:
time: 117 us; the launch traced here: 116 us
  starting transfers between devices  52.1 us (45%)
  waiting for transfers between devices  45 us (38%)
  Pallas kernels  13.6 us (12%)
  other arithmetic  3.12 us (3%)
  local copies, waits for them, and re-layouts  1.45 us (1%)
    ppermute x2, waiting for transfers between devices, row_halos(): return (pair, lax.ppermute(row(odd), ALL, between + across))  16.7 us
    ppermute x3, waiting for transfers between devices, local(): got = lax.ppermute(part, ('z', 'core'), folded(height, cores, reach))  15.3 us
    ppermute x3, starting transfers between devices, column_halos(): in_chip = lax.ppermute(edge((1 - core) * reach), 'core', [(0, 1), (1, 0)])  13.5 us
    ppermute x2, starting transfers between devices, row_halos(): return (pair, lax.ppermute(row(odd), ALL, between + across))  7.3 us
    ppermute x2, starting transfers between devices, row_halos(): lax.ppermute(row(1 - odd), ALL, both_ways([(at(i, k), at(i, k + 1)) for i...  7.09 us
    ppermute x1, starting transfers between devices, local(): other = lax.ppermute(mine, 'core', swap)  6.97 us
    ppermute x3, waiting for transfers between devices, column_halos(): lax.ppermute(edge(core * reach), ALL, both_ways([(at(i + 1, k), at(i + 2,...  6 us
    ppermute x2, waiting for transfers between devices, row_halos(): lax.ppermute(row(1 - odd), ALL, both_ways([(at(i, k), at(i, k + 1)) for i...  5.06 us
  transfers between devices with their start and end apart: 17, of which 11 were waited for; matrix products, arithmetic and copies ran while one was open for 2% of the time, Pallas kernels for 6%

profile of v8, /device:TPU:1, one launch (start us, length us, event | category | flops | bytes accessed | tf_op | source)
XLA Modules:
  0.0 116.2 jit_solution(8298221174393805795)
XLA Ops:
  0.6 0.0 copy-start.2
  0.6 0.0 copy-start.3
  0.7 1.3 %fusion.1 = (bf16[2,2,128,256]{3,2,1,0:T(8,128)(2,1)S(1)}, bf16[2,2,128,256]{3,2,1,0:T(8,128)(2,1)S(1)}) fusion(s32[]{:T(128)S(6)} %select_n.53, bf16[1,2,2,128,256]{4,3,2,1,0:T(8,128)(2,1)} %bitcast.38, bf16[1,2,2,128,256]{4,3,2,1,0:T(8,128)(2,1)} %bitcast.36, s32[]{:T(128)S(6)} %select_n.52), kind=kLoop, calls=%fused_computation.11 | loop fusion | flops 262144 | bytes 1048584 | tf_op jit(solution)/shard_map/jit(dynamic_index_in_dim)/squeeze | solution.py:250
  2.0 4.0 %collective-permute-start.3 = (bf16[2,2,128,256]{3,2,1,0:T(8,128)(2,1)S(1)}, bf16[2,2,128,256]{3,2,1,0:T(8,128)(2,1)S(1)}, u32[]{:S(2)}, u32[]{:S(2)}) collective-permute-start(bf16[2,2,128,256]{3,2,1,0:T(8,128)(2,1)S(1)} %get-tuple-element.57), channel_id=1, source_target_pairs={{1,2},{3,4},{5,6},{9,10},{11,12},{13,14},{17,18},{19,20},{21,22},{... | collective-permute-start | bytes 786440 | tf_op jit(solution)/shard_map/ppermute | solution.py:254
  6.0 2.7 %collective-permute-start.2 = (bf16[2,2,128,256]{3,2,1,0:T(8,128)(2,1)S(1)}, bf16[2,2,128,256]{3,2,1,0:T(8,128)(2,1)S(1)}, u32[]{:S(2)}, u32[]{:S(2)}) collective-permute-start(bf16[2,2,128,256]{3,2,1,0:T(8,128)(2,1)S(1)} %get-tuple-element.58), channel_id=1, source_target_pairs={{0,1},{2,3},{4,5},{6,7},{8,9},{10,11},{12,13},{14,15},{16,17},{18,... | collective-permute-start | bytes 786440 | tf_op jit(solution)/shard_map/ppermute | solution.py:251
  8.7 2.8 %collective-permute-start.1 = (bf16[2,2,2,16,256]{4,3,2,1,0:T(8,128)(2,1)S(1)}, bf16[2,2,2,16,256]{4,3,2,1,0:T(8,128)(2,1)S(1)}, u32[]{:S(2)}, u32[]{:S(2)}) collective-permute-start(bf16[2,2,2,16,256]{4,3,2,1,0:T(8,128)(2,1)S(1)} %get-tuple-element.59), channel_id=1, source_target_pairs={{8,16},{9,17},{10,18},{11,19},{12,20},{13,21},{14,22},{15,23},{24,... | collective-permute-start | bytes 196616 | tf_op jit(solution)/shard_map/ppermute | solution.py:266
  11.5 4.2 %collective-permute-start = (bf16[2,2,2,16,256]{4,3,2,1,0:T(8,128)(2,1)S(1)}, bf16[2,2,2,16,256]{4,3,2,1,0:T(8,128)(2,1)S(1)}, u32[]{:S(2)}, u32[]{:S(2)}) collective-permute-start(bf16[2,2,2,16,256]{4,3,2,1,0:T(8,128)(2,1)S(1)} %get-tuple-element.60), channel_id=1, source_target_pairs={{0,8},{8,0},{1,9},{9,1},{2,10},{10,2},{3,11},{11,3},{4,12},{12,4},... | collective-permute-start | bytes 196616 | tf_op jit(solution)/shard_map/ppermute | solution.py:267
  15.8 0.1 copy.11.strides
  15.9 0.1 pad_add_fusion.where.refs_0_
  15.9 0.0 collective-permute-done.1.next_chip
  15.9 0.7 collective-permute-done.in_chip
  16.7 1.3 %copy-done.1 = bf16[3,3,256,256]{3,2,1,0:T(8,128)(2,1)S(1)} copy-done((bf16[3,3,256,256]{3,2,1,0:T(8,128)(2,1)S(1)}, bf16[3,3,256,256]{3,2,1,0:T(8,128)(2,1)}, u32[]{:S(2)}) %copy-start.1) | copy-done | bytes 1179672
  18.0 2.0 %early.1 = (bf16[12,256,256]{2,1,0:T(8,128)(2,1)S(1)}, bf16[12,256,256]{2,1,0:T(8,128)(2,1)S(1)}, f32[512,256]{1,0:T(8,128)S(1)}, f32[512,256]{1,0:T(8,128)S(1)}) custom-call(s32[3]{0:T(128)S(1)} %pad_add_fusion.where.refs_0_, s32[2,16,3]{2,1,0:T(8,128)S(1)} %copy.11.strides, bf16[2,2,128,256]{3,2,1,0:T(8,128)(2,1)S(1)} %copy-done.3, ...), custom_call_target="tpu_custom_call" | custom-call | tf_op jit(solution)/shard_map/early/pallas_call | solution.py:308
  20.0 0.0 collective-permute-done.3.next_pair
  20.0 2.7 %collective-permute-done.2.pair = bf16[2,2,128,256]{3,2,1,0:T(8,128)(2,1)S(1)} collective-permute-done((bf16[2,2,128,256]{3,2,1,0:T(8,128)(2,1)S(1)}, bf16[2,2,128,256]{3,2,1,0:T(8,128)(2,1)S(1)}, u32[]{:S(2)}, u32[]{:S(2)}) %collective-permute-start.2) | collective-permute-done | bytes 262176 | tf_op jit(solution)/shard_map/ppermute | solution.py:251
  22.8 1.8 %collective-permute-start.4 = (bf16[2,2,2,16,256]{4,3,2,1,0:T(8,128)(2,1)S(1)}, bf16[2,2,2,16,256]{4,3,2,1,0:T(8,128)(2,1)S(1)}, u32[]{:S(2)}, u32[]{:S(2)}) collective-permute-start(bf16[2,2,2,16,256]{4,3,2,1,0:T(8,128)(2,1)S(1)} %pad_maximum_fusion), channel_id=1, source_target_pairs={{0,8},{8,0},{1,9},{9,1},{2,10},{10,2},{3,11},{11,3},{4,12},{12,4},... | collective-permute-start | bytes 196616 | tf_op jit(solution)/shard_map/ppermute | solution.py:267
  24.6 0.9 collective-permute-start.5
  25.5 0.0 collective-permute-done.4.in_chip
  25.5 2.8 %collective-permute-done.5.next_chip = bf16[2,2,2,16,256]{4,3,2,1,0:T(8,128)(2,1)S(1)} collective-permute-done((bf16[2,2,2,16,256]{4,3,2,1,0:T(8,128)(2,1)S(1)}, bf16[2,2,2,16,256]{4,3,2,1,0:T(8,128)(2,1)S(1)}, u32[]{:S(2)}, u32[]{:S(2)}) %collective-permute-start.5) | collective-permute-done | bytes 65568 | tf_op jit(solution)/shard_map/ppermute | solution.py:266
  28.4 4.1 %main.1 = (f32[2304,256]{1,0:T(8,128)S(1)}, bf16[2304,256]{1,0:T(8,128)(2,1)S(1)}, bf16[2,2,128,256]{3,2,1,0:T(8,128)(2,1)S(1)}) custom-call(s32[3]{0:T(128)S(1)} %pad_add_fusion.where.refs_0_, s32[2,16,3]{2,1,0:T(8,128)S(1)} %copy.11.strides, bf16[12,256,256]{2,1,0:T(8,128)(2,1)S(1)} %get-tuple-element.33.own_f, ...), custom_call_target="tpu_custom_call" | custom-call | tf_op jit(solution)/shard_map/main/pallas_call | solution.py:321
  32.5 4.2 %collective-permute-start.6 = (bf16[2304,256]{1,0:T(8,128)(2,1)S(1)}, bf16[2304,256]{1,0:T(8,128)(2,1)S(1)}, u32[]{:S(2)}, u32[]{:S(2)}) collective-permute-start(bf16[2304,256]{1,0:T(8,128)(2,1)S(1)} %get-tuple-element.40), channel_id=1, source_target_pairs={{0,8},{8,0},{1,9},{9,1},{2,10},{10,2},{3,11},{11,3},{4,12},{12,4},... | collective-permute-start | bytes 3538952 | tf_op jit(solution)/shard_map/ppermute | solution.py:342
  36.7 4.4 %collective-permute-start.7 = (bf16[1,2,128,256]{3,2,1,0:T(8,128)(2,1)S(1)}, bf16[1,2,128,256]{3,2,1,0:T(8,128)(2,1)S(1)}, u32[]{:S(2)}, u32[]{:S(2)}) collective-permute-start(bf16[1,2,128,256]{3,2,1,0:T(8,128)(2,1)S(1)} %get-tuple-element.66), channel_id=1, source_target_pairs={{0,1},{2,3},{4,5},{6,7},{8,9},{10,11},{12,13},{14,15},{16,17},{18,... | collective-permute-start | bytes 393224 | tf_op jit(solution)/shard_map/ppermute | solution.py:251
  41.1 0.0 collective-permute-done.6
  41.1 1.5 %add_convert_fusion = bf16[2304,256]{1,0:T(8,128)(2,1)} fusion(f32[2304,256]{1,0:T(8,128)S(1)} %get-tuple-element.39, bf16[2304,256]{1,0:T(8,128)(2,1)S(1)} %collective-permute-done.6), kind=kLoop, calls=%fused_computation.1 | loop fusion | flops 1769472 | bytes 4718592 | tf_op jit(solution)/shard_map/convert_element_type | solution.py:344
  42.6 2.4 %collective-permute-done.7.pair = bf16[1,2,128,256]{3,2,1,0:T(8,128)(2,1)S(1)} collective-permute-done((bf16[1,2,128,256]{3,2,1,0:T(8,128)(2,1)S(1)}, bf16[1,2,128,256]{3,2,1,0:T(8,128)(2,1)S(1)}, u32[]{:S(2)}, u32[]{:S(2)}) %collective-permute-start.7) | collective-permute-done | bytes 131104 | tf_op jit(solution)/shard_map/ppermute | solution.py:251
  45.0 4.1 %all-to-all-start = ((bf16[16,144,256]{2,1,0:T(8,128)(2,1)}), bf16[16,144,256]{2,1,0:T(8,128)(2,1)S(1)}, u32[]{:S(2)}, u32[]{:S(2)}) async-start(bf16[16,144,256]{2,1,0:T(8,128)(2,1)} %bitcast.41), calls=%async_computation | async-start | bytes 2359296 | tf_op jit(solution)/shard_map/all_to_all | solution.py:348
  49.1 3.3 %collective-permute-start.8 = (bf16[1,2,128,256]{3,2,1,0:T(8,128)(2,1)S(1)}, bf16[1,2,128,256]{3,2,1,0:T(8,128)(2,1)S(1)}, u32[]{:S(2)}, u32[]{:S(2)}) collective-permute-start(bf16[1,2,128,256]{3,2,1,0:T(8,128)(2,1)S(1)} %get-tuple-element.65), channel_id=1, source_target_pairs={{1,2},{3,4},{5,6},{9,10},{11,12},{13,14},{17,18},{19,20},{21,22},{... | collective-permute-start | bytes 393224 | tf_op jit(solution)/shard_map/ppermute | solution.py:254
  52.4 16.7 %collective-permute-done.8.next_pair = bf16[1,2,128,256]{3,2,1,0:T(8,128)(2,1)S(1)} collective-permute-done((bf16[1,2,128,256]{3,2,1,0:T(8,128)(2,1)S(1)}, bf16[1,2,128,256]{3,2,1,0:T(8,128)(2,1)S(1)}, u32[]{:S(2)}, u32[]{:S(2)}) %collective-permute-start.8) | collective-permute-done | bytes 131104 | tf_op jit(solution)/shard_map/ppermute | solution.py:254
  69.1 0.0 all-to-all-done
  69.1 0.2 convert_reduce_fusion
  69.2 0.1 collective-permute-start.9
  69.3 4.0 %collective-permute-done.9 = f32[144,256]{1,0:T(8,128)S(1)} collective-permute-done((f32[144,256]{1,0:T(8,128)S(1)}, f32[144,256]{1,0:T(8,128)S(1)}, u32[]{:S(2)}, u32[]{:S(2)}) %collective-permute-start.9) | collective-permute-done | bytes 147488 | tf_op jit(solution)/shard_map/ppermute | solution.py:354
  73.3 0.6 collective-permute-start.10
  73.9 5.7 %collective-permute-done.10 = f32[144,256]{1,0:T(8,128)S(1)} collective-permute-done((f32[144,256]{1,0:T(8,128)S(1)}, f32[144,256]{1,0:T(8,128)S(1)}, u32[]{:S(2)}, u32[]{:S(2)}) %collective-permute-start.10) | collective-permute-done | bytes 147488 | tf_op jit(solution)/shard_map/ppermute | solution.py:354
  79.6 0.4 collective-permute-start.11
  80.0 5.6 %collective-permute-done.11.got = f32[144,256]{1,0:T(8,128)S(1)} collective-permute-done((f32[144,256]{1,0:T(8,128)S(1)}, f32[144,256]{1,0:T(8,128)S(1)}, u32[]{:S(2)}, u32[]{:S(2)}) %collective-permute-start.11) | collective-permute-done | bytes 147488 | tf_op jit(solution)/shard_map/ppermute | solution.py:354
  85.6 1.1 copies.1
  86.7 4.0 %all-to-all-start.1 = ((bf16[16,144,256]{2,1,0:T(8,128)(2,1)}), bf16[16,144,256]{2,1,0:T(8,128)(2,1)S(1)}, u32[]{:S(2)}, u32[]{:S(2)}) async-start(bf16[16,144,256]{2,1,0:T(8,128)(2,1)} %copies.1), calls=%async_computation.1 | async-start | bytes 2359296 | tf_op jit(solution)/shard_map/all_to_all | solution.py:379
  90.8 7.4 %collective-permute-start.12 = (bf16[1,2,4,16,256]{4,3,2,1,0:T(8,128)(2,1)S(1)}, bf16[1,2,4,16,256]{4,3,2,1,0:T(8,128)(2,1)S(1)}, u32[]{:S(2)}, u32[]{:S(2)}) collective-permute-start(bf16[1,2,4,16,256]{4,3,2,1,0:T(8,128)(2,1)S(1)} %pad_maximum_fusion.2), channel_id=1, source_target_pairs={{0,8},{8,0},{1,9},{9,1},{2,10},{10,2},{3,11},{11,3},{4,12},{12,4},... | collective-permute-start | bytes 196616 | tf_op jit(solution)/shard_map/ppermute | solution.py:267
  98.3 0.1 collective-permute-start.13
  98.4 0.8 collective-permute-done.12.in_chip
  99.1 3.1 %collective-permute-done.13.next_chip = bf16[1,2,4,16,256]{4,3,2,1,0:T(8,128)(2,1)S(1)} collective-permute-done((bf16[1,2,4,16,256]{4,3,2,1,0:T(8,128)(2,1)S(1)}, bf16[1,2,4,16,256]{4,3,2,1,0:T(8,128)(2,1)S(1)}, u32[]{:S(2)}, u32[]{:S(2)}) %collective-permute-start.13) | collective-permute-done | bytes 65568 | tf_op jit(solution)/shard_map/ppermute | solution.py:266
  102.3 2.4 %back.1 = bf16[2,2,128,256]{3,2,1,0:T(8,128)(2,1)} custom-call(s32[3]{0:T(128)S(1)} %pad_add_fusion.where.refs_0_, s32[2,16,3]{2,1,0:T(8,128)S(1)} %copy.11.strides, bf16[2,2,128,256]{3,2,1,0:T(8,128)(2,1)S(1)} %copy-done.2, bf16[2,2,128,256]{3,2,1,0:T(8,128)(2,1)S(1)} %get-tuple-element.41.pre, bf16[1,2,128,256]{3,2,1,0:T(8,128)(2,1)S(1)} %collective-permute-done.7.pair, ...), custom_call_target="tpu_custom_call" | custom-call | tf_op jit(solution)/shard_map/back/pallas_call | solution.py:361
  104.7 0.0 all-to-all-done.1
  104.7 7.0 %collective-permute-start.14 = (bf16[2304,256]{1,0:T(8,128)(2,1)S(1)}, bf16[2304,256]{1,0:T(8,128)(2,1)S(1)}, u32[]{:S(2)}, u32[]{:S(2)}) collective-permute-start(bf16[2304,256]{1,0:T(8,128)(2,1)S(1)} %bitcast.34), channel_id=1, source_target_pairs={{0,8},{8,0},{1,9},{9,1},{2,10},{10,2},{3,11},{11,3},{4,12},{12,4},... | collective-permute-start | bytes 3538952 | tf_op jit(solution)/shard_map/ppermute | solution.py:381
  111.7 2.0 %own_part.1 = (f32[2304,256]{1,0:T(8,128)}, f32[2304,256]{1,0:T(8,128)}) custom-call(s32[3]{0:T(128)S(1)} %pad_add_fusion.where.refs_0_, bf16[2304,256]{1,0:T(8,128)(2,1)S(1)} %bitcast.35), custom_call_target="tpu_custom_call" | custom-call | tf_op jit(solution)/shard_map/own_part/pallas_call | solution.py:385
  113.7 0.4 collective-permute-done.14.refs_1_
  114.1 2.0 %other_part.1 = (f32[2304,256]{1,0:T(8,128)}, f32[2304,256]{1,0:T(8,128)}) custom-call(s32[3]{0:T(128)S(1)} %pad_add_fusion.where.refs_0_, bf16[2304,256]{1,0:T(8,128)(2,1)S(1)} %collective-permute-done.14.refs_1_, f32[2304,256]{1,0:T(8,128)} %get-tuple-element.51.refs_2_, ...), custom_call_target="tpu_custom_call", output_to_operand_aliasing={{0}: (2, {}), {1}: (3, {})} | custom-call | tf_op jit(solution)/shard_map/other_part/pallas_call | solution.py:394
  (21 shorter events, 0.2 us)
Async XLA Ops:
  0.6 8.1 %copy-start.2 = (bf16[2,2,128,256]{3,2,1,0:T(8,128)(2,1)S(1)}, bf16[2,2,128,256]{3,2,1,0:T(8,128)(2,1)}, u32[]{:S(2)}) copy-start(bf16[2,2,128,256]{3,2,1,0:T(8,128)(2,1)} %grad.3) | copy-start | bytes 786436
  0.6 8.0 %copy-start.3 = (bf16[2,2,128,256]{3,2,1,0:T(8,128)(2,1)S(1)}, bf16[2,2,128,256]{3,2,1,0:T(8,128)(2,1)}, u32[]{:S(2)}) copy-start(bf16[2,2,128,256]{3,2,1,0:T(8,128)(2,1)} %feat.1) | copy-start | bytes 786436
  0.7 15.1 %copy-start.4 = (s32[2,16,3]{1,0,2:T(2,128)S(1)}, s32[2,16,3]{1,0,2:T(2,128)}, u32[]{:S(2)}) copy-start(s32[2,16,3]{1,0,2:T(2,128)} %param.9) | copy-start | bytes 1156
  0.7 16.0 %copy-start = (bf16[3,3,256,256]{3,2,1,0:T(8,128)(2,1)S(1)}, bf16[3,3,256,256]{3,2,1,0:T(8,128)(2,1)}, u32[]{:S(2)}) copy-start(bf16[3,3,256,256]{3,2,1,0:T(8,128)(2,1)} %first_kernel.5) | copy-start | bytes 3538948
  2.0 18.0 %collective-permute-start.3 = (bf16[2,2,128,256]{3,2,1,0:T(8,128)(2,1)S(1)}, bf16[2,2,128,256]{3,2,1,0:T(8,128)(2,1)S(1)}, u32[]{:S(2)}, u32[]{:S(2)}) collective-permute-start(bf16[2,2,128,256]{3,2,1,0:T(8,128)(2,1)S(1)} %get-tuple-element.57), channel_id=1, source_target_pairs={{1,2},{3,4},{5,6},{9,10},{11,12},{13,14},{17,18},{19,20},{21,22},{... | collective-permute-start | bytes 786440 | tf_op jit(solution)/shard_map/ppermute | solution.py:254
  6.0 16.7 %collective-permute-start.2 = (bf16[2,2,128,256]{3,2,1,0:T(8,128)(2,1)S(1)}, bf16[2,2,128,256]{3,2,1,0:T(8,128)(2,1)S(1)}, u32[]{:S(2)}, u32[]{:S(2)}) collective-permute-start(bf16[2,2,128,256]{3,2,1,0:T(8,128)(2,1)S(1)} %get-tuple-element.58), channel_id=1, source_target_pairs={{0,1},{2,3},{4,5},{6,7},{8,9},{10,11},{12,13},{14,15},{16,17},{18,... | collective-permute-start | bytes 786440 | tf_op jit(solution)/shard_map/ppermute | solution.py:251
  8.7 7.2 %collective-permute-start.1 = (bf16[2,2,2,16,256]{4,3,2,1,0:T(8,128)(2,1)S(1)}, bf16[2,2,2,16,256]{4,3,2,1,0:T(8,128)(2,1)S(1)}, u32[]{:S(2)}, u32[]{:S(2)}) collective-permute-start(bf16[2,2,2,16,256]{4,3,2,1,0:T(8,128)(2,1)S(1)} %get-tuple-element.59), channel_id=1, source_target_pairs={{8,16},{9,17},{10,18},{11,19},{12,20},{13,21},{14,22},{15,23},{24,... | collective-permute-start | bytes 196616 | tf_op jit(solution)/shard_map/ppermute | solution.py:266
  11.5 5.1 %collective-permute-start = (bf16[2,2,2,16,256]{4,3,2,1,0:T(8,128)(2,1)S(1)}, bf16[2,2,2,16,256]{4,3,2,1,0:T(8,128)(2,1)S(1)}, u32[]{:S(2)}, u32[]{:S(2)}) collective-permute-start(bf16[2,2,2,16,256]{4,3,2,1,0:T(8,128)(2,1)S(1)} %get-tuple-element.60), channel_id=1, source_target_pairs={{0,8},{8,0},{1,9},{9,1},{2,10},{10,2},{3,11},{11,3},{4,12},{12,4},... | collective-permute-start | bytes 196616 | tf_op jit(solution)/shard_map/ppermute | solution.py:267
  16.7 1.3 %copy-start.1 = (bf16[3,3,256,256]{3,2,1,0:T(8,128)(2,1)S(1)}, bf16[3,3,256,256]{3,2,1,0:T(8,128)(2,1)}, u32[]{:S(2)}) copy-start(bf16[3,3,256,256]{3,2,1,0:T(8,128)(2,1)} %second_kernel.3) | copy-start | bytes 3538948
  22.8 2.8 %collective-permute-start.4 = (bf16[2,2,2,16,256]{4,3,2,1,0:T(8,128)(2,1)S(1)}, bf16[2,2,2,16,256]{4,3,2,1,0:T(8,128)(2,1)S(1)}, u32[]{:S(2)}, u32[]{:S(2)}) collective-permute-start(bf16[2,2,2,16,256]{4,3,2,1,0:T(8,128)(2,1)S(1)} %pad_maximum_fusion), channel_id=1, source_target_pairs={{0,8},{8,0},{1,9},{9,1},{2,10},{10,2},{3,11},{11,3},{4,12},{12,4},... | collective-permute-start | bytes 196616 | tf_op jit(solution)/shard_map/ppermute | solution.py:267
  24.6 3.8 %collective-permute-start.5 = (bf16[2,2,2,16,256]{4,3,2,1,0:T(8,128)(2,1)S(1)}, bf16[2,2,2,16,256]{4,3,2,1,0:T(8,128)(2,1)S(1)}, u32[]{:S(2)}, u32[]{:S(2)}) collective-permute-start(bf16[2,2,2,16,256]{4,3,2,1,0:T(8,128)(2,1)S(1)} %pad_maximum_fusion.1), channel_id=1, source_target_pairs={{8,16},{9,17},{10,18},{11,19},{12,20},{13,21},{14,22},{15,23},{24,... | collective-permute-start | bytes 196616 | tf_op jit(solution)/shard_map/ppermute | solution.py:266
  32.5 8.6 %collective-permute-start.6 = (bf16[2304,256]{1,0:T(8,128)(2,1)S(1)}, bf16[2304,256]{1,0:T(8,128)(2,1)S(1)}, u32[]{:S(2)}, u32[]{:S(2)}) collective-permute-start(bf16[2304,256]{1,0:T(8,128)(2,1)S(1)} %get-tuple-element.40), channel_id=1, source_target_pairs={{0,8},{8,0},{1,9},{9,1},{2,10},{10,2},{3,11},{11,3},{4,12},{12,4},... | collective-permute-start | bytes 3538952 | tf_op jit(solution)/shard_map/ppermute | solution.py:342
  36.7 8.2 %collective-permute-start.7 = (bf16[1,2,128,256]{3,2,1,0:T(8,128)(2,1)S(1)}, bf16[1,2,128,256]{3,2,1,0:T(8,128)(2,1)S(1)}, u32[]{:S(2)}, u32[]{:S(2)}) collective-permute-start(bf16[1,2,128,256]{3,2,1,0:T(8,128)(2,1)S(1)} %get-tuple-element.66), channel_id=1, source_target_pairs={{0,1},{2,3},{4,5},{6,7},{8,9},{10,11},{12,13},{14,15},{16,17},{18,... | collective-permute-start | bytes 393224 | tf_op jit(solution)/shard_map/ppermute | solution.py:251
  45.0 24.1 %all-to-all-start = ((bf16[16,144,256]{2,1,0:T(8,128)(2,1)}), bf16[16,144,256]{2,1,0:T(8,128)(2,1)S(1)}, u32[]{:S(2)}, u32[]{:S(2)}) async-start(bf16[16,144,256]{2,1,0:T(8,128)(2,1)} %bitcast.41), calls=%async_computation | async-start | bytes 2359296 | tf_op jit(solution)/shard_map/all_to_all | solution.py:348
  49.1 20.0 %collective-permute-start.8 = (bf16[1,2,128,256]{3,2,1,0:T(8,128)(2,1)S(1)}, bf16[1,2,128,256]{3,2,1,0:T(8,128)(2,1)S(1)}, u32[]{:S(2)}, u32[]{:S(2)}) collective-permute-start(bf16[1,2,128,256]{3,2,1,0:T(8,128)(2,1)S(1)} %get-tuple-element.65), channel_id=1, source_target_pairs={{1,2},{3,4},{5,6},{9,10},{11,12},{13,14},{17,18},{19,20},{21,22},{... | collective-permute-start | bytes 393224 | tf_op jit(solution)/shard_map/ppermute | solution.py:254
  69.2 4.1 %collective-permute-start.9 = (f32[144,256]{1,0:T(8,128)S(1)}, f32[144,256]{1,0:T(8,128)S(1)}, u32[]{:S(2)}, u32[]{:S(2)}) collective-permute-start(f32[144,256]{1,0:T(8,128)S(1)} %convert_reduce_fusion), channel_id=1, source_target_pairs={{0,16},{8,24},{16,0},{24,8},{32,48},{40,56},{48,32},{56,40},{64,80... | collective-permute-start | bytes 442376 | tf_op jit(solution)/shard_map/ppermute | solution.py:354
  73.3 6.3 %collective-permute-start.10 = (f32[144,256]{1,0:T(8,128)S(1)}, f32[144,256]{1,0:T(8,128)S(1)}, u32[]{:S(2)}, u32[]{:S(2)}) collective-permute-start(f32[144,256]{1,0:T(8,128)S(1)} %add.49), channel_id=1, source_target_pairs={{0,32},{8,104},{16,48},{24,120},{32,0},{40,72},{48,16},{56,88},{64... | collective-permute-start | bytes 442376 | tf_op jit(solution)/shard_map/ppermute | solution.py:354
  79.6 6.0 %collective-permute-start.11 = (f32[144,256]{1,0:T(8,128)S(1)}, f32[144,256]{1,0:T(8,128)S(1)}, u32[]{:S(2)}, u32[]{:S(2)}) collective-permute-start(f32[144,256]{1,0:T(8,128)S(1)} %add.50.part), channel_id=1, source_target_pairs={{0,112},{8,56},{16,96},{24,40},{32,80},{40,24},{48,64},{56,8},{64,... | collective-permute-start | bytes 442376 | tf_op jit(solution)/shard_map/ppermute | solution.py:354
  86.7 18.0 %all-to-all-start.1 = ((bf16[16,144,256]{2,1,0:T(8,128)(2,1)}), bf16[16,144,256]{2,1,0:T(8,128)(2,1)S(1)}, u32[]{:S(2)}, u32[]{:S(2)}) async-start(bf16[16,144,256]{2,1,0:T(8,128)(2,1)} %copies.1), calls=%async_computation.1 | async-start | bytes 2359296 | tf_op jit(solution)/shard_map/all_to_all | solution.py:379
  90.8 8.3 %collective-permute-start.12 = (bf16[1,2,4,16,256]{4,3,2,1,0:T(8,128)(2,1)S(1)}, bf16[1,2,4,16,256]{4,3,2,1,0:T(8,128)(2,1)S(1)}, u32[]{:S(2)}, u32[]{:S(2)}) collective-permute-start(bf16[1,2,4,16,256]{4,3,2,1,0:T(8,128)(2,1)S(1)} %pad_maximum_fusion.2), channel_id=1, source_target_pairs={{0,8},{8,0},{1,9},{9,1},{2,10},{10,2},{3,11},{11,3},{4,12},{12,4},... | collective-permute-start | bytes 196616 | tf_op jit(solution)/shard_map/ppermute | solution.py:267
  98.3 4.0 %collective-permute-start.13 = (bf16[1,2,4,16,256]{4,3,2,1,0:T(8,128)(2,1)S(1)}, bf16[1,2,4,16,256]{4,3,2,1,0:T(8,128)(2,1)S(1)}, u32[]{:S(2)}, u32[]{:S(2)}) collective-permute-start(bf16[1,2,4,16,256]{4,3,2,1,0:T(8,128)(2,1)S(1)} %pad_maximum_fusion.3), channel_id=1, source_target_pairs={{8,16},{9,17},{10,18},{11,19},{12,20},{13,21},{14,22},{15,23},{24,... | collective-permute-start | bytes 196616 | tf_op jit(solution)/shard_map/ppermute | solution.py:266
  104.7 9.4 %collective-permute-start.14 = (bf16[2304,256]{1,0:T(8,128)(2,1)S(1)}, bf16[2304,256]{1,0:T(8,128)(2,1)S(1)}, u32[]{:S(2)}, u32[]{:S(2)}) collective-permute-start(bf16[2304,256]{1,0:T(8,128)(2,1)S(1)} %bitcast.34), channel_id=1, source_target_pairs={{0,8},{8,0},{1,9},{9,1},{2,10},{10,2},{3,11},{11,3},{4,12},{12,4},... | collective-permute-start | bytes 3538952 | tf_op jit(solution)/shard_map/ppermute | solution.py:381

commit v9 on v7

--- a/solution.py
+++ b/solution.py
@@ -135,7 +135,7 @@
 
 
 def main_kernel(where, strides, own_f, own_g, pre_part, back_part, pair, next_pair, in_chip, next_chip,
-                first_kernel, second_kernel, keep, send, pre_grad, ext_f, ext_g, edge_f, edge_g, act, sums):
+                first_kernel, second_kernel, keep, send, pre_grad, ext_f, ext_g, edge_f, edge_g, act):
     lat, core = where[0], where[1]
     odd, second_core = where[2] == 1, core == 1
     mirror = lat == 0
@@ -172,29 +172,32 @@
         for s in range(2):
             pre_grad[s, row] = result[s * width : (s + 1) * width]
 
-    def place(value, k, col, owner):
-        at = (k * 3 + col) * 256
-        sums[jnp.where(core == owner, 0, 1), at : at + 256] = value
-
     def taps_of(own, edge, row, k, col):
         return own[OWN.index((row, k)) * 3 + col] if (row, k) in OWN else edge[row * 3 + col]
 
-    turned = act[...].T
-    above, below = turned[:, :half], turned[:, half:]
-    for col in range(3):
-        edge, upper = (dot(a, taps_of(own_g, edge_g, r, 0, col), NN) for r, a in enumerate((above, below)))
-        centre, lower = (
-            sum(dot(a, taps_of(own_g, edge_g, r, slot, col), NN) for r, a in enumerate((above, below))) for slot in (1, 2)
-        )
-        place(centre, 1, col, 1)
-        place(lower + jnp.where(mirror, edge, 0.0), 0, col, 1)
-        place(upper + jnp.where(mirror, 0.0, edge), 2, col, 1)
     rows = [jnp.concatenate([pre_grad[s, row] for s in range(2)], axis=0) for row in range(2)]
-    for k in range(3):
+
+    def products(first, second):
+        def place(out, value, k, col):
+            at = (k * 3 + col) * 256
+            out[at : at + 256] = value.astype(out.dtype)
+
+        turned = act[...].T
+        above, below = turned[:, :half], turned[:, half:]
         for col in range(3):
-            place(sum(dot(taps_of(own_f, edge_f, r, k, col), rows[r], TN) for r in range(2)), k, col, 0)
-    keep[...] = sums[0]
-    send[...] = sums[1].astype(jnp.bfloat16)
+            edge, upper = (dot(a, taps_of(own_g, edge_g, r, 0, col), NN) for r, a in enumerate((above, below)))
+            centre, lower = (
+                sum(dot(a, taps_of(own_g, edge_g, r, slot, col), NN) for r, a in enumerate((above, below))) for slot in (1, 2)
+            )
+            place(second, centre, 1, col)
+            place(second, lower + jnp.where(mirror, edge, 0.0), 0, col)
+            place(second, upper + jnp.where(mirror, 0.0, edge), 2, col)
+        for k in range(3):
+            for col in range(3):
+                place(first, sum(dot(taps_of(own_f, edge_f, r, k, col), rows[r], TN) for r in range(2)), k, col)
+
+    pl.when(core == 0)(lambda: products(keep, send))
+    pl.when(core != 0)(lambda: products(send, keep))
 
 
 def back_kernel(where, strides, grad, pre, pair, next_pair, in_chip, next_chip, first_kernel, out, ext, taps):
@@ -333,7 +336,6 @@
             edge,
             edge,
             pltpu.VMEM((cells, chans), jnp.bfloat16),
-            pltpu.VMEM((2,) + grads, jnp.float32),
         ],
         compiler_params=params,
         name="main",

time: 114 us -> 113 us (level)
  no operation moved by 1% of the time
where the time goes in v9:
time: 113 us
  starting transfers between devices  43.5 us (38%)
  waiting for transfers between devices  29.3 us (26%)
  blocking collectives  23.1 us (20%)
  Pallas kernels  12.7 us (11%)
  other arithmetic  1.95 us (2%)
  local copies, waits for them, and re-layouts  1.45 us (1%)
    all_to_all x1, blocking collectives, local(): spread = lax.all_to_all(total, PLANE, 0, 0, tiled=True)  23.1 us
    ppermute x3, starting transfers between devices, column_halos(): in_chip = lax.ppermute(edge((1 - core) * reach), 'core', [(0, 1), (1, 0)])  11.3 us
    ppermute x1, starting transfers between devices, local(): other = lax.ppermute(mine, 'core', swap)  6.39 us
    ppermute x2, waiting for transfers between devices, row_halos(): lax.ppermute(row(1 - odd), ALL, both_ways([(at(i, k), at(i, k + 1)) for i...  6.29 us
    ppermute x3, waiting for transfers between devices, column_halos(): lax.ppermute(edge(core * reach), ALL, both_ways([(at(i + 1, k), at(i + 2,...  6.03 us
    ppermute x3, waiting for transfers between devices, local(): got = lax.ppermute(part, ('z', 'core'), folded(height, cores, reach))  6.02 us
    ppermute x2, starting transfers between devices, row_halos(): return (pair, lax.ppermute(row(odd), ALL, between + across))  5.94 us
    ppermute x2, waiting for transfers between devices, row_halos(): return (pair, lax.ppermute(row(odd), ALL, between + across))  5.49 us
  transfers between devices with their start and end apart: 16, of which 12 were waited for; matrix products, arithmetic and copies ran while one was open for 0% of the time, Pallas kernels for 6%

profile of v9, /device:TPU:1, one launch (start us, length us, event | category | flops | bytes accessed | tf_op | source)
XLA Modules:
  0.0 113.0 jit_solution(7217180235538510185)
XLA Ops:
  0.6 0.0 copy-start.2
  0.6 0.0 copy-start.3
  0.7 0.0 copy-start.4
  0.7 1.3 %fusion.1 = (bf16[2,2,128,256]{3,2,1,0:T(8,128)(2,1)S(1)}, bf16[2,2,128,256]{3,2,1,0:T(8,128)(2,1)S(1)}) fusion(s32[]{:T(128)S(6)} %select_n.53, bf16[1,2,2,128,256]{4,3,2,1,0:T(8,128)(2,1)} %bitcast.41, bf16[1,2,2,128,256]{4,3,2,1,0:T(8,128)(2,1)} %bitcast.39, s32[]{:T(128)S(6)} %select_n.52), kind=kLoop, calls=%fused_computation.11 | loop fusion | flops 262144 | bytes 1048584 | tf_op jit(solution)/shard_map/jit(dynamic_index_in_dim)/squeeze | solution.py:253
  2.0 4.0 %collective-permute-start.3 = (bf16[2,2,128,256]{3,2,1,0:T(8,128)(2,1)S(1)}, bf16[2,2,128,256]{3,2,1,0:T(8,128)(2,1)S(1)}, u32[]{:S(2)}, u32[]{:S(2)}) collective-permute-start(bf16[2,2,128,256]{3,2,1,0:T(8,128)(2,1)S(1)} %get-tuple-element.55), channel_id=1, source_target_pairs={{1,2},{3,4},{5,6},{9,10},{11,12},{13,14},{17,18},{19,20},{21,22},{... | collective-permute-start | bytes 786440 | tf_op jit(solution)/shard_map/ppermute | solution.py:257
  6.0 2.7 %collective-permute-start.2 = (bf16[2,2,128,256]{3,2,1,0:T(8,128)(2,1)S(1)}, bf16[2,2,128,256]{3,2,1,0:T(8,128)(2,1)S(1)}, u32[]{:S(2)}, u32[]{:S(2)}) collective-permute-start(bf16[2,2,128,256]{3,2,1,0:T(8,128)(2,1)S(1)} %get-tuple-element.56), channel_id=1, source_target_pairs={{0,1},{2,3},{4,5},{6,7},{8,9},{10,11},{12,13},{14,15},{16,17},{18,... | collective-permute-start | bytes 786440 | tf_op jit(solution)/shard_map/ppermute | solution.py:254
  8.7 2.8 %collective-permute-start.1 = (bf16[2,2,2,16,256]{4,3,2,1,0:T(8,128)(2,1)S(1)}, bf16[2,2,2,16,256]{4,3,2,1,0:T(8,128)(2,1)S(1)}, u32[]{:S(2)}, u32[]{:S(2)}) collective-permute-start(bf16[2,2,2,16,256]{4,3,2,1,0:T(8,128)(2,1)S(1)} %get-tuple-element.57), channel_id=1, source_target_pairs={{8,16},{9,17},{10,18},{11,19},{12,20},{13,21},{14,22},{15,23},{24,... | collective-permute-start | bytes 196616 | tf_op jit(solution)/shard_map/ppermute | solution.py:269
  11.5 4.2 %collective-permute-start = (bf16[2,2,2,16,256]{4,3,2,1,0:T(8,128)(2,1)S(1)}, bf16[2,2,2,16,256]{4,3,2,1,0:T(8,128)(2,1)S(1)}, u32[]{:S(2)}, u32[]{:S(2)}) collective-permute-start(bf16[2,2,2,16,256]{4,3,2,1,0:T(8,128)(2,1)S(1)} %get-tuple-element.58), channel_id=1, source_target_pairs={{0,8},{8,0},{1,9},{9,1},{2,10},{10,2},{3,11},{11,3},{4,12},{12,4},... | collective-permute-start | bytes 196616 | tf_op jit(solution)/shard_map/ppermute | solution.py:270
  15.8 0.1 copy.11.strides
  15.9 0.1 pad_add_fusion.where.refs_0_
  15.9 0.0 collective-permute-done.1.next_chip
  15.9 0.7 collective-permute-done.in_chip
  16.7 1.3 %copy-done.1 = bf16[3,3,256,256]{3,2,1,0:T(8,128)(2,1)S(1)} copy-done((bf16[3,3,256,256]{3,2,1,0:T(8,128)(2,1)S(1)}, bf16[3,3,256,256]{3,2,1,0:T(8,128)(2,1)}, u32[]{:S(2)}) %copy-start.1) | copy-done | bytes 1179672
  18.0 2.0 %early.1 = (bf16[12,256,256]{2,1,0:T(8,128)(2,1)S(1)}, bf16[12,256,256]{2,1,0:T(8,128)(2,1)S(1)}, f32[512,256]{1,0:T(8,128)S(1)}, f32[512,256]{1,0:T(8,128)S(1)}) custom-call(s32[3]{0:T(128)S(1)} %pad_add_fusion.where.refs_0_, s32[2,16,3]{2,1,0:T(8,128)S(1)} %copy.11.strides, bf16[2,2,128,256]{3,2,1,0:T(8,128)(2,1)S(1)} %copy-done.3, ...), custom_call_target="tpu_custom_call" | custom-call | tf_op jit(solution)/shard_map/early/pallas_call | solution.py:311
  19.9 0.0 collective-permute-done.3.next_pair
  19.9 2.7 %collective-permute-done.2.pair = bf16[2,2,128,256]{3,2,1,0:T(8,128)(2,1)S(1)} collective-permute-done((bf16[2,2,128,256]{3,2,1,0:T(8,128)(2,1)S(1)}, bf16[2,2,128,256]{3,2,1,0:T(8,128)(2,1)S(1)}, u32[]{:S(2)}, u32[]{:S(2)}) %collective-permute-start.2) | collective-permute-done | bytes 262176 | tf_op jit(solution)/shard_map/ppermute | solution.py:254
  22.8 1.8 %collective-permute-start.4 = (bf16[2,2,2,16,256]{4,3,2,1,0:T(8,128)(2,1)S(1)}, bf16[2,2,2,16,256]{4,3,2,1,0:T(8,128)(2,1)S(1)}, u32[]{:S(2)}, u32[]{:S(2)}) collective-permute-start(bf16[2,2,2,16,256]{4,3,2,1,0:T(8,128)(2,1)S(1)} %pad_maximum_fusion), channel_id=1, source_target_pairs={{0,8},{8,0},{1,9},{9,1},{2,10},{10,2},{3,11},{11,3},{4,12},{12,4},... | collective-permute-start | bytes 196616 | tf_op jit(solution)/shard_map/ppermute | solution.py:270
  24.6 0.9 collective-permute-start.5
  25.5 0.0 collective-permute-done.4.in_chip
  25.5 2.8 %collective-permute-done.5.next_chip = bf16[2,2,2,16,256]{4,3,2,1,0:T(8,128)(2,1)S(1)} collective-permute-done((bf16[2,2,2,16,256]{4,3,2,1,0:T(8,128)(2,1)S(1)}, bf16[2,2,2,16,256]{4,3,2,1,0:T(8,128)(2,1)S(1)}, u32[]{:S(2)}, u32[]{:S(2)}) %collective-permute-start.5) | collective-permute-done | bytes 65568 | tf_op jit(solution)/shard_map/ppermute | solution.py:269
  28.4 3.3 %main.1 = (f32[2304,256]{1,0:T(8,128)S(1)}, bf16[2304,256]{1,0:T(8,128)(2,1)S(1)}, bf16[2,2,128,256]{3,2,1,0:T(8,128)(2,1)S(1)}) custom-call(s32[3]{0:T(128)S(1)} %pad_add_fusion.where.refs_0_, s32[2,16,3]{2,1,0:T(8,128)S(1)} %copy.11.strides, bf16[12,256,256]{2,1,0:T(8,128)(2,1)S(1)} %get-tuple-element.32.own_f, ...), custom_call_target="tpu_custom_call" | custom-call | tf_op jit(solution)/shard_map/main/pallas_call | solution.py:324
  31.7 4.2 %collective-permute-start.6 = (bf16[2304,256]{1,0:T(8,128)(2,1)S(1)}, bf16[2304,256]{1,0:T(8,128)(2,1)S(1)}, u32[]{:S(2)}, u32[]{:S(2)}) collective-permute-start(bf16[2304,256]{1,0:T(8,128)(2,1)S(1)} %get-tuple-element.39), channel_id=1, source_target_pairs={{0,8},{8,0},{1,9},{9,1},{2,10},{10,2},{3,11},{11,3},{4,12},{12,4},... | collective-permute-start | bytes 3538952 | tf_op jit(solution)/shard_map/ppermute | solution.py:344
  35.9 2.5 %collective-permute-done.6 = bf16[2304,256]{1,0:T(8,128)(2,1)S(1)} collective-permute-done((bf16[2304,256]{1,0:T(8,128)(2,1)S(1)}, bf16[2304,256]{1,0:T(8,128)(2,1)S(1)}, u32[]{:S(2)}, u32[]{:S(2)}) %collective-permute-start.6) | collective-permute-done | bytes 1179680 | tf_op jit(solution)/shard_map/ppermute | solution.py:344
  38.3 0.3 add_convert_fusion
  38.7 23.1 %all_to_all.10 = bf16[16,144,256]{2,1,0:T(8,128)(2,1)S(1)} all-to-all(bf16[16,144,256]{2,1,0:T(8,128)(2,1)S(1)} %bitcast.43), channel_id=1, replica_groups=mesh['yl'=2,'z'=8,'core'=2,'x'=4,'yh'=2] {'x','yh','yl'}, dimensions={0} | all-to-all | bytes 2359296 | tf_op jit(solution)/shard_map/all_to_all | solution.py:347
  61.7 0.2 convert_reduce_fusion
  61.9 0.1 collective-permute-start.7
  62.0 4.0 %collective-permute-done.7 = f32[144,256]{1,0:T(8,128)S(1)} collective-permute-done((f32[144,256]{1,0:T(8,128)S(1)}, f32[144,256]{1,0:T(8,128)S(1)}, u32[]{:S(2)}, u32[]{:S(2)}) %collective-permute-start.7) | collective-permute-done | bytes 147488 | tf_op jit(solution)/shard_map/ppermute | solution.py:355
  66.0 3.4 %collective-permute-start.8 = (f32[144,256]{1,0:T(8,128)S(1)}, f32[144,256]{1,0:T(8,128)S(1)}, u32[]{:S(2)}, u32[]{:S(2)}) collective-permute-start(f32[144,256]{1,0:T(8,128)S(1)} %add.49), channel_id=1, source_target_pairs={{0,32},{8,104},{16,48},{24,120},{32,0},{40,72},{48,16},{56,88},{64... | collective-permute-start | bytes 442376 | tf_op jit(solution)/shard_map/ppermute | solution.py:355
  69.4 1.4 %collective-permute-start.9 = (bf16[1,2,128,256]{3,2,1,0:T(8,128)(2,1)S(1)}, bf16[1,2,128,256]{3,2,1,0:T(8,128)(2,1)S(1)}, u32[]{:S(2)}, u32[]{:S(2)}) collective-permute-start(bf16[1,2,128,256]{3,2,1,0:T(8,128)(2,1)S(1)} %get-tuple-element.64), channel_id=1, source_target_pairs={{0,1},{2,3},{4,5},{6,7},{8,9},{10,11},{12,13},{14,15},{16,17},{18,... | collective-permute-start | bytes 393224 | tf_op jit(solution)/shard_map/ppermute | solution.py:254
  70.9 2.0 %collective-permute-done.8 = f32[144,256]{1,0:T(8,128)S(1)} collective-permute-done((f32[144,256]{1,0:T(8,128)S(1)}, f32[144,256]{1,0:T(8,128)S(1)}, u32[]{:S(2)}, u32[]{:S(2)}) %collective-permute-start.8) | collective-permute-done | bytes 147488 | tf_op jit(solution)/shard_map/ppermute | solution.py:355
  72.9 3.5 %collective-permute-done.9.pair = bf16[1,2,128,256]{3,2,1,0:T(8,128)(2,1)S(1)} collective-permute-done((bf16[1,2,128,256]{3,2,1,0:T(8,128)(2,1)S(1)}, bf16[1,2,128,256]{3,2,1,0:T(8,128)(2,1)S(1)}, u32[]{:S(2)}, u32[]{:S(2)}) %collective-permute-start.9) | collective-permute-done | bytes 131104 | tf_op jit(solution)/shard_map/ppermute | solution.py:254
  76.5 0.0 collective-permute-start.10
  76.5 1.9 %collective-permute-start.11 = (bf16[1,2,128,256]{3,2,1,0:T(8,128)(2,1)S(1)}, bf16[1,2,128,256]{3,2,1,0:T(8,128)(2,1)S(1)}, u32[]{:S(2)}, u32[]{:S(2)}) collective-permute-start(bf16[1,2,128,256]{3,2,1,0:T(8,128)(2,1)S(1)} %get-tuple-element.63), channel_id=1, source_target_pairs={{1,2},{3,4},{5,6},{9,10},{11,12},{13,14},{17,18},{19,20},{21,22},{... | collective-permute-start | bytes 393224 | tf_op jit(solution)/shard_map/ppermute | solution.py:257
  78.4 5.5 %collective-permute-done.11.next_pair = bf16[1,2,128,256]{3,2,1,0:T(8,128)(2,1)S(1)} collective-permute-done((bf16[1,2,128,256]{3,2,1,0:T(8,128)(2,1)S(1)}, bf16[1,2,128,256]{3,2,1,0:T(8,128)(2,1)S(1)}, u32[]{:S(2)}, u32[]{:S(2)}) %collective-permute-start.11) | collective-permute-done | bytes 131104 | tf_op jit(solution)/shard_map/ppermute | solution.py:257
  83.9 0.0 collective-permute-done.10.got
  83.9 1.1 copies.1
  85.0 3.8 %all-to-all-start.1 = ((bf16[16,144,256]{2,1,0:T(8,128)(2,1)}), bf16[16,144,256]{2,1,0:T(8,128)(2,1)S(1)}, u32[]{:S(2)}, u32[]{:S(2)}) async-start(bf16[16,144,256]{2,1,0:T(8,128)(2,1)} %copies.1), calls=%async_computation.1 | async-start | bytes 2359296 | tf_op jit(solution)/shard_map/all_to_all | solution.py:382
  88.9 5.3 %collective-permute-start.12 = (bf16[1,2,4,16,256]{4,3,2,1,0:T(8,128)(2,1)S(1)}, bf16[1,2,4,16,256]{4,3,2,1,0:T(8,128)(2,1)S(1)}, u32[]{:S(2)}, u32[]{:S(2)}) collective-permute-start(bf16[1,2,4,16,256]{4,3,2,1,0:T(8,128)(2,1)S(1)} %pad_maximum_fusion.2), channel_id=1, source_target_pairs={{0,8},{8,0},{1,9},{9,1},{2,10},{10,2},{3,11},{11,3},{4,12},{12,4},... | collective-permute-start | bytes 196616 | tf_op jit(solution)/shard_map/ppermute | solution.py:270
  94.2 0.4 collective-permute-start.13
  94.6 0.5 collective-permute-done.12.in_chip
  95.1 3.2 %collective-permute-done.13.next_chip = bf16[1,2,4,16,256]{4,3,2,1,0:T(8,128)(2,1)S(1)} collective-permute-done((bf16[1,2,4,16,256]{4,3,2,1,0:T(8,128)(2,1)S(1)}, bf16[1,2,4,16,256]{4,3,2,1,0:T(8,128)(2,1)S(1)}, u32[]{:S(2)}, u32[]{:S(2)}) %collective-permute-start.13) | collective-permute-done | bytes 65568 | tf_op jit(solution)/shard_map/ppermute | solution.py:269
  98.3 2.4 %back.1 = bf16[2,2,128,256]{3,2,1,0:T(8,128)(2,1)} custom-call(s32[3]{0:T(128)S(1)} %pad_add_fusion.where.refs_0_, s32[2,16,3]{2,1,0:T(8,128)S(1)} %copy.11.strides, bf16[2,2,128,256]{3,2,1,0:T(8,128)(2,1)S(1)} %copy-done.2, bf16[2,2,128,256]{3,2,1,0:T(8,128)(2,1)S(1)} %get-tuple-element.42.pre, bf16[1,2,128,256]{3,2,1,0:T(8,128)(2,1)S(1)} %collective-permute-done.9.pair, ...), custom_call_target="tpu_custom_call" | custom-call | tf_op jit(solution)/shard_map/back/pallas_call | solution.py:364
  100.7 1.3 %all-to-all-done.1 = bf16[16,144,256]{2,1,0:T(8,128)(2,1)S(1)} async-done(((bf16[16,144,256]{2,1,0:T(8,128)(2,1)}), bf16[16,144,256]{2,1,0:T(8,128)(2,1)S(1)}, u32[]{:S(2)}, u32[]{:S(2)}) %all-to-all-start.1) | async-done | bytes 1179680 | tf_op jit(solution)/shard_map/all_to_all | solution.py:382
  102.0 6.4 %collective-permute-start.14 = (bf16[2304,256]{1,0:T(8,128)(2,1)S(1)}, bf16[2304,256]{1,0:T(8,128)(2,1)S(1)}, u32[]{:S(2)}, u32[]{:S(2)}) collective-permute-start(bf16[2304,256]{1,0:T(8,128)(2,1)S(1)} %bitcast.37), channel_id=1, source_target_pairs={{0,8},{8,0},{1,9},{9,1},{2,10},{10,2},{3,11},{11,3},{4,12},{12,4},... | collective-permute-start | bytes 3538952 | tf_op jit(solution)/shard_map/ppermute | solution.py:384
  108.4 2.0 %own_part.1 = (f32[2304,256]{1,0:T(8,128)}, f32[2304,256]{1,0:T(8,128)}) custom-call(s32[3]{0:T(128)S(1)} %pad_add_fusion.where.refs_0_, bf16[2304,256]{1,0:T(8,128)(2,1)S(1)} %bitcast.38), custom_call_target="tpu_custom_call" | custom-call | tf_op jit(solution)/shard_map/own_part/pallas_call | solution.py:388
  110.4 0.4 collective-permute-done.14.refs_1_
  110.8 2.0 %other_part.1 = (f32[2304,256]{1,0:T(8,128)}, f32[2304,256]{1,0:T(8,128)}) custom-call(s32[3]{0:T(128)S(1)} %pad_add_fusion.where.refs_0_, bf16[2304,256]{1,0:T(8,128)(2,1)S(1)} %collective-permute-done.14.refs_1_, f32[2304,256]{1,0:T(8,128)} %get-tuple-element.49.refs_2_, ...), custom_call_target="tpu_custom_call", output_to_operand_aliasing={{0}: (2, {}), {1}: (3, {})} | custom-call | tf_op jit(solution)/shard_map/other_part/pallas_call | solution.py:397
  (20 shorter events, 0.2 us)
Async XLA Ops:
  0.6 8.1 %copy-start.2 = (bf16[2,2,128,256]{3,2,1,0:T(8,128)(2,1)S(1)}, bf16[2,2,128,256]{3,2,1,0:T(8,128)(2,1)}, u32[]{:S(2)}) copy-start(bf16[2,2,128,256]{3,2,1,0:T(8,128)(2,1)} %grad.3) | copy-start | bytes 786436
  0.6 8.0 %copy-start.3 = (bf16[2,2,128,256]{3,2,1,0:T(8,128)(2,1)S(1)}, bf16[2,2,128,256]{3,2,1,0:T(8,128)(2,1)}, u32[]{:S(2)}) copy-start(bf16[2,2,128,256]{3,2,1,0:T(8,128)(2,1)} %feat.1) | copy-start | bytes 786436
  0.7 15.1 %copy-start.4 = (s32[2,16,3]{1,0,2:T(2,128)S(1)}, s32[2,16,3]{1,0,2:T(2,128)}, u32[]{:S(2)}) copy-start(s32[2,16,3]{1,0,2:T(2,128)} %param.9) | copy-start | bytes 1156
  0.7 16.0 %copy-start = (bf16[3,3,256,256]{3,2,1,0:T(8,128)(2,1)S(1)}, bf16[3,3,256,256]{3,2,1,0:T(8,128)(2,1)}, u32[]{:S(2)}) copy-start(bf16[3,3,256,256]{3,2,1,0:T(8,128)(2,1)} %first_kernel.5) | copy-start | bytes 3538948
  2.0 18.0 %collective-permute-start.3 = (bf16[2,2,128,256]{3,2,1,0:T(8,128)(2,1)S(1)}, bf16[2,2,128,256]{3,2,1,0:T(8,128)(2,1)S(1)}, u32[]{:S(2)}, u32[]{:S(2)}) collective-permute-start(bf16[2,2,128,256]{3,2,1,0:T(8,128)(2,1)S(1)} %get-tuple-element.55), channel_id=1, source_target_pairs={{1,2},{3,4},{5,6},{9,10},{11,12},{13,14},{17,18},{19,20},{21,22},{... | collective-permute-start | bytes 786440 | tf_op jit(solution)/shard_map/ppermute | solution.py:257
  6.0 16.7 %collective-permute-start.2 = (bf16[2,2,128,256]{3,2,1,0:T(8,128)(2,1)S(1)}, bf16[2,2,128,256]{3,2,1,0:T(8,128)(2,1)S(1)}, u32[]{:S(2)}, u32[]{:S(2)}) collective-permute-start(bf16[2,2,128,256]{3,2,1,0:T(8,128)(2,1)S(1)} %get-tuple-element.56), channel_id=1, source_target_pairs={{0,1},{2,3},{4,5},{6,7},{8,9},{10,11},{12,13},{14,15},{16,17},{18,... | collective-permute-start | bytes 786440 | tf_op jit(solution)/shard_map/ppermute | solution.py:254
  8.7 7.2 %collective-permute-start.1 = (bf16[2,2,2,16,256]{4,3,2,1,0:T(8,128)(2,1)S(1)}, bf16[2,2,2,16,256]{4,3,2,1,0:T(8,128)(2,1)S(1)}, u32[]{:S(2)}, u32[]{:S(2)}) collective-permute-start(bf16[2,2,2,16,256]{4,3,2,1,0:T(8,128)(2,1)S(1)} %get-tuple-element.57), channel_id=1, source_target_pairs={{8,16},{9,17},{10,18},{11,19},{12,20},{13,21},{14,22},{15,23},{24,... | collective-permute-start | bytes 196616 | tf_op jit(solution)/shard_map/ppermute | solution.py:269
  11.5 5.1 %collective-permute-start = (bf16[2,2,2,16,256]{4,3,2,1,0:T(8,128)(2,1)S(1)}, bf16[2,2,2,16,256]{4,3,2,1,0:T(8,128)(2,1)S(1)}, u32[]{:S(2)}, u32[]{:S(2)}) collective-permute-start(bf16[2,2,2,16,256]{4,3,2,1,0:T(8,128)(2,1)S(1)} %get-tuple-element.58), channel_id=1, source_target_pairs={{0,8},{8,0},{1,9},{9,1},{2,10},{10,2},{3,11},{11,3},{4,12},{12,4},... | collective-permute-start | bytes 196616 | tf_op jit(solution)/shard_map/ppermute | solution.py:270
  16.7 1.3 %copy-start.1 = (bf16[3,3,256,256]{3,2,1,0:T(8,128)(2,1)S(1)}, bf16[3,3,256,256]{3,2,1,0:T(8,128)(2,1)}, u32[]{:S(2)}) copy-start(bf16[3,3,256,256]{3,2,1,0:T(8,128)(2,1)} %second_kernel.3) | copy-start | bytes 3538948
  22.8 2.8 %collective-permute-start.4 = (bf16[2,2,2,16,256]{4,3,2,1,0:T(8,128)(2,1)S(1)}, bf16[2,2,2,16,256]{4,3,2,1,0:T(8,128)(2,1)S(1)}, u32[]{:S(2)}, u32[]{:S(2)}) collective-permute-start(bf16[2,2,2,16,256]{4,3,2,1,0:T(8,128)(2,1)S(1)} %pad_maximum_fusion), channel_id=1, source_target_pairs={{0,8},{8,0},{1,9},{9,1},{2,10},{10,2},{3,11},{11,3},{4,12},{12,4},... | collective-permute-start | bytes 196616 | tf_op jit(solution)/shard_map/ppermute | solution.py:270
  24.6 3.8 %collective-permute-start.5 = (bf16[2,2,2,16,256]{4,3,2,1,0:T(8,128)(2,1)S(1)}, bf16[2,2,2,16,256]{4,3,2,1,0:T(8,128)(2,1)S(1)}, u32[]{:S(2)}, u32[]{:S(2)}) collective-permute-start(bf16[2,2,2,16,256]{4,3,2,1,0:T(8,128)(2,1)S(1)} %pad_maximum_fusion.1), channel_id=1, source_target_pairs={{8,16},{9,17},{10,18},{11,19},{12,20},{13,21},{14,22},{15,23},{24,... | collective-permute-start | bytes 196616 | tf_op jit(solution)/shard_map/ppermute | solution.py:269
  31.7 6.7 %collective-permute-start.6 = (bf16[2304,256]{1,0:T(8,128)(2,1)S(1)}, bf16[2304,256]{1,0:T(8,128)(2,1)S(1)}, u32[]{:S(2)}, u32[]{:S(2)}) collective-permute-start(bf16[2304,256]{1,0:T(8,128)(2,1)S(1)} %get-tuple-element.39), channel_id=1, source_target_pairs={{0,8},{8,0},{1,9},{9,1},{2,10},{10,2},{3,11},{11,3},{4,12},{12,4},... | collective-permute-start | bytes 3538952 | tf_op jit(solution)/shard_map/ppermute | solution.py:344
  61.9 4.1 %collective-permute-start.7 = (f32[144,256]{1,0:T(8,128)S(1)}, f32[144,256]{1,0:T(8,128)S(1)}, u32[]{:S(2)}, u32[]{:S(2)}) collective-permute-start(f32[144,256]{1,0:T(8,128)S(1)} %convert_reduce_fusion), channel_id=1, source_target_pairs={{0,16},{8,24},{16,0},{24,8},{32,48},{40,56},{48,32},{56,40},{64,80... | collective-permute-start | bytes 442376 | tf_op jit(solution)/shard_map/ppermute | solution.py:355
  66.0 6.9 %collective-permute-start.8 = (f32[144,256]{1,0:T(8,128)S(1)}, f32[144,256]{1,0:T(8,128)S(1)}, u32[]{:S(2)}, u32[]{:S(2)}) collective-permute-start(f32[144,256]{1,0:T(8,128)S(1)} %add.49), channel_id=1, source_target_pairs={{0,32},{8,104},{16,48},{24,120},{32,0},{40,72},{48,16},{56,88},{64... | collective-permute-start | bytes 442376 | tf_op jit(solution)/shard_map/ppermute | solution.py:355
  69.4 7.0 %collective-permute-start.9 = (bf16[1,2,128,256]{3,2,1,0:T(8,128)(2,1)S(1)}, bf16[1,2,128,256]{3,2,1,0:T(8,128)(2,1)S(1)}, u32[]{:S(2)}, u32[]{:S(2)}) collective-permute-start(bf16[1,2,128,256]{3,2,1,0:T(8,128)(2,1)S(1)} %get-tuple-element.64), channel_id=1, source_target_pairs={{0,1},{2,3},{4,5},{6,7},{8,9},{10,11},{12,13},{14,15},{16,17},{18,... | collective-permute-start | bytes 393224 | tf_op jit(solution)/shard_map/ppermute | solution.py:254
  76.5 7.4 %collective-permute-start.10 = (f32[144,256]{1,0:T(8,128)S(1)}, f32[144,256]{1,0:T(8,128)S(1)}, u32[]{:S(2)}, u32[]{:S(2)}) collective-permute-start(f32[144,256]{1,0:T(8,128)S(1)} %add.50.part), channel_id=1, source_target_pairs={{0,112},{8,56},{16,96},{24,40},{32,80},{40,24},{48,64},{56,8},{64,... | collective-permute-start | bytes 442376 | tf_op jit(solution)/shard_map/ppermute | solution.py:355
  76.5 7.4 %collective-permute-start.11 = (bf16[1,2,128,256]{3,2,1,0:T(8,128)(2,1)S(1)}, bf16[1,2,128,256]{3,2,1,0:T(8,128)(2,1)S(1)}, u32[]{:S(2)}, u32[]{:S(2)}) collective-permute-start(bf16[1,2,128,256]{3,2,1,0:T(8,128)(2,1)S(1)} %get-tuple-element.63), channel_id=1, source_target_pairs={{1,2},{3,4},{5,6},{9,10},{11,12},{13,14},{17,18},{19,20},{21,22},{... | collective-permute-start | bytes 393224 | tf_op jit(solution)/shard_map/ppermute | solution.py:257
  85.0 17.0 %all-to-all-start.1 = ((bf16[16,144,256]{2,1,0:T(8,128)(2,1)}), bf16[16,144,256]{2,1,0:T(8,128)(2,1)S(1)}, u32[]{:S(2)}, u32[]{:S(2)}) async-start(bf16[16,144,256]{2,1,0:T(8,128)(2,1)} %copies.1), calls=%async_computation.1 | async-start | bytes 2359296 | tf_op jit(solution)/shard_map/all_to_all | solution.py:382
  88.9 6.2 %collective-permute-start.12 = (bf16[1,2,4,16,256]{4,3,2,1,0:T(8,128)(2,1)S(1)}, bf16[1,2,4,16,256]{4,3,2,1,0:T(8,128)(2,1)S(1)}, u32[]{:S(2)}, u32[]{:S(2)}) collective-permute-start(bf16[1,2,4,16,256]{4,3,2,1,0:T(8,128)(2,1)S(1)} %pad_maximum_fusion.2), channel_id=1, source_target_pairs={{0,8},{8,0},{1,9},{9,1},{2,10},{10,2},{3,11},{11,3},{4,12},{12,4},... | collective-permute-start | bytes 196616 | tf_op jit(solution)/shard_map/ppermute | solution.py:270
  94.2 4.1 %collective-permute-start.13 = (bf16[1,2,4,16,256]{4,3,2,1,0:T(8,128)(2,1)S(1)}, bf16[1,2,4,16,256]{4,3,2,1,0:T(8,128)(2,1)S(1)}, u32[]{:S(2)}, u32[]{:S(2)}) collective-permute-start(bf16[1,2,4,16,256]{4,3,2,1,0:T(8,128)(2,1)S(1)} %pad_maximum_fusion.3), channel_id=1, source_target_pairs={{8,16},{9,17},{10,18},{11,19},{12,20},{13,21},{14,22},{15,23},{24,... | collective-permute-start | bytes 196616 | tf_op jit(solution)/shard_map/ppermute | solution.py:269
  102.0 8.9 %collective-permute-start.14 = (bf16[2304,256]{1,0:T(8,128)(2,1)S(1)}, bf16[2304,256]{1,0:T(8,128)(2,1)S(1)}, u32[]{:S(2)}, u32[]{:S(2)}) collective-permute-start(bf16[2304,256]{1,0:T(8,128)(2,1)S(1)} %bitcast.37), channel_id=1, source_target_pairs={{0,8},{8,0},{1,9},{9,1},{2,10},{10,2},{3,11},{11,3},{4,12},{12,4},... | collective-permute-start | bytes 3538952 | tf_op jit(solution)/shard_map/ppermute | solution.py:384

commit v10 on v9

--- a/solution.py
+++ b/solution.py
@@ -357,8 +357,8 @@
             part = part + got
         reach *= 2
         if reach == height:
-            part, pair = lax.optimization_barrier((part, pair))
-    got, next_pair = lax.optimization_barrier((got, next_pair))
+            part, next_pair = lax.optimization_barrier((part, next_pair))
+    got, pair = lax.optimization_barrier((got, pair))
     above, below = ordered(pair, next_pair)
     around = (pair, next_pair) + column_halos([above, pre_field, below], width, lon_count, lat_count)
     input_grad = pl.pallas_call(

time: 113 us -> 115 us (1.018)
  waiting for transfers between devices: 29.3 us -> 35.3 us
  starting transfers between devices: 43.5 us -> 39 us
    all_to_all x1, waiting for transfers between devices: 1.29 us -> 5.6 us  [local(): mine = lax.all_to_all(copies, PLANE, 0, 0, tiled=True).reshape(grads)]
    ppermute x1, starting transfers between devices: 6.39 us -> 4 us  [local(): other = lax.ppermute(mine, 'core', swap)]
    ppermute x3, starting transfers between devices: 11.3 us -> 9.42 us  [column_halos(): in_chip = lax.ppermute(edge((1 - core) * reach), 'core', [(0, 1), (1, 0)])]
    ppermute x2, waiting for transfers between devices: 5.49 us -> 6.66 us  [row_halos(): return (pair, lax.ppermute(row(odd), ALL, between + across))]
  transfers between devices with their start and end apart: 16 -> 16, of which waited for: 12 -> 13; matrix products, arithmetic and copies ran while one was open for 0% -> 0% of each run, Pallas kernels for 6% -> 6%
where the time goes in v10:
time: 115 us; the launch traced here: 114 us
  starting transfers between devices  39 us (34%)
  waiting for transfers between devices  35.3 us (31%)
  blocking collectives  23.1 us (20%)
  Pallas kernels  12.7 us (11%)
  other arithmetic  1.95 us (2%)
  local copies, waits for them, and re-layouts  1.45 us (1%)
    all_to_all x1, blocking collectives, local(): spread = lax.all_to_all(total, PLANE, 0, 0, tiled=True)  23.1 us
    ppermute x3, starting transfers between devices, column_halos(): in_chip = lax.ppermute(edge((1 - core) * reach), 'core', [(0, 1), (1, 0)])  9.42 us
    ppermute x2, waiting for transfers between devices, row_halos(): lax.ppermute(row(1 - odd), ALL, both_ways([(at(i, k), at(i, k + 1)) for i...  7.13 us
    ppermute x2, waiting for transfers between devices, row_halos(): return (pair, lax.ppermute(row(odd), ALL, between + across))  6.66 us
    ppermute x3, waiting for transfers between devices, local(): got = lax.ppermute(part, ('z', 'core'), folded(height, cores, reach))  6.11 us
    ppermute x3, waiting for transfers between devices, column_halos(): lax.ppermute(edge(core * reach), ALL, both_ways([(at(i + 1, k), at(i + 2,...  6.03 us
    ppermute x2, starting transfers between devices, row_halos(): return (pair, lax.ppermute(row(odd), ALL, between + across))  5.95 us
    all_to_all x1, waiting for transfers between devices, local(): mine = lax.all_to_all(copies, PLANE, 0, 0, tiled=True).reshape(grads)  5.6 us
  transfers between devices with their start and end apart: 16, of which 13 were waited for; matrix products, arithmetic and copies ran while one was open for 0% of the time, Pallas kernels for 6%

profile of v10, /device:TPU:1, one launch (start us, length us, event | category | flops | bytes accessed | tf_op | source)
XLA Modules:
  0.0 114.5 jit_solution(8892140228419365793)
XLA Ops:
  0.6 0.0 copy-start.2
  0.6 0.0 copy-start.3
  0.7 1.3 %fusion.1 = (bf16[2,2,128,256]{3,2,1,0:T(8,128)(2,1)S(1)}, bf16[2,2,128,256]{3,2,1,0:T(8,128)(2,1)S(1)}) fusion(s32[]{:T(128)S(6)} %select_n.53, bf16[1,2,2,128,256]{4,3,2,1,0:T(8,128)(2,1)} %bitcast.41, bf16[1,2,2,128,256]{4,3,2,1,0:T(8,128)(2,1)} %bitcast.39, s32[]{:T(128)S(6)} %select_n.52), kind=kLoop, calls=%fused_computation.11 | loop fusion | flops 262144 | bytes 1048584 | tf_op jit(solution)/shard_map/jit(dynamic_index_in_dim)/squeeze | solution.py:253
  2.0 4.0 %collective-permute-start.3 = (bf16[2,2,128,256]{3,2,1,0:T(8,128)(2,1)S(1)}, bf16[2,2,128,256]{3,2,1,0:T(8,128)(2,1)S(1)}, u32[]{:S(2)}, u32[]{:S(2)}) collective-permute-start(bf16[2,2,128,256]{3,2,1,0:T(8,128)(2,1)S(1)} %get-tuple-element.55), channel_id=1, source_target_pairs={{1,2},{3,4},{5,6},{9,10},{11,12},{13,14},{17,18},{19,20},{21,22},{... | collective-permute-start | bytes 786440 | tf_op jit(solution)/shard_map/ppermute | solution.py:257
  6.0 2.7 %collective-permute-start.2 = (bf16[2,2,128,256]{3,2,1,0:T(8,128)(2,1)S(1)}, bf16[2,2,128,256]{3,2,1,0:T(8,128)(2,1)S(1)}, u32[]{:S(2)}, u32[]{:S(2)}) collective-permute-start(bf16[2,2,128,256]{3,2,1,0:T(8,128)(2,1)S(1)} %get-tuple-element.56), channel_id=1, source_target_pairs={{0,1},{2,3},{4,5},{6,7},{8,9},{10,11},{12,13},{14,15},{16,17},{18,... | collective-permute-start | bytes 786440 | tf_op jit(solution)/shard_map/ppermute | solution.py:254
  8.7 0.0 copy-done.2
  8.7 2.8 %collective-permute-start.1 = (bf16[2,2,2,16,256]{4,3,2,1,0:T(8,128)(2,1)S(1)}, bf16[2,2,2,16,256]{4,3,2,1,0:T(8,128)(2,1)S(1)}, u32[]{:S(2)}, u32[]{:S(2)}) collective-permute-start(bf16[2,2,2,16,256]{4,3,2,1,0:T(8,128)(2,1)S(1)} %get-tuple-element.57), channel_id=1, source_target_pairs={{8,16},{9,17},{10,18},{11,19},{12,20},{13,21},{14,22},{15,23},{24,... | collective-permute-start | bytes 196616 | tf_op jit(solution)/shard_map/ppermute | solution.py:269
  11.5 4.2 %collective-permute-start = (bf16[2,2,2,16,256]{4,3,2,1,0:T(8,128)(2,1)S(1)}, bf16[2,2,2,16,256]{4,3,2,1,0:T(8,128)(2,1)S(1)}, u32[]{:S(2)}, u32[]{:S(2)}) collective-permute-start(bf16[2,2,2,16,256]{4,3,2,1,0:T(8,128)(2,1)S(1)} %get-tuple-element.58), channel_id=1, source_target_pairs={{0,8},{8,0},{1,9},{9,1},{2,10},{10,2},{3,11},{11,3},{4,12},{12,4},... | collective-permute-start | bytes 196616 | tf_op jit(solution)/shard_map/ppermute | solution.py:270
  15.8 0.1 copy.11.strides
  15.9 0.1 pad_add_fusion.where.refs_0_
  15.9 0.0 collective-permute-done.1.next_chip
  15.9 0.7 collective-permute-done.in_chip
  16.7 1.3 %copy-done.1 = bf16[3,3,256,256]{3,2,1,0:T(8,128)(2,1)S(1)} copy-done((bf16[3,3,256,256]{3,2,1,0:T(8,128)(2,1)S(1)}, bf16[3,3,256,256]{3,2,1,0:T(8,128)(2,1)}, u32[]{:S(2)}) %copy-start.1) | copy-done | bytes 1179672
  18.0 2.0 %early.1 = (bf16[12,256,256]{2,1,0:T(8,128)(2,1)S(1)}, bf16[12,256,256]{2,1,0:T(8,128)(2,1)S(1)}, f32[512,256]{1,0:T(8,128)S(1)}, f32[512,256]{1,0:T(8,128)S(1)}) custom-call(s32[3]{0:T(128)S(1)} %pad_add_fusion.where.refs_0_, s32[2,16,3]{2,1,0:T(8,128)S(1)} %copy.11.strides, bf16[2,2,128,256]{3,2,1,0:T(8,128)(2,1)S(1)} %copy-done.3, ...), custom_call_target="tpu_custom_call" | custom-call | tf_op jit(solution)/shard_map/early/pallas_call | solution.py:311
  19.9 0.0 collective-permute-done.3.next_pair
  19.9 2.7 %collective-permute-done.2.pair = bf16[2,2,128,256]{3,2,1,0:T(8,128)(2,1)S(1)} collective-permute-done((bf16[2,2,128,256]{3,2,1,0:T(8,128)(2,1)S(1)}, bf16[2,2,128,256]{3,2,1,0:T(8,128)(2,1)S(1)}, u32[]{:S(2)}, u32[]{:S(2)}) %collective-permute-start.2) | collective-permute-done | bytes 262176 | tf_op jit(solution)/shard_map/ppermute | solution.py:254
  22.8 1.8 %collective-permute-start.4 = (bf16[2,2,2,16,256]{4,3,2,1,0:T(8,128)(2,1)S(1)}, bf16[2,2,2,16,256]{4,3,2,1,0:T(8,128)(2,1)S(1)}, u32[]{:S(2)}, u32[]{:S(2)}) collective-permute-start(bf16[2,2,2,16,256]{4,3,2,1,0:T(8,128)(2,1)S(1)} %pad_maximum_fusion), channel_id=1, source_target_pairs={{0,8},{8,0},{1,9},{9,1},{2,10},{10,2},{3,11},{11,3},{4,12},{12,4},... | collective-permute-start | bytes 196616 | tf_op jit(solution)/shard_map/ppermute | solution.py:270
  24.6 0.9 collective-permute-start.5
  25.5 0.0 collective-permute-done.4.in_chip
  25.5 2.8 %collective-permute-done.5.next_chip = bf16[2,2,2,16,256]{4,3,2,1,0:T(8,128)(2,1)S(1)} collective-permute-done((bf16[2,2,2,16,256]{4,3,2,1,0:T(8,128)(2,1)S(1)}, bf16[2,2,2,16,256]{4,3,2,1,0:T(8,128)(2,1)S(1)}, u32[]{:S(2)}, u32[]{:S(2)}) %collective-permute-start.5) | collective-permute-done | bytes 65568 | tf_op jit(solution)/shard_map/ppermute | solution.py:269
  28.4 3.3 %main.1 = (f32[2304,256]{1,0:T(8,128)S(1)}, bf16[2304,256]{1,0:T(8,128)(2,1)S(1)}, bf16[2,2,128,256]{3,2,1,0:T(8,128)(2,1)S(1)}) custom-call(s32[3]{0:T(128)S(1)} %pad_add_fusion.where.refs_0_, s32[2,16,3]{2,1,0:T(8,128)S(1)} %copy.11.strides, bf16[12,256,256]{2,1,0:T(8,128)(2,1)S(1)} %get-tuple-element.32.own_f, ...), custom_call_target="tpu_custom_call" | custom-call | tf_op jit(solution)/shard_map/main/pallas_call | solution.py:324
  31.7 4.2 %collective-permute-start.6 = (bf16[2304,256]{1,0:T(8,128)(2,1)S(1)}, bf16[2304,256]{1,0:T(8,128)(2,1)S(1)}, u32[]{:S(2)}, u32[]{:S(2)}) collective-permute-start(bf16[2304,256]{1,0:T(8,128)(2,1)S(1)} %get-tuple-element.39), channel_id=1, source_target_pairs={{0,8},{8,0},{1,9},{9,1},{2,10},{10,2},{3,11},{11,3},{4,12},{12,4},... | collective-permute-start | bytes 3538952 | tf_op jit(solution)/shard_map/ppermute | solution.py:344
  35.9 2.5 %collective-permute-done.6 = bf16[2304,256]{1,0:T(8,128)(2,1)S(1)} collective-permute-done((bf16[2304,256]{1,0:T(8,128)(2,1)S(1)}, bf16[2304,256]{1,0:T(8,128)(2,1)S(1)}, u32[]{:S(2)}, u32[]{:S(2)}) %collective-permute-start.6) | collective-permute-done | bytes 1179680 | tf_op jit(solution)/shard_map/ppermute | solution.py:344
  38.3 0.3 add_convert_fusion
  38.7 23.1 %all_to_all.10 = bf16[16,144,256]{2,1,0:T(8,128)(2,1)S(1)} all-to-all(bf16[16,144,256]{2,1,0:T(8,128)(2,1)S(1)} %bitcast.43), channel_id=1, replica_groups=mesh['yl'=2,'z'=8,'core'=2,'x'=4,'yh'=2] {'x','yh','yl'}, dimensions={0} | all-to-all | bytes 2359296 | tf_op jit(solution)/shard_map/all_to_all | solution.py:347
  61.7 0.2 convert_reduce_fusion
  61.9 0.1 collective-permute-start.7
  62.0 4.0 %collective-permute-done.7 = f32[144,256]{1,0:T(8,128)S(1)} collective-permute-done((f32[144,256]{1,0:T(8,128)S(1)}, f32[144,256]{1,0:T(8,128)S(1)}, u32[]{:S(2)}, u32[]{:S(2)}) %collective-permute-start.7) | collective-permute-done | bytes 147488 | tf_op jit(solution)/shard_map/ppermute | solution.py:355
  66.0 3.4 %collective-permute-start.8 = (f32[144,256]{1,0:T(8,128)S(1)}, f32[144,256]{1,0:T(8,128)S(1)}, u32[]{:S(2)}, u32[]{:S(2)}) collective-permute-start(f32[144,256]{1,0:T(8,128)S(1)} %add.49), channel_id=1, source_target_pairs={{0,32},{8,104},{16,48},{24,120},{32,0},{40,72},{48,16},{56,88},{64... | collective-permute-start | bytes 442376 | tf_op jit(solution)/shard_map/ppermute | solution.py:355
  69.4 1.9 %collective-permute-start.9 = (bf16[1,2,128,256]{3,2,1,0:T(8,128)(2,1)S(1)}, bf16[1,2,128,256]{3,2,1,0:T(8,128)(2,1)S(1)}, u32[]{:S(2)}, u32[]{:S(2)}) collective-permute-start(bf16[1,2,128,256]{3,2,1,0:T(8,128)(2,1)S(1)} %get-tuple-element.64), channel_id=1, source_target_pairs={{1,2},{3,4},{5,6},{9,10},{11,12},{13,14},{17,18},{19,20},{21,22},{... | collective-permute-start | bytes 393224 | tf_op jit(solution)/shard_map/ppermute | solution.py:257
  71.4 1.6 %collective-permute-done.8 = f32[144,256]{1,0:T(8,128)S(1)} collective-permute-done((f32[144,256]{1,0:T(8,128)S(1)}, f32[144,256]{1,0:T(8,128)S(1)}, u32[]{:S(2)}, u32[]{:S(2)}) %collective-permute-start.8) | collective-permute-done | bytes 147488 | tf_op jit(solution)/shard_map/ppermute | solution.py:355
  72.9 6.7 %collective-permute-done.9.next_pair = bf16[1,2,128,256]{3,2,1,0:T(8,128)(2,1)S(1)} collective-permute-done((bf16[1,2,128,256]{3,2,1,0:T(8,128)(2,1)S(1)}, bf16[1,2,128,256]{3,2,1,0:T(8,128)(2,1)S(1)}, u32[]{:S(2)}, u32[]{:S(2)}) %collective-permute-start.9) | collective-permute-done | bytes 131104 | tf_op jit(solution)/shard_map/ppermute | solution.py:257
  79.6 0.0 collective-permute-start.10
  79.6 0.9 collective-permute-start.11
  80.5 4.4 %collective-permute-done.11.pair = bf16[1,2,128,256]{3,2,1,0:T(8,128)(2,1)S(1)} collective-permute-done((bf16[1,2,128,256]{3,2,1,0:T(8,128)(2,1)S(1)}, bf16[1,2,128,256]{3,2,1,0:T(8,128)(2,1)S(1)}, u32[]{:S(2)}, u32[]{:S(2)}) %collective-permute-start.11) | collective-permute-done | bytes 131104 | tf_op jit(solution)/shard_map/ppermute | solution.py:254
  84.9 0.6 collective-permute-done.10.got
  85.5 1.1 copies.1
  86.6 3.7 %all-to-all-start.1 = ((bf16[16,144,256]{2,1,0:T(8,128)(2,1)}), bf16[16,144,256]{2,1,0:T(8,128)(2,1)S(1)}, u32[]{:S(2)}, u32[]{:S(2)}) async-start(bf16[16,144,256]{2,1,0:T(8,128)(2,1)} %copies.1), calls=%async_computation.1 | async-start | bytes 2359296 | tf_op jit(solution)/shard_map/all_to_all | solution.py:382
  90.4 3.4 %collective-permute-start.12 = (bf16[1,2,4,16,256]{4,3,2,1,0:T(8,128)(2,1)S(1)}, bf16[1,2,4,16,256]{4,3,2,1,0:T(8,128)(2,1)S(1)}, u32[]{:S(2)}, u32[]{:S(2)}) collective-permute-start(bf16[1,2,4,16,256]{4,3,2,1,0:T(8,128)(2,1)S(1)} %pad_maximum_fusion.2), channel_id=1, source_target_pairs={{0,8},{8,0},{1,9},{9,1},{2,10},{10,2},{3,11},{11,3},{4,12},{12,4},... | collective-permute-start | bytes 196616 | tf_op jit(solution)/shard_map/ppermute | solution.py:270
  93.8 0.8 collective-permute-start.13
  94.6 0.1 collective-permute-done.12.in_chip
  94.7 3.2 %collective-permute-done.13.next_chip = bf16[1,2,4,16,256]{4,3,2,1,0:T(8,128)(2,1)S(1)} collective-permute-done((bf16[1,2,4,16,256]{4,3,2,1,0:T(8,128)(2,1)S(1)}, bf16[1,2,4,16,256]{4,3,2,1,0:T(8,128)(2,1)S(1)}, u32[]{:S(2)}, u32[]{:S(2)}) %collective-permute-start.13) | collective-permute-done | bytes 65568 | tf_op jit(solution)/shard_map/ppermute | solution.py:269
  97.9 2.4 %back.1 = bf16[2,2,128,256]{3,2,1,0:T(8,128)(2,1)} custom-call(s32[3]{0:T(128)S(1)} %pad_add_fusion.where.refs_0_, s32[2,16,3]{2,1,0:T(8,128)S(1)} %copy.11.strides, bf16[2,2,128,256]{3,2,1,0:T(8,128)(2,1)S(1)} %copy-done.2, bf16[2,2,128,256]{3,2,1,0:T(8,128)(2,1)S(1)} %get-tuple-element.42.pre, bf16[1,2,128,256]{3,2,1,0:T(8,128)(2,1)S(1)} %collective-permute-done.11.pair, ...), custom_call_target="tpu_custom_call" | custom-call | tf_op jit(solution)/shard_map/back/pallas_call | solution.py:364
  100.2 5.6 %all-to-all-done.1 = bf16[16,144,256]{2,1,0:T(8,128)(2,1)S(1)} async-done(((bf16[16,144,256]{2,1,0:T(8,128)(2,1)}), bf16[16,144,256]{2,1,0:T(8,128)(2,1)S(1)}, u32[]{:S(2)}, u32[]{:S(2)}) %all-to-all-start.1) | async-done | bytes 1179680 | tf_op jit(solution)/shard_map/all_to_all | solution.py:382
  105.8 4.0 %collective-permute-start.14 = (bf16[2304,256]{1,0:T(8,128)(2,1)S(1)}, bf16[2304,256]{1,0:T(8,128)(2,1)S(1)}, u32[]{:S(2)}, u32[]{:S(2)}) collective-permute-start(bf16[2304,256]{1,0:T(8,128)(2,1)S(1)} %bitcast.37), channel_id=1, source_target_pairs={{0,8},{8,0},{1,9},{9,1},{2,10},{10,2},{3,11},{11,3},{4,12},{12,4},... | collective-permute-start | bytes 3538952 | tf_op jit(solution)/shard_map/ppermute | solution.py:384
  109.8 2.0 %own_part.1 = (f32[2304,256]{1,0:T(8,128)}, f32[2304,256]{1,0:T(8,128)}) custom-call(s32[3]{0:T(128)S(1)} %pad_add_fusion.where.refs_0_, bf16[2304,256]{1,0:T(8,128)(2,1)S(1)} %bitcast.38), custom_call_target="tpu_custom_call" | custom-call | tf_op jit(solution)/shard_map/own_part/pallas_call | solution.py:388
  111.8 0.4 collective-permute-done.14.refs_1_
  112.3 2.0 %other_part.1 = (f32[2304,256]{1,0:T(8,128)}, f32[2304,256]{1,0:T(8,128)}) custom-call(s32[3]{0:T(128)S(1)} %pad_add_fusion.where.refs_0_, bf16[2304,256]{1,0:T(8,128)(2,1)S(1)} %collective-permute-done.14.refs_1_, f32[2304,256]{1,0:T(8,128)} %get-tuple-element.49.refs_2_, ...), custom_call_target="tpu_custom_call", output_to_operand_aliasing={{0}: (2, {}), {1}: (3, {})} | custom-call | tf_op jit(solution)/shard_map/other_part/pallas_call | solution.py:397
  (20 shorter events, 0.2 us)
Async XLA Ops:
  0.6 8.1 %copy-start.2 = (bf16[2,2,128,256]{3,2,1,0:T(8,128)(2,1)S(1)}, bf16[2,2,128,256]{3,2,1,0:T(8,128)(2,1)}, u32[]{:S(2)}) copy-start(bf16[2,2,128,256]{3,2,1,0:T(8,128)(2,1)} %grad.3) | copy-start | bytes 786436
  0.6 8.0 %copy-start.3 = (bf16[2,2,128,256]{3,2,1,0:T(8,128)(2,1)S(1)}, bf16[2,2,128,256]{3,2,1,0:T(8,128)(2,1)}, u32[]{:S(2)}) copy-start(bf16[2,2,128,256]{3,2,1,0:T(8,128)(2,1)} %feat.1) | copy-start | bytes 786436
  0.7 15.1 %copy-start.4 = (s32[2,16,3]{1,0,2:T(2,128)S(1)}, s32[2,16,3]{1,0,2:T(2,128)}, u32[]{:S(2)}) copy-start(s32[2,16,3]{1,0,2:T(2,128)} %param.9) | copy-start | bytes 1156
  0.7 16.0 %copy-start = (bf16[3,3,256,256]{3,2,1,0:T(8,128)(2,1)S(1)}, bf16[3,3,256,256]{3,2,1,0:T(8,128)(2,1)}, u32[]{:S(2)}) copy-start(bf16[3,3,256,256]{3,2,1,0:T(8,128)(2,1)} %first_kernel.5) | copy-start | bytes 3538948
  2.0 18.0 %collective-permute-start.3 = (bf16[2,2,128,256]{3,2,1,0:T(8,128)(2,1)S(1)}, bf16[2,2,128,256]{3,2,1,0:T(8,128)(2,1)S(1)}, u32[]{:S(2)}, u32[]{:S(2)}) collective-permute-start(bf16[2,2,128,256]{3,2,1,0:T(8,128)(2,1)S(1)} %get-tuple-element.55), channel_id=1, source_target_pairs={{1,2},{3,4},{5,6},{9,10},{11,12},{13,14},{17,18},{19,20},{21,22},{... | collective-permute-start | bytes 786440 | tf_op jit(solution)/shard_map/ppermute | solution.py:257
  6.0 16.7 %collective-permute-start.2 = (bf16[2,2,128,256]{3,2,1,0:T(8,128)(2,1)S(1)}, bf16[2,2,128,256]{3,2,1,0:T(8,128)(2,1)S(1)}, u32[]{:S(2)}, u32[]{:S(2)}) collective-permute-start(bf16[2,2,128,256]{3,2,1,0:T(8,128)(2,1)S(1)} %get-tuple-element.56), channel_id=1, source_target_pairs={{0,1},{2,3},{4,5},{6,7},{8,9},{10,11},{12,13},{14,15},{16,17},{18,... | collective-permute-start | bytes 786440 | tf_op jit(solution)/shard_map/ppermute | solution.py:254
  8.7 7.2 %collective-permute-start.1 = (bf16[2,2,2,16,256]{4,3,2,1,0:T(8,128)(2,1)S(1)}, bf16[2,2,2,16,256]{4,3,2,1,0:T(8,128)(2,1)S(1)}, u32[]{:S(2)}, u32[]{:S(2)}) collective-permute-start(bf16[2,2,2,16,256]{4,3,2,1,0:T(8,128)(2,1)S(1)} %get-tuple-element.57), channel_id=1, source_target_pairs={{8,16},{9,17},{10,18},{11,19},{12,20},{13,21},{14,22},{15,23},{24,... | collective-permute-start | bytes 196616 | tf_op jit(solution)/shard_map/ppermute | solution.py:269
  11.5 5.1 %collective-permute-start = (bf16[2,2,2,16,256]{4,3,2,1,0:T(8,128)(2,1)S(1)}, bf16[2,2,2,16,256]{4,3,2,1,0:T(8,128)(2,1)S(1)}, u32[]{:S(2)}, u32[]{:S(2)}) collective-permute-start(bf16[2,2,2,16,256]{4,3,2,1,0:T(8,128)(2,1)S(1)} %get-tuple-element.58), channel_id=1, source_target_pairs={{0,8},{8,0},{1,9},{9,1},{2,10},{10,2},{3,11},{11,3},{4,12},{12,4},... | collective-permute-start | bytes 196616 | tf_op jit(solution)/shard_map/ppermute | solution.py:270
  16.7 1.3 %copy-start.1 = (bf16[3,3,256,256]{3,2,1,0:T(8,128)(2,1)S(1)}, bf16[3,3,256,256]{3,2,1,0:T(8,128)(2,1)}, u32[]{:S(2)}) copy-start(bf16[3,3,256,256]{3,2,1,0:T(8,128)(2,1)} %second_kernel.3) | copy-start | bytes 3538948
  22.8 2.8 %collective-permute-start.4 = (bf16[2,2,2,16,256]{4,3,2,1,0:T(8,128)(2,1)S(1)}, bf16[2,2,2,16,256]{4,3,2,1,0:T(8,128)(2,1)S(1)}, u32[]{:S(2)}, u32[]{:S(2)}) collective-permute-start(bf16[2,2,2,16,256]{4,3,2,1,0:T(8,128)(2,1)S(1)} %pad_maximum_fusion), channel_id=1, source_target_pairs={{0,8},{8,0},{1,9},{9,1},{2,10},{10,2},{3,11},{11,3},{4,12},{12,4},... | collective-permute-start | bytes 196616 | tf_op jit(solution)/shard_map/ppermute | solution.py:270
  24.6 3.8 %collective-permute-start.5 = (bf16[2,2,2,16,256]{4,3,2,1,0:T(8,128)(2,1)S(1)}, bf16[2,2,2,16,256]{4,3,2,1,0:T(8,128)(2,1)S(1)}, u32[]{:S(2)}, u32[]{:S(2)}) collective-permute-start(bf16[2,2,2,16,256]{4,3,2,1,0:T(8,128)(2,1)S(1)} %pad_maximum_fusion.1), channel_id=1, source_target_pairs={{8,16},{9,17},{10,18},{11,19},{12,20},{13,21},{14,22},{15,23},{24,... | collective-permute-start | bytes 196616 | tf_op jit(solution)/shard_map/ppermute | solution.py:269
  31.7 6.7 %collective-permute-start.6 = (bf16[2304,256]{1,0:T(8,128)(2,1)S(1)}, bf16[2304,256]{1,0:T(8,128)(2,1)S(1)}, u32[]{:S(2)}, u32[]{:S(2)}) collective-permute-start(bf16[2304,256]{1,0:T(8,128)(2,1)S(1)} %get-tuple-element.39), channel_id=1, source_target_pairs={{0,8},{8,0},{1,9},{9,1},{2,10},{10,2},{3,11},{11,3},{4,12},{12,4},... | collective-permute-start | bytes 3538952 | tf_op jit(solution)/shard_map/ppermute | solution.py:344
  61.9 4.1 %collective-permute-start.7 = (f32[144,256]{1,0:T(8,128)S(1)}, f32[144,256]{1,0:T(8,128)S(1)}, u32[]{:S(2)}, u32[]{:S(2)}) collective-permute-start(f32[144,256]{1,0:T(8,128)S(1)} %convert_reduce_fusion), channel_id=1, source_target_pairs={{0,16},{8,24},{16,0},{24,8},{32,48},{40,56},{48,32},{56,40},{64,80... | collective-permute-start | bytes 442376 | tf_op jit(solution)/shard_map/ppermute | solution.py:355
  66.0 6.9 %collective-permute-start.8 = (f32[144,256]{1,0:T(8,128)S(1)}, f32[144,256]{1,0:T(8,128)S(1)}, u32[]{:S(2)}, u32[]{:S(2)}) collective-permute-start(f32[144,256]{1,0:T(8,128)S(1)} %add.49), channel_id=1, source_target_pairs={{0,32},{8,104},{16,48},{24,120},{32,0},{40,72},{48,16},{56,88},{64... | collective-permute-start | bytes 442376 | tf_op jit(solution)/shard_map/ppermute | solution.py:355
  69.4 10.2 %collective-permute-start.9 = (bf16[1,2,128,256]{3,2,1,0:T(8,128)(2,1)S(1)}, bf16[1,2,128,256]{3,2,1,0:T(8,128)(2,1)S(1)}, u32[]{:S(2)}, u32[]{:S(2)}) collective-permute-start(bf16[1,2,128,256]{3,2,1,0:T(8,128)(2,1)S(1)} %get-tuple-element.64), channel_id=1, source_target_pairs={{1,2},{3,4},{5,6},{9,10},{11,12},{13,14},{17,18},{19,20},{21,22},{... | collective-permute-start | bytes 393224 | tf_op jit(solution)/shard_map/ppermute | solution.py:257
  79.6 5.9 %collective-permute-start.10 = (f32[144,256]{1,0:T(8,128)S(1)}, f32[144,256]{1,0:T(8,128)S(1)}, u32[]{:S(2)}, u32[]{:S(2)}) collective-permute-start(f32[144,256]{1,0:T(8,128)S(1)} %add.50.part), channel_id=1, source_target_pairs={{0,112},{8,56},{16,96},{24,40},{32,80},{40,24},{48,64},{56,8},{64,... | collective-permute-start | bytes 442376 | tf_op jit(solution)/shard_map/ppermute | solution.py:355
  79.6 5.3 %collective-permute-start.11 = (bf16[1,2,128,256]{3,2,1,0:T(8,128)(2,1)S(1)}, bf16[1,2,128,256]{3,2,1,0:T(8,128)(2,1)S(1)}, u32[]{:S(2)}, u32[]{:S(2)}) collective-permute-start(bf16[1,2,128,256]{3,2,1,0:T(8,128)(2,1)S(1)} %get-tuple-element.63), channel_id=1, source_target_pairs={{0,1},{2,3},{4,5},{6,7},{8,9},{10,11},{12,13},{14,15},{16,17},{18,... | collective-permute-start | bytes 393224 | tf_op jit(solution)/shard_map/ppermute | solution.py:254
  86.6 19.2 %all-to-all-start.1 = ((bf16[16,144,256]{2,1,0:T(8,128)(2,1)}), bf16[16,144,256]{2,1,0:T(8,128)(2,1)S(1)}, u32[]{:S(2)}, u32[]{:S(2)}) async-start(bf16[16,144,256]{2,1,0:T(8,128)(2,1)} %copies.1), calls=%async_computation.1 | async-start | bytes 2359296 | tf_op jit(solution)/shard_map/all_to_all | solution.py:382
  90.4 4.3 %collective-permute-start.12 = (bf16[1,2,4,16,256]{4,3,2,1,0:T(8,128)(2,1)S(1)}, bf16[1,2,4,16,256]{4,3,2,1,0:T(8,128)(2,1)S(1)}, u32[]{:S(2)}, u32[]{:S(2)}) collective-permute-start(bf16[1,2,4,16,256]{4,3,2,1,0:T(8,128)(2,1)S(1)} %pad_maximum_fusion.2), channel_id=1, source_target_pairs={{0,8},{8,0},{1,9},{9,1},{2,10},{10,2},{3,11},{11,3},{4,12},{12,4},... | collective-permute-start | bytes 196616 | tf_op jit(solution)/shard_map/ppermute | solution.py:270
  93.8 4.1 %collective-permute-start.13 = (bf16[1,2,4,16,256]{4,3,2,1,0:T(8,128)(2,1)S(1)}, bf16[1,2,4,16,256]{4,3,2,1,0:T(8,128)(2,1)S(1)}, u32[]{:S(2)}, u32[]{:S(2)}) collective-permute-start(bf16[1,2,4,16,256]{4,3,2,1,0:T(8,128)(2,1)S(1)} %pad_maximum_fusion.3), channel_id=1, source_target_pairs={{8,16},{9,17},{10,18},{11,19},{12,20},{13,21},{14,22},{15,23},{24,... | collective-permute-start | bytes 196616 | tf_op jit(solution)/shard_map/ppermute | solution.py:269
  105.8 6.5 %collective-permute-start.14 = (bf16[2304,256]{1,0:T(8,128)(2,1)S(1)}, bf16[2304,256]{1,0:T(8,128)(2,1)S(1)}, u32[]{:S(2)}, u32[]{:S(2)}) collective-permute-start(bf16[2304,256]{1,0:T(8,128)(2,1)S(1)} %bitcast.37), channel_id=1, source_target_pairs={{0,8},{8,0},{1,9},{9,1},{2,10},{10,2},{3,11},{11,3},{4,12},{12,4},... | collective-permute-start | bytes 3538952 | tf_op jit(solution)/shard_map/ppermute | solution.py:384

commit v11 on v9

--- a/solution.py
+++ b/solution.py
@@ -135,7 +135,7 @@
 
 
 def main_kernel(where, strides, own_f, own_g, pre_part, back_part, pair, next_pair, in_chip, next_chip,
-                first_kernel, second_kernel, keep, send, pre_grad, ext_f, ext_g, edge_f, edge_g, act):
+                first_kernel, second_kernel, pre_grad, act, edge_f, edge_g, ext_f, ext_g):
     lat, core = where[0], where[1]
     odd, second_core = where[2] == 1, core == 1
     mirror = lat == 0
@@ -172,16 +172,19 @@
         for s in range(2):
             pre_grad[s, row] = result[s * width : (s + 1) * width]
 
+
+def weight_kernel(owner, where, own_f, own_g, edge_f, edge_g, act, pre_grad, out):
+    mirror = where[0] == 0
+    half = act.shape[0] // 2
+
     def taps_of(own, edge, row, k, col):
         return own[OWN.index((row, k)) * 3 + col] if (row, k) in OWN else edge[row * 3 + col]
 
-    rows = [jnp.concatenate([pre_grad[s, row] for s in range(2)], axis=0) for row in range(2)]
-
-    def products(first, second):
-        def place(out, value, k, col):
-            at = (k * 3 + col) * 256
-            out[at : at + 256] = value.astype(out.dtype)
-
+    def place(value, k, col):
+        at = (k * 3 + col) * 256
+        out[at : at + 256] = value.astype(out.dtype)
+
+    def second():
         turned = act[...].T
         above, below = turned[:, :half], turned[:, half:]
         for col in range(3):
@@ -189,15 +192,18 @@
             centre, lower = (
                 sum(dot(a, taps_of(own_g, edge_g, r, slot, col), NN) for r, a in enumerate((above, below))) for slot in (1, 2)
             )
-            place(second, centre, 1, col)
-            place(second, lower + jnp.where(mirror, edge, 0.0), 0, col)
-            place(second, upper + jnp.where(mirror, 0.0, edge), 2, col)
+            place(centre, 1, col)
+            place(lower + jnp.where(mirror, edge, 0.0), 0, col)
+            place(upper + jnp.where(mirror, 0.0, edge), 2, col)
+
+    def first():
+        rows = [jnp.concatenate([pre_grad[s, row] for s in range(2)], axis=0) for row in range(2)]
         for k in range(3):
             for col in range(3):
-                place(first, sum(dot(taps_of(own_f, edge_f, r, k, col), rows[r], TN) for r in range(2)), k, col)
-
-    pl.when(core == 0)(lambda: products(keep, send))
-    pl.when(core != 0)(lambda: products(send, keep))
+                place(sum(dot(taps_of(own_f, edge_f, r, k, col), rows[r], TN) for r in range(2)), k, col)
+
+    pl.when(where[1] == owner)(first)
+    pl.when(where[1] != owner)(second)
 
 
 def back_kernel(where, strides, grad, pre, pair, next_pair, in_chip, next_chip, first_kernel, out, ext, taps):
@@ -320,26 +326,33 @@
     )(where, strides, features, out_grad, *own_columns, first_kernel, second_kernel)
     early, rows_around = lax.optimization_barrier((early, rows_around))
     corners = column_halos(ordered(*rows_around), width, lon_count, lat_count)
-    edge = pltpu.VMEM((6, half, chans), jnp.bfloat16)
-    keep, send, pre_grad = pl.pallas_call(
+    edge = jax.ShapeDtypeStruct((6, half, chans), jnp.bfloat16)
+    pre_grad, act, *edges = pl.pallas_call(
         main_kernel,
         out_shape=[
-            jax.ShapeDtypeStruct(grads, jnp.float32),
-            jax.ShapeDtypeStruct(grads, jnp.bfloat16),
             jax.ShapeDtypeStruct(features.shape, jnp.bfloat16),
+            jax.ShapeDtypeStruct((cells, chans), jnp.bfloat16),
+            edge,
+            edge,
         ],
         in_specs=[smem, smem] + [vmem] * 10,
-        out_specs=[vmem] * 3,
-        scratch_shapes=[
-            ext_rows,
-            ext_rows,
-            edge,
-            edge,
-            pltpu.VMEM((cells, chans), jnp.bfloat16),
-        ],
+        out_specs=[vmem] * 4,
+        scratch_shapes=[ext_rows, ext_rows],
         compiler_params=params,
         name="main",
     )(where, strides, *early, *rows_around, *corners, first_kernel, second_kernel)
+
+    def weights(owner, kind, name):
+        return pl.pallas_call(
+            lambda *refs: weight_kernel(owner, *refs),
+            out_shape=jax.ShapeDtypeStruct(grads, kind),
+            in_specs=[smem] + [vmem] * 6,
+            out_specs=vmem,
+            compiler_params=params,
+            name=name,
+        )(where, *early[:2], *edges, act, pre_grad)
+
+    send, keep = weights(1, jnp.bfloat16, "sent"), weights(0, jnp.float32, "kept")
 
     total = keep + lax.ppermute(send, "core", swap).astype(jnp.float32)
     planes, height, cores = lax.axis_size(PLANE), lax.axis_size("z"), lax.axis_size("core")

time: 113 us -> 113 us (level)
    ppermute x1, waiting for transfers between devices: 2.47 us -> 1.09 us  [local(): total = keep + lax.ppermute(send, 'core', swap).astype(jnp.float32)]
    pallas_call x1 -> x3, Pallas kernels: 3.26 us -> 4.52 us  [the longest x2 2.75 us: weights(): pl.pallas_call(lambda *refs: weight_kernel(owner, *refs), out_shape=jax.S...]
    unnamed x11 -> x15, local copies, waits for them, and re-layouts: 1.38 us -> 2.39 us
  transfers between devices with their start and end apart: 16 -> 16, of which waited for: 12 -> 12; matrix products, arithmetic and copies ran while one was open for 0% -> 0% of each run, Pallas kernels for 6% -> 7%
where the time goes in v11:
time: 113 us
  starting transfers between devices  43.4 us (38%)
  waiting for transfers between devices  28.3 us (25%)
  blocking collectives  23.1 us (20%)
  Pallas kernels  12.9 us (11%)
  local copies, waits for them, and re-layouts  2.47 us (2%)
  other arithmetic  1.91 us (2%)
    all_to_all x1, blocking collectives, local(): spread = lax.all_to_all(total, PLANE, 0, 0, tiled=True)  23.1 us
    ppermute x3, starting transfers between devices, column_halos(): in_chip = lax.ppermute(edge((1 - core) * reach), 'core', [(0, 1), (1, 0)])  11.2 us
    ppermute x2, waiting for transfers between devices, row_halos(): lax.ppermute(row(1 - odd), ALL, both_ways([(at(i, k), at(i, k + 1)) for i...  6.34 us
    ppermute x1, starting transfers between devices, local(): other = lax.ppermute(mine, 'core', swap)  6.27 us
    ppermute x3, waiting for transfers between devices, column_halos(): lax.ppermute(edge(core * reach), ALL, both_ways([(at(i + 1, k), at(i + 2,...  6.03 us
    ppermute x3, waiting for transfers between devices, local(): got = lax.ppermute(part, ('z', 'core'), folded(height, cores, reach))  6.02 us
    ppermute x2, starting transfers between devices, row_halos(): return (pair, lax.ppermute(row(odd), ALL, between + across))  5.94 us
    ppermute x2, waiting for transfers between devices, row_halos(): return (pair, lax.ppermute(row(odd), ALL, between + across))  5.49 us
  transfers between devices with their start and end apart: 16, of which 12 were waited for; matrix products, arithmetic and copies ran while one was open for 0% of the time, Pallas kernels for 7%

profile of v11, /device:TPU:1, one launch (start us, length us, event | category | flops | bytes accessed | tf_op | source)
XLA Modules:
  0.0 113.1 jit_solution(15777236916418560912)
XLA Ops:
  0.7 1.3 %fusion.1 = (bf16[2,2,128,256]{3,2,1,0:T(8,128)(2,1)S(1)}, bf16[2,2,128,256]{3,2,1,0:T(8,128)(2,1)S(1)}) fusion(s32[]{:T(128)S(6)} %select_n.53, bf16[1,2,2,128,256]{4,3,2,1,0:T(8,128)(2,1)} %bitcast.41, bf16[1,2,2,128,256]{4,3,2,1,0:T(8,128)(2,1)} %bitcast.39, s32[]{:T(128)S(6)} %select_n.52), kind=kLoop, calls=%fused_computation.11 | loop fusion | flops 262144 | bytes 1048584 | tf_op jit(solution)/shard_map/jit(dynamic_index_in_dim)/squeeze | solution.py:259
  2.0 4.0 %collective-permute-start.3 = (bf16[2,2,128,256]{3,2,1,0:T(8,128)(2,1)S(1)}, bf16[2,2,128,256]{3,2,1,0:T(8,128)(2,1)S(1)}, u32[]{:S(2)}, u32[]{:S(2)}) collective-permute-start(bf16[2,2,128,256]{3,2,1,0:T(8,128)(2,1)S(1)} %get-tuple-element.57), channel_id=1, source_target_pairs={{1,2},{3,4},{5,6},{9,10},{11,12},{13,14},{17,18},{19,20},{21,22},{... | collective-permute-start | bytes 786440 | tf_op jit(solution)/shard_map/ppermute | solution.py:263
  6.0 2.7 %collective-permute-start.2 = (bf16[2,2,128,256]{3,2,1,0:T(8,128)(2,1)S(1)}, bf16[2,2,128,256]{3,2,1,0:T(8,128)(2,1)S(1)}, u32[]{:S(2)}, u32[]{:S(2)}) collective-permute-start(bf16[2,2,128,256]{3,2,1,0:T(8,128)(2,1)S(1)} %get-tuple-element.58), channel_id=1, source_target_pairs={{0,1},{2,3},{4,5},{6,7},{8,9},{10,11},{12,13},{14,15},{16,17},{18,... | collective-permute-start | bytes 786440 | tf_op jit(solution)/shard_map/ppermute | solution.py:260
  8.7 2.8 %collective-permute-start.1 = (bf16[2,2,2,16,256]{4,3,2,1,0:T(8,128)(2,1)S(1)}, bf16[2,2,2,16,256]{4,3,2,1,0:T(8,128)(2,1)S(1)}, u32[]{:S(2)}, u32[]{:S(2)}) collective-permute-start(bf16[2,2,2,16,256]{4,3,2,1,0:T(8,128)(2,1)S(1)} %get-tuple-element.59), channel_id=1, source_target_pairs={{8,16},{9,17},{10,18},{11,19},{12,20},{13,21},{14,22},{15,23},{24,... | collective-permute-start | bytes 196616 | tf_op jit(solution)/shard_map/ppermute | solution.py:275
  11.5 4.2 %collective-permute-start = (bf16[2,2,2,16,256]{4,3,2,1,0:T(8,128)(2,1)S(1)}, bf16[2,2,2,16,256]{4,3,2,1,0:T(8,128)(2,1)S(1)}, u32[]{:S(2)}, u32[]{:S(2)}) collective-permute-start(bf16[2,2,2,16,256]{4,3,2,1,0:T(8,128)(2,1)S(1)} %get-tuple-element.60), channel_id=1, source_target_pairs={{0,8},{8,0},{1,9},{9,1},{2,10},{10,2},{3,11},{11,3},{4,12},{12,4},... | collective-permute-start | bytes 196616 | tf_op jit(solution)/shard_map/ppermute | solution.py:276
  15.8 0.1 copy.10.strides
  15.9 0.1 pad_add_fusion.where.refs_0_
  15.9 0.7 collective-permute-done.in_chip
  16.7 1.3 %copy-done.1 = bf16[3,3,256,256]{3,2,1,0:T(8,128)(2,1)S(1)} copy-done((bf16[3,3,256,256]{3,2,1,0:T(8,128)(2,1)S(1)}, bf16[3,3,256,256]{3,2,1,0:T(8,128)(2,1)}, u32[]{:S(2)}) %copy-start.1) | copy-done | bytes 1179672
  18.0 1.9 %early.1 = (bf16[12,256,256]{2,1,0:T(8,128)(2,1)S(1)}, bf16[12,256,256]{2,1,0:T(8,128)(2,1)S(1)}, f32[512,256]{1,0:T(8,128)S(1)}, f32[512,256]{1,0:T(8,128)S(1)}) custom-call(s32[3]{0:T(128)S(1)} %pad_add_fusion.where.refs_0_, s32[2,16,3]{2,1,0:T(8,128)S(1)} %copy.10.strides, bf16[2,2,128,256]{3,2,1,0:T(8,128)(2,1)S(1)} %copy-done.5, ...), custom_call_target="tpu_custom_call" | custom-call | tf_op jit(solution)/shard_map/early/pallas_call | solution.py:317
  19.9 0.0 copy-start.2
  19.9 0.0 collective-permute-done.3.next_pair
  19.9 2.8 %collective-permute-done.2.pair = bf16[2,2,128,256]{3,2,1,0:T(8,128)(2,1)S(1)} collective-permute-done((bf16[2,2,128,256]{3,2,1,0:T(8,128)(2,1)S(1)}, bf16[2,2,128,256]{3,2,1,0:T(8,128)(2,1)S(1)}, u32[]{:S(2)}, u32[]{:S(2)}) %collective-permute-start.2) | collective-permute-done | bytes 262176 | tf_op jit(solution)/shard_map/ppermute | solution.py:260
  22.8 1.8 %collective-permute-start.4 = (bf16[2,2,2,16,256]{4,3,2,1,0:T(8,128)(2,1)S(1)}, bf16[2,2,2,16,256]{4,3,2,1,0:T(8,128)(2,1)S(1)}, u32[]{:S(2)}, u32[]{:S(2)}) collective-permute-start(bf16[2,2,2,16,256]{4,3,2,1,0:T(8,128)(2,1)S(1)} %pad_maximum_fusion), channel_id=1, source_target_pairs={{0,8},{8,0},{1,9},{9,1},{2,10},{10,2},{3,11},{11,3},{4,12},{12,4},... | collective-permute-start | bytes 196616 | tf_op jit(solution)/shard_map/ppermute | solution.py:276
  24.6 0.9 collective-permute-start.5
  25.5 0.0 collective-permute-done.4.in_chip
  25.5 2.8 %collective-permute-done.5.next_chip = bf16[2,2,2,16,256]{4,3,2,1,0:T(8,128)(2,1)S(1)} collective-permute-done((bf16[2,2,2,16,256]{4,3,2,1,0:T(8,128)(2,1)S(1)}, bf16[2,2,2,16,256]{4,3,2,1,0:T(8,128)(2,1)S(1)}, u32[]{:S(2)}, u32[]{:S(2)}) %collective-permute-start.5) | collective-permute-done | bytes 65568 | tf_op jit(solution)/shard_map/ppermute | solution.py:275
  28.4 1.8 %main.1 = (bf16[2,2,128,256]{3,2,1,0:T(8,128)(2,1)S(1)}, bf16[512,256]{1,0:T(8,128)(2,1)S(1)}, bf16[6,256,256]{2,1,0:T(8,128)(2,1)S(1)}, bf16[6,256,256]{2,1,0:T(8,128)(2,1)S(1)}) custom-call(s32[3]{0:T(128)S(1)} %pad_add_fusion.where.refs_0_, s32[2,16,3]{2,1,0:T(8,128)S(1)} %copy.10.strides, bf16[12,256,256]{2,1,0:T(8,128)(2,1)S(1)} %get-tuple-element.33.own_f.refs_1_, ...), custom_call_target="tpu_custom_call" | custom-call | tf_op jit(solution)/shard_map/main/pallas_call | solution.py:330
  30.2 1.4 %sent.1 = bf16[2304,256]{1,0:T(8,128)(2,1)S(1)} custom-call(s32[3]{0:T(128)S(1)} %pad_add_fusion.where.refs_0_, bf16[12,256,256]{2,1,0:T(8,128)(2,1)S(1)} %get-tuple-element.33.own_f.refs_1_, bf16[12,256,256]{2,1,0:T(8,128)(2,1)S(1)} %get-tuple-element.34.own_g.refs_2_, bf16[6,256,256]{2,1,0:T(8,128)(2,1)S(1)} %get-tuple-element.39.refs_3_, ...), custom_call_target="tpu_custom_call" | custom-call | tf_op jit(solution)/shard_map/sent/pallas_call | solution.py:346
  31.6 4.2 %collective-permute-start.6 = (bf16[2304,256]{1,0:T(8,128)(2,1)S(1)}, bf16[2304,256]{1,0:T(8,128)(2,1)S(1)}, u32[]{:S(2)}, u32[]{:S(2)}) collective-permute-start(bf16[2304,256]{1,0:T(8,128)(2,1)S(1)} %sent.1), channel_id=1, source_target_pairs={{0,8},{8,0},{1,9},{9,1},{2,10},{10,2},{3,11},{11,3},{4,12},{12,4},... | collective-permute-start | bytes 3538952 | tf_op jit(solution)/shard_map/ppermute | solution.py:357
  35.8 1.4 %kept.1 = f32[2304,256]{1,0:T(8,128)S(1)} custom-call(s32[3]{0:T(128)S(1)} %pad_add_fusion.where.refs_0_, bf16[12,256,256]{2,1,0:T(8,128)(2,1)S(1)} %get-tuple-element.33.own_f.refs_1_, bf16[12,256,256]{2,1,0:T(8,128)(2,1)S(1)} %get-tuple-element.34.own_g.refs_2_, bf16[6,256,256]{2,1,0:T(8,128)(2,1)S(1)} %get-tuple-element.39.refs_3_, ...), custom_call_target="tpu_custom_call" | custom-call | tf_op jit(solution)/shard_map/kept/pallas_call | solution.py:346
  37.1 1.1 collective-permute-done.6
  38.2 0.3 add_convert_fusion
  38.5 23.1 %all_to_all.10 = bf16[16,144,256]{2,1,0:T(8,128)(2,1)S(1)} all-to-all(bf16[16,144,256]{2,1,0:T(8,128)(2,1)S(1)} %bitcast.43), channel_id=1, replica_groups=mesh['yl'=2,'z'=8,'core'=2,'x'=4,'yh'=2] {'x','yh','yl'}, dimensions={0} | all-to-all | bytes 2359296 | tf_op jit(solution)/shard_map/all_to_all | solution.py:360
  61.6 0.2 convert_reduce_fusion
  61.7 0.1 collective-permute-start.7
  61.8 4.0 %collective-permute-done.7 = f32[144,256]{1,0:T(8,128)S(1)} collective-permute-done((f32[144,256]{1,0:T(8,128)S(1)}, f32[144,256]{1,0:T(8,128)S(1)}, u32[]{:S(2)}, u32[]{:S(2)}) %collective-permute-start.7) | collective-permute-done | bytes 147488 | tf_op jit(solution)/shard_map/ppermute | solution.py:368
  65.8 3.4 %collective-permute-start.8 = (f32[144,256]{1,0:T(8,128)S(1)}, f32[144,256]{1,0:T(8,128)S(1)}, u32[]{:S(2)}, u32[]{:S(2)}) collective-permute-start(f32[144,256]{1,0:T(8,128)S(1)} %add.49), channel_id=1, source_target_pairs={{0,32},{8,104},{16,48},{24,120},{32,0},{40,72},{48,16},{56,88},{64... | collective-permute-start | bytes 442376 | tf_op jit(solution)/shard_map/ppermute | solution.py:368
  69.3 1.4 %collective-permute-start.9 = (bf16[1,2,128,256]{3,2,1,0:T(8,128)(2,1)S(1)}, bf16[1,2,128,256]{3,2,1,0:T(8,128)(2,1)S(1)}, u32[]{:S(2)}, u32[]{:S(2)}) collective-permute-start(bf16[1,2,128,256]{3,2,1,0:T(8,128)(2,1)S(1)} %get-tuple-element.66), channel_id=1, source_target_pairs={{0,1},{2,3},{4,5},{6,7},{8,9},{10,11},{12,13},{14,15},{16,17},{18,... | collective-permute-start | bytes 393224 | tf_op jit(solution)/shard_map/ppermute | solution.py:260
  70.7 2.0 %collective-permute-done.8 = f32[144,256]{1,0:T(8,128)S(1)} collective-permute-done((f32[144,256]{1,0:T(8,128)S(1)}, f32[144,256]{1,0:T(8,128)S(1)}, u32[]{:S(2)}, u32[]{:S(2)}) %collective-permute-start.8) | collective-permute-done | bytes 147488 | tf_op jit(solution)/shard_map/ppermute | solution.py:368
  72.8 3.6 %collective-permute-done.9.pair = bf16[1,2,128,256]{3,2,1,0:T(8,128)(2,1)S(1)} collective-permute-done((bf16[1,2,128,256]{3,2,1,0:T(8,128)(2,1)S(1)}, bf16[1,2,128,256]{3,2,1,0:T(8,128)(2,1)S(1)}, u32[]{:S(2)}, u32[]{:S(2)}) %collective-permute-start.9) | collective-permute-done | bytes 131104 | tf_op jit(solution)/shard_map/ppermute | solution.py:260
  76.3 1.9 %collective-permute-start.11 = (bf16[1,2,128,256]{3,2,1,0:T(8,128)(2,1)S(1)}, bf16[1,2,128,256]{3,2,1,0:T(8,128)(2,1)S(1)}, u32[]{:S(2)}, u32[]{:S(2)}) collective-permute-start(bf16[1,2,128,256]{3,2,1,0:T(8,128)(2,1)S(1)} %get-tuple-element.65), channel_id=1, source_target_pairs={{1,2},{3,4},{5,6},{9,10},{11,12},{13,14},{17,18},{19,20},{21,22},{... | collective-permute-start | bytes 393224 | tf_op jit(solution)/shard_map/ppermute | solution.py:263
  78.3 5.5 %collective-permute-done.11.next_pair = bf16[1,2,128,256]{3,2,1,0:T(8,128)(2,1)S(1)} collective-permute-done((bf16[1,2,128,256]{3,2,1,0:T(8,128)(2,1)S(1)}, bf16[1,2,128,256]{3,2,1,0:T(8,128)(2,1)S(1)}, u32[]{:S(2)}, u32[]{:S(2)}) %collective-permute-start.11) | collective-permute-done | bytes 131104 | tf_op jit(solution)/shard_map/ppermute | solution.py:263
  83.7 0.0 collective-permute-done.10.got
  83.7 0.1 copies.1
  83.8 0.0 copy-start.3
  83.8 1.0 copy-done.3
  84.8 4.0 %all-to-all-start.1 = ((bf16[16,144,256]{2,1,0:T(8,128)(2,1)}), bf16[16,144,256]{2,1,0:T(8,128)(2,1)S(1)}, u32[]{:S(2)}, u32[]{:S(2)}) async-start(bf16[16,144,256]{2,1,0:T(8,128)(2,1)} %copy-done.3), calls=%async_computation.1 | async-start | bytes 2359296 | tf_op jit(solution)/shard_map/all_to_all | solution.py:395
  89.0 5.1 %collective-permute-start.12 = (bf16[1,2,4,16,256]{4,3,2,1,0:T(8,128)(2,1)S(1)}, bf16[1,2,4,16,256]{4,3,2,1,0:T(8,128)(2,1)S(1)}, u32[]{:S(2)}, u32[]{:S(2)}) collective-permute-start(bf16[1,2,4,16,256]{4,3,2,1,0:T(8,128)(2,1)S(1)} %pad_maximum_fusion.2), channel_id=1, source_target_pairs={{0,8},{8,0},{1,9},{9,1},{2,10},{10,2},{3,11},{11,3},{4,12},{12,4},... | collective-permute-start | bytes 196616 | tf_op jit(solution)/shard_map/ppermute | solution.py:276
  94.1 0.4 collective-permute-start.13
  94.5 0.5 collective-permute-done.12.in_chip
  95.0 3.2 %collective-permute-done.13.next_chip = bf16[1,2,4,16,256]{4,3,2,1,0:T(8,128)(2,1)S(1)} collective-permute-done((bf16[1,2,4,16,256]{4,3,2,1,0:T(8,128)(2,1)S(1)}, bf16[1,2,4,16,256]{4,3,2,1,0:T(8,128)(2,1)S(1)}, u32[]{:S(2)}, u32[]{:S(2)}) %collective-permute-start.13) | collective-permute-done | bytes 65568 | tf_op jit(solution)/shard_map/ppermute | solution.py:275
  98.2 2.4 %back.1 = bf16[2,2,128,256]{3,2,1,0:T(8,128)(2,1)} custom-call(s32[3]{0:T(128)S(1)} %pad_add_fusion.where.refs_0_, s32[2,16,3]{2,1,0:T(8,128)S(1)} %copy.10.strides, bf16[2,2,128,256]{3,2,1,0:T(8,128)(2,1)S(1)} %copy-done.4, bf16[2,2,128,256]{3,2,1,0:T(8,128)(2,1)S(1)} %get-tuple-element.44.refs_6_.pre, ...), custom_call_target="tpu_custom_call" | custom-call | tf_op jit(solution)/shard_map/back/pallas_call | solution.py:377
  100.5 1.6 %all-to-all-done.1 = bf16[16,144,256]{2,1,0:T(8,128)(2,1)S(1)} async-done(((bf16[16,144,256]{2,1,0:T(8,128)(2,1)}), bf16[16,144,256]{2,1,0:T(8,128)(2,1)S(1)}, u32[]{:S(2)}, u32[]{:S(2)}) %all-to-all-start.1) | async-done | bytes 1179680 | tf_op jit(solution)/shard_map/all_to_all | solution.py:395
  102.2 6.3 %collective-permute-start.14 = (bf16[2304,256]{1,0:T(8,128)(2,1)S(1)}, bf16[2304,256]{1,0:T(8,128)(2,1)S(1)}, u32[]{:S(2)}, u32[]{:S(2)}) collective-permute-start(bf16[2304,256]{1,0:T(8,128)(2,1)S(1)} %bitcast.37), channel_id=1, source_target_pairs={{0,8},{8,0},{1,9},{9,1},{2,10},{10,2},{3,11},{11,3},{4,12},{12,4},... | collective-permute-start | bytes 3538952 | tf_op jit(solution)/shard_map/ppermute | solution.py:397
  108.4 2.0 %own_part.1 = (f32[2304,256]{1,0:T(8,128)}, f32[2304,256]{1,0:T(8,128)}) custom-call(s32[3]{0:T(128)S(1)} %pad_add_fusion.where.refs_0_, bf16[2304,256]{1,0:T(8,128)(2,1)S(1)} %bitcast.38), custom_call_target="tpu_custom_call" | custom-call | tf_op jit(solution)/shard_map/own_part/pallas_call | solution.py:401
  110.5 0.4 collective-permute-done.14.refs_1_
  110.9 2.0 %other_part.1 = (f32[2304,256]{1,0:T(8,128)}, f32[2304,256]{1,0:T(8,128)}) custom-call(s32[3]{0:T(128)S(1)} %pad_add_fusion.where.refs_0_, bf16[2304,256]{1,0:T(8,128)(2,1)S(1)} %collective-permute-done.14.refs_1_, f32[2304,256]{1,0:T(8,128)} %get-tuple-element.51.refs_2_, ...), custom_call_target="tpu_custom_call", output_to_operand_aliasing={{0}: (2, {}), {1}: (3, {})} | custom-call | tf_op jit(solution)/shard_map/other_part/pallas_call | solution.py:410
  (26 shorter events, 0.3 us)
Async XLA Ops:
  0.6 8.1 %copy-start.4 = (bf16[2,2,128,256]{3,2,1,0:T(8,128)(2,1)S(1)}, bf16[2,2,128,256]{3,2,1,0:T(8,128)(2,1)}, u32[]{:S(2)}) copy-start(bf16[2,2,128,256]{3,2,1,0:T(8,128)(2,1)} %grad.3) | copy-start | bytes 786436
  0.6 8.0 %copy-start.5 = (bf16[2,2,128,256]{3,2,1,0:T(8,128)(2,1)S(1)}, bf16[2,2,128,256]{3,2,1,0:T(8,128)(2,1)}, u32[]{:S(2)}) copy-start(bf16[2,2,128,256]{3,2,1,0:T(8,128)(2,1)} %feat.1) | copy-start | bytes 786436
  0.7 15.1 %copy-start.6 = (s32[2,16,3]{1,0,2:T(2,128)S(1)}, s32[2,16,3]{1,0,2:T(2,128)}, u32[]{:S(2)}) copy-start(s32[2,16,3]{1,0,2:T(2,128)} %param.9) | copy-start | bytes 1156
  0.7 16.0 %copy-start = (bf16[3,3,256,256]{3,2,1,0:T(8,128)(2,1)S(1)}, bf16[3,3,256,256]{3,2,1,0:T(8,128)(2,1)}, u32[]{:S(2)}) copy-start(bf16[3,3,256,256]{3,2,1,0:T(8,128)(2,1)} %first_kernel.5) | copy-start | bytes 3538948
  2.0 17.9 %collective-permute-start.3 = (bf16[2,2,128,256]{3,2,1,0:T(8,128)(2,1)S(1)}, bf16[2,2,128,256]{3,2,1,0:T(8,128)(2,1)S(1)}, u32[]{:S(2)}, u32[]{:S(2)}) collective-permute-start(bf16[2,2,128,256]{3,2,1,0:T(8,128)(2,1)S(1)} %get-tuple-element.57), channel_id=1, source_target_pairs={{1,2},{3,4},{5,6},{9,10},{11,12},{13,14},{17,18},{19,20},{21,22},{... | collective-permute-start | bytes 786440 | tf_op jit(solution)/shard_map/ppermute | solution.py:263
  6.0 16.7 %collective-permute-start.2 = (bf16[2,2,128,256]{3,2,1,0:T(8,128)(2,1)S(1)}, bf16[2,2,128,256]{3,2,1,0:T(8,128)(2,1)S(1)}, u32[]{:S(2)}, u32[]{:S(2)}) collective-permute-start(bf16[2,2,128,256]{3,2,1,0:T(8,128)(2,1)S(1)} %get-tuple-element.58), channel_id=1, source_target_pairs={{0,1},{2,3},{4,5},{6,7},{8,9},{10,11},{12,13},{14,15},{16,17},{18,... | collective-permute-start | bytes 786440 | tf_op jit(solution)/shard_map/ppermute | solution.py:260
  8.7 7.2 %collective-permute-start.1 = (bf16[2,2,2,16,256]{4,3,2,1,0:T(8,128)(2,1)S(1)}, bf16[2,2,2,16,256]{4,3,2,1,0:T(8,128)(2,1)S(1)}, u32[]{:S(2)}, u32[]{:S(2)}) collective-permute-start(bf16[2,2,2,16,256]{4,3,2,1,0:T(8,128)(2,1)S(1)} %get-tuple-element.59), channel_id=1, source_target_pairs={{8,16},{9,17},{10,18},{11,19},{12,20},{13,21},{14,22},{15,23},{24,... | collective-permute-start | bytes 196616 | tf_op jit(solution)/shard_map/ppermute | solution.py:275
  11.5 5.1 %collective-permute-start = (bf16[2,2,2,16,256]{4,3,2,1,0:T(8,128)(2,1)S(1)}, bf16[2,2,2,16,256]{4,3,2,1,0:T(8,128)(2,1)S(1)}, u32[]{:S(2)}, u32[]{:S(2)}) collective-permute-start(bf16[2,2,2,16,256]{4,3,2,1,0:T(8,128)(2,1)S(1)} %get-tuple-element.60), channel_id=1, source_target_pairs={{0,8},{8,0},{1,9},{9,1},{2,10},{10,2},{3,11},{11,3},{4,12},{12,4},... | collective-permute-start | bytes 196616 | tf_op jit(solution)/shard_map/ppermute | solution.py:276
  16.7 1.3 %copy-start.1 = (bf16[3,3,256,256]{3,2,1,0:T(8,128)(2,1)S(1)}, bf16[3,3,256,256]{3,2,1,0:T(8,128)(2,1)}, u32[]{:S(2)}) copy-start(bf16[3,3,256,256]{3,2,1,0:T(8,128)(2,1)} %second_kernel.3) | copy-start | bytes 3538948
  19.9 8.5 %copy-start.2 = (bf16[3,3,256,256]{3,2,1,0:T(8,128)(2,1)S(1)}, bf16[3,3,256,256]{3,2,1,0:T(8,128)(2,1)}, u32[]{:S(2)}) copy-start(bf16[3,3,256,256]{3,2,1,0:T(8,128)(2,1)} %second_kernel.3) | copy-start | bytes 3538948
  22.8 2.8 %collective-permute-start.4 = (bf16[2,2,2,16,256]{4,3,2,1,0:T(8,128)(2,1)S(1)}, bf16[2,2,2,16,256]{4,3,2,1,0:T(8,128)(2,1)S(1)}, u32[]{:S(2)}, u32[]{:S(2)}) collective-permute-start(bf16[2,2,2,16,256]{4,3,2,1,0:T(8,128)(2,1)S(1)} %pad_maximum_fusion), channel_id=1, source_target_pairs={{0,8},{8,0},{1,9},{9,1},{2,10},{10,2},{3,11},{11,3},{4,12},{12,4},... | collective-permute-start | bytes 196616 | tf_op jit(solution)/shard_map/ppermute | solution.py:276
  24.6 3.8 %collective-permute-start.5 = (bf16[2,2,2,16,256]{4,3,2,1,0:T(8,128)(2,1)S(1)}, bf16[2,2,2,16,256]{4,3,2,1,0:T(8,128)(2,1)S(1)}, u32[]{:S(2)}, u32[]{:S(2)}) collective-permute-start(bf16[2,2,2,16,256]{4,3,2,1,0:T(8,128)(2,1)S(1)} %pad_maximum_fusion.1), channel_id=1, source_target_pairs={{8,16},{9,17},{10,18},{11,19},{12,20},{13,21},{14,22},{15,23},{24,... | collective-permute-start | bytes 196616 | tf_op jit(solution)/shard_map/ppermute | solution.py:275
  31.6 6.7 %collective-permute-start.6 = (bf16[2304,256]{1,0:T(8,128)(2,1)S(1)}, bf16[2304,256]{1,0:T(8,128)(2,1)S(1)}, u32[]{:S(2)}, u32[]{:S(2)}) collective-permute-start(bf16[2304,256]{1,0:T(8,128)(2,1)S(1)} %sent.1), channel_id=1, source_target_pairs={{0,8},{8,0},{1,9},{9,1},{2,10},{10,2},{3,11},{11,3},{4,12},{12,4},... | collective-permute-start | bytes 3538952 | tf_op jit(solution)/shard_map/ppermute | solution.py:357
  61.7 4.1 %collective-permute-start.7 = (f32[144,256]{1,0:T(8,128)S(1)}, f32[144,256]{1,0:T(8,128)S(1)}, u32[]{:S(2)}, u32[]{:S(2)}) collective-permute-start(f32[144,256]{1,0:T(8,128)S(1)} %convert_reduce_fusion), channel_id=1, source_target_pairs={{0,16},{8,24},{16,0},{24,8},{32,48},{40,56},{48,32},{56,40},{64,80... | collective-permute-start | bytes 442376 | tf_op jit(solution)/shard_map/ppermute | solution.py:368
  65.8 6.9 %collective-permute-start.8 = (f32[144,256]{1,0:T(8,128)S(1)}, f32[144,256]{1,0:T(8,128)S(1)}, u32[]{:S(2)}, u32[]{:S(2)}) collective-permute-start(f32[144,256]{1,0:T(8,128)S(1)} %add.49), channel_id=1, source_target_pairs={{0,32},{8,104},{16,48},{24,120},{32,0},{40,72},{48,16},{56,88},{64... | collective-permute-start | bytes 442376 | tf_op jit(solution)/shard_map/ppermute | solution.py:368
  69.3 7.1 %collective-permute-start.9 = (bf16[1,2,128,256]{3,2,1,0:T(8,128)(2,1)S(1)}, bf16[1,2,128,256]{3,2,1,0:T(8,128)(2,1)S(1)}, u32[]{:S(2)}, u32[]{:S(2)}) collective-permute-start(bf16[1,2,128,256]{3,2,1,0:T(8,128)(2,1)S(1)} %get-tuple-element.66), channel_id=1, source_target_pairs={{0,1},{2,3},{4,5},{6,7},{8,9},{10,11},{12,13},{14,15},{16,17},{18,... | collective-permute-start | bytes 393224 | tf_op jit(solution)/shard_map/ppermute | solution.py:260
  76.3 7.4 %collective-permute-start.10 = (f32[144,256]{1,0:T(8,128)S(1)}, f32[144,256]{1,0:T(8,128)S(1)}, u32[]{:S(2)}, u32[]{:S(2)}) collective-permute-start(f32[144,256]{1,0:T(8,128)S(1)} %add.50.part), channel_id=1, source_target_pairs={{0,112},{8,56},{16,96},{24,40},{32,80},{40,24},{48,64},{56,8},{64,... | collective-permute-start | bytes 442376 | tf_op jit(solution)/shard_map/ppermute | solution.py:368
  76.3 7.4 %collective-permute-start.11 = (bf16[1,2,128,256]{3,2,1,0:T(8,128)(2,1)S(1)}, bf16[1,2,128,256]{3,2,1,0:T(8,128)(2,1)S(1)}, u32[]{:S(2)}, u32[]{:S(2)}) collective-permute-start(bf16[1,2,128,256]{3,2,1,0:T(8,128)(2,1)S(1)} %get-tuple-element.65), channel_id=1, source_target_pairs={{1,2},{3,4},{5,6},{9,10},{11,12},{13,14},{17,18},{19,20},{21,22},{... | collective-permute-start | bytes 393224 | tf_op jit(solution)/shard_map/ppermute | solution.py:263
  83.8 1.0 copy-start.3
  84.8 17.3 %all-to-all-start.1 = ((bf16[16,144,256]{2,1,0:T(8,128)(2,1)}), bf16[16,144,256]{2,1,0:T(8,128)(2,1)S(1)}, u32[]{:S(2)}, u32[]{:S(2)}) async-start(bf16[16,144,256]{2,1,0:T(8,128)(2,1)} %copy-done.3), calls=%async_computation.1 | async-start | bytes 2359296 | tf_op jit(solution)/shard_map/all_to_all | solution.py:395
  89.0 6.0 %collective-permute-start.12 = (bf16[1,2,4,16,256]{4,3,2,1,0:T(8,128)(2,1)S(1)}, bf16[1,2,4,16,256]{4,3,2,1,0:T(8,128)(2,1)S(1)}, u32[]{:S(2)}, u32[]{:S(2)}) collective-permute-start(bf16[1,2,4,16,256]{4,3,2,1,0:T(8,128)(2,1)S(1)} %pad_maximum_fusion.2), channel_id=1, source_target_pairs={{0,8},{8,0},{1,9},{9,1},{2,10},{10,2},{3,11},{11,3},{4,12},{12,4},... | collective-permute-start | bytes 196616 | tf_op jit(solution)/shard_map/ppermute | solution.py:276
  94.1 4.1 %collective-permute-start.13 = (bf16[1,2,4,16,256]{4,3,2,1,0:T(8,128)(2,1)S(1)}, bf16[1,2,4,16,256]{4,3,2,1,0:T(8,128)(2,1)S(1)}, u32[]{:S(2)}, u32[]{:S(2)}) collective-permute-start(bf16[1,2,4,16,256]{4,3,2,1,0:T(8,128)(2,1)S(1)} %pad_maximum_fusion.3), channel_id=1, source_target_pairs={{8,16},{9,17},{10,18},{11,19},{12,20},{13,21},{14,22},{15,23},{24,... | collective-permute-start | bytes 196616 | tf_op jit(solution)/shard_map/ppermute | solution.py:275
  102.2 8.7 %collective-permute-start.14 = (bf16[2304,256]{1,0:T(8,128)(2,1)S(1)}, bf16[2304,256]{1,0:T(8,128)(2,1)S(1)}, u32[]{:S(2)}, u32[]{:S(2)}) collective-permute-start(bf16[2304,256]{1,0:T(8,128)(2,1)S(1)} %bitcast.37), channel_id=1, source_target_pairs={{0,8},{8,0},{1,9},{9,1},{2,10},{10,2},{3,11},{11,3},{4,12},{12,4},... | collective-permute-start | bytes 3538952 | tf_op jit(solution)/shard_map/ppermute | solution.py:397

commit v12 on v9

--- a/solution.py
+++ b/solution.py
@@ -356,7 +356,7 @@
         if reach < height:
             part = part + got
         reach *= 2
-        if reach == height:
+        if reach == height // 2:
             part, pair = lax.optimization_barrier((part, pair))
     got, next_pair = lax.optimization_barrier((got, next_pair))
     above, below = ordered(pair, next_pair)

time: 113 us -> 114 us (level)
  starting transfers between devices: 43.5 us -> 49.9 us
  waiting for transfers between devices: 29.3 us -> 23.8 us
    ppermute x3, starting transfers between devices: 11.3 us -> 14 us  [column_halos(): in_chip = lax.ppermute(edge((1 - core) * reach), 'core', [(0, 1), (1, 0)])]
    ppermute x2, waiting for transfers between devices: 6.29 us -> 4.19 us  [row_halos(): lax.ppermute(row(1 - odd), ALL, both_ways([(at(i, k), at(i, k + 1)) for i...]
    ppermute x3, starting transfers between devices: 3.49 us -> 4.98 us  [local(): got = lax.ppermute(part, ('z', 'core'), folded(height, cores, reach))]
    all_to_all x1, waiting for transfers between devices: 1.29 us -> 0.01 us  [local(): mine = lax.all_to_all(copies, PLANE, 0, 0, tiled=True).reshape(grads)]
  transfers between devices with their start and end apart: 16 -> 16, of which waited for: 12 -> 10; matrix products, arithmetic and copies ran while one was open for 0% -> 0% of each run, Pallas kernels for 6% -> 6%
where the time goes in v12:
time: 114 us
  starting transfers between devices  49.9 us (44%)
  waiting for transfers between devices  23.8 us (21%)
  blocking collectives  23.1 us (20%)
  Pallas kernels  12.7 us (11%)
  other arithmetic  1.95 us (2%)
  local copies, waits for them, and re-layouts  1.46 us (1%)
    all_to_all x1, blocking collectives, local(): spread = lax.all_to_all(total, PLANE, 0, 0, tiled=True)  23.1 us
    ppermute x3, starting transfers between devices, column_halos(): in_chip = lax.ppermute(edge((1 - core) * reach), 'core', [(0, 1), (1, 0)])  14 us
    ppermute x1, starting transfers between devices, local(): other = lax.ppermute(mine, 'core', swap)  7.1 us
    ppermute x2, starting transfers between devices, row_halos(): return (pair, lax.ppermute(row(odd), ALL, between + across))  6.09 us
    ppermute x3, waiting for transfers between devices, column_halos(): lax.ppermute(edge(core * reach), ALL, both_ways([(at(i + 1, k), at(i + 2,...  5.5 us
    ppermute x3, waiting for transfers between devices, local(): got = lax.ppermute(part, ('z', 'core'), folded(height, cores, reach))  5.37 us
    ppermute x2, waiting for transfers between devices, row_halos(): return (pair, lax.ppermute(row(odd), ALL, between + across))  5.04 us
    ppermute x3, starting transfers between devices, local(): got = lax.ppermute(part, ('z', 'core'), folded(height, cores, reach))  4.98 us
  transfers between devices with their start and end apart: 16, of which 10 were waited for; matrix products, arithmetic and copies ran while one was open for 0% of the time, Pallas kernels for 6%

profile of v12, /device:TPU:1, one launch (start us, length us, event | category | flops | bytes accessed | tf_op | source)
XLA Modules:
  0.0 113.9 jit_solution(6453563874542391928)
XLA Ops:
  0.6 0.0 copy-start.2
  0.6 0.0 copy-start.3
  0.7 1.3 %fusion.1 = (bf16[2,2,128,256]{3,2,1,0:T(8,128)(2,1)S(1)}, bf16[2,2,128,256]{3,2,1,0:T(8,128)(2,1)S(1)}) fusion(s32[]{:T(128)S(6)} %select_n.53, bf16[1,2,2,128,256]{4,3,2,1,0:T(8,128)(2,1)} %bitcast.41, bf16[1,2,2,128,256]{4,3,2,1,0:T(8,128)(2,1)} %bitcast.39, s32[]{:T(128)S(6)} %select_n.52), kind=kLoop, calls=%fused_computation.11 | loop fusion | flops 262144 | bytes 1048584 | tf_op jit(solution)/shard_map/jit(dynamic_index_in_dim)/squeeze | solution.py:253
  2.0 4.0 %collective-permute-start.3 = (bf16[2,2,128,256]{3,2,1,0:T(8,128)(2,1)S(1)}, bf16[2,2,128,256]{3,2,1,0:T(8,128)(2,1)S(1)}, u32[]{:S(2)}, u32[]{:S(2)}) collective-permute-start(bf16[2,2,128,256]{3,2,1,0:T(8,128)(2,1)S(1)} %get-tuple-element.55), channel_id=1, source_target_pairs={{1,2},{3,4},{5,6},{9,10},{11,12},{13,14},{17,18},{19,20},{21,22},{... | collective-permute-start | bytes 786440 | tf_op jit(solution)/shard_map/ppermute | solution.py:257
  6.0 2.7 %collective-permute-start.2 = (bf16[2,2,128,256]{3,2,1,0:T(8,128)(2,1)S(1)}, bf16[2,2,128,256]{3,2,1,0:T(8,128)(2,1)S(1)}, u32[]{:S(2)}, u32[]{:S(2)}) collective-permute-start(bf16[2,2,128,256]{3,2,1,0:T(8,128)(2,1)S(1)} %get-tuple-element.56), channel_id=1, source_target_pairs={{0,1},{2,3},{4,5},{6,7},{8,9},{10,11},{12,13},{14,15},{16,17},{18,... | collective-permute-start | bytes 786440 | tf_op jit(solution)/shard_map/ppermute | solution.py:254
  8.7 0.0 copy-done.2
  8.7 2.8 %collective-permute-start.1 = (bf16[2,2,2,16,256]{4,3,2,1,0:T(8,128)(2,1)S(1)}, bf16[2,2,2,16,256]{4,3,2,1,0:T(8,128)(2,1)S(1)}, u32[]{:S(2)}, u32[]{:S(2)}) collective-permute-start(bf16[2,2,2,16,256]{4,3,2,1,0:T(8,128)(2,1)S(1)} %get-tuple-element.57), channel_id=1, source_target_pairs={{8,16},{9,17},{10,18},{11,19},{12,20},{13,21},{14,22},{15,23},{24,... | collective-permute-start | bytes 196616 | tf_op jit(solution)/shard_map/ppermute | solution.py:269
  11.5 4.2 %collective-permute-start = (bf16[2,2,2,16,256]{4,3,2,1,0:T(8,128)(2,1)S(1)}, bf16[2,2,2,16,256]{4,3,2,1,0:T(8,128)(2,1)S(1)}, u32[]{:S(2)}, u32[]{:S(2)}) collective-permute-start(bf16[2,2,2,16,256]{4,3,2,1,0:T(8,128)(2,1)S(1)} %get-tuple-element.58), channel_id=1, source_target_pairs={{0,8},{8,0},{1,9},{9,1},{2,10},{10,2},{3,11},{11,3},{4,12},{12,4},... | collective-permute-start | bytes 196616 | tf_op jit(solution)/shard_map/ppermute | solution.py:270
  15.8 0.1 copy.11.strides
  15.9 0.1 pad_add_fusion.where.refs_0_
  15.9 0.0 collective-permute-done.1.next_chip
  15.9 0.7 collective-permute-done.in_chip
  16.7 1.3 %copy-done.1 = bf16[3,3,256,256]{3,2,1,0:T(8,128)(2,1)S(1)} copy-done((bf16[3,3,256,256]{3,2,1,0:T(8,128)(2,1)S(1)}, bf16[3,3,256,256]{3,2,1,0:T(8,128)(2,1)}, u32[]{:S(2)}) %copy-start.1) | copy-done | bytes 1179672
  18.0 2.0 %early.1 = (bf16[12,256,256]{2,1,0:T(8,128)(2,1)S(1)}, bf16[12,256,256]{2,1,0:T(8,128)(2,1)S(1)}, f32[512,256]{1,0:T(8,128)S(1)}, f32[512,256]{1,0:T(8,128)S(1)}) custom-call(s32[3]{0:T(128)S(1)} %pad_add_fusion.where.refs_0_, s32[2,16,3]{2,1,0:T(8,128)S(1)} %copy.11.strides, bf16[2,2,128,256]{3,2,1,0:T(8,128)(2,1)S(1)} %copy-done.3, ...), custom_call_target="tpu_custom_call" | custom-call | tf_op jit(solution)/shard_map/early/pallas_call | solution.py:311
  19.9 0.0 collective-permute-done.3.next_pair
  19.9 2.7 %collective-permute-done.2.pair = bf16[2,2,128,256]{3,2,1,0:T(8,128)(2,1)S(1)} collective-permute-done((bf16[2,2,128,256]{3,2,1,0:T(8,128)(2,1)S(1)}, bf16[2,2,128,256]{3,2,1,0:T(8,128)(2,1)S(1)}, u32[]{:S(2)}, u32[]{:S(2)}) %collective-permute-start.2) | collective-permute-done | bytes 262176 | tf_op jit(solution)/shard_map/ppermute | solution.py:254
  22.8 1.8 %collective-permute-start.4 = (bf16[2,2,2,16,256]{4,3,2,1,0:T(8,128)(2,1)S(1)}, bf16[2,2,2,16,256]{4,3,2,1,0:T(8,128)(2,1)S(1)}, u32[]{:S(2)}, u32[]{:S(2)}) collective-permute-start(bf16[2,2,2,16,256]{4,3,2,1,0:T(8,128)(2,1)S(1)} %pad_maximum_fusion), channel_id=1, source_target_pairs={{0,8},{8,0},{1,9},{9,1},{2,10},{10,2},{3,11},{11,3},{4,12},{12,4},... | collective-permute-start | bytes 196616 | tf_op jit(solution)/shard_map/ppermute | solution.py:270
  24.6 0.9 collective-permute-start.5
  25.5 0.0 collective-permute-done.4.in_chip
  25.5 2.8 %collective-permute-done.5.next_chip = bf16[2,2,2,16,256]{4,3,2,1,0:T(8,128)(2,1)S(1)} collective-permute-done((bf16[2,2,2,16,256]{4,3,2,1,0:T(8,128)(2,1)S(1)}, bf16[2,2,2,16,256]{4,3,2,1,0:T(8,128)(2,1)S(1)}, u32[]{:S(2)}, u32[]{:S(2)}) %collective-permute-start.5) | collective-permute-done | bytes 65568 | tf_op jit(solution)/shard_map/ppermute | solution.py:269
  28.4 3.3 %main.1 = (f32[2304,256]{1,0:T(8,128)S(1)}, bf16[2304,256]{1,0:T(8,128)(2,1)S(1)}, bf16[2,2,128,256]{3,2,1,0:T(8,128)(2,1)S(1)}) custom-call(s32[3]{0:T(128)S(1)} %pad_add_fusion.where.refs_0_, s32[2,16,3]{2,1,0:T(8,128)S(1)} %copy.11.strides, bf16[12,256,256]{2,1,0:T(8,128)(2,1)S(1)} %get-tuple-element.32.own_f, ...), custom_call_target="tpu_custom_call" | custom-call | tf_op jit(solution)/shard_map/main/pallas_call | solution.py:324
  31.7 4.2 %collective-permute-start.6 = (bf16[2304,256]{1,0:T(8,128)(2,1)S(1)}, bf16[2304,256]{1,0:T(8,128)(2,1)S(1)}, u32[]{:S(2)}, u32[]{:S(2)}) collective-permute-start(bf16[2304,256]{1,0:T(8,128)(2,1)S(1)} %get-tuple-element.39), channel_id=1, source_target_pairs={{0,8},{8,0},{1,9},{9,1},{2,10},{10,2},{3,11},{11,3},{4,12},{12,4},... | collective-permute-start | bytes 3538952 | tf_op jit(solution)/shard_map/ppermute | solution.py:344
  35.9 2.5 %collective-permute-done.6 = bf16[2304,256]{1,0:T(8,128)(2,1)S(1)} collective-permute-done((bf16[2304,256]{1,0:T(8,128)(2,1)S(1)}, bf16[2304,256]{1,0:T(8,128)(2,1)S(1)}, u32[]{:S(2)}, u32[]{:S(2)}) %collective-permute-start.6) | collective-permute-done | bytes 1179680 | tf_op jit(solution)/shard_map/ppermute | solution.py:344
  38.3 0.3 add_convert_fusion
  38.7 23.1 %all_to_all.10 = bf16[16,144,256]{2,1,0:T(8,128)(2,1)S(1)} all-to-all(bf16[16,144,256]{2,1,0:T(8,128)(2,1)S(1)} %bitcast.43), channel_id=1, replica_groups=mesh['yl'=2,'z'=8,'core'=2,'x'=4,'yh'=2] {'x','yh','yl'}, dimensions={0} | all-to-all | bytes 2359296 | tf_op jit(solution)/shard_map/all_to_all | solution.py:347
  61.7 0.2 convert_reduce_fusion
  61.9 0.1 collective-permute-start.7
  62.0 1.4 %collective-permute-start.8 = (bf16[1,2,128,256]{3,2,1,0:T(8,128)(2,1)S(1)}, bf16[1,2,128,256]{3,2,1,0:T(8,128)(2,1)S(1)}, u32[]{:S(2)}, u32[]{:S(2)}) collective-permute-start(bf16[1,2,128,256]{3,2,1,0:T(8,128)(2,1)S(1)} %get-tuple-element.64), channel_id=1, source_target_pairs={{0,1},{2,3},{4,5},{6,7},{8,9},{10,11},{12,13},{14,15},{16,17},{18,... | collective-permute-start | bytes 393224 | tf_op jit(solution)/shard_map/ppermute | solution.py:254
  63.5 2.5 %collective-permute-done.7 = f32[144,256]{1,0:T(8,128)S(1)} collective-permute-done((f32[144,256]{1,0:T(8,128)S(1)}, f32[144,256]{1,0:T(8,128)S(1)}, u32[]{:S(2)}, u32[]{:S(2)}) %collective-permute-start.7) | collective-permute-done | bytes 147488 | tf_op jit(solution)/shard_map/ppermute | solution.py:355
  66.0 1.4 %collective-permute-done.8.pair = bf16[1,2,128,256]{3,2,1,0:T(8,128)(2,1)S(1)} collective-permute-done((bf16[1,2,128,256]{3,2,1,0:T(8,128)(2,1)S(1)}, bf16[1,2,128,256]{3,2,1,0:T(8,128)(2,1)S(1)}, u32[]{:S(2)}, u32[]{:S(2)}) %collective-permute-start.8) | collective-permute-done | bytes 131104 | tf_op jit(solution)/shard_map/ppermute | solution.py:254
  67.4 4.7 %collective-permute-start.9 = (f32[144,256]{1,0:T(8,128)S(1)}, f32[144,256]{1,0:T(8,128)S(1)}, u32[]{:S(2)}, u32[]{:S(2)}) collective-permute-start(f32[144,256]{1,0:T(8,128)S(1)} %add.49), channel_id=1, source_target_pairs={{0,32},{8,104},{16,48},{24,120},{32,0},{40,72},{48,16},{56,88},{64... | collective-permute-start | bytes 442376 | tf_op jit(solution)/shard_map/ppermute | solution.py:355
  72.2 2.9 %collective-permute-done.9 = f32[144,256]{1,0:T(8,128)S(1)} collective-permute-done((f32[144,256]{1,0:T(8,128)S(1)}, f32[144,256]{1,0:T(8,128)S(1)}, u32[]{:S(2)}, u32[]{:S(2)}) %collective-permute-start.9) | collective-permute-done | bytes 147488 | tf_op jit(solution)/shard_map/ppermute | solution.py:355
  75.1 0.1 collective-permute-start.10
  75.2 2.1 %collective-permute-start.11 = (bf16[1,2,128,256]{3,2,1,0:T(8,128)(2,1)S(1)}, bf16[1,2,128,256]{3,2,1,0:T(8,128)(2,1)S(1)}, u32[]{:S(2)}, u32[]{:S(2)}) collective-permute-start(bf16[1,2,128,256]{3,2,1,0:T(8,128)(2,1)S(1)} %get-tuple-element.63), channel_id=1, source_target_pairs={{1,2},{3,4},{5,6},{9,10},{11,12},{13,14},{17,18},{19,20},{21,22},{... | collective-permute-start | bytes 393224 | tf_op jit(solution)/shard_map/ppermute | solution.py:257
  77.3 5.0 %collective-permute-done.11.next_pair = bf16[1,2,128,256]{3,2,1,0:T(8,128)(2,1)S(1)} collective-permute-done((bf16[1,2,128,256]{3,2,1,0:T(8,128)(2,1)S(1)}, bf16[1,2,128,256]{3,2,1,0:T(8,128)(2,1)S(1)}, u32[]{:S(2)}, u32[]{:S(2)}) %collective-permute-start.11) | collective-permute-done | bytes 131104 | tf_op jit(solution)/shard_map/ppermute | solution.py:257
  82.3 0.0 collective-permute-done.10.got
  82.3 1.1 copies.1
  83.4 4.5 %all-to-all-start.1 = ((bf16[16,144,256]{2,1,0:T(8,128)(2,1)}), bf16[16,144,256]{2,1,0:T(8,128)(2,1)S(1)}, u32[]{:S(2)}, u32[]{:S(2)}) async-start(bf16[16,144,256]{2,1,0:T(8,128)(2,1)} %copies.1), calls=%async_computation.1 | async-start | bytes 2359296 | tf_op jit(solution)/shard_map/all_to_all | solution.py:382
  88.1 7.9 %collective-permute-start.12 = (bf16[1,2,4,16,256]{4,3,2,1,0:T(8,128)(2,1)S(1)}, bf16[1,2,4,16,256]{4,3,2,1,0:T(8,128)(2,1)S(1)}, u32[]{:S(2)}, u32[]{:S(2)}) collective-permute-start(bf16[1,2,4,16,256]{4,3,2,1,0:T(8,128)(2,1)S(1)} %pad_maximum_fusion.2), channel_id=1, source_target_pairs={{0,8},{8,0},{1,9},{9,1},{2,10},{10,2},{3,11},{11,3},{4,12},{12,4},... | collective-permute-start | bytes 196616 | tf_op jit(solution)/shard_map/ppermute | solution.py:270
  96.0 1.1 collective-permute-start.13
  97.2 0.0 collective-permute-done.12.in_chip
  97.2 2.6 %collective-permute-done.13.next_chip = bf16[1,2,4,16,256]{4,3,2,1,0:T(8,128)(2,1)S(1)} collective-permute-done((bf16[1,2,4,16,256]{4,3,2,1,0:T(8,128)(2,1)S(1)}, bf16[1,2,4,16,256]{4,3,2,1,0:T(8,128)(2,1)S(1)}, u32[]{:S(2)}, u32[]{:S(2)}) %collective-permute-start.13) | collective-permute-done | bytes 65568 | tf_op jit(solution)/shard_map/ppermute | solution.py:269
  99.8 2.4 %back.1 = bf16[2,2,128,256]{3,2,1,0:T(8,128)(2,1)} custom-call(s32[3]{0:T(128)S(1)} %pad_add_fusion.where.refs_0_, s32[2,16,3]{2,1,0:T(8,128)S(1)} %copy.11.strides, bf16[2,2,128,256]{3,2,1,0:T(8,128)(2,1)S(1)} %copy-done.2, bf16[2,2,128,256]{3,2,1,0:T(8,128)(2,1)S(1)} %get-tuple-element.42.pre, bf16[1,2,128,256]{3,2,1,0:T(8,128)(2,1)S(1)} %collective-permute-done.8.pair, ...), custom_call_target="tpu_custom_call" | custom-call | tf_op jit(solution)/shard_map/back/pallas_call | solution.py:364
  102.2 0.0 all-to-all-done.1
  102.2 7.1 %collective-permute-start.14 = (bf16[2304,256]{1,0:T(8,128)(2,1)S(1)}, bf16[2304,256]{1,0:T(8,128)(2,1)S(1)}, u32[]{:S(2)}, u32[]{:S(2)}) collective-permute-start(bf16[2304,256]{1,0:T(8,128)(2,1)S(1)} %bitcast.37), channel_id=1, source_target_pairs={{0,8},{8,0},{1,9},{9,1},{2,10},{10,2},{3,11},{11,3},{4,12},{12,4},... | collective-permute-start | bytes 3538952 | tf_op jit(solution)/shard_map/ppermute | solution.py:384
  109.3 2.0 %own_part.1 = (f32[2304,256]{1,0:T(8,128)}, f32[2304,256]{1,0:T(8,128)}) custom-call(s32[3]{0:T(128)S(1)} %pad_add_fusion.where.refs_0_, bf16[2304,256]{1,0:T(8,128)(2,1)S(1)} %bitcast.38), custom_call_target="tpu_custom_call" | custom-call | tf_op jit(solution)/shard_map/own_part/pallas_call | solution.py:388
  111.3 0.4 collective-permute-done.14.refs_1_
  111.7 2.0 %other_part.1 = (f32[2304,256]{1,0:T(8,128)}, f32[2304,256]{1,0:T(8,128)}) custom-call(s32[3]{0:T(128)S(1)} %pad_add_fusion.where.refs_0_, bf16[2304,256]{1,0:T(8,128)(2,1)S(1)} %collective-permute-done.14.refs_1_, f32[2304,256]{1,0:T(8,128)} %get-tuple-element.49.refs_2_, ...), custom_call_target="tpu_custom_call", output_to_operand_aliasing={{0}: (2, {}), {1}: (3, {})} | custom-call | tf_op jit(solution)/shard_map/other_part/pallas_call | solution.py:397
  (20 shorter events, 0.2 us)
Async XLA Ops:
  0.6 8.1 %copy-start.2 = (bf16[2,2,128,256]{3,2,1,0:T(8,128)(2,1)S(1)}, bf16[2,2,128,256]{3,2,1,0:T(8,128)(2,1)}, u32[]{:S(2)}) copy-start(bf16[2,2,128,256]{3,2,1,0:T(8,128)(2,1)} %grad.3) | copy-start | bytes 786436
  0.6 8.0 %copy-start.3 = (bf16[2,2,128,256]{3,2,1,0:T(8,128)(2,1)S(1)}, bf16[2,2,128,256]{3,2,1,0:T(8,128)(2,1)}, u32[]{:S(2)}) copy-start(bf16[2,2,128,256]{3,2,1,0:T(8,128)(2,1)} %feat.1) | copy-start | bytes 786436
  0.7 15.1 %copy-start.4 = (s32[2,16,3]{1,0,2:T(2,128)S(1)}, s32[2,16,3]{1,0,2:T(2,128)}, u32[]{:S(2)}) copy-start(s32[2,16,3]{1,0,2:T(2,128)} %param.9) | copy-start | bytes 1156
  0.7 16.0 %copy-start = (bf16[3,3,256,256]{3,2,1,0:T(8,128)(2,1)S(1)}, bf16[3,3,256,256]{3,2,1,0:T(8,128)(2,1)}, u32[]{:S(2)}) copy-start(bf16[3,3,256,256]{3,2,1,0:T(8,128)(2,1)} %first_kernel.5) | copy-start | bytes 3538948
  2.0 18.0 %collective-permute-start.3 = (bf16[2,2,128,256]{3,2,1,0:T(8,128)(2,1)S(1)}, bf16[2,2,128,256]{3,2,1,0:T(8,128)(2,1)S(1)}, u32[]{:S(2)}, u32[]{:S(2)}) collective-permute-start(bf16[2,2,128,256]{3,2,1,0:T(8,128)(2,1)S(1)} %get-tuple-element.55), channel_id=1, source_target_pairs={{1,2},{3,4},{5,6},{9,10},{11,12},{13,14},{17,18},{19,20},{21,22},{... | collective-permute-start | bytes 786440 | tf_op jit(solution)/shard_map/ppermute | solution.py:257
  6.0 16.7 %collective-permute-start.2 = (bf16[2,2,128,256]{3,2,1,0:T(8,128)(2,1)S(1)}, bf16[2,2,128,256]{3,2,1,0:T(8,128)(2,1)S(1)}, u32[]{:S(2)}, u32[]{:S(2)}) collective-permute-start(bf16[2,2,128,256]{3,2,1,0:T(8,128)(2,1)S(1)} %get-tuple-element.56), channel_id=1, source_target_pairs={{0,1},{2,3},{4,5},{6,7},{8,9},{10,11},{12,13},{14,15},{16,17},{18,... | collective-permute-start | bytes 786440 | tf_op jit(solution)/shard_map/ppermute | solution.py:254
  8.7 7.2 %collective-permute-start.1 = (bf16[2,2,2,16,256]{4,3,2,1,0:T(8,128)(2,1)S(1)}, bf16[2,2,2,16,256]{4,3,2,1,0:T(8,128)(2,1)S(1)}, u32[]{:S(2)}, u32[]{:S(2)}) collective-permute-start(bf16[2,2,2,16,256]{4,3,2,1,0:T(8,128)(2,1)S(1)} %get-tuple-element.57), channel_id=1, source_target_pairs={{8,16},{9,17},{10,18},{11,19},{12,20},{13,21},{14,22},{15,23},{24,... | collective-permute-start | bytes 196616 | tf_op jit(solution)/shard_map/ppermute | solution.py:269
  11.5 5.1 %collective-permute-start = (bf16[2,2,2,16,256]{4,3,2,1,0:T(8,128)(2,1)S(1)}, bf16[2,2,2,16,256]{4,3,2,1,0:T(8,128)(2,1)S(1)}, u32[]{:S(2)}, u32[]{:S(2)}) collective-permute-start(bf16[2,2,2,16,256]{4,3,2,1,0:T(8,128)(2,1)S(1)} %get-tuple-element.58), channel_id=1, source_target_pairs={{0,8},{8,0},{1,9},{9,1},{2,10},{10,2},{3,11},{11,3},{4,12},{12,4},... | collective-permute-start | bytes 196616 | tf_op jit(solution)/shard_map/ppermute | solution.py:270
  16.7 1.3 %copy-start.1 = (bf16[3,3,256,256]{3,2,1,0:T(8,128)(2,1)S(1)}, bf16[3,3,256,256]{3,2,1,0:T(8,128)(2,1)}, u32[]{:S(2)}) copy-start(bf16[3,3,256,256]{3,2,1,0:T(8,128)(2,1)} %second_kernel.3) | copy-start | bytes 3538948
  22.8 2.8 %collective-permute-start.4 = (bf16[2,2,2,16,256]{4,3,2,1,0:T(8,128)(2,1)S(1)}, bf16[2,2,2,16,256]{4,3,2,1,0:T(8,128)(2,1)S(1)}, u32[]{:S(2)}, u32[]{:S(2)}) collective-permute-start(bf16[2,2,2,16,256]{4,3,2,1,0:T(8,128)(2,1)S(1)} %pad_maximum_fusion), channel_id=1, source_target_pairs={{0,8},{8,0},{1,9},{9,1},{2,10},{10,2},{3,11},{11,3},{4,12},{12,4},... | collective-permute-start | bytes 196616 | tf_op jit(solution)/shard_map/ppermute | solution.py:270
  24.6 3.8 %collective-permute-start.5 = (bf16[2,2,2,16,256]{4,3,2,1,0:T(8,128)(2,1)S(1)}, bf16[2,2,2,16,256]{4,3,2,1,0:T(8,128)(2,1)S(1)}, u32[]{:S(2)}, u32[]{:S(2)}) collective-permute-start(bf16[2,2,2,16,256]{4,3,2,1,0:T(8,128)(2,1)S(1)} %pad_maximum_fusion.1), channel_id=1, source_target_pairs={{8,16},{9,17},{10,18},{11,19},{12,20},{13,21},{14,22},{15,23},{24,... | collective-permute-start | bytes 196616 | tf_op jit(solution)/shard_map/ppermute | solution.py:269
  31.7 6.7 %collective-permute-start.6 = (bf16[2304,256]{1,0:T(8,128)(2,1)S(1)}, bf16[2304,256]{1,0:T(8,128)(2,1)S(1)}, u32[]{:S(2)}, u32[]{:S(2)}) collective-permute-start(bf16[2304,256]{1,0:T(8,128)(2,1)S(1)} %get-tuple-element.39), channel_id=1, source_target_pairs={{0,8},{8,0},{1,9},{9,1},{2,10},{10,2},{3,11},{11,3},{4,12},{12,4},... | collective-permute-start | bytes 3538952 | tf_op jit(solution)/shard_map/ppermute | solution.py:344
  61.9 4.1 %collective-permute-start.7 = (f32[144,256]{1,0:T(8,128)S(1)}, f32[144,256]{1,0:T(8,128)S(1)}, u32[]{:S(2)}, u32[]{:S(2)}) collective-permute-start(f32[144,256]{1,0:T(8,128)S(1)} %convert_reduce_fusion), channel_id=1, source_target_pairs={{0,16},{8,24},{16,0},{24,8},{32,48},{40,56},{48,32},{56,40},{64,80... | collective-permute-start | bytes 442376 | tf_op jit(solution)/shard_map/ppermute | solution.py:355
  62.0 5.4 %collective-permute-start.8 = (bf16[1,2,128,256]{3,2,1,0:T(8,128)(2,1)S(1)}, bf16[1,2,128,256]{3,2,1,0:T(8,128)(2,1)S(1)}, u32[]{:S(2)}, u32[]{:S(2)}) collective-permute-start(bf16[1,2,128,256]{3,2,1,0:T(8,128)(2,1)S(1)} %get-tuple-element.64), channel_id=1, source_target_pairs={{0,1},{2,3},{4,5},{6,7},{8,9},{10,11},{12,13},{14,15},{16,17},{18,... | collective-permute-start | bytes 393224 | tf_op jit(solution)/shard_map/ppermute | solution.py:254
  67.4 7.6 %collective-permute-start.9 = (f32[144,256]{1,0:T(8,128)S(1)}, f32[144,256]{1,0:T(8,128)S(1)}, u32[]{:S(2)}, u32[]{:S(2)}) collective-permute-start(f32[144,256]{1,0:T(8,128)S(1)} %add.49), channel_id=1, source_target_pairs={{0,32},{8,104},{16,48},{24,120},{32,0},{40,72},{48,16},{56,88},{64... | collective-permute-start | bytes 442376 | tf_op jit(solution)/shard_map/ppermute | solution.py:355
  75.1 7.3 %collective-permute-start.10 = (f32[144,256]{1,0:T(8,128)S(1)}, f32[144,256]{1,0:T(8,128)S(1)}, u32[]{:S(2)}, u32[]{:S(2)}) collective-permute-start(f32[144,256]{1,0:T(8,128)S(1)} %add.50.part), channel_id=1, source_target_pairs={{0,112},{8,56},{16,96},{24,40},{32,80},{40,24},{48,64},{56,8},{64,... | collective-permute-start | bytes 442376 | tf_op jit(solution)/shard_map/ppermute | solution.py:355
  75.2 7.1 %collective-permute-start.11 = (bf16[1,2,128,256]{3,2,1,0:T(8,128)(2,1)S(1)}, bf16[1,2,128,256]{3,2,1,0:T(8,128)(2,1)S(1)}, u32[]{:S(2)}, u32[]{:S(2)}) collective-permute-start(bf16[1,2,128,256]{3,2,1,0:T(8,128)(2,1)S(1)} %get-tuple-element.63), channel_id=1, source_target_pairs={{1,2},{3,4},{5,6},{9,10},{11,12},{13,14},{17,18},{19,20},{21,22},{... | collective-permute-start | bytes 393224 | tf_op jit(solution)/shard_map/ppermute | solution.py:257
  83.4 18.7 %all-to-all-start.1 = ((bf16[16,144,256]{2,1,0:T(8,128)(2,1)}), bf16[16,144,256]{2,1,0:T(8,128)(2,1)S(1)}, u32[]{:S(2)}, u32[]{:S(2)}) async-start(bf16[16,144,256]{2,1,0:T(8,128)(2,1)} %copies.1), calls=%async_computation.1 | async-start | bytes 2359296 | tf_op jit(solution)/shard_map/all_to_all | solution.py:382
  88.1 9.1 %collective-permute-start.12 = (bf16[1,2,4,16,256]{4,3,2,1,0:T(8,128)(2,1)S(1)}, bf16[1,2,4,16,256]{4,3,2,1,0:T(8,128)(2,1)S(1)}, u32[]{:S(2)}, u32[]{:S(2)}) collective-permute-start(bf16[1,2,4,16,256]{4,3,2,1,0:T(8,128)(2,1)S(1)} %pad_maximum_fusion.2), channel_id=1, source_target_pairs={{0,8},{8,0},{1,9},{9,1},{2,10},{10,2},{3,11},{11,3},{4,12},{12,4},... | collective-permute-start | bytes 196616 | tf_op jit(solution)/shard_map/ppermute | solution.py:270
  96.0 3.8 %collective-permute-start.13 = (bf16[1,2,4,16,256]{4,3,2,1,0:T(8,128)(2,1)S(1)}, bf16[1,2,4,16,256]{4,3,2,1,0:T(8,128)(2,1)S(1)}, u32[]{:S(2)}, u32[]{:S(2)}) collective-permute-start(bf16[1,2,4,16,256]{4,3,2,1,0:T(8,128)(2,1)S(1)} %pad_maximum_fusion.3), channel_id=1, source_target_pairs={{8,16},{9,17},{10,18},{11,19},{12,20},{13,21},{14,22},{15,23},{24,... | collective-permute-start | bytes 196616 | tf_op jit(solution)/shard_map/ppermute | solution.py:269
  102.2 9.6 %collective-permute-start.14 = (bf16[2304,256]{1,0:T(8,128)(2,1)S(1)}, bf16[2304,256]{1,0:T(8,128)(2,1)S(1)}, u32[]{:S(2)}, u32[]{:S(2)}) collective-permute-start(bf16[2304,256]{1,0:T(8,128)(2,1)S(1)} %bitcast.37), channel_id=1, source_target_pairs={{0,8},{8,0},{1,9},{9,1},{2,10},{10,2},{3,11},{11,3},{4,12},{12,4},... | collective-permute-start | bytes 3538952 | tf_op jit(solution)/shard_map/ppermute | solution.py:384
